TPU v7x, 32 devices: a whole 2x2x4 slice. The times are simulated.
32 devices in a mesh: dp: 8 (over y, x, core), mp: 4 (over z).
Axes of the slice: x: 2, y: 2, z: 4, core: 2. Of those that a mesh axis runs over, the one named last changes fastest.
Arguments:
- users_list: int32 [32, 256], P(('dp', 'mp')), may hold values from 0 to 1023, as said below
- items_list: int32 [32, 256], P(('dp', 'mp')), may hold values from 0 to 1023, as said below
- days_list: int32 [32, 32], P(('dp', 'mp')), may hold values from 0 to 255, as said below
- status: int32 [32, 32, 256, 256], P(('dp', 'mp')), may hold values from 0 to 2
- user_factor: float32 [1024, 256], P('dp', 'mp'), may hold values from -2.4 to 2.4
- user_first: float32 [1024, 256], P('dp', 'mp'), may hold values from -6 to 6
- user_second: float32 [1024, 256], P('dp', 'mp'), may hold values from 0.05 to 2
- item_factor: float32 [1024, 256], P('dp', 'mp'), may hold values from -2.4 to 2.4
- item_first: float32 [1024, 256], P('dp', 'mp'), may hold values from -6 to 6
- item_second: float32 [1024, 256], P('dp', 'mp'), may hold values from 0.05 to 2
- day_factor: float32 [256, 256], P('dp', 'mp'), may hold values from -2.4 to 2.4
- day_first: float32 [256, 256], P('dp', 'mp'), may hold values from -6 to 6
- day_second: float32 [256, 256], P('dp', 'mp'), may hold values from 1 to 3000
Outputs:
- new_user_factor: float32 [1024, 256], P('dp', 'mp')
- new_user_first: float32 [1024, 256], P('dp', 'mp')
- new_user_second: float32 [1024, 256], P('dp', 'mp')
- new_item_factor: float32 [1024, 256], P('dp', 'mp')
- new_item_first: float32 [1024, 256], P('dp', 'mp')
- new_item_second: float32 [1024, 256], P('dp', 'mp')
- new_day_factor: float32 [256, 256], P('dp', 'mp')
- new_day_first: float32 [256, 256], P('dp', 'mp')
- new_day_second: float32 [256, 256], P('dp', 'mp')
Inputs may be any that keep to these rules, and one draw needn't show every extreme that they name: `users_list`: the 256 users of a block are distinct; at most 48 of them lie in the rows n * 128 to (n + 1) * 128 - 1 of one index n of dp, and one such index holds exactly 48 users of every block. `items_list`: the 256 items of a block are distinct; at most 48 of them lie in the rows n * 128 to (n + 1) * 128 - 1 of one index n of dp, and one such index holds exactly 48 items of every block. `days_list`: the 32 days of a block are distinct; at most 8 of them lie in the rows n * 32 to (n + 1) * 32 - 1 of one index n of dp, and one such index holds exactly 8 days of every block.
All inputs are finite; a program needn't handle non-finite values.
Results may differ from a plain program's by a relative error of at most 0.0044.
Values may be sent and summed in bfloat16 or wider, within the bound.
No kernel may reach another device: no remote copies, remote signals or barrier semaphores. Data moves between devices by JAX's collectives and lax.ppermute only.
A program may use at most 64 MiB of HBM per device.

v0:
```python
import jax
import jax.numpy as jnp
from jax import lax
from jax.sharding import PartitionSpec as P

beta_one = 0.9
beta_two = 0.99
bias_one = 1.0 - 0.9**10
bias_two = 1.0 - 0.99**10
learn_rate = 0.01
epsilon = 1e-08
loss_scale = 0.0625
zero_weight = 2.0


def block_grads(user_row_values, item_row_values, day_row_values, block_status):
    day_count = day_row_values.shape[0]
    user_count = user_row_values.shape[0]
    scaled = day_row_values[:, None, :] * user_row_values[None, :, :]
    scaled_flat = scaled.reshape(day_count * user_count, -1)
    logits = jnp.einsum(
        "nr,ir->ni", scaled_flat, item_row_values, preferred_element_type=jnp.float32
    )
    chance = jax.nn.sigmoid(logits)
    status_flat = block_status.reshape(day_count * user_count, -1)
    residual = loss_scale * (
        jnp.where(status_flat == 1, chance - 1.0, 0.0)
        + jnp.where(status_flat == 2, zero_weight * chance, 0.0)
    )
    residual = residual.astype(jnp.bfloat16)
    projected = jnp.dot(residual, item_row_values, preferred_element_type=jnp.float32).reshape(
        day_count, user_count, -1
    )
    user_gradient = jnp.sum(projected * day_row_values[:, None, :].astype(jnp.float32), axis=0)
    day_gradient = jnp.sum(projected * user_row_values[None, :, :].astype(jnp.float32), axis=1)
    item_gradient = jnp.einsum(
        "ni,nr->ir", residual, scaled_flat, preferred_element_type=jnp.float32
    )
    return (user_gradient, item_gradient, day_gradient)


def adam_update(factor, first, second, gradient):
    first_new = beta_one * first + (1.0 - beta_one) * gradient
    second_new = beta_two * second + (1.0 - beta_two) * gradient * gradient
    change = learn_rate * (first_new / bias_one) / (jnp.sqrt(second_new / bias_two) + epsilon)
    return (factor - change, first_new, second_new)


def slot_layout(wanted_row_list, locally_kept_lines, line_bundles):
    holder_index = wanted_row_list // locally_kept_lines
    local_row = wanted_row_list % locally_kept_lines
    onehot = (
        holder_index[:, :, None] == jnp.arange(line_bundles, dtype=jnp.int32)[None, None, :]
    ).astype(jnp.int32)
    before = jnp.cumsum(onehot, axis=1) - onehot
    slot_position_index = jnp.sum(before * onehot, axis=2)
    return (holder_index, local_row, slot_position_index)


def build_needed_catalogs(desired_line_catalogs, locally_kept_counts, place_limits, line_bundles):
    buffers = []
    for wanted_row_list, locally_kept_lines, place_limit in zip(
        desired_line_catalogs, locally_kept_counts, place_limits
    ):
        holder_index, local_row, slot_position_index = slot_layout(
            wanted_row_list, locally_kept_lines, line_bundles
        )
        blocks = jnp.broadcast_to(
            jnp.arange(wanted_row_list.shape[0], dtype=jnp.int32)[:, None], wanted_row_list.shape
        )
        blank_slots = jnp.full((line_bundles, wanted_row_list.shape[0], place_limit), -1, jnp.int32)
        buffers.append(blank_slots.at[holder_index, blocks, slot_position_index].set(local_row))
    return jnp.concatenate(buffers, axis=2)


def collect_needed_lines(desired_line_catalogs, locally_kept_counts, place_limits, line_bundles):
    return lax.all_to_all(
        build_needed_catalogs(
            desired_line_catalogs, locally_kept_counts, place_limits, line_bundles
        ),
        "dp",
        split_axis=0,
        concat_axis=0,
        tiled=True,
    )


def serve_needed_lines(needed_line_numbers, loading_tables, place_limits):
    pieces = []
    offset = 0
    for loading_table, place_limit in zip(loading_tables, place_limits):
        wanted = needed_line_numbers[:, :, offset : offset + place_limit]
        taken_rows = jnp.take(
            loading_table, jnp.clip(wanted, 0, loading_table.shape[0] - 1), axis=0
        )
        pieces.append(
            jnp.where((wanted >= 0)[..., None], taken_rows, jnp.zeros((), loading_table.dtype))
        )
        offset = offset + place_limit
    return jnp.concatenate(pieces, axis=2)


def slot_targets(place_layout, place_limit):
    holder_index, slot_position_index = place_layout
    return holder_index[0] * place_limit + slot_position_index[0]


def pick_lines(arrived_lines, place_layouts, place_limits, line_bundles):
    picked = []
    offset = 0
    for place_layout, place_limit in zip(place_layouts, place_limits):
        flat_slots = arrived_lines[:, 0, offset : offset + place_limit, :].reshape(
            line_bundles * place_limit, -1
        )
        target = slot_targets(place_layout, place_limit)
        selector = (
            target[:, None] == jnp.arange(line_bundles * place_limit, dtype=jnp.int32)[None, :]
        ).astype(jnp.bfloat16)
        picked.append(
            jnp.dot(selector, flat_slots, preferred_element_type=jnp.float32).astype(jnp.bfloat16)
        )
        offset = offset + place_limit
    return picked


def derivative_place_numbers(slope_numbers, place_layouts, place_limits, line_bundles):
    pieces = []
    for row_gradient, place_layout, place_limit in zip(slope_numbers, place_layouts, place_limits):
        target = slot_targets(place_layout, place_limit)
        placer = (
            jnp.arange(line_bundles * place_limit, dtype=jnp.int32)[:, None] == target[None, :]
        ).astype(jnp.float32)
        placed = jnp.dot(
            placer,
            row_gradient,
            precision=lax.Precision.HIGHEST,
            preferred_element_type=jnp.float32,
        )
        pieces.append(placed.reshape(line_bundles, place_limit, -1))
    return jnp.concatenate(pieces, axis=1)[:, None, :, :]


def keeper_slope_totals(arrived_lines, needed_line_numbers, locally_kept_counts, place_limits):
    totals = []
    offset = 0
    for locally_kept_lines, place_limit in zip(locally_kept_counts, place_limits):
        wanted = needed_line_numbers[:, :, offset : offset + place_limit].reshape(-1)
        values = arrived_lines[:, :, offset : offset + place_limit, :].reshape(wanted.shape[0], -1)
        onehot = (
            jnp.arange(locally_kept_lines, dtype=jnp.int32)[:, None] == wanted[None, :]
        ).astype(jnp.float32)
        totals.append(
            jnp.dot(
                onehot, values, precision=lax.Precision.HIGHEST, preferred_element_type=jnp.float32
            )
        )
        offset = offset + place_limit
    return totals


def local(
    users_list,
    items_list,
    days_list,
    status,
    user_factor,
    user_first,
    user_second,
    item_factor,
    item_first,
    item_second,
    day_factor,
    day_first,
    day_second,
):
    line_bundles = lax.axis_size("dp")
    place_limits = (
        max(2, 3 * users_list.shape[1] // (2 * line_bundles)),
        max(2, 3 * items_list.shape[1] // (2 * line_bundles)),
        max(2, 2 * days_list.shape[1] // line_bundles),
    )
    locally_kept_counts = (user_factor.shape[0], item_factor.shape[0], day_factor.shape[0])
    loading_tables = (
        user_factor.astype(jnp.bfloat16),
        item_factor.astype(jnp.bfloat16),
        day_factor.astype(jnp.bfloat16),
    )
    own_lists = (users_list, items_list, days_list)
    place_layouts = []
    for wanted_row_list, locally_kept_lines in zip(own_lists, locally_kept_counts):
        holder_index, local_row, slot_position_index = slot_layout(
            wanted_row_list, locally_kept_lines, line_bundles
        )
        place_layouts.append((holder_index, slot_position_index))
    bundled_line_catalogs = (
        lax.all_gather(users_list, "mp", axis=0, tiled=True),
        lax.all_gather(items_list, "mp", axis=0, tiled=True),
        lax.all_gather(days_list, "mp", axis=0, tiled=True),
    )
    needed_line_numbers = collect_needed_lines(
        bundled_line_catalogs, locally_kept_counts, place_limits, line_bundles
    )
    served_lines = serve_needed_lines(needed_line_numbers, loading_tables, place_limits)
    arrived_lines = lax.all_to_all(
        lax.all_to_all(served_lines, "dp", split_axis=0, concat_axis=0, tiled=True),
        "mp",
        split_axis=1,
        concat_axis=3,
        tiled=True,
    )
    user_row_values, item_row_values, day_row_values = pick_lines(
        arrived_lines, place_layouts, place_limits, line_bundles
    )
    user_gradient, item_gradient, day_gradient = block_grads(
        user_row_values, item_row_values, day_row_values, status[0]
    )
    slot_storage = derivative_place_numbers(
        (user_gradient, item_gradient, day_gradient), place_layouts, place_limits, line_bundles
    )
    returned_lines = lax.all_to_all(
        lax.all_to_all(
            slot_storage.astype(jnp.bfloat16), "dp", split_axis=0, concat_axis=0, tiled=True
        ),
        "mp",
        split_axis=3,
        concat_axis=1,
        tiled=True,
    ).astype(slot_storage.dtype)
    user_gradient_sum, item_gradient_sum, day_gradient_sum = keeper_slope_totals(
        returned_lines, needed_line_numbers, locally_kept_counts, place_limits
    )
    new_user_factor, new_user_first, new_user_second = adam_update(
        user_factor, user_first, user_second, user_gradient_sum
    )
    new_item_factor, new_item_first, new_item_second = adam_update(
        item_factor, item_first, item_second, item_gradient_sum
    )
    new_day_factor, new_day_first, new_day_second = adam_update(
        day_factor, day_first, day_second, day_gradient_sum
    )
    return (
        new_user_factor,
        new_user_first,
        new_user_second,
        new_item_factor,
        new_item_first,
        new_item_second,
        new_day_factor,
        new_day_first,
        new_day_second,
    )


def solution(mesh):
    placed = (
        P(("dp", "mp"), None),
        P(("dp", "mp"), None),
        P(("dp", "mp"), None),
        P(("dp", "mp"), None, None, None),
        P("dp", "mp"),
        P("dp", "mp"),
        P("dp", "mp"),
        P("dp", "mp"),
        P("dp", "mp"),
        P("dp", "mp"),
        P("dp", "mp"),
        P("dp", "mp"),
        P("dp", "mp"),
    )
    return jax.shard_map(
        local,
        mesh=mesh,
        in_specs=placed,
        out_specs=(
            P("dp", "mp"),
            P("dp", "mp"),
            P("dp", "mp"),
            P("dp", "mp"),
            P("dp", "mp"),
            P("dp", "mp"),
            P("dp", "mp"),
            P("dp", "mp"),
            P("dp", "mp"),
        ),
        check_vma=False,
    )
```

profile of v0, /device:TPU:0, one launch (start us, length us, event | category | flops | bytes accessed | tf_op | source)
XLA Modules:
  0.0 159.7 jit_solution(16536680708248613087)
XLA Ops:
  0.7 12.8 %all-gather.2 = s32[4,1,32]{2,1,0:T(1,128)S(1)} all-gather(s32[1,1,32]{2,1,0:T(1,128)} %bitcast.240), channel_id=1, replica_groups=mesh['dp'=8,'mp'=4] {'mp'}, dimensions={0}, use_global_device_ids=true | all-gather | bytes 640 | tf_op jit(solution)/shard_map/all_gather | solution.py:198
  13.6 7.9 %all-gather.1 = s32[4,1,256]{2,1,0:T(1,128)S(1)} all-gather(s32[1,1,256]{2,1,0:T(1,128)} %bitcast.227), channel_id=1, replica_groups=mesh['dp'=8,'mp'=4] {'mp'}, dimensions={0}, use_global_device_ids=true | all-gather | bytes 5120 | tf_op jit(solution)/shard_map/all_gather | solution.py:197
  21.5 9.7 %all-gather = s32[4,1,256]{2,1,0:T(1,128)S(1)} all-gather(s32[1,1,256]{2,1,0:T(1,128)} %bitcast.228), channel_id=1, replica_groups=mesh['dp'=8,'mp'=4] {'mp'}, dimensions={0}, use_global_device_ids=true | all-gather | bytes 5120 | tf_op jit(solution)/shard_map/all_gather | solution.py:196
  31.3 2.3 %reduce-window.30 = s32[4,8,2,128]{3,1,2,0:T(8,128)S(1)} reduce-window(s32[4,8,2,128]{3,1,2,0:T(8,128)S(1)} %fusion.26, s32[]{:T(128)} %constant.177.clone.1), window={size=1x1x1x128 pad=0_0x0_0x0_0x127_0}, to_apply=%region_4.5 | reduce-window | flops 1040384 | bytes 65540 | tf_op jit(solution)/shard_map/reduce-window.2
  33.6 2.3 %reduce-window.26 = s32[4,8,2,128]{3,1,2,0:T(8,128)S(1)} reduce-window(s32[4,8,2,128]{3,1,2,0:T(8,128)S(1)} %fusion.25, s32[]{:T(128)} %constant.177.clone.1), window={size=1x1x1x128 pad=0_0x0_0x0_0x127_0}, to_apply=%region_0.1 | reduce-window | flops 1040384 | bytes 65540 | tf_op jit(solution)/shard_map/reduce-window
  38.1 4.3 %scatter_custom_fusion.1 = s32[1536]{0:T(1024)S(1)} fusion(s32[1024]{0:T(1024)S(1)} %bitcast.239, s32[1024]{0:T(1024)S(1)} %bitcast.236, s32[]{:T(128)} %constant.175.clone.1), kind=kCustom, calls=%fused_computation.152 | custom fusion | bytes 6148
  42.5 4.3 %scatter_custom_fusion.2 = s32[1536]{0:T(1024)S(1)} fusion(s32[1024]{0:T(1024)S(1)} %bitcast.238, s32[1024]{0:T(1024)S(1)} %bitcast.237, s32[]{:T(128)} %constant.175.clone.1), kind=kCustom, calls=%fused_computation.150 | custom fusion | bytes 6148
  47.4 8.2 %scatter_fusion = s32[8,4,8]{2,0,1:T(8,128)S(1)} fusion(s32[8,4,8]{2,0,1:T(8,128)S(1)} %broadcast_in_dim.73, s32[128]{0:T(128)S(1)} %reshape.575, s32[128]{0:T(128)S(1)} %reshape.577), kind=kCustom, calls=%fused_computation.3 | custom fusion | bytes 3072 | tf_op jit(solution)/shard_map/scatter | solution.py:72
  56.3 3.7 %all-to-all-start = ((s32[8,4,104]{2,1,0:T(4,128)}), s32[8,4,104]{2,1,0:T(4,128)S(1)}, u32[]{:S(2)}, u32[]{:S(2)}) async-start(s32[8,4,104]{2,1,0:T(4,128)} %pad_add_fusion), calls=%async_computation | async-start | bytes 32768 | tf_op jit(solution)/shard_map/all_to_all | solution.py:77
  62.3 6.1 %broadcast_compare_fusion.1 = (pred[1,32,256,256]{3,2,1,0:T(32,128)(4,1)}, pred[1,32,256,256]{3,2,1,0:T(32,128)(4,1)}) fusion(s32[1,32,256,256]{3,2,1,0:T(8,128)} %param.18), kind=kLoop, calls=%fused_computation.14 | loop fusion | flops 4194304 | bytes 12582912 | tf_op jit(solution)/shard_map/eq | solution.py:27
  69.1 3.2 %gather_fusion.2 = bf16[1536,64]{1,0:T(8,128)(2,1)S(1)} fusion(bf16[128,64]{1,0:T(8,128)(2,1)S(1)} %copy.133, s32[2048]{0:T(1024)S(1)} %pad_clamp_fusion), kind=kCustom, calls=%fused_computation.1.clone | custom fusion | bytes 399360 | tf_op jit(solution)/shard_map/jit(_take)/gather | solution.py:93
  72.6 3.2 %gather_fusion.1 = bf16[1536,64]{1,0:T(8,128)(2,1)S(1)} fusion(bf16[128,64]{1,0:T(8,128)(2,1)S(1)} %copy.131, s32[2048]{0:T(1024)S(1)} %pad_clamp_fusion.1), kind=kCustom, calls=%fused_computation.clone | custom fusion | bytes 399360 | tf_op jit(solution)/shard_map/jit(_take)/gather | solution.py:93
  76.1 0.9 gather_fusion
  77.7 1.3 pad_maximum_fusion
  79.0 4.2 %all-to-all-start.1 = ((bf16[8,4,104,64]{2,3,1,0:T(8,128)(2,1)}), bf16[8,4,104,64]{2,3,1,0:T(8,128)(2,1)S(1)}, u32[]{:S(2)}, u32[]{:S(2)}) async-start(bf16[8,4,104,64]{2,3,1,0:T(8,128)(2,1)} %pad_maximum_fusion), calls=%async_computation.1 | async-start | bytes 1048576 | tf_op jit(solution)/shard_map/all_to_all | solution.py:205
  83.3 9.6 %all-to-all-done.1 = bf16[8,4,104,64]{2,3,1,0:T(8,128)(2,1)S(1)} async-done(((bf16[8,4,104,64]{2,3,1,0:T(8,128)(2,1)}), bf16[8,4,104,64]{2,3,1,0:T(8,128)(2,1)S(1)}, u32[]{:S(2)}, u32[]{:S(2)}) %all-to-all-start.1) | async-done | bytes 426016 | tf_op jit(solution)/shard_map/all_to_all | solution.py:205
  92.9 0.8 copy.136
  93.8 3.6 %all-to-all-start.2 = ((bf16[8,4,104,64]{2,3,0,1:T(8,128)(2,1)}), bf16[8,4,104,64]{2,3,0,1:T(8,128)(2,1)S(1)}, u32[]{:S(2)}, u32[]{:S(2)}) async-start(bf16[8,4,104,64]{2,3,0,1:T(8,128)(2,1)} %copy.136), calls=%async_computation.2 | async-start | bytes 1048576 | tf_op jit(solution)/shard_map/all_to_all | solution.py:204
  97.5 12.2 %all-to-all-done.2 = bf16[8,4,104,64]{2,3,0,1:T(8,128)(2,1)S(1)} async-done(((bf16[8,4,104,64]{2,3,0,1:T(8,128)(2,1)}), bf16[8,4,104,64]{2,3,0,1:T(8,128)(2,1)S(1)}, u32[]{:S(2)}, u32[]{:S(2)}) %all-to-all-start.2) | async-done | bytes 426016 | tf_op jit(solution)/shard_map/all_to_all | solution.py:204
  112.8 4.5 %multiply_convert_fusion = bf16[8192,256]{1,0:T(8,128)(2,1)S(1)} fusion(pred[1,32,256,256]{3,2,1,0:T(32,128)(4,1)S(1)} %copy-done.1, pred[1,32,256,256]{3,2,1,0:T(32,128)(4,1)S(1)} %copy-done, bf16[8192,256]{1,0:T(8,128)(2,1)S(1)} %bitcast.206, bf16[256,256]{1,0:T(8,128)(2,1)S(1)} %convolution_convert_fusion.2), kind=kOutput, calls=%fused_computation.12 | convolution fusion | flops 1094713344 | bytes 12713984 | tf_op jit(solution)/shard_map/nr,ir->ni/dot_general | solution.py:21
  117.2 1.3 fusion.75
  118.5 1.3 multiply_reduce_fusion
  120.2 1.1 multiply_reduce_fusion.1
  121.9 12.9 %all_to_all.51 = bf16[8,1,104,256]{3,2,1,0:T(8,128)(2,1)S(1)} all-to-all(bf16[8,1,104,256]{3,2,1,0:T(8,128)(2,1)S(1)} %maximum_bitcast_fusion), channel_id=1, replica_groups=mesh['dp'=8,'mp'=4] {'dp'}, dimensions={0} | all-to-all | bytes 851968 | tf_op jit(solution)/shard_map/all_to_all | solution.py:221
  134.8 1.1 copy.142
  135.9 3.7 %all-to-all-start.4 = ((bf16[8,1,104,256]{2,0,1,3:T(8,128)(2,1)}), bf16[8,1,104,256]{2,0,1,3:T(8,128)(2,1)S(1)}, u32[]{:S(2)}, u32[]{:S(2)}) async-start(bf16[8,1,104,256]{2,0,1,3:T(8,128)(2,1)} %copy.142), calls=%async_computation.4 | async-start | bytes 1048576 | tf_op jit(solution)/shard_map/all_to_all | solution.py:220
  139.9 14.0 %all-to-all-done.4 = bf16[8,1,104,256]{2,0,1,3:T(8,128)(2,1)S(1)} async-done(((bf16[8,1,104,256]{2,0,1,3:T(8,128)(2,1)}), bf16[8,1,104,256]{2,0,1,3:T(8,128)(2,1)S(1)}, u32[]{:S(2)}, u32[]{:S(2)}) %all-to-all-start.4) | async-done | bytes 426016 | tf_op jit(solution)/shard_map/all_to_all | solution.py:220
  155.1 0.8 reshape.541
  156.3 0.8 reshape.540
  157.1 0.8 divide_subtract_fusion.2
  157.9 0.9 divide_subtract_fusion
  158.8 0.9 divide_subtract_fusion.1
  (139 shorter events, 13.8 us)
Async XLA Ops:
  0.6 59.4 %copy-start.9 = (s32[1,32]{1,0:T(1,128)S(1)}, s32[1,32]{1,0:T(1,128)}, u32[]{:S(2)}) copy-start(s32[1,32]{1,0:T(1,128)} %param.17) | copy-start | bytes 388
  0.7 59.4 %copy-start.7 = (s32[1,256]{1,0:T(1,128)S(1)}, s32[1,256]{1,0:T(1,128)}, u32[]{:S(2)}) copy-start(s32[1,256]{1,0:T(1,128)} %param.16) | copy-start | bytes 3076
  0.7 59.4 %copy-start.8 = (s32[1,256]{1,0:T(1,128)S(1)}, s32[1,256]{1,0:T(1,128)}, u32[]{:S(2)}) copy-start(s32[1,256]{1,0:T(1,128)} %param.15) | copy-start | bytes 3076
  56.3 12.4 %all-to-all-start = ((s32[8,4,104]{2,1,0:T(4,128)}), s32[8,4,104]{2,1,0:T(4,128)S(1)}, u32[]{:S(2)}, u32[]{:S(2)}) async-start(s32[8,4,104]{2,1,0:T(4,128)} %pad_add_fusion), calls=%async_computation | async-start | bytes 32768 | tf_op jit(solution)/shard_map/all_to_all | solution.py:77
  62.2 6.1 %copy-start.2 = (f32[32,64]{1,0:T(8,128)S(1)}, f32[32,64]{1,0:T(8,128)}, u32[]{:S(2)}) copy-start(f32[32,64]{1,0:T(8,128)} %param.25) | copy-start | bytes 24580
  62.2 6.1 %copy-start.4 = (f32[128,64]{0,1:T(8,128)S(1)}, f32[128,64]{0,1:T(8,128)}, u32[]{:S(2)}) copy-start(f32[128,64]{0,1:T(8,128)} %param.19) | copy-start | bytes 98308
  62.3 6.2 %copy-start.3 = (f32[128,64]{0,1:T(8,128)S(1)}, f32[128,64]{0,1:T(8,128)}, u32[]{:S(2)}) copy-start(f32[128,64]{0,1:T(8,128)} %param.22) | copy-start | bytes 98308
  79.0 13.9 %all-to-all-start.1 = ((bf16[8,4,104,64]{2,3,1,0:T(8,128)(2,1)}), bf16[8,4,104,64]{2,3,1,0:T(8,128)(2,1)S(1)}, u32[]{:S(2)}, u32[]{:S(2)}) async-start(bf16[8,4,104,64]{2,3,1,0:T(8,128)(2,1)} %pad_maximum_fusion), calls=%async_computation.1 | async-start | bytes 1048576 | tf_op jit(solution)/shard_map/all_to_all | solution.py:205
  93.8 15.9 %all-to-all-start.2 = ((bf16[8,4,104,64]{2,3,0,1:T(8,128)(2,1)}), bf16[8,4,104,64]{2,3,0,1:T(8,128)(2,1)S(1)}, u32[]{:S(2)}, u32[]{:S(2)}) async-start(bf16[8,4,104,64]{2,3,0,1:T(8,128)(2,1)} %copy.136), calls=%async_computation.2 | async-start | bytes 1048576 | tf_op jit(solution)/shard_map/all_to_all | solution.py:204
  110.5 1.6 copy-start
  110.7 2.1 %copy-start.1 = (pred[1,32,256,256]{3,2,1,0:T(32,128)(4,1)S(1)}, pred[1,32,256,256]{3,2,1,0:T(32,128)(4,1)}, u32[]{:S(2)}) copy-start(pred[1,32,256,256]{3,2,1,0:T(32,128)(4,1)} %get-tuple-element.28) | copy-start | bytes 6291460
  135.9 18.0 %all-to-all-start.4 = ((bf16[8,1,104,256]{2,0,1,3:T(8,128)(2,1)}), bf16[8,1,104,256]{2,0,1,3:T(8,128)(2,1)S(1)}, u32[]{:S(2)}, u32[]{:S(2)}) async-start(bf16[8,1,104,256]{2,0,1,3:T(8,128)(2,1)} %copy.142), calls=%async_computation.4 | async-start | bytes 1048576 | tf_op jit(solution)/shard_map/all_to_all | solution.py:220
  139.7 17.4 %copy-start.5 = (f32[32,64]{1,0:T(8,128)S(1)}, f32[32,64]{1,0:T(8,128)}, u32[]{:S(2)}) copy-start(f32[32,64]{1,0:T(8,128)} %param.26) | copy-start | bytes 24580
  139.7 17.4 %copy-start.6 = (f32[32,64]{1,0:T(8,128)S(1)}, f32[32,64]{1,0:T(8,128)}, u32[]{:S(2)}) copy-start(f32[32,64]{1,0:T(8,128)} %param.27) | copy-start | bytes 24580
  139.9 18.0 %copy-start.10 = (f32[128,64]{0,1:T(8,128)S(1)}, f32[128,64]{0,1:T(8,128)}, u32[]{:S(2)}) copy-start(f32[128,64]{0,1:T(8,128)} %param.23) | copy-start | bytes 98308
  139.9 18.0 %copy-start.11 = (f32[128,64]{0,1:T(8,128)S(1)}, f32[128,64]{0,1:T(8,128)}, u32[]{:S(2)}) copy-start(f32[128,64]{0,1:T(8,128)} %param.24) | copy-start | bytes 98308
  154.0 4.8 %copy-start.12 = (f32[128,64]{0,1:T(8,128)S(1)}, f32[128,64]{0,1:T(8,128)}, u32[]{:S(2)}) copy-start(f32[128,64]{0,1:T(8,128)} %param.20) | copy-start | bytes 98308
  154.0 4.8 %copy-start.13 = (f32[128,64]{0,1:T(8,128)S(1)}, f32[128,64]{0,1:T(8,128)}, u32[]{:S(2)}) copy-start(f32[128,64]{0,1:T(8,128)} %param.21) | copy-start | bytes 98308
where the time goes:
time: 160 us
  blocking collectives  43.4 us (27%)
  waiting for transfers between devices  35.8 us (22%)
  local copies, waits for them, and re-layouts  34 us (21%)
  other arithmetic  18.6 us (12%)
  starting transfers between devices  15.3 us (10%)
  matrix products  11.3 us (7%)
    all_to_all x1, waiting for transfers between devices, local(): lax.all_to_all(lax.all_to_all(slot_storage.astype(jnp.bfloat16), 'dp', sp...  14 us
    all_to_all x1, blocking collectives, local(): lax.all_to_all(slot_storage.astype(jnp.bfloat16), 'dp', split_axis=0, con...  12.9 us
    all_gather x1, blocking collectives, local(): lax.all_gather(days_list, 'mp', axis=0, tiled=True)  12.8 us
    all_to_all x1, waiting for transfers between devices, local(): lax.all_to_all(lax.all_to_all(served_lines, 'dp', split_axis=0, concat_ax...  12.2 us
    unnamed x34, local copies, waits for them, and re-layouts  9.76 us
    all_gather x1, blocking collectives, local(): lax.all_gather(users_list, 'mp', axis=0, tiled=True)  9.74 us
    all_to_all x1, waiting for transfers between devices, local(): lax.all_to_all(served_lines, 'dp', split_axis=0, concat_axis=0, tiled=True)  9.64 us
    scatter x4, local copies, waits for them, and re-layouts, build_needed_catalogs(): blank_slots.at[holder_index, blocks, slot_position_index].set(local_row)  8.36 us
  transfers between devices with their start and end apart: 4, of which 3 were waited for; matrix products, arithmetic and copies ran while one was open for 6% of the time, Pallas kernels for 0%

commit v1 on v0

v1 whole, which is shorter than its diff:
```python
import functools

import jax
import jax.numpy as jnp
from jax import lax
from jax.experimental import pallas as pl
from jax.experimental.pallas import tpu as pltpu
from jax.sharding import PartitionSpec as P

beta_one = 0.9
beta_two = 0.99
bias_one = 1.0 - 0.9**10
bias_two = 1.0 - 0.99**10
learn_rate = 0.01
epsilon = 1e-08
loss_scale = 0.0625

LANES = 128
DAYS_PER_STEP = 4

f32 = jnp.float32
bf16 = jnp.bfloat16


class Packing:
    def __init__(self, row_counts, columns):
        self.columns = columns
        self.parts = LANES // columns
        self.row_counts = row_counts
        self.packed = tuple(rows // self.parts for rows in row_counts)
        padded = [-(-rows // 16) * 16 for rows in self.packed]
        self.padded = tuple(padded)
        self.starts = tuple(sum(padded[:t]) for t in range(len(padded)))
        self.height = sum(padded)


def pack_kernel(packing, user_ref, item_ref, day_ref, out_ref):
    for t, ref in enumerate((user_ref, item_ref, day_ref)):
        rows = packing.packed[t]
        parts = [ref[p * rows : (p + 1) * rows, :] for p in range(packing.parts)]
        if packing.padded[t] != rows:
            blank = jnp.zeros((packing.padded[t] - rows, packing.columns), f32)
            parts = [jnp.concatenate([part, blank], axis=0) for part in parts]
        wide = jnp.concatenate(parts, axis=1).astype(bf16)
        out_ref[packing.starts[t] : packing.starts[t] + packing.padded[t], :] = wide


def lane_spread(packing, holders):
    wide = holders * LANES
    narrow = holders * packing.columns
    lane = lax.broadcasted_iota(jnp.int32, (wide, narrow), 0)
    column = lax.broadcasted_iota(jnp.int32, (wide, narrow), 1)
    target = (lane // LANES) * packing.columns + lane % packing.columns
    return jnp.where(target == column, 1.0, 0.0).astype(bf16)


def lane_part(packing, rows, holders):
    lane = lax.broadcasted_iota(jnp.int32, (rows, holders * LANES), 1)
    return (lane % LANES) // packing.columns


def split_rows(packing, t, numbers):
    owner = numbers // packing.row_counts[t]
    local = numbers % packing.row_counts[t]
    return owner * packing.padded[t] + local % packing.packed[t], local // packing.packed[t]


def block_kernel(
    packing,
    owners,
    holders,
    days_per_step,
    user_row_ref,
    item_row_ref,
    day_row_ref,
    user_col_ref,
    item_col_ref,
    day_col_ref,
    table_ref,
    status_ref,
    out_ref,
    users,
    items,
    items_half_t,
    days,
    user_gradient,
    item_gradient,
    day_gradient,
):
    step = pl.program_id(0)
    user_count = users.shape[0]

    def pick(t, numbers):
        slots, part = split_rows(packing, t, numbers)
        rows = numbers.shape[0]
        depth = owners * packing.padded[t]
        selector = jnp.where(
            slots == lax.broadcasted_iota(jnp.int32, (rows, depth), 1), 1.0, 0.0
        ).astype(bf16)
        start = packing.starts[t]
        wide = jnp.concatenate(
            [
                jnp.dot(
                    selector,
                    table_ref[:, m, start : start + packing.padded[t], :].reshape(depth, LANES),
                    preferred_element_type=f32,
                )
                for m in range(holders)
            ],
            axis=1,
        )
        wide = jnp.where(lane_part(packing, rows, holders) == part, wide, 0.0).astype(bf16)
        return jnp.dot(wide, lane_spread(packing, holders), preferred_element_type=f32)

    @pl.when(step == 0)
    def _():
        users[...] = pick(0, user_col_ref[...])
        item_values = pick(1, item_col_ref[...])
        items[...] = item_values.astype(bf16)
        items_half_t[...] = (0.5 * item_values).T.astype(bf16)
        days[...] = pick(2, day_col_ref[...])
        user_gradient[...] = jnp.zeros_like(user_gradient)
        item_gradient[...] = jnp.zeros_like(item_gradient)

    for j in range(days_per_step):
        k = step * days_per_step + j
        day = days[pl.ds(k, 1), :]
        user_values = users[...]
        scaled = (day * user_values).astype(bf16)
        half_logits = jnp.dot(scaled, items_half_t[...], preferred_element_type=f32)
        state = status_ref[0, j]
        residual = (
            (0.5 * loss_scale)
            * state.astype(f32)
            * (jnp.tanh(half_logits) + jnp.where(state == 1, -1.0, 1.0))
        ).astype(bf16)
        projected = jnp.dot(residual, items[...], preferred_element_type=f32)
        user_gradient[...] += projected * day
        day_gradient[pl.ds(k, 1), :] = jnp.sum(projected * user_values, axis=0, keepdims=True)
        item_gradient[...] += lax.dot_general(
            residual, scaled, (((0,), (0,)), ((), ())), preferred_element_type=f32
        )

    def place(t, numbers, gradient):
        slots, part = split_rows(packing, t, numbers[1])
        _, part_col = split_rows(packing, t, numbers[0])
        count = gradient.shape[0]
        depth = owners * packing.padded[t]
        placer = jnp.where(
            lax.broadcasted_iota(jnp.int32, (depth, count), 0) == slots, 1.0, 0.0
        ).astype(bf16)
        wide = lax.dot_general(
            gradient.astype(bf16),
            lane_spread(packing, holders),
            (((1,), (1,)), ((), ())),
            preferred_element_type=f32,
        )
        wide = jnp.where(lane_part(packing, count, holders) == part_col, wide, 0.0).astype(bf16)
        placed = jnp.dot(placer, wide, preferred_element_type=f32)
        start = packing.starts[t]
        for m in range(holders):
            out_ref[:, m, start : start + packing.padded[t], :] = placed[
                :, m * LANES : (m + 1) * LANES
            ].reshape(owners, packing.padded[t], LANES)

    @pl.when(step == pl.num_programs(0) - 1)
    def _():
        place(0, (user_col_ref[...], user_row_ref[...]), user_gradient[...])
        place(1, (item_col_ref[...], item_row_ref[...]), item_gradient[...])
        place(2, (day_col_ref[...], day_row_ref[...]), day_gradient[...])


def adam_kernel(packing, gradient_ref, *refs):
    for t in range(3):
        factor, first, second = refs[3 * t : 3 * t + 3]
        new_factor, new_first, new_second = refs[9 + 3 * t : 12 + 3 * t]
        rows, columns = packing.packed[t], packing.columns
        start = packing.starts[t]
        wide = gradient_ref[start : start + packing.padded[t], :]
        gradient = jnp.concatenate(
            [wide[:rows, p * columns : (p + 1) * columns] for p in range(packing.parts)], axis=0
        )
        first_value = beta_one * first[...] + (1.0 - beta_one) * gradient
        second_value = beta_two * second[...] + (1.0 - beta_two) * gradient * gradient
        change = (
            learn_rate
            * (first_value / bias_one)
            / (jnp.sqrt(second_value / bias_two) + epsilon)
        )
        new_factor[...] = factor[...] - change
        new_first[...] = first_value
        new_second[...] = second_value


def local(
    users_list,
    items_list,
    days_list,
    status,
    user_factor,
    user_first,
    user_second,
    item_factor,
    item_first,
    item_second,
    day_factor,
    day_first,
    day_second,
):
    owners = lax.axis_size("dp")
    holders = lax.axis_size("mp")
    columns = user_factor.shape[1]
    rank = columns * holders
    packing = Packing((user_factor.shape[0], item_factor.shape[0], day_factor.shape[0]), columns)
    user_count, item_count, day_count = (
        users_list.shape[1],
        items_list.shape[1],
        days_list.shape[1],
    )
    packed = pl.pallas_call(
        functools.partial(pack_kernel, packing),
        out_shape=jax.ShapeDtypeStruct((packing.height, LANES), bf16),
        name="pack",
    )(user_factor, item_factor, day_factor)
    table = lax.all_gather(packed, ("dp", "mp"), axis=0).reshape(
        owners, holders, packing.height, LANES
    )
    whole = lambda shape: pl.BlockSpec(shape, lambda s: (0,) * len(shape))
    dense = pl.pallas_call(
        functools.partial(block_kernel, packing, owners, holders, DAYS_PER_STEP),
        out_shape=jax.ShapeDtypeStruct(table.shape, f32),
        grid=(day_count // DAYS_PER_STEP,),
        in_specs=[
            whole((1, user_count)),
            whole((1, item_count)),
            whole((1, day_count)),
            whole((user_count, 1)),
            whole((item_count, 1)),
            whole((day_count, 1)),
            whole(table.shape),
            pl.BlockSpec(
                (1, DAYS_PER_STEP, user_count, item_count), lambda s: (0, s, 0, 0)
            ),
        ],
        out_specs=whole(table.shape),
        scratch_shapes=[
            pltpu.VMEM((user_count, rank), f32),
            pltpu.VMEM((item_count, rank), bf16),
            pltpu.VMEM((rank, item_count), bf16),
            pltpu.VMEM((day_count, rank), f32),
            pltpu.VMEM((user_count, rank), f32),
            pltpu.VMEM((item_count, rank), f32),
            pltpu.VMEM((day_count, rank), f32),
        ],
        compiler_params=pltpu.CompilerParams(vmem_limit_bytes=48 * 1024 * 1024),
        name="block_gradients",
    )(
        users_list,
        items_list,
        days_list,
        users_list.reshape(user_count, 1),
        items_list.reshape(item_count, 1),
        days_list.reshape(day_count, 1),
        table,
        status,
    )
    gradient = lax.psum_scatter(
        dense.reshape(owners * holders, packing.height, LANES),
        ("dp", "mp"),
        scatter_dimension=0,
        tiled=False,
    )
    states = (
        user_factor,
        user_first,
        user_second,
        item_factor,
        item_first,
        item_second,
        day_factor,
        day_first,
        day_second,
    )
    return pl.pallas_call(
        functools.partial(adam_kernel, packing),
        out_shape=tuple(jax.ShapeDtypeStruct(a.shape, a.dtype) for a in states),
        name="adam",
    )(gradient, *states)


def solution(mesh):
    block = P(("dp", "mp"), None)
    piece = P("dp", "mp")
    return jax.shard_map(
        local,
        mesh=mesh,
        in_specs=(block, block, block, P(("dp", "mp"), None, None, None)) + (piece,) * 9,
        out_specs=(piece,) * 9,
        check_vma=False,
    )
```

time: 160 us -> 203 us (1.27)
  waiting for transfers between devices: 35.8 us -> 149 us
  blocking collectives: 43.4 us -> 0 us
  other arithmetic: 18.6 us -> 0 us
  Pallas kernels: 0 us -> 17.3 us
  starting transfers between devices: 15.3 us -> 0.08 us
  between operations: 1.32 us -> 14.1 us
  local copies, waits for them, and re-layouts: 34 us -> 21.4 us
  matrix products: 11.3 us -> 0 us
    reduce_scatter x0 -> x1, waiting for transfers between devices: none -> 94.5 us  [local(): lax.psum_scatter(dense.reshape(owners * holders, packing.height, LANES),...]
    all_gather x0 -> x1, waiting for transfers between devices: none -> 54.5 us  [local(): lax.all_gather(packed, ('dp', 'mp'), axis=0)]
    all_to_all x4 -> x0, waiting for transfers between devices: 35.8 us -> none  [the longest x1 14 us: local(): lax.all_to_all(lax.all_to_all(slot_storage.astype(jnp.bfloat16), 'dp', sp...]
    all_gather x3 -> x0, blocking collectives: 30.5 us -> none  [the longest x1 12.8 us: local(): lax.all_gather(days_list, 'mp', axis=0, tiled=True)]
    pallas_call x0 -> x3, Pallas kernels: none -> 17.3 us  [the longest x1 13.8 us: local(): pl.pallas_call(functools.partial(block_kernel, packing, owners, holders,...]
    all_to_all x4 -> x0, starting transfers between devices: 15.3 us -> none  [the longest x1 4.19 us: local(): lax.all_to_all(served_lines, 'dp', split_axis=0, concat_axis=0, tiled=True)]
    all_to_all x1 -> x0, blocking collectives: 12.9 us -> none  [local(): lax.all_to_all(slot_storage.astype(jnp.bfloat16), 'dp', split_axis=0, con...]
    dot_general x12 -> x0, matrix products: 11.3 us -> none  [the longest x1 4.46 us: block_grads(): jnp.einsum('nr,ir->ni', scaled_flat, item_row_values, preferred_element_t...]
  transfers between devices with their start and end apart: 4 -> 2, of which waited for: 3 -> 2; matrix products, arithmetic and copies ran while one was open for 6% -> 3% of each run, Pallas kernels for 0% -> 0%
where the time goes in v1:
time: 203 us; the launch traced here: 202 us
  waiting for transfers between devices  149 us (73%)
  local copies, waits for them, and re-layouts  21.4 us (11%)
  Pallas kernels  17.3 us (9%)
  between operations  14.1 us (7%)
    reduce_scatter x1, waiting for transfers between devices, local(): lax.psum_scatter(dense.reshape(owners * holders, packing.height, LANES),...  94.5 us
    all_gather x1, waiting for transfers between devices, local(): lax.all_gather(packed, ('dp', 'mp'), axis=0)  54.5 us
    pallas_call x1, Pallas kernels, local(): pl.pallas_call(functools.partial(block_kernel, packing, owners, holders,...  13.8 us
    unnamed x22, local copies, waits for them, and re-layouts  9.83 us
    pallas_call x6, local copies, waits for them, and re-layouts, local(): pl.pallas_call(functools.partial(adam_kernel, packing), out_shape=tuple((...  9.22 us
  transfers between devices with their start and end apart: 2, of which 2 were waited for; matrix products, arithmetic and copies ran while one was open for 3% of the time, Pallas kernels for 0%

profile of v1, /device:TPU:0, one launch (start us, length us, event | category | flops | bytes accessed | tf_op | source)
XLA Modules:
  0.0 201.8 jit_solution(7637015191469500703)
XLA Ops:
  7.2 0.0 all-gather.3.cloned.1.call-start
  7.2 1.5 copy.37.user_ref.refs_0_
  8.7 1.5 copy.38.item_ref.refs_3_
  10.2 1.6 pack.1
  11.7 0.0 all-gather.3.cloned.1.call-update
  11.8 0.0 reduce-scatter.2.cloned.1.call-start
  11.8 0.8 copy.39.user_col_ref
  12.6 0.8 copy.40.item_col_ref
  13.4 0.7 copy.41.day_col_ref
  14.2 54.5 %all-gather.3.cloned.1.call-done = bf16[4608,128]{1,0:T(8,128)(2,1)} async-done(((bf16[144,128]{1,0:T(8,128)(2,1)}), bf16[4608,128]{1,0:T(8,128)(2,1)}) %all-gather.3.cloned.1.call-update) | async-done | bytes 1179664 | tf_op jit(solution)/shard_map/all_gather | solution.py:225
  68.7 1.3 copy-done
  70.0 0.7 copy-done.1
  70.7 0.7 copy-done.2
  71.3 0.7 copy-done.3
  72.0 13.8 %block_gradients.1 = f32[8,4,144,128]{3,2,1,0:T(8,128)} custom-call(s32[1,256]{1,0:T(1,128)S(1)} %copy-done.1, s32[1,256]{1,0:T(1,128)S(1)} %copy-done.2, s32[1,32]{1,0:T(1,128)S(1)} %copy-done.3, s32[256,1]{1,0:T(8,128)S(1)} %copy.39.user_col_ref, s32[256,1]{1,0:T(8,128)S(1)} %copy.40.item_col_ref, s32[32,1]{1,0:T(8,128)S(1)} %copy.41.day_col_ref, ...), custom_call_target="tpu_custom_call" | custom-call | tf_op jit(solution)/shard_map/block_gradients/pallas_call | solution.py:229
  85.8 0.0 reduce-scatter.2.cloned.1.call-update
  85.8 0.7 copy-done.4
  86.5 0.7 copy.43.refs_1_
  87.2 0.0 copy-done.5
  87.2 0.7 copy.44.refs_2_
  88.0 0.0 copy-done.6
  88.0 0.7 copy.46.refs_4_
  88.7 0.0 copy-done.7
  88.7 0.7 copy.47.refs_5_
  89.4 94.5 %reduce-scatter.2.cloned.1.call-done = f32[1,144,128]{2,1,0:T(8,128)} async-done(((f32[32,144,128]{2,1,0:T(8,128)}), f32[1,144,128]{2,1,0:T(8,128)}) %reduce-scatter.2.cloned.1.call-update) | async-done | bytes 73744 | tf_op jit(solution)/shard_map/reduce_scatter | solution.py:267
  183.9 1.9 adam.1
  185.8 1.5 copy.48
  187.3 1.5 copy.49
  188.8 1.5 copy.50
  190.4 1.5 copy.51
  191.9 1.5 copy.52
  193.5 1.5 copy.53
  (8 shorter events, 0.0 us)
Async XLA Ops:
  7.2 61.5 %all-gather.3.cloned.1.call-start = ((), (), s32[]{:S(2)}) async-start(), calls=%async_computation.2 | async-start | bytes 1216512 | tf_op jit(solution)/shard_map/all_gather | solution.py:225
  11.8 172.1 %reduce-scatter.2.cloned.1.call-start = ((), (), s32[]{:S(2)}) async-start(), calls=%async_computation.1 | async-start | bytes 2433024 | tf_op jit(solution)/shard_map/reduce_scatter | solution.py:267
  68.7 1.3 copy-start
  70.0 0.7 copy-start.1
  70.7 0.7 copy-start.2
  71.3 0.7 copy-start.3
  85.8 0.8 copy-start.4
  85.8 1.5 copy-start.5
  85.8 2.2 %copy-start.6 = (f32[128,64]{0,1:T(8,128)S(1)}, f32[128,64]{0,1:T(8,128)}, u32[]{:S(2)}) copy-start(f32[128,64]{0,1:T(8,128)} %param.21) | copy-start | bytes 98308
  85.8 2.9 %copy-start.7 = (f32[128,64]{0,1:T(8,128)S(1)}, f32[128,64]{0,1:T(8,128)}, u32[]{:S(2)}) copy-start(f32[128,64]{0,1:T(8,128)} %param.22) | copy-start | bytes 98308
Sparse Core Ops, SparseCore 0:
  11.9 56.7 all-gather.2
  85.9 97.8 reduce-scatter.1

commit v2 on v1

v2 whole, which is shorter than its diff:
```python
import functools

import jax
import jax.numpy as jnp
from jax import lax
from jax.experimental import pallas as pl
from jax.experimental.pallas import tpu as pltpu
from jax.sharding import PartitionSpec as P

beta_one = 0.9
beta_two = 0.99
bias_one = 1.0 - 0.9**10
bias_two = 1.0 - 0.99**10
learn_rate = 0.01
epsilon = 1e-08
loss_scale = 0.0625

LANES = 128
DAYS_PER_STEP = 4
VMEM_LIMIT = 56 * 1024 * 1024

f32 = jnp.float32
bf16 = jnp.bfloat16


class Sizes:
    def __init__(self, owners, holders, columns, row_counts, list_counts):
        self.owners = owners
        self.holders = holders
        self.columns = columns
        self.rank = columns * holders
        self.row_counts = row_counts
        self.list_counts = list_counts
        limits = (
            max(2, 3 * list_counts[0] // (2 * owners)),
            max(2, 3 * list_counts[1] // (2 * owners)),
            max(2, 2 * list_counts[2] // owners),
        )
        self.slots = tuple(-(-limit // 16) * 16 for limit in limits)
        self.slot_starts = (0, self.slots[0], self.slots[0] + self.slots[1])
        self.slot_rows = sum(self.slots)
        self.list_starts = (0, list_counts[0], list_counts[0] + list_counts[1])
        self.day_parts = LANES // columns
        self.day_packed = -(-(row_counts[2] // self.day_parts) // 16) * 16
        self.piece_rows = 2 * columns + self.day_packed


def iota(shape, dimension):
    return lax.broadcasted_iota(jnp.int32, shape, dimension)


def onehot(condition):
    return jnp.where(condition, 1.0, 0.0).astype(bf16)


def dot_nt(a, b):
    return lax.dot_general(a, b, (((1,), (1,)), ((), ())), preferred_element_type=f32)


def pack_days(sizes, days):
    rows = sizes.row_counts[2] // sizes.day_parts
    parts = [days[p * rows : (p + 1) * rows] for p in range(sizes.day_parts)]
    if rows != sizes.day_packed:
        blank = jnp.zeros((sizes.day_packed - rows, days.shape[1]), days.dtype)
        parts = [jnp.concatenate([part, blank], axis=0) for part in parts]
    return jnp.concatenate(parts, axis=1)


def unpack_days(sizes, packed):
    rows = sizes.row_counts[2] // sizes.day_parts
    return jnp.concatenate(
        [
            packed[:rows, p * sizes.columns : (p + 1) * sizes.columns]
            for p in range(sizes.day_parts)
        ],
        axis=0,
    )


def pack_kernel(sizes, user_ref, item_ref, day_ref, out_ref):
    columns = sizes.columns
    out_ref[:columns, :] = user_ref[...].astype(bf16)
    out_ref[columns : 2 * columns, :] = item_ref[...].astype(bf16)
    out_ref[2 * columns :, :] = pack_days(sizes, day_ref[...]).astype(bf16)


def slot_kernel(sizes, me_ref, *refs):
    owners = sizes.owners
    lists = refs[:owners]
    outs = refs[owners:]
    me = me_ref[0]
    for t in range(3):
        serve_ref, sum_ref, pick_ref, place_ref = outs[4 * t : 4 * t + 4]
        count, rows, slots = sizes.list_counts[t], sizes.row_counts[t], sizes.slots[t]
        start = sizes.list_starts[t]
        numbers = jnp.concatenate([ref[:, start : start + count] for ref in lists], axis=0)
        owner = numbers // rows
        row = numbers % rows
        earlier = onehot(iota((count, count), 0) < iota((count, count), 1))
        mine = owner == me
        position = jnp.dot(onehot(mine), earlier, preferred_element_type=f32).astype(jnp.int32)
        position = jnp.where(mine, position, -1)
        for s in range(owners):
            slot_hot = onehot(iota((slots, count), 0) == position[s : s + 1])
            row_hot = onehot(iota((rows, count), 0) == row[s : s + 1])
            serve_ref[s * slots : (s + 1) * slots, :] = dot_nt(slot_hot, row_hot).astype(bf16)
        sum_ref[...] = serve_ref[...].astype(f32).T.astype(bf16)
        own = owner[0:1]
        owner_hot = iota((owners, count), 0) == own
        before = jnp.dot(onehot(owner_hot), earlier, preferred_element_type=f32)
        position = jnp.sum(jnp.where(owner_hot, before, 0.0), axis=0, keepdims=True)
        target = lax.bitwise_xor(own, jnp.full_like(own, me)) * slots + position.astype(jnp.int32)
        place = jnp.where(iota((owners * slots, count), 0) == target, 1.0, 0.0)
        place_ref[...] = place.astype(bf16)
        pick_ref[...] = place.T.astype(bf16)


def serve_kernel(sizes, *refs):
    holders, owners, columns = sizes.holders, sizes.owners, sizes.columns
    pieces = refs[:holders]
    selectors = refs[holders : holders + 3]
    outs = refs[holders + 3 :]
    for t in range(3):
        if t < 2:
            table = jnp.concatenate(
                [ref[t * columns : (t + 1) * columns, :] for ref in pieces], axis=0
            )
            rows = dot_nt(selectors[t][...], table)
        else:
            table = jnp.concatenate(
                [unpack_days(sizes, ref[2 * columns :, :].astype(f32)) for ref in pieces], axis=1
            ).astype(bf16)
            rows = jnp.dot(selectors[t][...], table, preferred_element_type=f32)
        rows = rows.astype(bf16)
        start, slots = sizes.slot_starts[t], sizes.slots[t]
        for s in range(owners):
            outs[s][start : start + slots, :] = rows[s * slots : (s + 1) * slots]


def block_kernel(sizes, days_per_step, *refs):
    owners = sizes.owners
    arrived = refs[:owners]
    picks = refs[owners : owners + 3]
    places = refs[owners + 3 : owners + 6]
    status_ref = refs[owners + 6]
    outs = refs[owners + 7 : 2 * owners + 7]
    users, items, items_half_t, days, user_gradient, item_gradient, day_gradient = refs[
        2 * owners + 7 :
    ]
    step = pl.program_id(0)

    def pick(t):
        start, slots = sizes.slot_starts[t], sizes.slots[t]
        rows = jnp.concatenate([ref[start : start + slots, :] for ref in arrived], axis=0)
        return jnp.dot(picks[t][...], rows, preferred_element_type=f32)

    @pl.when(step == 0)
    def _():
        users[...] = pick(0)
        item_values = pick(1)
        items[...] = item_values.astype(bf16)
        items_half_t[...] = (0.5 * item_values).T.astype(bf16)
        days[...] = pick(2)
        user_gradient[...] = jnp.zeros_like(user_gradient)
        item_gradient[...] = jnp.zeros_like(item_gradient)

    for j in range(days_per_step):
        k = step * days_per_step + j
        day = days[pl.ds(k, 1), :]
        user_values = users[...]
        scaled = (day * user_values).astype(bf16)
        half_logits = jnp.dot(scaled, items_half_t[...], preferred_element_type=f32)
        state = status_ref[0, j]
        residual = (
            (0.5 * loss_scale)
            * state.astype(f32)
            * (jnp.tanh(half_logits) + jnp.where(state == 1, -1.0, 1.0))
        ).astype(bf16)
        projected = jnp.dot(residual, items[...], preferred_element_type=f32)
        user_gradient[...] += projected * day
        day_gradient[pl.ds(k, 1), :] = jnp.sum(projected * user_values, axis=0, keepdims=True)
        item_gradient[...] += lax.dot_general(
            residual, scaled, (((0,), (0,)), ((), ())), preferred_element_type=f32
        )

    @pl.when(step == pl.num_programs(0) - 1)
    def _():
        for t, gradient in enumerate((user_gradient, item_gradient, day_gradient)):
            start, slots = sizes.slot_starts[t], sizes.slots[t]
            placed = jnp.dot(
                places[t][...], gradient[...].astype(bf16), preferred_element_type=f32
            ).astype(bf16)
            for s in range(owners):
                outs[s][start : start + slots, :] = placed[s * slots : (s + 1) * slots]


def sum_kernel(sizes, *refs):
    holders, owners, columns = sizes.holders, sizes.owners, sizes.columns
    arrived = refs[:owners]
    selectors = refs[owners : owners + 3]
    outs = refs[owners + 3 :]
    for t in range(3):
        start, slots = sizes.slot_starts[t], sizes.slots[t]
        rows = jnp.concatenate([ref[start : start + slots, :] for ref in arrived], axis=0)
        total = jnp.dot(selectors[t][...], rows, preferred_element_type=f32)
        if t < 2:
            turned = total.T.astype(bf16)
            for j in range(holders):
                outs[j][t * columns : (t + 1) * columns, :] = turned[
                    j * columns : (j + 1) * columns
                ]
        else:
            for j in range(holders):
                outs[j][2 * columns :, :] = pack_days(
                    sizes, total[:, j * columns : (j + 1) * columns]
                ).astype(bf16)


def adam_kernel(sizes, *refs):
    holders, columns = sizes.holders, sizes.columns
    pieces = refs[:holders]
    states = refs[holders : holders + 9]
    outs = refs[holders + 9 :]
    total = pieces[0][...].astype(f32)
    for ref in pieces[1:]:
        total = total + ref[...].astype(f32)
    for t in range(3):
        if t < 2:
            gradient = total[t * columns : (t + 1) * columns]
        else:
            gradient = unpack_days(sizes, total[2 * columns :])
        factor, first, second = states[3 * t : 3 * t + 3]
        new_factor, new_first, new_second = outs[3 * t : 3 * t + 3]
        first_value = beta_one * first[...] + (1.0 - beta_one) * gradient
        second_value = beta_two * second[...] + (1.0 - beta_two) * gradient * gradient
        change = (
            learn_rate
            * (first_value / bias_one)
            / (jnp.sqrt(second_value / bias_two) + epsilon)
        )
        new_factor[...] = factor[...] - change
        new_first[...] = first_value
        new_second[...] = second_value


def swap_all(arrays, axis, size):
    return [arrays[0]] + [
        lax.ppermute(arrays[s], axis, [(i, i ^ s) for i in range(size)]) for s in range(1, size)
    ]


def local(
    users_list,
    items_list,
    days_list,
    status,
    user_factor,
    user_first,
    user_second,
    item_factor,
    item_first,
    item_second,
    day_factor,
    day_first,
    day_second,
):
    owners = lax.axis_size("dp")
    holders = lax.axis_size("mp")
    row_counts = (user_factor.shape[0], item_factor.shape[0], day_factor.shape[0])
    list_counts = (users_list.shape[1], items_list.shape[1], days_list.shape[1])
    sizes = Sizes(owners, holders, user_factor.shape[1], row_counts, list_counts)
    params = pltpu.CompilerParams(vmem_limit_bytes=VMEM_LIMIT)
    shape = jax.ShapeDtypeStruct

    numbers = jnp.concatenate([users_list, items_list, days_list], axis=1)
    lists = swap_all([numbers] * owners, "dp", owners)
    piece = pl.pallas_call(
        functools.partial(pack_kernel, sizes),
        out_shape=shape((sizes.piece_rows, LANES), bf16),
        compiler_params=params,
        name="pack",
    )(user_factor.T, item_factor.T, day_factor)
    pieces = swap_all([piece] * holders, "mp", holders)

    selector_shapes = []
    for t in range(3):
        flat = owners * sizes.slots[t]
        selector_shapes += [
            shape((flat, row_counts[t]), bf16),
            shape((row_counts[t], flat), bf16),
            shape((list_counts[t], flat), bf16),
            shape((flat, list_counts[t]), bf16),
        ]
    selectors = pl.pallas_call(
        functools.partial(slot_kernel, sizes),
        out_shape=tuple(selector_shapes),
        in_specs=[pl.BlockSpec(memory_space=pltpu.SMEM)]
        + [pl.BlockSpec(memory_space=pltpu.VMEM)] * owners,
        compiler_params=params,
        name="slots",
    )(lax.axis_index("dp").astype(jnp.int32).reshape(1), *lists)
    serves, sums, picks, places = (selectors[n::4] for n in range(4))

    served = pl.pallas_call(
        functools.partial(serve_kernel, sizes),
        out_shape=tuple([shape((sizes.slot_rows, sizes.rank), bf16)] * owners),
        compiler_params=params,
        name="serve",
    )(*pieces, *serves)
    arrived = swap_all(served, "dp", owners)

    whole = lambda a: pl.BlockSpec(a.shape, lambda s: (0,) * len(a.shape))
    inputs = [*arrived, *picks, *places]
    users, items, days = list_counts
    gradients = pl.pallas_call(
        functools.partial(block_kernel, sizes, DAYS_PER_STEP),
        out_shape=tuple(shape(a.shape, bf16) for a in arrived),
        grid=(days // DAYS_PER_STEP,),
        in_specs=[whole(a) for a in inputs]
        + [pl.BlockSpec((1, DAYS_PER_STEP, users, items), lambda s: (0, s, 0, 0))],
        out_specs=tuple(whole(a) for a in arrived),
        scratch_shapes=[
            pltpu.VMEM((users, sizes.rank), f32),
            pltpu.VMEM((items, sizes.rank), bf16),
            pltpu.VMEM((sizes.rank, items), bf16),
            pltpu.VMEM((days, sizes.rank), f32),
            pltpu.VMEM((users, sizes.rank), f32),
            pltpu.VMEM((items, sizes.rank), f32),
            pltpu.VMEM((days, sizes.rank), f32),
        ],
        compiler_params=params,
        name="block_gradients",
    )(*inputs, status)
    returned = swap_all(gradients, "dp", owners)

    totals = pl.pallas_call(
        functools.partial(sum_kernel, sizes),
        out_shape=tuple([shape(piece.shape, bf16)] * holders),
        compiler_params=params,
        name="row_sums",
    )(*returned, *sums)
    column_totals = swap_all(totals, "mp", holders)

    states = (
        user_factor.T,
        user_first.T,
        user_second.T,
        item_factor.T,
        item_first.T,
        item_second.T,
        day_factor,
        day_first,
        day_second,
    )
    updated = pl.pallas_call(
        functools.partial(adam_kernel, sizes),
        out_shape=tuple(shape(a.shape, a.dtype) for a in states),
        compiler_params=params,
        name="adam",
    )(*column_totals, *states)
    return tuple(a.T for a in updated[:6]) + tuple(updated[6:])


def solution(mesh):
    block = P(("dp", "mp"), None)
    piece = P("dp", "mp")
    return jax.shard_map(
        local,
        mesh=mesh,
        in_specs=(block, block, block, P(("dp", "mp"), None, None, None)) + (piece,) * 9,
        out_specs=(piece,) * 9,
        check_vma=False,
    )
```

time: 203 us -> 76.8 us (0.38)
  waiting for transfers between devices: 149 us -> 20.7 us
  starting transfers between devices: 0.08 us -> 28.2 us
  local copies, waits for them, and re-layouts: 21.4 us -> 4.99 us
  between operations: 14.1 us -> 0.84 us
  Pallas kernels: 17.3 us -> 21.5 us
    reduce_scatter x1 -> x0, waiting for transfers between devices: 94.5 us -> none  [local(): lax.psum_scatter(dense.reshape(owners * holders, packing.height, LANES),...]
    all_gather x1 -> x0, waiting for transfers between devices: 54.5 us -> none  [local(): lax.all_gather(packed, ('dp', 'mp'), axis=0)]
    ppermute x0 -> x27, starting transfers between devices: none -> 28.2 us  [swap_all(): lax.ppermute(arrays[s], axis, [(i, i ^ s) for i in range(size)])]
    ppermute x0 -> x27, waiting for transfers between devices: none -> 20.7 us  [swap_all(): lax.ppermute(arrays[s], axis, [(i, i ^ s) for i in range(size)])]
    pallas_call x6 -> x0, local copies, waits for them, and re-layouts: 9.22 us -> none  [local(): pl.pallas_call(functools.partial(adam_kernel, packing), out_shape=tuple((...]
    unnamed x22 -> x58, local copies, waits for them, and re-layouts: 9.83 us -> 4.33 us
    pallas_call x3 -> x6, Pallas kernels: 17.3 us -> 21.5 us  [the longest x1 11.6 us: local(): pl.pallas_call(functools.partial(block_kernel, sizes, DAYS_PER_STEP), out...]
    reshape x3 -> x0, local copies, waits for them, and re-layouts: 2.36 us -> none  [the longest x1 0.81 us: local(): items_list.reshape(item_count, 1)]
  transfers between devices with their start and end apart: 2 -> 27, of which waited for: 2 -> 16; matrix products, arithmetic and copies ran while one was open for 3% -> 3% of each run, Pallas kernels for 0% -> 3%
where the time goes in v2:
time: 76.8 us; the launch traced here: 76.2 us
  starting transfers between devices  28.2 us (37%)
  Pallas kernels  21.5 us (28%)
  waiting for transfers between devices  20.7 us (27%)
  local copies, waits for them, and re-layouts  4.99 us (6%)
  between operations  0.84 us (1%)
    ppermute x27, starting transfers between devices, swap_all(): lax.ppermute(arrays[s], axis, [(i, i ^ s) for i in range(size)])  28.2 us
    ppermute x27, waiting for transfers between devices, swap_all(): lax.ppermute(arrays[s], axis, [(i, i ^ s) for i in range(size)])  20.7 us
    pallas_call x1, Pallas kernels, local(): pl.pallas_call(functools.partial(block_kernel, sizes, DAYS_PER_STEP), out...  11.6 us
    unnamed x58, local copies, waits for them, and re-layouts  4.33 us
    pallas_call x1, Pallas kernels, local(): pl.pallas_call(functools.partial(slot_kernel, sizes), out_shape=tuple(sel...  2.56 us
    pallas_call x1, Pallas kernels, local(): pl.pallas_call(functools.partial(sum_kernel, sizes), out_shape=tuple([sha...  2.16 us
    pallas_call x1, Pallas kernels, local(): pl.pallas_call(functools.partial(serve_kernel, sizes), out_shape=tuple([s...  2.07 us
    pallas_call x1, Pallas kernels, local(): pl.pallas_call(functools.partial(adam_kernel, sizes), out_shape=tuple((sh...  1.66 us
  transfers between devices with their start and end apart: 27, of which 16 were waited for; matrix products, arithmetic and copies ran while one was open for 3% of the time, Pallas kernels for 3%

profile of v2, /device:TPU:0, one launch (start us, length us, event | category | flops | bytes accessed | tf_op | source)
XLA Modules:
  0.0 76.2 jit_solution(15565015998358309585)
XLA Ops:
  0.6 1.5 %pack.1.refs_0_ = bf16[144,128]{1,0:T(8,128)(2,1)} custom-call(f32[64,128]{1,0:T(8,128)} %bitcast.13, f32[64,128]{1,0:T(8,128)} %bitcast.15, f32[32,64]{1,0:T(8,128)} %refs_10_.1), custom_call_target="tpu_custom_call" | custom-call | tf_op jit(solution)/shard_map/pack/pallas_call | solution.py:277
  2.1 5.0 %collective-permute-start.2 = (bf16[144,128]{1,0:T(8,128)(2,1)}, bf16[144,128]{1,0:T(8,128)(2,1)S(1)}, u32[]{:S(2)}, u32[]{:S(2)}) collective-permute-start(bf16[144,128]{1,0:T(8,128)(2,1)} %pack.1.refs_0_), channel_id=1, source_target_pairs={{0,3},{1,2},{2,1},{3,0},{4,7},{5,6},{6,5},{7,4},{8,11},{9,10},{10,... | collective-permute-start | bytes 110600 | tf_op jit(solution)/shard_map/ppermute | solution.py:248
  7.7 0.7 constant_dynamic-update-slice_fusion.2
  8.4 0.7 constant_dynamic-update-slice_fusion.1
  9.7 1.3 %collective-permute-start.9 = (s32[1,544]{1,0:T(1,128)S(1)}, s32[1,544]{1,0:T(1,128)S(1)}, u32[]{:S(2)}, u32[]{:S(2)}) collective-permute-start(s32[1,544]{1,0:T(1,128)S(1)} %constant_dynamic-update-slice_fusion.refs_0_), channel_id=1, source_target_pairs={{0,28},{4,24},{8,20},{12,16},{16,12},{20,8},{24,4},{28,0},{1,29},{... | collective-permute-start | bytes 6536 | tf_op jit(solution)/shard_map/ppermute | solution.py:248
  11.1 1.4 %collective-permute-start.8 = (s32[1,544]{1,0:T(1,128)S(1)}, s32[1,544]{1,0:T(1,128)S(1)}, u32[]{:S(2)}, u32[]{:S(2)}) collective-permute-start(s32[1,544]{1,0:T(1,128)S(1)} %constant_dynamic-update-slice_fusion.refs_0_), channel_id=1, source_target_pairs={{0,24},{4,28},{8,16},{12,20},{16,8},{20,12},{24,0},{28,4},{1,25},{... | collective-permute-start | bytes 6536 | tf_op jit(solution)/shard_map/ppermute | solution.py:248
  12.4 1.2 %collective-permute-done.9.refs_7_ = s32[1,544]{1,0:T(1,128)S(1)} collective-permute-done((s32[1,544]{1,0:T(1,128)S(1)}, s32[1,544]{1,0:T(1,128)S(1)}, u32[]{:S(2)}, u32[]{:S(2)}) %collective-permute-start.9) | collective-permute-done | bytes 2208 | tf_op jit(solution)/shard_map/ppermute | solution.py:248
  14.1 1.5 %collective-permute-done.8.refs_6_ = s32[1,544]{1,0:T(1,128)S(1)} collective-permute-done((s32[1,544]{1,0:T(1,128)S(1)}, s32[1,544]{1,0:T(1,128)S(1)}, u32[]{:S(2)}, u32[]{:S(2)}) %collective-permute-start.8) | collective-permute-done | bytes 2208 | tf_op jit(solution)/shard_map/ppermute | solution.py:248
  16.7 1.4 %collective-permute-start.5 = (s32[1,544]{1,0:T(1,128)S(1)}, s32[1,544]{1,0:T(1,128)S(1)}, u32[]{:S(2)}, u32[]{:S(2)}) collective-permute-start(s32[1,544]{1,0:T(1,128)S(1)} %constant_dynamic-update-slice_fusion.refs_0_), channel_id=1, source_target_pairs={{0,12},{4,8},{8,4},{12,0},{16,28},{20,24},{24,20},{28,16},{1,13},{... | collective-permute-start | bytes 6536 | tf_op jit(solution)/shard_map/ppermute | solution.py:248
  18.1 1.0 %collective-permute-done.6.refs_4_ = s32[1,544]{1,0:T(1,128)S(1)} collective-permute-done((s32[1,544]{1,0:T(1,128)S(1)}, s32[1,544]{1,0:T(1,128)S(1)}, u32[]{:S(2)}, u32[]{:S(2)}) %collective-permute-start.6) | collective-permute-done | bytes 2208 | tf_op jit(solution)/shard_map/ppermute | solution.py:248
  19.8 2.9 %collective-permute-done.4.refs_2_ = s32[1,544]{1,0:T(1,128)S(1)} collective-permute-done((s32[1,544]{1,0:T(1,128)S(1)}, s32[1,544]{1,0:T(1,128)S(1)}, u32[]{:S(2)}, u32[]{:S(2)}) %collective-permute-start.4) | collective-permute-done | bytes 2208 | tf_op jit(solution)/shard_map/ppermute | solution.py:248
  23.3 2.6 %slots.1 = (bf16[384,128]{1,0:T(8,128)(2,1)}, bf16[128,384]{1,0:T(8,128)(2,1)}, bf16[256,384]{1,0:T(8,128)(2,1)}, bf16[384,256]{1,0:T(8,128)(2,1)}, bf16[384,128...) custom-call(s32[1]{0:T(128)} %bitcast.2.me_ref, ...), custom_call_target="tpu_custom_call" | custom-call | tf_op jit(solution)/shard_map/slots/pallas_call | solution.py:294
  26.6 2.1 %serve.1 = (bf16[112,256]{1,0:T(8,128)(2,1)}, bf16[112,256]{1,0:T(8,128)(2,1)}, bf16[112,256]{1,0:T(8,128)(2,1)}, bf16[112,256]{1,0:T(8,128)(2,1)}, bf16[112,256...) custom-call(bf16[144,128]{1,0:T(8,128)(2,1)} %pack.1.refs_0_, ...), custom_call_target="tpu_custom_call" | custom-call | tf_op jit(solution)/shard_map/serve/pallas_call | solution.py:304
  29.2 1.3 %collective-permute-start.12 = (bf16[112,256]{1,0:T(8,128)(2,1)}, bf16[112,256]{1,0:T(8,128)(2,1)S(1)}, u32[]{:S(2)}, u32[]{:S(2)}) collective-permute-start(bf16[112,256]{1,0:T(8,128)(2,1)} %get-tuple-element.56), channel_id=1, source_target_pairs={{0,12},{4,8},{8,4},{12,0},{16,28},{20,24},{24,20},{28,16},{1,13},{... | collective-permute-start | bytes 172040 | tf_op jit(solution)/shard_map/ppermute | solution.py:248
  31.0 1.2 %collective-permute-start.14 = (bf16[112,256]{1,0:T(8,128)(2,1)}, bf16[112,256]{1,0:T(8,128)(2,1)S(1)}, u32[]{:S(2)}, u32[]{:S(2)}) collective-permute-start(bf16[112,256]{1,0:T(8,128)(2,1)} %get-tuple-element.58), channel_id=1, source_target_pairs={{0,20},{4,16},{8,28},{12,24},{16,4},{20,0},{24,12},{28,8},{1,21},{... | collective-permute-start | bytes 172040 | tf_op jit(solution)/shard_map/ppermute | solution.py:248
  32.2 1.4 %collective-permute-start.15 = (bf16[112,256]{1,0:T(8,128)(2,1)}, bf16[112,256]{1,0:T(8,128)(2,1)S(1)}, u32[]{:S(2)}, u32[]{:S(2)}) collective-permute-start(bf16[112,256]{1,0:T(8,128)(2,1)} %get-tuple-element.59), channel_id=1, source_target_pairs={{0,24},{4,28},{8,16},{12,20},{16,8},{20,12},{24,0},{28,4},{1,25},{... | collective-permute-start | bytes 172040 | tf_op jit(solution)/shard_map/ppermute | solution.py:248
  33.6 1.3 %collective-permute-start.16 = (bf16[112,256]{1,0:T(8,128)(2,1)}, bf16[112,256]{1,0:T(8,128)(2,1)S(1)}, u32[]{:S(2)}, u32[]{:S(2)}) collective-permute-start(bf16[112,256]{1,0:T(8,128)(2,1)} %get-tuple-element.60), channel_id=1, source_target_pairs={{0,28},{4,24},{8,20},{12,16},{16,12},{20,8},{24,4},{28,0},{1,29},{... | collective-permute-start | bytes 172040 | tf_op jit(solution)/shard_map/ppermute | solution.py:248
  35.5 2.1 %collective-permute-done.15.refs_6_ = bf16[112,256]{1,0:T(8,128)(2,1)S(1)} collective-permute-done((bf16[112,256]{1,0:T(8,128)(2,1)}, bf16[112,256]{1,0:T(8,128)(2,1)S(1)}, u32[]{:S(2)}, u32[]{:S(2)}) %collective-permute-start.15) | collective-permute-done | bytes 57376 | tf_op jit(solution)/shard_map/ppermute | solution.py:248
  37.6 1.1 %collective-permute-done.16.refs_7_ = bf16[112,256]{1,0:T(8,128)(2,1)S(1)} collective-permute-done((bf16[112,256]{1,0:T(8,128)(2,1)}, bf16[112,256]{1,0:T(8,128)(2,1)S(1)}, u32[]{:S(2)}, u32[]{:S(2)}) %collective-permute-start.16) | collective-permute-done | bytes 57376 | tf_op jit(solution)/shard_map/ppermute | solution.py:248
  39.3 11.6 %block_gradients.1 = (bf16[112,256]{1,0:T(8,128)(2,1)}, bf16[112,256]{1,0:T(8,128)(2,1)}, bf16[112,256]{1,0:T(8,128)(2,1)}, bf16[112,256]{1,0:T(8,128)(2,1)}, bf...) custom-call(bf16[112,256]{1,0:T(8,128)(2,1)} %get-tuple-element.53.refs_, ...), custom_call_target="tpu_custom_call" | custom-call | tf_op jit(solution)/shard_map/block_gradients/pallas_call | solution.py:315
  51.7 1.1 %collective-permute-start.19 = (bf16[112,256]{1,0:T(8,128)(2,1)}, bf16[112,256]{1,0:T(8,128)(2,1)S(1)}, u32[]{:S(2)}, u32[]{:S(2)}) collective-permute-start(bf16[112,256]{1,0:T(8,128)(2,1)} %get-tuple-element.70), channel_id=1, source_target_pairs={{0,12},{4,8},{8,4},{12,0},{16,28},{20,24},{24,20},{28,16},{1,13},{... | collective-permute-start | bytes 172040 | tf_op jit(solution)/shard_map/ppermute | solution.py:248
  53.4 1.2 %collective-permute-start.21 = (bf16[112,256]{1,0:T(8,128)(2,1)}, bf16[112,256]{1,0:T(8,128)(2,1)S(1)}, u32[]{:S(2)}, u32[]{:S(2)}) collective-permute-start(bf16[112,256]{1,0:T(8,128)(2,1)} %get-tuple-element.72), channel_id=1, source_target_pairs={{0,20},{4,16},{8,28},{12,24},{16,4},{20,0},{24,12},{28,8},{1,21},{... | collective-permute-start | bytes 172040 | tf_op jit(solution)/shard_map/ppermute | solution.py:248
  54.6 1.5 %collective-permute-start.22 = (bf16[112,256]{1,0:T(8,128)(2,1)}, bf16[112,256]{1,0:T(8,128)(2,1)S(1)}, u32[]{:S(2)}, u32[]{:S(2)}) collective-permute-start(bf16[112,256]{1,0:T(8,128)(2,1)} %get-tuple-element.73), channel_id=1, source_target_pairs={{0,24},{4,28},{8,16},{12,20},{16,8},{20,12},{24,0},{28,4},{1,25},{... | collective-permute-start | bytes 172040 | tf_op jit(solution)/shard_map/ppermute | solution.py:248
  56.1 1.1 %collective-permute-start.23 = (bf16[112,256]{1,0:T(8,128)(2,1)}, bf16[112,256]{1,0:T(8,128)(2,1)S(1)}, u32[]{:S(2)}, u32[]{:S(2)}) collective-permute-start(bf16[112,256]{1,0:T(8,128)(2,1)} %get-tuple-element.74), channel_id=1, source_target_pairs={{0,28},{4,24},{8,20},{12,16},{16,12},{20,8},{24,4},{28,0},{1,29},{... | collective-permute-start | bytes 172040 | tf_op jit(solution)/shard_map/ppermute | solution.py:248
  58.1 1.8 %collective-permute-done.22.refs_6_ = bf16[112,256]{1,0:T(8,128)(2,1)S(1)} collective-permute-done((bf16[112,256]{1,0:T(8,128)(2,1)}, bf16[112,256]{1,0:T(8,128)(2,1)S(1)}, u32[]{:S(2)}, u32[]{:S(2)}) %collective-permute-start.22) | collective-permute-done | bytes 57376 | tf_op jit(solution)/shard_map/ppermute | solution.py:248
  59.9 1.2 %collective-permute-done.23.refs_7_ = bf16[112,256]{1,0:T(8,128)(2,1)S(1)} collective-permute-done((bf16[112,256]{1,0:T(8,128)(2,1)}, bf16[112,256]{1,0:T(8,128)(2,1)S(1)}, u32[]{:S(2)}, u32[]{:S(2)}) %collective-permute-start.23) | collective-permute-done | bytes 57376 | tf_op jit(solution)/shard_map/ppermute | solution.py:248
  61.7 2.2 %row_sums.1 = (bf16[144,128]{1,0:T(8,128)(2,1)}, bf16[144,128]{1,0:T(8,128)(2,1)}, bf16[144,128]{1,0:T(8,128)(2,1)}, bf16[144,128]{1,0:T(8,128)(2,1)}) custom-call(bf16[112,256]{1,0:T(8,128)(2,1)} %get-tuple-element.67.refs_0_, bf16[112,256]{1,0:T(8,128)(2,1)} %copy-done, bf16[112,256]{1,0:T(8,128)(2,1)} %copy-done.1, bf16[112,256]{1,0:T(8,128)(2,1)} %copy-done.2, ...), custom_call_target="tpu_custom_call" | custom-call | tf_op jit(solution)/shard_map/row_sums/pallas_call | solution.py:336
  63.9 1.7 %collective-permute-start.24 = (bf16[144,128]{1,0:T(8,128)(2,1)}, bf16[144,128]{1,0:T(8,128)(2,1)S(1)}, u32[]{:S(2)}, u32[]{:S(2)}) collective-permute-start(bf16[144,128]{1,0:T(8,128)(2,1)} %get-tuple-element.79), channel_id=1, source_target_pairs={{0,1},{1,0},{2,3},{3,2},{4,5},{5,4},{6,7},{7,6},{8,9},{9,8},{10,11... | collective-permute-start | bytes 110600 | tf_op jit(solution)/shard_map/ppermute | solution.py:248
  65.6 2.4 %collective-permute-start.25 = (bf16[144,128]{1,0:T(8,128)(2,1)}, bf16[144,128]{1,0:T(8,128)(2,1)S(1)}, u32[]{:S(2)}, u32[]{:S(2)}) collective-permute-start(bf16[144,128]{1,0:T(8,128)(2,1)} %get-tuple-element.80), channel_id=1, source_target_pairs={{0,2},{1,3},{2,0},{3,1},{4,6},{5,7},{6,4},{7,5},{8,10},{9,11},{10,... | collective-permute-start | bytes 110600 | tf_op jit(solution)/shard_map/ppermute | solution.py:248
  68.3 3.0 %collective-permute-done.25.refs_2_ = bf16[144,128]{1,0:T(8,128)(2,1)S(1)} collective-permute-done((bf16[144,128]{1,0:T(8,128)(2,1)}, bf16[144,128]{1,0:T(8,128)(2,1)S(1)}, u32[]{:S(2)}, u32[]{:S(2)}) %collective-permute-start.25) | collective-permute-done | bytes 36896 | tf_op jit(solution)/shard_map/ppermute | solution.py:248
  71.3 2.7 %collective-permute-done.26.refs_3_ = bf16[144,128]{1,0:T(8,128)(2,1)S(1)} collective-permute-done((bf16[144,128]{1,0:T(8,128)(2,1)}, bf16[144,128]{1,0:T(8,128)(2,1)S(1)}, u32[]{:S(2)}, u32[]{:S(2)}) %collective-permute-start.26) | collective-permute-done | bytes 36896 | tf_op jit(solution)/shard_map/ppermute | solution.py:248
  74.6 1.7 %adam.1 = (f32[64,128]{1,0:T(8,128)}, f32[64,128]{1,0:T(8,128)}, f32[64,128]{1,0:T(8,128)}, f32[64,128]{1,0:T(8,128)}, f32[64,128]{1,0:T(8,128)}, /*index=5*/f32...) custom-call(bf16[144,128]{1,0:T(8,128)(2,1)} %get-tuple-element.78.refs_0_, ...), custom_call_target="tpu_custom_call" | custom-call | tf_op jit(solution)/shard_map/adam/pallas_call | solution.py:355
  (87 shorter events, 10.7 us)
Async XLA Ops:
  2.1 23.8 %collective-permute-start.2 = (bf16[144,128]{1,0:T(8,128)(2,1)}, bf16[144,128]{1,0:T(8,128)(2,1)S(1)}, u32[]{:S(2)}, u32[]{:S(2)}) collective-permute-start(bf16[144,128]{1,0:T(8,128)(2,1)} %pack.1.refs_0_), channel_id=1, source_target_pairs={{0,3},{1,2},{2,1},{3,0},{4,7},{5,6},{6,5},{7,4},{8,11},{9,10},{10,... | collective-permute-start | bytes 110600 | tf_op jit(solution)/shard_map/ppermute | solution.py:248
  7.1 18.8 %collective-permute-start.1 = (bf16[144,128]{1,0:T(8,128)(2,1)}, bf16[144,128]{1,0:T(8,128)(2,1)S(1)}, u32[]{:S(2)}, u32[]{:S(2)}) collective-permute-start(bf16[144,128]{1,0:T(8,128)(2,1)} %pack.1.refs_0_), channel_id=1, source_target_pairs={{0,2},{1,3},{2,0},{3,1},{4,6},{5,7},{6,4},{7,5},{8,10},{9,11},{10,... | collective-permute-start | bytes 110600 | tf_op jit(solution)/shard_map/ppermute | solution.py:248
  7.2 18.8 %collective-permute-start = (bf16[144,128]{1,0:T(8,128)(2,1)}, bf16[144,128]{1,0:T(8,128)(2,1)S(1)}, u32[]{:S(2)}, u32[]{:S(2)}) collective-permute-start(bf16[144,128]{1,0:T(8,128)(2,1)} %pack.1.refs_0_), channel_id=1, source_target_pairs={{0,1},{1,0},{2,3},{3,2},{4,5},{5,4},{6,7},{7,6},{8,9},{9,8},{10,11... | collective-permute-start | bytes 110600 | tf_op jit(solution)/shard_map/ppermute | solution.py:248
  9.7 13.0 %copy-start.20 = (s32[1,544]{1,0:T(1,128)}, s32[1,544]{1,0:T(1,128)S(1)}, u32[]{:S(2)}) copy-start(s32[1,544]{1,0:T(1,128)S(1)} %constant_dynamic-update-slice_fusion.refs_0_) | copy-start | bytes 6532
  9.7 3.9 %collective-permute-start.9 = (s32[1,544]{1,0:T(1,128)S(1)}, s32[1,544]{1,0:T(1,128)S(1)}, u32[]{:S(2)}, u32[]{:S(2)}) collective-permute-start(s32[1,544]{1,0:T(1,128)S(1)} %constant_dynamic-update-slice_fusion.refs_0_), channel_id=1, source_target_pairs={{0,28},{4,24},{8,20},{12,16},{16,12},{20,8},{24,4},{28,0},{1,29},{... | collective-permute-start | bytes 6536 | tf_op jit(solution)/shard_map/ppermute | solution.py:248
  11.1 4.5 %collective-permute-start.8 = (s32[1,544]{1,0:T(1,128)S(1)}, s32[1,544]{1,0:T(1,128)S(1)}, u32[]{:S(2)}, u32[]{:S(2)}) collective-permute-start(s32[1,544]{1,0:T(1,128)S(1)} %constant_dynamic-update-slice_fusion.refs_0_), channel_id=1, source_target_pairs={{0,24},{4,28},{8,16},{12,20},{16,8},{20,12},{24,0},{28,4},{1,25},{... | collective-permute-start | bytes 6536 | tf_op jit(solution)/shard_map/ppermute | solution.py:248
  13.7 9.1 %copy-start.21 = (s32[1,544]{1,0:T(1,128)}, s32[1,544]{1,0:T(1,128)S(1)}, u32[]{:S(2)}) copy-start(s32[1,544]{1,0:T(1,128)S(1)} %collective-permute-done.9.refs_7_) | copy-start | bytes 6532
  13.7 3.0 %collective-permute-start.7 = (s32[1,544]{1,0:T(1,128)S(1)}, s32[1,544]{1,0:T(1,128)S(1)}, u32[]{:S(2)}, u32[]{:S(2)}) collective-permute-start(s32[1,544]{1,0:T(1,128)S(1)} %constant_dynamic-update-slice_fusion.refs_0_), channel_id=1, source_target_pairs={{0,20},{4,16},{8,28},{12,24},{16,4},{20,0},{24,12},{28,8},{1,21},{... | collective-permute-start | bytes 6536 | tf_op jit(solution)/shard_map/ppermute | solution.py:248
  15.6 7.2 %copy-start.22 = (s32[1,544]{1,0:T(1,128)}, s32[1,544]{1,0:T(1,128)S(1)}, u32[]{:S(2)}) copy-start(s32[1,544]{1,0:T(1,128)S(1)} %collective-permute-done.8.refs_6_) | copy-start | bytes 6532
  15.6 3.6 %collective-permute-start.6 = (s32[1,544]{1,0:T(1,128)S(1)}, s32[1,544]{1,0:T(1,128)S(1)}, u32[]{:S(2)}, u32[]{:S(2)}) collective-permute-start(s32[1,544]{1,0:T(1,128)S(1)} %constant_dynamic-update-slice_fusion.refs_0_), channel_id=1, source_target_pairs={{0,16},{4,20},{8,24},{12,28},{16,0},{20,4},{24,8},{28,12},{1,17},{... | collective-permute-start | bytes 6536 | tf_op jit(solution)/shard_map/ppermute | solution.py:248
  16.7 3.0 %collective-permute-start.5 = (s32[1,544]{1,0:T(1,128)S(1)}, s32[1,544]{1,0:T(1,128)S(1)}, u32[]{:S(2)}, u32[]{:S(2)}) collective-permute-start(s32[1,544]{1,0:T(1,128)S(1)} %constant_dynamic-update-slice_fusion.refs_0_), channel_id=1, source_target_pairs={{0,12},{4,8},{8,4},{12,0},{16,28},{20,24},{24,20},{28,16},{1,13},{... | collective-permute-start | bytes 6536 | tf_op jit(solution)/shard_map/ppermute | solution.py:248
  19.2 3.6 %collective-permute-start.4 = (s32[1,544]{1,0:T(1,128)S(1)}, s32[1,544]{1,0:T(1,128)S(1)}, u32[]{:S(2)}, u32[]{:S(2)}) collective-permute-start(s32[1,544]{1,0:T(1,128)S(1)} %constant_dynamic-update-slice_fusion.refs_0_), channel_id=1, source_target_pairs={{0,8},{4,12},{8,0},{12,4},{16,24},{20,28},{24,16},{28,20},{1,9},{5... | collective-permute-start | bytes 6536 | tf_op jit(solution)/shard_map/ppermute | solution.py:248
  19.7 3.1 %collective-permute-start.3 = (s32[1,544]{1,0:T(1,128)S(1)}, s32[1,544]{1,0:T(1,128)S(1)}, u32[]{:S(2)}, u32[]{:S(2)}) collective-permute-start(s32[1,544]{1,0:T(1,128)S(1)} %constant_dynamic-update-slice_fusion.refs_0_), channel_id=1, source_target_pairs={{0,4},{4,0},{8,12},{12,8},{16,20},{20,16},{24,28},{28,24},{1,5},{5... | collective-permute-start | bytes 6536 | tf_op jit(solution)/shard_map/ppermute | solution.py:248
  28.6 3.6 %collective-permute-start.10 = (bf16[112,256]{1,0:T(8,128)(2,1)}, bf16[112,256]{1,0:T(8,128)(2,1)S(1)}, u32[]{:S(2)}, u32[]{:S(2)}) collective-permute-start(bf16[112,256]{1,0:T(8,128)(2,1)} %get-tuple-element.54), channel_id=1, source_target_pairs={{0,4},{4,0},{8,12},{12,8},{16,20},{20,16},{24,28},{28,24},{1,5},{5... | collective-permute-start | bytes 172040 | tf_op jit(solution)/shard_map/ppermute | solution.py:248
  28.6 5.0 %collective-permute-start.11 = (bf16[112,256]{1,0:T(8,128)(2,1)}, bf16[112,256]{1,0:T(8,128)(2,1)S(1)}, u32[]{:S(2)}, u32[]{:S(2)}) collective-permute-start(bf16[112,256]{1,0:T(8,128)(2,1)} %get-tuple-element.55), channel_id=1, source_target_pairs={{0,8},{4,12},{8,0},{12,4},{16,24},{20,28},{24,16},{28,20},{1,9},{5... | collective-permute-start | bytes 172040 | tf_op jit(solution)/shard_map/ppermute | solution.py:248
  29.2 5.7 %collective-permute-start.12 = (bf16[112,256]{1,0:T(8,128)(2,1)}, bf16[112,256]{1,0:T(8,128)(2,1)S(1)}, u32[]{:S(2)}, u32[]{:S(2)}) collective-permute-start(bf16[112,256]{1,0:T(8,128)(2,1)} %get-tuple-element.56), channel_id=1, source_target_pairs={{0,12},{4,8},{8,4},{12,0},{16,28},{20,24},{24,20},{28,16},{1,13},{... | collective-permute-start | bytes 172040 | tf_op jit(solution)/shard_map/ppermute | solution.py:248
  30.5 4.9 %collective-permute-start.13 = (bf16[112,256]{1,0:T(8,128)(2,1)}, bf16[112,256]{1,0:T(8,128)(2,1)S(1)}, u32[]{:S(2)}, u32[]{:S(2)}) collective-permute-start(bf16[112,256]{1,0:T(8,128)(2,1)} %get-tuple-element.57), channel_id=1, source_target_pairs={{0,16},{4,20},{8,24},{12,28},{16,0},{20,4},{24,8},{28,12},{1,17},{... | collective-permute-start | bytes 172040 | tf_op jit(solution)/shard_map/ppermute | solution.py:248
  31.0 4.5 %collective-permute-start.14 = (bf16[112,256]{1,0:T(8,128)(2,1)}, bf16[112,256]{1,0:T(8,128)(2,1)S(1)}, u32[]{:S(2)}, u32[]{:S(2)}) collective-permute-start(bf16[112,256]{1,0:T(8,128)(2,1)} %get-tuple-element.58), channel_id=1, source_target_pairs={{0,20},{4,16},{8,28},{12,24},{16,4},{20,0},{24,12},{28,8},{1,21},{... | collective-permute-start | bytes 172040 | tf_op jit(solution)/shard_map/ppermute | solution.py:248
  32.2 6.5 %copy-start.7 = (bf16[112,256]{1,0:T(8,128)(2,1)}, bf16[112,256]{1,0:T(8,128)(2,1)S(1)}, u32[]{:S(2)}) copy-start(bf16[112,256]{1,0:T(8,128)(2,1)S(1)} %collective-permute-done.10.refs_1_) | copy-start | bytes 172036
  32.2 5.4 %collective-permute-start.15 = (bf16[112,256]{1,0:T(8,128)(2,1)}, bf16[112,256]{1,0:T(8,128)(2,1)S(1)}, u32[]{:S(2)}, u32[]{:S(2)}) collective-permute-start(bf16[112,256]{1,0:T(8,128)(2,1)} %get-tuple-element.59), channel_id=1, source_target_pairs={{0,24},{4,28},{8,16},{12,20},{16,8},{20,12},{24,0},{28,4},{1,25},{... | collective-permute-start | bytes 172040 | tf_op jit(solution)/shard_map/ppermute | solution.py:248
  33.6 5.0 %collective-permute-start.16 = (bf16[112,256]{1,0:T(8,128)(2,1)}, bf16[112,256]{1,0:T(8,128)(2,1)S(1)}, u32[]{:S(2)}, u32[]{:S(2)}) collective-permute-start(bf16[112,256]{1,0:T(8,128)(2,1)} %get-tuple-element.60), channel_id=1, source_target_pairs={{0,28},{4,24},{8,20},{12,16},{16,12},{20,8},{24,4},{28,0},{1,29},{... | collective-permute-start | bytes 172040 | tf_op jit(solution)/shard_map/ppermute | solution.py:248
  50.9 3.7 %collective-permute-start.17 = (bf16[112,256]{1,0:T(8,128)(2,1)}, bf16[112,256]{1,0:T(8,128)(2,1)S(1)}, u32[]{:S(2)}, u32[]{:S(2)}) collective-permute-start(bf16[112,256]{1,0:T(8,128)(2,1)} %get-tuple-element.68), channel_id=1, source_target_pairs={{0,4},{4,0},{8,12},{12,8},{16,20},{20,16},{24,28},{28,24},{1,5},{5... | collective-permute-start | bytes 172040 | tf_op jit(solution)/shard_map/ppermute | solution.py:248
  51.1 5.0 %collective-permute-start.18 = (bf16[112,256]{1,0:T(8,128)(2,1)}, bf16[112,256]{1,0:T(8,128)(2,1)S(1)}, u32[]{:S(2)}, u32[]{:S(2)}) collective-permute-start(bf16[112,256]{1,0:T(8,128)(2,1)} %get-tuple-element.69), channel_id=1, source_target_pairs={{0,8},{4,12},{8,0},{12,4},{16,24},{20,28},{24,16},{28,20},{1,9},{5... | collective-permute-start | bytes 172040 | tf_op jit(solution)/shard_map/ppermute | solution.py:248
  51.7 5.5 %collective-permute-start.19 = (bf16[112,256]{1,0:T(8,128)(2,1)}, bf16[112,256]{1,0:T(8,128)(2,1)S(1)}, u32[]{:S(2)}, u32[]{:S(2)}) collective-permute-start(bf16[112,256]{1,0:T(8,128)(2,1)} %get-tuple-element.70), channel_id=1, source_target_pairs={{0,12},{4,8},{8,4},{12,0},{16,28},{20,24},{24,20},{28,16},{1,13},{... | collective-permute-start | bytes 172040 | tf_op jit(solution)/shard_map/ppermute | solution.py:248
  52.8 4.9 %collective-permute-start.20 = (bf16[112,256]{1,0:T(8,128)(2,1)}, bf16[112,256]{1,0:T(8,128)(2,1)S(1)}, u32[]{:S(2)}, u32[]{:S(2)}) collective-permute-start(bf16[112,256]{1,0:T(8,128)(2,1)} %get-tuple-element.71), channel_id=1, source_target_pairs={{0,16},{4,20},{8,24},{12,28},{16,0},{20,4},{24,8},{28,12},{1,17},{... | collective-permute-start | bytes 172040 | tf_op jit(solution)/shard_map/ppermute | solution.py:248
  53.4 4.6 %collective-permute-start.21 = (bf16[112,256]{1,0:T(8,128)(2,1)}, bf16[112,256]{1,0:T(8,128)(2,1)S(1)}, u32[]{:S(2)}, u32[]{:S(2)}) collective-permute-start(bf16[112,256]{1,0:T(8,128)(2,1)} %get-tuple-element.72), channel_id=1, source_target_pairs={{0,20},{4,16},{8,28},{12,24},{16,4},{20,0},{24,12},{28,8},{1,21},{... | collective-permute-start | bytes 172040 | tf_op jit(solution)/shard_map/ppermute | solution.py:248
  54.6 6.5 %copy-start = (bf16[112,256]{1,0:T(8,128)(2,1)}, bf16[112,256]{1,0:T(8,128)(2,1)S(1)}, u32[]{:S(2)}) copy-start(bf16[112,256]{1,0:T(8,128)(2,1)S(1)} %collective-permute-done.17.refs_1_) | copy-start | bytes 172036
  54.6 5.3 %collective-permute-start.22 = (bf16[112,256]{1,0:T(8,128)(2,1)}, bf16[112,256]{1,0:T(8,128)(2,1)S(1)}, u32[]{:S(2)}, u32[]{:S(2)}) collective-permute-start(bf16[112,256]{1,0:T(8,128)(2,1)} %get-tuple-element.73), channel_id=1, source_target_pairs={{0,24},{4,28},{8,16},{12,20},{16,8},{20,12},{24,0},{28,4},{1,25},{... | collective-permute-start | bytes 172040 | tf_op jit(solution)/shard_map/ppermute | solution.py:248
  56.1 5.0 %collective-permute-start.23 = (bf16[112,256]{1,0:T(8,128)(2,1)}, bf16[112,256]{1,0:T(8,128)(2,1)S(1)}, u32[]{:S(2)}, u32[]{:S(2)}) collective-permute-start(bf16[112,256]{1,0:T(8,128)(2,1)} %get-tuple-element.74), channel_id=1, source_target_pairs={{0,28},{4,24},{8,20},{12,16},{16,12},{20,8},{24,4},{28,0},{1,29},{... | collective-permute-start | bytes 172040 | tf_op jit(solution)/shard_map/ppermute | solution.py:248
  63.9 4.4 %collective-permute-start.24 = (bf16[144,128]{1,0:T(8,128)(2,1)}, bf16[144,128]{1,0:T(8,128)(2,1)S(1)}, u32[]{:S(2)}, u32[]{:S(2)}) collective-permute-start(bf16[144,128]{1,0:T(8,128)(2,1)} %get-tuple-element.79), channel_id=1, source_target_pairs={{0,1},{1,0},{2,3},{3,2},{4,5},{5,4},{6,7},{7,6},{8,9},{9,8},{10,11... | collective-permute-start | bytes 110600 | tf_op jit(solution)/shard_map/ppermute | solution.py:248
  65.6 5.7 %collective-permute-start.25 = (bf16[144,128]{1,0:T(8,128)(2,1)}, bf16[144,128]{1,0:T(8,128)(2,1)S(1)}, u32[]{:S(2)}, u32[]{:S(2)}) collective-permute-start(bf16[144,128]{1,0:T(8,128)(2,1)} %get-tuple-element.80), channel_id=1, source_target_pairs={{0,2},{1,3},{2,0},{3,1},{4,6},{5,7},{6,4},{7,5},{8,10},{9,11},{10,... | collective-permute-start | bytes 110600 | tf_op jit(solution)/shard_map/ppermute | solution.py:248
  68.0 6.0 %collective-permute-start.26 = (bf16[144,128]{1,0:T(8,128)(2,1)}, bf16[144,128]{1,0:T(8,128)(2,1)S(1)}, u32[]{:S(2)}, u32[]{:S(2)}) collective-permute-start(bf16[144,128]{1,0:T(8,128)(2,1)} %get-tuple-element.81), channel_id=1, source_target_pairs={{0,3},{1,2},{2,1},{3,0},{4,7},{5,6},{6,5},{7,4},{8,11},{9,10},{10,... | collective-permute-start | bytes 110600 | tf_op jit(solution)/shard_map/ppermute | solution.py:248
  (23 other events, 58.9 us)

commit v3 on v2

v3 whole, which is shorter than its diff:
```python
import functools

import jax
import jax.numpy as jnp
from jax import lax
from jax.experimental import pallas as pl
from jax.experimental.pallas import tpu as pltpu
from jax.sharding import PartitionSpec as P

beta_one = 0.9
beta_two = 0.99
bias_one = 1.0 - 0.9**10
bias_two = 1.0 - 0.99**10
learn_rate = 0.01
epsilon = 1e-08
loss_scale = 0.0625

LANES = 128
DAYS_PER_STEP = 4
SMALL_VMEM = 16 * 1024 * 1024
BLOCK_VMEM = 32 * 1024 * 1024

f32 = jnp.float32
bf16 = jnp.bfloat16


class Sizes:
    def __init__(self, owners, holders, columns, row_counts, list_counts):
        self.owners = owners
        self.holders = holders
        self.columns = columns
        self.rank = columns * holders
        self.row_counts = row_counts
        self.list_counts = list_counts
        limits = (
            max(2, 3 * list_counts[0] // (2 * owners)),
            max(2, 3 * list_counts[1] // (2 * owners)),
            max(2, 2 * list_counts[2] // owners),
        )
        self.slots = tuple(-(-(limit + t // 2) // 16) * 16 for t, limit in enumerate(limits))
        self.note_row = limits[2]
        self.slot_starts = (0, self.slots[0], self.slots[0] + self.slots[1])
        self.slot_rows = sum(self.slots)
        self.day_parts = LANES // columns
        self.day_packed = -(-(row_counts[2] // self.day_parts) // 16) * 16
        self.piece_rows = 2 * columns + self.day_packed
        self.day_chunks = self.rank // LANES
        self.table_rows = 2 * self.rank + self.day_chunks * row_counts[2]


def iota(shape, dimension):
    return lax.broadcasted_iota(jnp.int32, shape, dimension)


def onehot(condition):
    return jnp.where(condition, 1.0, 0.0).astype(bf16)


def dot_nt(a, b):
    return lax.dot_general(a, b, (((1,), (1,)), ((), ())), preferred_element_type=f32)


def pack_days(sizes, days):
    rows = sizes.row_counts[2] // sizes.day_parts
    parts = [days[p * rows : (p + 1) * rows] for p in range(sizes.day_parts)]
    if rows != sizes.day_packed:
        blank = jnp.zeros((sizes.day_packed - rows, days.shape[1]), days.dtype)
        parts = [jnp.concatenate([part, blank], axis=0) for part in parts]
    return jnp.concatenate(parts, axis=1)


def unpack_days(sizes, packed):
    rows = sizes.row_counts[2] // sizes.day_parts
    return jnp.concatenate(
        [
            packed[:rows, p * sizes.columns : (p + 1) * sizes.columns]
            for p in range(sizes.day_parts)
        ],
        axis=0,
    )


def pack_kernel(sizes, user_ref, item_ref, day_ref, out_ref):
    columns = sizes.columns
    out_ref[:columns, :] = user_ref[...].astype(bf16)
    out_ref[columns : 2 * columns, :] = item_ref[...].astype(bf16)
    out_ref[2 * columns :, :] = pack_days(sizes, day_ref[...]).astype(bf16)


def slot_kernel(sizes, me_ref, *refs):
    owners = sizes.owners
    lists, picks, places, note_ref = refs[:3], refs[3:6], refs[6:9], refs[9]
    me = me_ref[0]
    notes = [[] for _ in range(owners)]
    for t in range(3):
        count, rows, slots = sizes.list_counts[t], sizes.row_counts[t], sizes.slots[t]
        number = lists[t][...]
        owner = number // rows
        row = number % rows
        partner = lax.bitwise_xor(owner, jnp.full_like(owner, me))
        picks[t][...] = onehot(iota((owners * rows, count), 0) == partner * rows + row)
        earlier = onehot(iota((count, count), 0) < iota((count, count), 1))
        owner_hot = iota((owners, count), 0) == owner
        before = jnp.dot(onehot(owner_hot), earlier, preferred_element_type=f32)
        position = jnp.sum(jnp.where(owner_hot, before, 0.0), axis=0, keepdims=True)
        target = partner * slots + position.astype(jnp.int32)
        place = onehot(iota((owners * slots, count), 0) == target)
        places[t][...] = place
        following = (row + 1).astype(bf16)
        for s in range(owners):
            notes[s].append(dot_nt(following, place[s * slots : (s + 1) * slots]) - 1.0)
    blank = jnp.full((1, sizes.rank - sizes.slot_rows), -1.0, f32)
    note_ref[...] = jnp.concatenate(
        [jnp.concatenate(note + [blank], axis=1) for note in notes], axis=0
    )


def table_kernel(sizes, *refs):
    pieces, out_ref = refs[:-1], refs[-1]
    columns, rank, day_rows = sizes.columns, sizes.rank, sizes.row_counts[2]
    for j, ref in enumerate(pieces):
        for t in range(2):
            out_ref[t * rank + j * columns : t * rank + (j + 1) * columns, :] = ref[
                t * columns : (t + 1) * columns, :
            ]
    days = jnp.concatenate(
        [unpack_days(sizes, ref[2 * columns :, :].astype(f32)) for ref in pieces], axis=1
    ).astype(bf16)
    for chunk in range(sizes.day_chunks):
        start = 2 * rank + chunk * day_rows
        out_ref[start : start + day_rows, :] = days[:, chunk * LANES : (chunk + 1) * LANES]


def block_kernel(sizes, days_per_step, *refs):
    owners, rank, day_rows = sizes.owners, sizes.rank, sizes.row_counts[2]
    tables = refs[:owners]
    picks = refs[owners : owners + 3]
    places = refs[owners + 3 : owners + 6]
    note_ref, status_ref = refs[owners + 6 : owners + 8]
    outs = refs[owners + 8 : 2 * owners + 8]
    users, items, items_half_t, days, user_gradient, item_gradient, day_gradient = refs[
        2 * owners + 8 :
    ]
    step = pl.program_id(0)

    def pick(t):
        table = jnp.concatenate([ref[t * rank : (t + 1) * rank, :] for ref in tables], axis=1)
        return jnp.dot(table, picks[t][...], preferred_element_type=f32)

    @pl.when(step == 0)
    def _():
        users[...] = pick(0).T
        items_t = pick(1)
        items[...] = items_t.T.astype(bf16)
        items_half_t[...] = (0.5 * items_t).astype(bf16)
        starts = [2 * rank + chunk * day_rows for chunk in range(sizes.day_chunks)]
        day_table = jnp.concatenate(
            [
                jnp.concatenate([ref[start : start + day_rows, :] for start in starts], axis=1)
                for ref in tables
            ],
            axis=0,
        )
        days[...] = lax.dot_general(
            picks[2][...], day_table, (((0,), (0,)), ((), ())), preferred_element_type=f32
        )
        user_gradient[...] = jnp.zeros_like(user_gradient)
        item_gradient[...] = jnp.zeros_like(item_gradient)

    for j in range(days_per_step):
        k = step * days_per_step + j
        day = days[pl.ds(k, 1), :]
        user_values = users[...]
        scaled = (day * user_values).astype(bf16)
        half_logits = jnp.dot(scaled, items_half_t[...], preferred_element_type=f32)
        state = status_ref[0, j]
        residual = (
            (0.5 * loss_scale)
            * state.astype(f32)
            * (jnp.tanh(half_logits) + jnp.where(state == 1, -1.0, 1.0))
        ).astype(bf16)
        projected = jnp.dot(residual, items[...], preferred_element_type=f32)
        user_gradient[...] += projected * day
        day_gradient[pl.ds(k, 1), :] = jnp.sum(projected * user_values, axis=0, keepdims=True)
        item_gradient[...] += lax.dot_general(
            residual, scaled, (((0,), (0,)), ((), ())), preferred_element_type=f32
        )

    @pl.when(step == pl.num_programs(0) - 1)
    def _():
        for t, gradient in enumerate((user_gradient, item_gradient, day_gradient)):
            start, slots = sizes.slot_starts[t], sizes.slots[t]
            placed = jnp.dot(
                places[t][...], gradient[...].astype(bf16), preferred_element_type=f32
            )
            for s in range(owners):
                rows = placed[s * slots : (s + 1) * slots]
                if t == 2:
                    note = iota(rows.shape, 0) == sizes.note_row
                    rows = jnp.where(note, note_ref[s : s + 1, :], rows)
                outs[s][start : start + slots, :] = rows.astype(bf16)


def sum_kernel(sizes, *refs):
    holders, owners, columns = sizes.holders, sizes.owners, sizes.columns
    arrived, outs = refs[:owners], refs[owners:]
    day_start = sizes.slot_starts[2]
    totals = [0.0, 0.0, 0.0]
    for ref in arrived:
        notes = ref[day_start : day_start + sizes.slots[2], :].astype(f32)
        rows = notes[sizes.note_row : sizes.note_row + 1, : sizes.slot_rows].astype(jnp.int32)
        for t in range(3):
            start, slots = sizes.slot_starts[t], sizes.slots[t]
            shape = (sizes.row_counts[t], sizes.slot_rows)
            slot = iota(shape, 1)
            mine = (slot >= start) & (slot < start + slots)
            selector = onehot((iota(shape, 0) == rows) & mine)
            totals[t] = totals[t] + jnp.dot(selector, ref[...], preferred_element_type=f32)
    for t in range(3):
        if t < 2:
            turned = totals[t].T.astype(bf16)
            for j in range(holders):
                outs[j][t * columns : (t + 1) * columns, :] = turned[
                    j * columns : (j + 1) * columns
                ]
        else:
            for j in range(holders):
                outs[j][2 * columns :, :] = pack_days(
                    sizes, totals[t][:, j * columns : (j + 1) * columns]
                ).astype(bf16)


def adam_kernel(sizes, *refs):
    holders, columns = sizes.holders, sizes.columns
    pieces = refs[:holders]
    states = refs[holders : holders + 9]
    outs = refs[holders + 9 :]
    total = pieces[0][...].astype(f32)
    for ref in pieces[1:]:
        total = total + ref[...].astype(f32)
    for t in range(3):
        if t < 2:
            gradient = total[t * columns : (t + 1) * columns]
        else:
            gradient = unpack_days(sizes, total[2 * columns :])
        factor, first, second = states[3 * t : 3 * t + 3]
        new_factor, new_first, new_second = outs[3 * t : 3 * t + 3]
        first_value = beta_one * first[...] + (1.0 - beta_one) * gradient
        second_value = beta_two * second[...] + (1.0 - beta_two) * gradient * gradient
        change = (
            learn_rate
            * (first_value / bias_one)
            / (jnp.sqrt(second_value / bias_two) + epsilon)
        )
        new_factor[...] = factor[...] - change
        new_first[...] = first_value
        new_second[...] = second_value


def swap(array, axis, size, bits):
    return lax.ppermute(array, axis, [(i, i ^ bits) for i in range(size)])


def local(
    users_list,
    items_list,
    days_list,
    status,
    user_factor,
    user_first,
    user_second,
    item_factor,
    item_first,
    item_second,
    day_factor,
    day_first,
    day_second,
):
    owners = lax.axis_size("dp")
    holders = lax.axis_size("mp")
    row_counts = (user_factor.shape[0], item_factor.shape[0], day_factor.shape[0])
    list_counts = (users_list.shape[1], items_list.shape[1], days_list.shape[1])
    sizes = Sizes(owners, holders, user_factor.shape[1], row_counts, list_counts)
    shape = jax.ShapeDtypeStruct
    small = pltpu.CompilerParams(vmem_limit_bytes=SMALL_VMEM)

    piece = pl.pallas_call(
        functools.partial(pack_kernel, sizes),
        out_shape=shape((sizes.piece_rows, LANES), bf16),
        compiler_params=small,
        name="pack",
    )(user_factor.T, item_factor.T, day_factor)
    pieces = [piece] + [swap(piece, "mp", holders, bits) for bits in range(1, holders)]

    picks_places_notes = pl.pallas_call(
        functools.partial(slot_kernel, sizes),
        out_shape=tuple(
            [shape((owners * row_counts[t], list_counts[t]), bf16) for t in range(3)]
            + [shape((owners * sizes.slots[t], list_counts[t]), bf16) for t in range(3)]
            + [shape((owners, sizes.rank), f32)]
        ),
        in_specs=[pl.BlockSpec(memory_space=pltpu.SMEM)]
        + [pl.BlockSpec(memory_space=pltpu.VMEM)] * 3,
        compiler_params=small,
        name="slots",
    )(lax.axis_index("dp").astype(jnp.int32).reshape(1), users_list, items_list, days_list)

    table = pl.pallas_call(
        functools.partial(table_kernel, sizes),
        out_shape=shape((sizes.table_rows, LANES), bf16),
        compiler_params=small,
        name="table",
    )(*pieces)
    tables = {0: table}
    for bits in range(2, owners, 2):
        tables[bits] = swap(table, "dp", owners, bits)
    for bits in range(0, owners, 2):
        tables[bits + 1] = swap(tables[bits], "dp", owners, 1)

    whole = lambda a: pl.BlockSpec(a.shape, lambda s: (0,) * len(a.shape))
    inputs = [*[tables[bits] for bits in range(owners)], *picks_places_notes]
    users, items, days = list_counts
    message = shape((sizes.slot_rows, sizes.rank), bf16)
    gradients = pl.pallas_call(
        functools.partial(block_kernel, sizes, DAYS_PER_STEP),
        out_shape=tuple([message] * owners),
        grid=(days // DAYS_PER_STEP,),
        in_specs=[whole(a) for a in inputs]
        + [pl.BlockSpec((1, DAYS_PER_STEP, users, items), lambda s: (0, s, 0, 0))],
        out_specs=tuple([whole(message)] * owners),
        scratch_shapes=[
            pltpu.VMEM((users, sizes.rank), f32),
            pltpu.VMEM((items, sizes.rank), bf16),
            pltpu.VMEM((sizes.rank, items), bf16),
            pltpu.VMEM((days, sizes.rank), f32),
            pltpu.VMEM((users, sizes.rank), f32),
            pltpu.VMEM((items, sizes.rank), f32),
            pltpu.VMEM((days, sizes.rank), f32),
        ],
        compiler_params=pltpu.CompilerParams(vmem_limit_bytes=BLOCK_VMEM),
        name="block_gradients",
    )(*inputs, status)
    crossed = [swap(gradients[bits + 1], "dp", owners, 1) for bits in range(0, owners, 2)]
    returned = [gradients[0], crossed[0]]
    for bits in range(2, owners, 2):
        returned.append(swap(gradients[bits], "dp", owners, bits))
        returned.append(swap(crossed[bits // 2], "dp", owners, bits))

    totals = pl.pallas_call(
        functools.partial(sum_kernel, sizes),
        out_shape=tuple([shape(piece.shape, bf16)] * holders),
        compiler_params=small,
        name="row_sums",
    )(*returned)
    column_totals = [totals[0]] + [
        swap(totals[bits], "mp", holders, bits) for bits in range(1, holders)
    ]

    states = (
        user_factor.T,
        user_first.T,
        user_second.T,
        item_factor.T,
        item_first.T,
        item_second.T,
        day_factor,
        day_first,
        day_second,
    )
    updated = pl.pallas_call(
        functools.partial(adam_kernel, sizes),
        out_shape=tuple(shape(a.shape, a.dtype) for a in states),
        compiler_params=small,
        name="adam",
    )(*column_totals, *states)
    return tuple(a.T for a in updated[:6]) + tuple(updated[6:])


def solution(mesh):
    block = P(("dp", "mp"), None)
    piece = P("dp", "mp")
    return jax.shard_map(
        local,
        mesh=mesh,
        in_specs=(block, block, block, P(("dp", "mp"), None, None, None)) + (piece,) * 9,
        out_specs=(piece,) * 9,
        check_vma=False,
    )
```

time: 76.8 us -> 59.8 us (0.78)
  Pallas kernels: 21.5 us -> 10.9 us
  starting transfers between devices: 28.2 us -> 22.2 us
  waiting for transfers between devices: 20.7 us -> 17.8 us
  local copies, waits for them, and re-layouts: 4.99 us -> 7.65 us
    ppermute x27 -> x23, starting transfers between devices: 28.2 us -> 22.2 us  [swap(): return lax.ppermute(array, axis, [(i, i ^ bits) for i in range(size)])]
    pallas_call x2, Pallas kernels: 4.63 us -> 1.27 us  [the longest x1 1.12 us: local(): pl.pallas_call(functools.partial(slot_kernel, sizes), out_shape=tuple([sh...]
    pallas_call x1, Pallas kernels: 11.6 us -> 8.31 us  [local(): pl.pallas_call(functools.partial(block_kernel, sizes, DAYS_PER_STEP), out...]
    unnamed x58 -> x32, local copies, waits for them, and re-layouts: 4.33 us -> 7.65 us
    ppermute x27 -> x23, waiting for transfers between devices: 20.7 us -> 17.8 us  [swap(): return lax.ppermute(array, axis, [(i, i ^ bits) for i in range(size)])]
    pallas_call x1, Pallas kernels: 2.16 us -> 0.56 us  [local(): pl.pallas_call(functools.partial(sum_kernel, sizes), out_shape=tuple([sha...]
    pallas_call x1, Pallas kernels: 1.46 us -> 0.07 us  [local(): pl.pallas_call(functools.partial(pack_kernel, sizes), out_shape=shape((si...]
    pallas_call x1, Pallas kernels: 1.66 us -> 0.74 us  [local(): pl.pallas_call(functools.partial(adam_kernel, sizes), out_shape=tuple((sh...]
  transfers between devices with their start and end apart: 27 -> 23, of which waited for: 16 -> 11; matrix products, arithmetic and copies ran while one was open for 3% -> 0% of each run, Pallas kernels for 3% -> 2%
where the time goes in v3:
time: 59.8 us; the launch traced here: 59.4 us
  starting transfers between devices  22.2 us (37%)
  waiting for transfers between devices  17.8 us (30%)
  Pallas kernels  10.9 us (18%)
  local copies, waits for them, and re-layouts  7.65 us (13%)
  between operations  0.84 us (1%)
    ppermute x23, starting transfers between devices, swap(): return lax.ppermute(array, axis, [(i, i ^ bits) for i in range(size)])  22.2 us
    ppermute x23, waiting for transfers between devices, swap(): return lax.ppermute(array, axis, [(i, i ^ bits) for i in range(size)])  17.8 us
    pallas_call x1, Pallas kernels, local(): pl.pallas_call(functools.partial(block_kernel, sizes, DAYS_PER_STEP), out...  8.31 us
    unnamed x32, local copies, waits for them, and re-layouts  7.65 us
  transfers between devices with their start and end apart: 23, of which 11 were waited for; matrix products, arithmetic and copies ran while one was open for 0% of the time, Pallas kernels for 2%

profile of v3, /device:TPU:0, one launch (start us, length us, event | category | flops | bytes accessed | tf_op | source)
XLA Modules:
  0.0 59.4 jit_solution(9007817588985175170)
XLA Ops:
  0.7 0.7 %copy-done.1 = f32[128,64]{0,1:T(8,128)S(1)} copy-done((f32[128,64]{0,1:T(8,128)S(1)}, f32[128,64]{0,1:T(8,128)}, u32[]{:S(2)}) %copy-start.1) | copy-done | bytes 32792
  1.4 0.8 %copy-done.3 = f32[128,64]{0,1:T(8,128)S(1)} copy-done((f32[128,64]{0,1:T(8,128)S(1)}, f32[128,64]{0,1:T(8,128)}, u32[]{:S(2)}) %copy-start.3) | copy-done | bytes 32792
  2.2 0.7 %copy-done.5 = f32[32,64]{1,0:T(8,128)S(1)} copy-done((f32[32,64]{1,0:T(8,128)S(1)}, f32[32,64]{1,0:T(8,128)}, u32[]{:S(2)}) %copy-start.5) | copy-done | bytes 8216
  3.0 5.1 %collective-permute-start.2 = (bf16[144,128]{1,0:T(8,128)(2,1)S(1)}, bf16[144,128]{1,0:T(8,128)(2,1)S(1)}, u32[]{:S(2)}, u32[]{:S(2)}) collective-permute-start(bf16[144,128]{1,0:T(8,128)(2,1)S(1)} %pack.1.refs_0_), channel_id=1, source_target_pairs={{0,3},{1,2},{2,1},{3,0},{4,7},{5,6},{6,5},{7,4},{8,11},{9,10},{10,... | collective-permute-start | bytes 110600 | tf_op jit(solution)/shard_map/ppermute | solution.py:261
  8.1 0.6 %collective-permute-start = (bf16[144,128]{1,0:T(8,128)(2,1)S(1)}, bf16[144,128]{1,0:T(8,128)(2,1)S(1)}, u32[]{:S(2)}, u32[]{:S(2)}) collective-permute-start(bf16[144,128]{1,0:T(8,128)(2,1)S(1)} %pack.1.refs_0_), channel_id=1, source_target_pairs={{0,1},{1,0},{2,3},{3,2},{4,5},{5,4},{6,7},{7,6},{8,9},{9,8},{10,11... | collective-permute-start | bytes 110600 | tf_op jit(solution)/shard_map/ppermute | solution.py:261
  8.7 1.3 %collective-permute-done.2.refs_3_ = bf16[144,128]{1,0:T(8,128)(2,1)S(1)} collective-permute-done((bf16[144,128]{1,0:T(8,128)(2,1)S(1)}, bf16[144,128]{1,0:T(8,128)(2,1)S(1)}, u32[]{:S(2)}, u32[]{:S(2)}) %collective-permute-start.2) | collective-permute-done | bytes 36896 | tf_op jit(solution)/shard_map/ppermute | solution.py:261
  10.0 2.9 %collective-permute-done.1.refs_2_ = bf16[144,128]{1,0:T(8,128)(2,1)S(1)} collective-permute-done((bf16[144,128]{1,0:T(8,128)(2,1)S(1)}, bf16[144,128]{1,0:T(8,128)(2,1)S(1)}, u32[]{:S(2)}, u32[]{:S(2)}) %collective-permute-start.1) | collective-permute-done | bytes 36896 | tf_op jit(solution)/shard_map/ppermute | solution.py:261
  13.1 2.5 %collective-permute-start.8 = (bf16[576,128]{1,0:T(8,128)(2,1)S(1)}, bf16[576,128]{1,0:T(8,128)(2,1)S(1)}, u32[]{:S(2)}, u32[]{:S(2)}) collective-permute-start(bf16[576,128]{1,0:T(8,128)(2,1)S(1)} %table.1.refs_0_), channel_id=1, source_target_pairs={{0,24},{4,28},{8,16},{12,20},{16,8},{20,12},{24,0},{28,4},{1,25},{... | collective-permute-start | bytes 442376 | tf_op jit(solution)/shard_map/ppermute | solution.py:261
  16.6 4.1 %collective-permute-done.8.refs_6_ = bf16[576,128]{1,0:T(8,128)(2,1)S(1)} collective-permute-done((bf16[576,128]{1,0:T(8,128)(2,1)S(1)}, bf16[576,128]{1,0:T(8,128)(2,1)S(1)}, u32[]{:S(2)}, u32[]{:S(2)}) %collective-permute-start.8) | collective-permute-done | bytes 147488 | tf_op jit(solution)/shard_map/ppermute | solution.py:261
  20.7 0.8 %collective-permute-done.6.refs_4_ = bf16[576,128]{1,0:T(8,128)(2,1)S(1)} collective-permute-done((bf16[576,128]{1,0:T(8,128)(2,1)S(1)}, bf16[576,128]{1,0:T(8,128)(2,1)S(1)}, u32[]{:S(2)}, u32[]{:S(2)}) %collective-permute-start.6) | collective-permute-done | bytes 147488 | tf_op jit(solution)/shard_map/ppermute | solution.py:261
  22.0 0.7 %copy-done.13 = s32[1,256]{1,0:T(1,128)S(1)} copy-done((s32[1,256]{1,0:T(1,128)S(1)}, s32[1,256]{1,0:T(1,128)}, u32[]{:S(2)}) %copy-start.13) | copy-done | bytes 1048
  22.7 0.7 %copy-done.14 = s32[1,256]{1,0:T(1,128)S(1)} copy-done((s32[1,256]{1,0:T(1,128)S(1)}, s32[1,256]{1,0:T(1,128)}, u32[]{:S(2)}) %copy-start.14) | copy-done | bytes 1048
  23.4 0.7 %copy-done.15 = s32[1,32]{1,0:T(1,128)S(1)} copy-done((s32[1,32]{1,0:T(1,128)S(1)}, s32[1,32]{1,0:T(1,128)}, u32[]{:S(2)}) %copy-start.15) | copy-done | bytes 152
  24.0 1.1 %slots.1 = (bf16[1024,256]{1,0:T(8,128)(2,1)S(1)}, bf16[1024,256]{1,0:T(8,128)(2,1)S(1)}, bf16[256,32]{1,0:T(8,128)(2,1)S(1)}, bf16[384,256]{1,0:T(8,128)(2,1)S(...) custom-call(s32[1]{0:T(128)} %bitcast.2.me_ref, s32[1,256]{1,0:T(1,128)S(1)} %copy-done.13, ...), custom_call_target="tpu_custom_call" | custom-call | tf_op jit(solution)/shard_map/slots/pallas_call | solution.py:295
  25.2 3.4 %copy-done = s32[1,32,256,256]{3,2,1,0:T(8,128)S(1)} copy-done((s32[1,32,256,256]{3,2,1,0:T(8,128)S(1)}, s32[1,32,256,256]{3,2,1,0:T(8,128)}, u32[]{:S(2)}) %copy-start) | copy-done | bytes 8388632
  28.6 8.3 %block_gradients.1 = (bf16[112,256]{1,0:T(8,128)(2,1)S(1)}, bf16[112,256]{1,0:T(8,128)(2,1)S(1)}, bf16[112,256]{1,0:T(8,128)(2,1)S(1)}, bf16[112,256]{1,0:T(8,12...) custom-call(bf16[576,128]{1,0:T(8,128)(2,1)S(1)} %table.1.refs_0_, ...), custom_call_target="tpu_custom_call" | custom-call | tf_op jit(solution)/shard_map/block_gradients/pallas_call | solution.py:324
  37.0 1.5 %collective-permute-start.11 = (bf16[112,256]{1,0:T(8,128)(2,1)S(1)}, bf16[112,256]{1,0:T(8,128)(2,1)S(1)}, u32[]{:S(2)}, u32[]{:S(2)}) collective-permute-start(bf16[112,256]{1,0:T(8,128)(2,1)S(1)} %get-tuple-element.46), channel_id=1, source_target_pairs={{0,8},{4,12},{8,0},{12,4},{16,24},{20,28},{24,16},{28,20},{1,9},{5... | collective-permute-start | bytes 172040 | tf_op jit(solution)/shard_map/ppermute | solution.py:261
  39.0 0.8 %collective-permute-start.14 = (bf16[112,256]{1,0:T(8,128)(2,1)S(1)}, bf16[112,256]{1,0:T(8,128)(2,1)S(1)}, u32[]{:S(2)}, u32[]{:S(2)}) collective-permute-start(bf16[112,256]{1,0:T(8,128)(2,1)S(1)} %get-tuple-element.48), channel_id=1, source_target_pairs={{0,16},{4,20},{8,24},{12,28},{16,0},{20,4},{24,8},{28,12},{1,17},{... | collective-permute-start | bytes 172040 | tf_op jit(solution)/shard_map/ppermute | solution.py:261
  39.8 1.5 %collective-permute-done.11.refs_2_ = bf16[112,256]{1,0:T(8,128)(2,1)S(1)} collective-permute-done((bf16[112,256]{1,0:T(8,128)(2,1)S(1)}, bf16[112,256]{1,0:T(8,128)(2,1)S(1)}, u32[]{:S(2)}, u32[]{:S(2)}) %collective-permute-start.11) | collective-permute-done | bytes 57376 | tf_op jit(solution)/shard_map/ppermute | solution.py:261
  41.3 1.6 %collective-permute-start.17 = (bf16[112,256]{1,0:T(8,128)(2,1)S(1)}, bf16[112,256]{1,0:T(8,128)(2,1)S(1)}, u32[]{:S(2)}, u32[]{:S(2)}) collective-permute-start(bf16[112,256]{1,0:T(8,128)(2,1)S(1)} %get-tuple-element.50), channel_id=1, source_target_pairs={{0,24},{4,28},{8,16},{12,20},{16,8},{20,12},{24,0},{28,4},{1,25},{... | collective-permute-start | bytes 172040 | tf_op jit(solution)/shard_map/ppermute | solution.py:261
  42.9 1.2 %collective-permute-start.13 = (bf16[112,256]{1,0:T(8,128)(2,1)S(1)}, bf16[112,256]{1,0:T(8,128)(2,1)S(1)}, u32[]{:S(2)}, u32[]{:S(2)}) collective-permute-start(bf16[112,256]{1,0:T(8,128)(2,1)S(1)} %collective-permute-done.12), channel_id=1, source_target_pairs={{0,8},{4,12},{8,0},{12,4},{16,24},{20,28},{24,16},{28,20},{1,9},{5... | collective-permute-start | bytes 172040 | tf_op jit(solution)/shard_map/ppermute | solution.py:261
  44.1 0.7 %collective-permute-start.16 = (bf16[112,256]{1,0:T(8,128)(2,1)S(1)}, bf16[112,256]{1,0:T(8,128)(2,1)S(1)}, u32[]{:S(2)}, u32[]{:S(2)}) collective-permute-start(bf16[112,256]{1,0:T(8,128)(2,1)S(1)} %collective-permute-done.15), channel_id=1, source_target_pairs={{0,16},{4,20},{8,24},{12,28},{16,0},{20,4},{24,8},{28,12},{1,17},{... | collective-permute-start | bytes 172040 | tf_op jit(solution)/shard_map/ppermute | solution.py:261
  44.8 1.6 %collective-permute-start.19 = (bf16[112,256]{1,0:T(8,128)(2,1)S(1)}, bf16[112,256]{1,0:T(8,128)(2,1)S(1)}, u32[]{:S(2)}, u32[]{:S(2)}) collective-permute-start(bf16[112,256]{1,0:T(8,128)(2,1)S(1)} %collective-permute-done.18), channel_id=1, source_target_pairs={{0,24},{4,28},{8,16},{12,20},{16,8},{20,12},{24,0},{28,4},{1,25},{... | collective-permute-start | bytes 172040 | tf_op jit(solution)/shard_map/ppermute | solution.py:261
  46.4 0.7 %collective-permute-done.13.refs_3_ = bf16[112,256]{1,0:T(8,128)(2,1)S(1)} collective-permute-done((bf16[112,256]{1,0:T(8,128)(2,1)S(1)}, bf16[112,256]{1,0:T(8,128)(2,1)S(1)}, u32[]{:S(2)}, u32[]{:S(2)}) %collective-permute-start.13) | collective-permute-done | bytes 57376 | tf_op jit(solution)/shard_map/ppermute | solution.py:261
  47.2 1.5 %collective-permute-done.16.refs_5_ = bf16[112,256]{1,0:T(8,128)(2,1)S(1)} collective-permute-done((bf16[112,256]{1,0:T(8,128)(2,1)S(1)}, bf16[112,256]{1,0:T(8,128)(2,1)S(1)}, u32[]{:S(2)}, u32[]{:S(2)}) %collective-permute-start.16) | collective-permute-done | bytes 57376 | tf_op jit(solution)/shard_map/ppermute | solution.py:261
  48.6 1.3 %collective-permute-done.19.refs_7_ = bf16[112,256]{1,0:T(8,128)(2,1)S(1)} collective-permute-done((bf16[112,256]{1,0:T(8,128)(2,1)S(1)}, bf16[112,256]{1,0:T(8,128)(2,1)S(1)}, u32[]{:S(2)}, u32[]{:S(2)}) %collective-permute-start.19) | collective-permute-done | bytes 57376 | tf_op jit(solution)/shard_map/ppermute | solution.py:261
  49.9 0.6 row_sums.1
  50.5 2.3 %collective-permute-start.21 = (bf16[144,128]{1,0:T(8,128)(2,1)S(1)}, bf16[144,128]{1,0:T(8,128)(2,1)S(1)}, u32[]{:S(2)}, u32[]{:S(2)}) collective-permute-start(bf16[144,128]{1,0:T(8,128)(2,1)S(1)} %get-tuple-element.54), channel_id=1, source_target_pairs={{0,2},{1,3},{2,0},{3,1},{4,6},{5,7},{6,4},{7,5},{8,10},{9,11},{10,... | collective-permute-start | bytes 110600 | tf_op jit(solution)/shard_map/ppermute | solution.py:261
  52.8 2.1 %collective-permute-start.22 = (bf16[144,128]{1,0:T(8,128)(2,1)S(1)}, bf16[144,128]{1,0:T(8,128)(2,1)S(1)}, u32[]{:S(2)}, u32[]{:S(2)}) collective-permute-start(bf16[144,128]{1,0:T(8,128)(2,1)S(1)} %get-tuple-element.55), channel_id=1, source_target_pairs={{0,3},{1,2},{2,1},{3,0},{4,7},{5,6},{6,5},{7,4},{8,11},{9,10},{10,... | collective-permute-start | bytes 110600 | tf_op jit(solution)/shard_map/ppermute | solution.py:261
  54.9 0.9 %collective-permute-done.21.refs_2_ = bf16[144,128]{1,0:T(8,128)(2,1)S(1)} collective-permute-done((bf16[144,128]{1,0:T(8,128)(2,1)S(1)}, bf16[144,128]{1,0:T(8,128)(2,1)S(1)}, u32[]{:S(2)}, u32[]{:S(2)}) %collective-permute-start.21) | collective-permute-done | bytes 36896 | tf_op jit(solution)/shard_map/ppermute | solution.py:261
  55.8 2.7 %collective-permute-done.22.refs_3_ = bf16[144,128]{1,0:T(8,128)(2,1)S(1)} collective-permute-done((bf16[144,128]{1,0:T(8,128)(2,1)S(1)}, bf16[144,128]{1,0:T(8,128)(2,1)S(1)}, u32[]{:S(2)}, u32[]{:S(2)}) %collective-permute-start.22) | collective-permute-done | bytes 36896 | tf_op jit(solution)/shard_map/ppermute | solution.py:261
  58.6 0.7 %adam.1 = (f32[64,128]{1,0:T(8,128)}, f32[64,128]{1,0:T(8,128)}, f32[64,128]{1,0:T(8,128)}, f32[64,128]{1,0:T(8,128)}, f32[64,128]{1,0:T(8,128)}, /*index=5*/f32...) custom-call(bf16[144,128]{1,0:T(8,128)(2,1)S(1)} %get-tuple-element.52.refs_0_, ...), custom_call_target="tpu_custom_call" | custom-call | tf_op jit(solution)/shard_map/adam/pallas_call | solution.py:370
  (52 shorter events, 2.7 us)
Async XLA Ops:
  2.9 55.7 %copy-start.2 = (f32[128,64]{0,1:T(8,128)S(1)}, f32[128,64]{0,1:T(8,128)}, u32[]{:S(2)}) copy-start(f32[128,64]{0,1:T(8,128)} %param.17) | copy-start | bytes 98308
  2.9 55.7 %copy-start.4 = (f32[128,64]{0,1:T(8,128)S(1)}, f32[128,64]{0,1:T(8,128)}, u32[]{:S(2)}) copy-start(f32[128,64]{0,1:T(8,128)} %param.20) | copy-start | bytes 98308
  2.9 55.7 %copy-start.6 = (f32[32,64]{1,0:T(8,128)S(1)}, f32[32,64]{1,0:T(8,128)}, u32[]{:S(2)}) copy-start(f32[32,64]{1,0:T(8,128)} %refs_10_.1) | copy-start | bytes 24580
  2.9 55.7 %copy-start.7 = (f32[128,64]{0,1:T(8,128)S(1)}, f32[128,64]{0,1:T(8,128)}, u32[]{:S(2)}) copy-start(f32[128,64]{0,1:T(8,128)} %param.18) | copy-start | bytes 98308
  2.9 55.7 %copy-start.8 = (f32[128,64]{0,1:T(8,128)S(1)}, f32[128,64]{0,1:T(8,128)}, u32[]{:S(2)}) copy-start(f32[128,64]{0,1:T(8,128)} %param.19) | copy-start | bytes 98308
  2.9 55.7 %copy-start.9 = (f32[128,64]{0,1:T(8,128)S(1)}, f32[128,64]{0,1:T(8,128)}, u32[]{:S(2)}) copy-start(f32[128,64]{0,1:T(8,128)} %param.21) | copy-start | bytes 98308
  2.9 55.7 %copy-start.10 = (f32[128,64]{0,1:T(8,128)S(1)}, f32[128,64]{0,1:T(8,128)}, u32[]{:S(2)}) copy-start(f32[128,64]{0,1:T(8,128)} %param.22) | copy-start | bytes 98308
  2.9 55.7 %copy-start.11 = (f32[32,64]{1,0:T(8,128)S(1)}, f32[32,64]{1,0:T(8,128)}, u32[]{:S(2)}) copy-start(f32[32,64]{1,0:T(8,128)} %refs_11_.1) | copy-start | bytes 24580
  2.9 55.7 %copy-start.12 = (f32[32,64]{1,0:T(8,128)S(1)}, f32[32,64]{1,0:T(8,128)}, u32[]{:S(2)}) copy-start(f32[32,64]{1,0:T(8,128)} %refs_12_.1) | copy-start | bytes 24580
  3.0 7.0 %collective-permute-start.2 = (bf16[144,128]{1,0:T(8,128)(2,1)S(1)}, bf16[144,128]{1,0:T(8,128)(2,1)S(1)}, u32[]{:S(2)}, u32[]{:S(2)}) collective-permute-start(bf16[144,128]{1,0:T(8,128)(2,1)S(1)} %pack.1.refs_0_), channel_id=1, source_target_pairs={{0,3},{1,2},{2,1},{3,0},{4,7},{5,6},{6,5},{7,4},{8,11},{9,10},{10,... | collective-permute-start | bytes 110600 | tf_op jit(solution)/shard_map/ppermute | solution.py:261
  8.1 4.9 %collective-permute-start.1 = (bf16[144,128]{1,0:T(8,128)(2,1)S(1)}, bf16[144,128]{1,0:T(8,128)(2,1)S(1)}, u32[]{:S(2)}, u32[]{:S(2)}) collective-permute-start(bf16[144,128]{1,0:T(8,128)(2,1)S(1)} %pack.1.refs_0_), channel_id=1, source_target_pairs={{0,2},{1,3},{2,0},{3,1},{4,6},{5,7},{6,4},{7,5},{8,10},{9,11},{10,... | collective-permute-start | bytes 110600 | tf_op jit(solution)/shard_map/ppermute | solution.py:261
  8.1 4.9 %collective-permute-start = (bf16[144,128]{1,0:T(8,128)(2,1)S(1)}, bf16[144,128]{1,0:T(8,128)(2,1)S(1)}, u32[]{:S(2)}, u32[]{:S(2)}) collective-permute-start(bf16[144,128]{1,0:T(8,128)(2,1)S(1)} %pack.1.refs_0_), channel_id=1, source_target_pairs={{0,1},{1,0},{2,3},{3,2},{4,5},{5,4},{6,7},{7,6},{8,9},{9,8},{10,11... | collective-permute-start | bytes 110600 | tf_op jit(solution)/shard_map/ppermute | solution.py:261
  13.1 7.6 %collective-permute-start.8 = (bf16[576,128]{1,0:T(8,128)(2,1)S(1)}, bf16[576,128]{1,0:T(8,128)(2,1)S(1)}, u32[]{:S(2)}, u32[]{:S(2)}) collective-permute-start(bf16[576,128]{1,0:T(8,128)(2,1)S(1)} %table.1.refs_0_), channel_id=1, source_target_pairs={{0,24},{4,28},{8,16},{12,20},{16,8},{20,12},{24,0},{28,4},{1,25},{... | collective-permute-start | bytes 442376 | tf_op jit(solution)/shard_map/ppermute | solution.py:261
  15.5 6.0 %collective-permute-start.6 = (bf16[576,128]{1,0:T(8,128)(2,1)S(1)}, bf16[576,128]{1,0:T(8,128)(2,1)S(1)}, u32[]{:S(2)}, u32[]{:S(2)}) collective-permute-start(bf16[576,128]{1,0:T(8,128)(2,1)S(1)} %table.1.refs_0_), channel_id=1, source_target_pairs={{0,16},{4,20},{8,24},{12,28},{16,0},{20,4},{24,8},{28,12},{1,17},{... | collective-permute-start | bytes 442376 | tf_op jit(solution)/shard_map/ppermute | solution.py:261
  16.0 5.4 %collective-permute-start.4 = (bf16[576,128]{1,0:T(8,128)(2,1)S(1)}, bf16[576,128]{1,0:T(8,128)(2,1)S(1)}, u32[]{:S(2)}, u32[]{:S(2)}) collective-permute-start(bf16[576,128]{1,0:T(8,128)(2,1)S(1)} %table.1.refs_0_), channel_id=1, source_target_pairs={{0,8},{4,12},{8,0},{12,4},{16,24},{20,28},{24,16},{28,20},{1,9},{5... | collective-permute-start | bytes 442376 | tf_op jit(solution)/shard_map/ppermute | solution.py:261
  16.6 8.6 %collective-permute-start.3 = (bf16[576,128]{1,0:T(8,128)(2,1)S(1)}, bf16[576,128]{1,0:T(8,128)(2,1)S(1)}, u32[]{:S(2)}, u32[]{:S(2)}) collective-permute-start(bf16[576,128]{1,0:T(8,128)(2,1)S(1)} %table.1.refs_0_), channel_id=1, source_target_pairs={{0,4},{4,0},{8,12},{12,8},{16,20},{20,16},{24,28},{28,24},{1,5},{5... | collective-permute-start | bytes 442376 | tf_op jit(solution)/shard_map/ppermute | solution.py:261
  20.7 4.4 %collective-permute-start.9 = (bf16[576,128]{1,0:T(8,128)(2,1)S(1)}, bf16[576,128]{1,0:T(8,128)(2,1)S(1)}, u32[]{:S(2)}, u32[]{:S(2)}) collective-permute-start(bf16[576,128]{1,0:T(8,128)(2,1)S(1)} %collective-permute-done.8.refs_6_), channel_id=1, source_target_pairs={{0,4},{4,0},{8,12},{12,8},{16,20},{20,16},{24,28},{28,24},{1,5},{5... | collective-permute-start | bytes 442376 | tf_op jit(solution)/shard_map/ppermute | solution.py:261
  21.5 3.7 %collective-permute-start.7 = (bf16[576,128]{1,0:T(8,128)(2,1)S(1)}, bf16[576,128]{1,0:T(8,128)(2,1)S(1)}, u32[]{:S(2)}, u32[]{:S(2)}) collective-permute-start(bf16[576,128]{1,0:T(8,128)(2,1)S(1)} %collective-permute-done.6.refs_4_), channel_id=1, source_target_pairs={{0,4},{4,0},{8,12},{12,8},{16,20},{20,16},{24,28},{28,24},{1,5},{5... | collective-permute-start | bytes 442376 | tf_op jit(solution)/shard_map/ppermute | solution.py:261
  21.5 3.7 %collective-permute-start.5 = (bf16[576,128]{1,0:T(8,128)(2,1)S(1)}, bf16[576,128]{1,0:T(8,128)(2,1)S(1)}, u32[]{:S(2)}, u32[]{:S(2)}) collective-permute-start(bf16[576,128]{1,0:T(8,128)(2,1)S(1)} %collective-permute-done.4.refs_2_), channel_id=1, source_target_pairs={{0,4},{4,0},{8,12},{12,8},{16,20},{20,16},{24,28},{28,24},{1,5},{5... | collective-permute-start | bytes 442376 | tf_op jit(solution)/shard_map/ppermute | solution.py:261
  36.9 2.1 %collective-permute-start.10 = (bf16[112,256]{1,0:T(8,128)(2,1)S(1)}, bf16[112,256]{1,0:T(8,128)(2,1)S(1)}, u32[]{:S(2)}, u32[]{:S(2)}) collective-permute-start(bf16[112,256]{1,0:T(8,128)(2,1)S(1)} %get-tuple-element.45), channel_id=1, source_target_pairs={{0,4},{4,0},{8,12},{12,8},{16,20},{20,16},{24,28},{28,24},{1,5},{5... | collective-permute-start | bytes 172040 | tf_op jit(solution)/shard_map/ppermute | solution.py:261
  37.0 4.3 %collective-permute-start.11 = (bf16[112,256]{1,0:T(8,128)(2,1)S(1)}, bf16[112,256]{1,0:T(8,128)(2,1)S(1)}, u32[]{:S(2)}, u32[]{:S(2)}) collective-permute-start(bf16[112,256]{1,0:T(8,128)(2,1)S(1)} %get-tuple-element.46), channel_id=1, source_target_pairs={{0,8},{4,12},{8,0},{12,4},{16,24},{20,28},{24,16},{28,20},{1,9},{5... | collective-permute-start | bytes 172040 | tf_op jit(solution)/shard_map/ppermute | solution.py:261
  38.4 4.4 %collective-permute-start.12 = (bf16[112,256]{1,0:T(8,128)(2,1)S(1)}, bf16[112,256]{1,0:T(8,128)(2,1)S(1)}, u32[]{:S(2)}, u32[]{:S(2)}) collective-permute-start(bf16[112,256]{1,0:T(8,128)(2,1)S(1)} %get-tuple-element.47), channel_id=1, source_target_pairs={{0,4},{4,0},{8,12},{12,8},{16,20},{20,16},{24,28},{28,24},{1,5},{5... | collective-permute-start | bytes 172040 | tf_op jit(solution)/shard_map/ppermute | solution.py:261
  38.5 5.6 %collective-permute-start.15 = (bf16[112,256]{1,0:T(8,128)(2,1)S(1)}, bf16[112,256]{1,0:T(8,128)(2,1)S(1)}, u32[]{:S(2)}, u32[]{:S(2)}) collective-permute-start(bf16[112,256]{1,0:T(8,128)(2,1)S(1)} %get-tuple-element.49), channel_id=1, source_target_pairs={{0,4},{4,0},{8,12},{12,8},{16,20},{20,16},{24,28},{28,24},{1,5},{5... | collective-permute-start | bytes 172040 | tf_op jit(solution)/shard_map/ppermute | solution.py:261
  38.9 5.9 %collective-permute-start.18 = (bf16[112,256]{1,0:T(8,128)(2,1)S(1)}, bf16[112,256]{1,0:T(8,128)(2,1)S(1)}, u32[]{:S(2)}, u32[]{:S(2)}) collective-permute-start(bf16[112,256]{1,0:T(8,128)(2,1)S(1)} %get-tuple-element.51), channel_id=1, source_target_pairs={{0,4},{4,0},{8,12},{12,8},{16,20},{20,16},{24,28},{28,24},{1,5},{5... | collective-permute-start | bytes 172040 | tf_op jit(solution)/shard_map/ppermute | solution.py:261
  39.0 7.4 %collective-permute-start.14 = (bf16[112,256]{1,0:T(8,128)(2,1)S(1)}, bf16[112,256]{1,0:T(8,128)(2,1)S(1)}, u32[]{:S(2)}, u32[]{:S(2)}) collective-permute-start(bf16[112,256]{1,0:T(8,128)(2,1)S(1)} %get-tuple-element.48), channel_id=1, source_target_pairs={{0,16},{4,20},{8,24},{12,28},{16,0},{20,4},{24,8},{28,12},{1,17},{... | collective-permute-start | bytes 172040 | tf_op jit(solution)/shard_map/ppermute | solution.py:261
  41.3 5.1 %collective-permute-start.17 = (bf16[112,256]{1,0:T(8,128)(2,1)S(1)}, bf16[112,256]{1,0:T(8,128)(2,1)S(1)}, u32[]{:S(2)}, u32[]{:S(2)}) collective-permute-start(bf16[112,256]{1,0:T(8,128)(2,1)S(1)} %get-tuple-element.50), channel_id=1, source_target_pairs={{0,24},{4,28},{8,16},{12,20},{16,8},{20,12},{24,0},{28,4},{1,25},{... | collective-permute-start | bytes 172040 | tf_op jit(solution)/shard_map/ppermute | solution.py:261
  42.9 4.3 %collective-permute-start.13 = (bf16[112,256]{1,0:T(8,128)(2,1)S(1)}, bf16[112,256]{1,0:T(8,128)(2,1)S(1)}, u32[]{:S(2)}, u32[]{:S(2)}) collective-permute-start(bf16[112,256]{1,0:T(8,128)(2,1)S(1)} %collective-permute-done.12), channel_id=1, source_target_pairs={{0,8},{4,12},{8,0},{12,4},{16,24},{20,28},{24,16},{28,20},{1,9},{5... | collective-permute-start | bytes 172040 | tf_op jit(solution)/shard_map/ppermute | solution.py:261
  44.1 4.5 %collective-permute-start.16 = (bf16[112,256]{1,0:T(8,128)(2,1)S(1)}, bf16[112,256]{1,0:T(8,128)(2,1)S(1)}, u32[]{:S(2)}, u32[]{:S(2)}) collective-permute-start(bf16[112,256]{1,0:T(8,128)(2,1)S(1)} %collective-permute-done.15), channel_id=1, source_target_pairs={{0,16},{4,20},{8,24},{12,28},{16,0},{20,4},{24,8},{28,12},{1,17},{... | collective-permute-start | bytes 172040 | tf_op jit(solution)/shard_map/ppermute | solution.py:261
  44.8 5.1 %collective-permute-start.19 = (bf16[112,256]{1,0:T(8,128)(2,1)S(1)}, bf16[112,256]{1,0:T(8,128)(2,1)S(1)}, u32[]{:S(2)}, u32[]{:S(2)}) collective-permute-start(bf16[112,256]{1,0:T(8,128)(2,1)S(1)} %collective-permute-done.18), channel_id=1, source_target_pairs={{0,24},{4,28},{8,16},{12,20},{16,8},{20,12},{24,0},{28,4},{1,25},{... | collective-permute-start | bytes 172040 | tf_op jit(solution)/shard_map/ppermute | solution.py:261
  50.4 4.5 %collective-permute-start.20 = (bf16[144,128]{1,0:T(8,128)(2,1)S(1)}, bf16[144,128]{1,0:T(8,128)(2,1)S(1)}, u32[]{:S(2)}, u32[]{:S(2)}) collective-permute-start(bf16[144,128]{1,0:T(8,128)(2,1)S(1)} %get-tuple-element.53), channel_id=1, source_target_pairs={{0,1},{1,0},{2,3},{3,2},{4,5},{5,4},{6,7},{7,6},{8,9},{9,8},{10,11... | collective-permute-start | bytes 110600 | tf_op jit(solution)/shard_map/ppermute | solution.py:261
  50.5 5.3 %collective-permute-start.21 = (bf16[144,128]{1,0:T(8,128)(2,1)S(1)}, bf16[144,128]{1,0:T(8,128)(2,1)S(1)}, u32[]{:S(2)}, u32[]{:S(2)}) collective-permute-start(bf16[144,128]{1,0:T(8,128)(2,1)S(1)} %get-tuple-element.54), channel_id=1, source_target_pairs={{0,2},{1,3},{2,0},{3,1},{4,6},{5,7},{6,4},{7,5},{8,10},{9,11},{10,... | collective-permute-start | bytes 110600 | tf_op jit(solution)/shard_map/ppermute | solution.py:261
  52.8 5.8 %collective-permute-start.22 = (bf16[144,128]{1,0:T(8,128)(2,1)S(1)}, bf16[144,128]{1,0:T(8,128)(2,1)S(1)}, u32[]{:S(2)}, u32[]{:S(2)}) collective-permute-start(bf16[144,128]{1,0:T(8,128)(2,1)S(1)} %get-tuple-element.55), channel_id=1, source_target_pairs={{0,3},{1,2},{2,1},{3,0},{4,7},{5,6},{6,5},{7,4},{8,11},{9,10},{10,... | collective-permute-start | bytes 110600 | tf_op jit(solution)/shard_map/ppermute | solution.py:261
  (7 other events, 7.6 us)

commit v4 on v3

--- a/solution.py
+++ b/solution.py
@@ -18,7 +18,8 @@
 LANES = 128
 DAYS_PER_STEP = 4
 SMALL_VMEM = 16 * 1024 * 1024
-BLOCK_VMEM = 32 * 1024 * 1024
+BLOCK_VMEM = 48 * 1024 * 1024
+PACK_VMEM = 56 * 1024 * 1024
 
 f32 = jnp.float32
 bf16 = jnp.bfloat16
@@ -80,16 +81,29 @@
     )
 
 
-def pack_kernel(sizes, user_ref, item_ref, day_ref, out_ref):
+def fetch(sources, targets, semaphores):
+    copies = [
+        pltpu.make_async_copy(source, target, semaphores.at[n])
+        for n, (source, target) in enumerate(zip(sources, targets))
+    ]
+    for copy in copies:
+        copy.start()
+    for copy in copies:
+        copy.wait()
+
+
+def pack_kernel(sizes, user_hbm, item_hbm, day_hbm, out_ref, user, item, day, semaphores):
     columns = sizes.columns
-    out_ref[:columns, :] = user_ref[...].astype(bf16)
-    out_ref[columns : 2 * columns, :] = item_ref[...].astype(bf16)
-    out_ref[2 * columns :, :] = pack_days(sizes, day_ref[...]).astype(bf16)
+    fetch((user_hbm, item_hbm, day_hbm), (user, item, day), semaphores)
+    out_ref[:columns, :] = user[...].astype(bf16)
+    out_ref[columns : 2 * columns, :] = item[...].astype(bf16)
+    out_ref[2 * columns :, :] = pack_days(sizes, day[...]).astype(bf16)
 
 
 def slot_kernel(sizes, me_ref, *refs):
     owners = sizes.owners
-    lists, picks, places, note_ref = refs[:3], refs[3:6], refs[6:9], refs[9]
+    picks, places, note_ref, lists = refs[3:6], refs[6:9], refs[9], refs[10:13]
+    fetch(refs[:3], lists, refs[13])
     me = me_ref[0]
     notes = [[] for _ in range(owners)]
     for t in range(3):
@@ -116,7 +130,7 @@
 
 
 def table_kernel(sizes, *refs):
-    pieces, out_ref = refs[:-1], refs[-1]
+    pieces, out_ref = refs[:-2], refs[-1]
     columns, rank, day_rows = sizes.columns, sizes.rank, sizes.row_counts[2]
     for j, ref in enumerate(pieces):
         for t in range(2):
@@ -136,77 +150,103 @@
     tables = refs[:owners]
     picks = refs[owners : owners + 3]
     places = refs[owners + 3 : owners + 6]
-    note_ref, status_ref = refs[owners + 6 : owners + 8]
-    outs = refs[owners + 8 : 2 * owners + 8]
-    users, items, items_half_t, days, user_gradient, item_gradient, day_gradient = refs[
-        2 * owners + 8 :
-    ]
-    step = pl.program_id(0)
+    note_ref, status_hbm, own_ref, other_ref = refs[owners + 6 : owners + 10]
+    (
+        users,
+        items,
+        items_half_t,
+        days,
+        user_gradient,
+        item_gradient,
+        day_gradient,
+        status,
+        semaphores,
+    ) = refs[owners + 10 :]
+    steps = status.shape[0] // days_per_step
+
+    def status_copy(step):
+        chunk = pl.ds(step * days_per_step, days_per_step)
+        return pltpu.make_async_copy(
+            status_hbm.at[0, chunk], status.at[chunk], semaphores.at[step]
+        )
+
+    for step in range(steps):
+        status_copy(step).start()
 
     def pick(t):
         table = jnp.concatenate([ref[t * rank : (t + 1) * rank, :] for ref in tables], axis=1)
         return jnp.dot(table, picks[t][...], preferred_element_type=f32)
 
-    @pl.when(step == 0)
-    def _():
-        users[...] = pick(0).T
-        items_t = pick(1)
-        items[...] = items_t.T.astype(bf16)
-        items_half_t[...] = (0.5 * items_t).astype(bf16)
-        starts = [2 * rank + chunk * day_rows for chunk in range(sizes.day_chunks)]
-        day_table = jnp.concatenate(
-            [
-                jnp.concatenate([ref[start : start + day_rows, :] for start in starts], axis=1)
-                for ref in tables
-            ],
-            axis=0,
-        )
-        days[...] = lax.dot_general(
-            picks[2][...], day_table, (((0,), (0,)), ((), ())), preferred_element_type=f32
-        )
-        user_gradient[...] = jnp.zeros_like(user_gradient)
-        item_gradient[...] = jnp.zeros_like(item_gradient)
-
-    for j in range(days_per_step):
-        k = step * days_per_step + j
-        day = days[pl.ds(k, 1), :]
-        user_values = users[...]
-        scaled = (day * user_values).astype(bf16)
-        half_logits = jnp.dot(scaled, items_half_t[...], preferred_element_type=f32)
-        state = status_ref[0, j]
-        residual = (
-            (0.5 * loss_scale)
-            * state.astype(f32)
-            * (jnp.tanh(half_logits) + jnp.where(state == 1, -1.0, 1.0))
-        ).astype(bf16)
-        projected = jnp.dot(residual, items[...], preferred_element_type=f32)
-        user_gradient[...] += projected * day
-        day_gradient[pl.ds(k, 1), :] = jnp.sum(projected * user_values, axis=0, keepdims=True)
-        item_gradient[...] += lax.dot_general(
-            residual, scaled, (((0,), (0,)), ((), ())), preferred_element_type=f32
-        )
-
-    @pl.when(step == pl.num_programs(0) - 1)
-    def _():
-        for t, gradient in enumerate((user_gradient, item_gradient, day_gradient)):
-            start, slots = sizes.slot_starts[t], sizes.slots[t]
-            placed = jnp.dot(
-                places[t][...], gradient[...].astype(bf16), preferred_element_type=f32
+    users[...] = pick(0).T
+    items_t = pick(1)
+    items[...] = items_t.T.astype(bf16)
+    items_half_t[...] = (0.5 * items_t).astype(bf16)
+    starts = [2 * rank + chunk * day_rows for chunk in range(sizes.day_chunks)]
+    day_table = jnp.concatenate(
+        [
+            jnp.concatenate([ref[start : start + day_rows, :] for start in starts], axis=1)
+            for ref in tables
+        ],
+        axis=0,
+    )
+    days[...] = lax.dot_general(
+        picks[2][...], day_table, (((0,), (0,)), ((), ())), preferred_element_type=f32
+    )
+    user_gradient[...] = jnp.zeros_like(user_gradient)
+    item_gradient[...] = jnp.zeros_like(item_gradient)
+
+    @pl.loop(0, steps)
+    def _(step):
+        status_copy(step).wait()
+        for j in range(days_per_step):
+            k = step * days_per_step + j
+            day = days[pl.ds(k, 1), :]
+            user_values = users[...]
+            scaled = (day * user_values).astype(bf16)
+            half_logits = jnp.dot(scaled, items_half_t[...], preferred_element_type=f32)
+            state = status[k]
+            residual = (
+                (0.5 * loss_scale)
+                * state.astype(f32)
+                * (jnp.tanh(half_logits) + jnp.where(state == 1, -1.0, 1.0))
+            ).astype(bf16)
+            projected = jnp.dot(residual, items[...], preferred_element_type=f32)
+            user_gradient[...] += projected * day
+            day_gradient[pl.ds(k, 1), :] = jnp.sum(projected * user_values, axis=0, keepdims=True)
+            item_gradient[...] += lax.dot_general(
+                residual, scaled, (((0,), (0,)), ((), ())), preferred_element_type=f32
             )
-            for s in range(owners):
-                rows = placed[s * slots : (s + 1) * slots]
-                if t == 2:
-                    note = iota(rows.shape, 0) == sizes.note_row
-                    rows = jnp.where(note, note_ref[s : s + 1, :], rows)
-                outs[s][start : start + slots, :] = rows.astype(bf16)
+
+    for t, gradient in enumerate((user_gradient, item_gradient, day_gradient)):
+        start, slots = sizes.slot_starts[t], sizes.slots[t]
+        placed = jnp.dot(places[t][...], gradient[...].astype(bf16), preferred_element_type=f32)
+        for s in range(owners):
+            rows = placed[s * slots : (s + 1) * slots]
+            if t == 2:
+                note = iota(rows.shape, 0) == sizes.note_row
+                rows = jnp.where(note, note_ref[s : s + 1, :], rows)
+            out = (own_ref, other_ref)[s % 2]
+            first = (s // 2) * sizes.slot_rows + start
+            out[first : first + slots, :] = rows.astype(bf16)
+
+
+def merge_kernel(sizes, own_ref, crossed_ref, *outs):
+    rows = sizes.slot_rows
+    for n, out in enumerate(outs):
+        start = (n + 1) * rows
+        out[:rows, :] = own_ref[start : start + rows, :]
+        out[rows:, :] = crossed_ref[start : start + rows, :]
 
 
 def sum_kernel(sizes, *refs):
-    holders, owners, columns = sizes.holders, sizes.owners, sizes.columns
-    arrived, outs = refs[:owners], refs[owners:]
+    holders, columns = sizes.holders, sizes.columns
+    inputs = sizes.owners // 2 + 1
+    arrived, outs = refs[:inputs], refs[inputs:]
     day_start = sizes.slot_starts[2]
     totals = [0.0, 0.0, 0.0]
-    for ref in arrived:
+    messages = [ref.at[: sizes.slot_rows] for ref in arrived]
+    messages += [ref.at[sizes.slot_rows :] for ref in arrived[2:]]
+    for ref in messages:
         notes = ref[day_start : day_start + sizes.slots[2], :].astype(f32)
         rows = notes[sizes.note_row : sizes.note_row + 1, : sizes.slot_rows].astype(jnp.int32)
         for t in range(3):
@@ -284,12 +324,17 @@
     shape = jax.ShapeDtypeStruct
     small = pltpu.CompilerParams(vmem_limit_bytes=SMALL_VMEM)
 
+    hbm = pl.BlockSpec(memory_space=pltpu.HBM)
+    tables_in = (user_factor.T, item_factor.T, day_factor)
     piece = pl.pallas_call(
         functools.partial(pack_kernel, sizes),
         out_shape=shape((sizes.piece_rows, LANES), bf16),
-        compiler_params=small,
+        in_specs=[hbm] * 3,
+        scratch_shapes=[pltpu.VMEM(a.shape, f32) for a in tables_in]
+        + [pltpu.SemaphoreType.DMA((3,))],
+        compiler_params=pltpu.CompilerParams(vmem_limit_bytes=PACK_VMEM),
         name="pack",
-    )(user_factor.T, item_factor.T, day_factor)
+    )(*tables_in)
     pieces = [piece] + [swap(piece, "mp", holders, bits) for bits in range(1, holders)]
 
     picks_places_notes = pl.pallas_call(
@@ -299,8 +344,9 @@
             + [shape((owners * sizes.slots[t], list_counts[t]), bf16) for t in range(3)]
             + [shape((owners, sizes.rank), f32)]
         ),
-        in_specs=[pl.BlockSpec(memory_space=pltpu.SMEM)]
-        + [pl.BlockSpec(memory_space=pltpu.VMEM)] * 3,
+        in_specs=[pl.BlockSpec(memory_space=pltpu.SMEM)] + [hbm] * 3,
+        scratch_shapes=[pltpu.VMEM((1, count), jnp.int32) for count in list_counts]
+        + [pltpu.SemaphoreType.DMA((3,))],
         compiler_params=small,
         name="slots",
     )(lax.axis_index("dp").astype(jnp.int32).reshape(1), users_list, items_list, days_list)
@@ -310,24 +356,21 @@
         out_shape=shape((sizes.table_rows, LANES), bf16),
         compiler_params=small,
         name="table",
-    )(*pieces)
+    )(*pieces, picks_places_notes[6])
     tables = {0: table}
     for bits in range(2, owners, 2):
         tables[bits] = swap(table, "dp", owners, bits)
     for bits in range(0, owners, 2):
         tables[bits + 1] = swap(tables[bits], "dp", owners, 1)
 
-    whole = lambda a: pl.BlockSpec(a.shape, lambda s: (0,) * len(a.shape))
     inputs = [*[tables[bits] for bits in range(owners)], *picks_places_notes]
     users, items, days = list_counts
-    message = shape((sizes.slot_rows, sizes.rank), bf16)
-    gradients = pl.pallas_call(
+    steps = days // DAYS_PER_STEP
+    half = shape((owners // 2 * sizes.slot_rows, sizes.rank), bf16)
+    own, other = pl.pallas_call(
         functools.partial(block_kernel, sizes, DAYS_PER_STEP),
-        out_shape=tuple([message] * owners),
-        grid=(days // DAYS_PER_STEP,),
-        in_specs=[whole(a) for a in inputs]
-        + [pl.BlockSpec((1, DAYS_PER_STEP, users, items), lambda s: (0, s, 0, 0))],
-        out_specs=tuple([whole(message)] * owners),
+        out_shape=(half, half),
+        in_specs=[pl.BlockSpec(memory_space=pltpu.VMEM)] * len(inputs) + [hbm],
         scratch_shapes=[
             pltpu.VMEM((users, sizes.rank), f32),
             pltpu.VMEM((items, sizes.rank), bf16),
@@ -336,15 +379,22 @@
             pltpu.VMEM((users, sizes.rank), f32),
             pltpu.VMEM((items, sizes.rank), f32),
             pltpu.VMEM((days, sizes.rank), f32),
+            pltpu.VMEM((days, users, items), jnp.int32),
+            pltpu.SemaphoreType.DMA((steps,)),
         ],
         compiler_params=pltpu.CompilerParams(vmem_limit_bytes=BLOCK_VMEM),
         name="block_gradients",
     )(*inputs, status)
-    crossed = [swap(gradients[bits + 1], "dp", owners, 1) for bits in range(0, owners, 2)]
-    returned = [gradients[0], crossed[0]]
-    for bits in range(2, owners, 2):
-        returned.append(swap(gradients[bits], "dp", owners, bits))
-        returned.append(swap(crossed[bits // 2], "dp", owners, bits))
+    crossed = swap(other, "dp", owners, 1)
+    message = shape((2 * sizes.slot_rows, sizes.rank), bf16)
+    merged = pl.pallas_call(
+        functools.partial(merge_kernel, sizes),
+        out_shape=tuple([message] * (owners // 2 - 1)),
+        compiler_params=small,
+        name="merge",
+    )(own, crossed)
+    returned = [own, crossed]
+    returned += [swap(merged[bits // 2 - 1], "dp", owners, bits) for bits in range(2, owners, 2)]
 
     totals = pl.pallas_call(
         functools.partial(sum_kernel, sizes),

time: 59.8 us -> 54.2 us (0.906)
  local copies, waits for them, and re-layouts: 7.65 us -> 2.82 us
  starting transfers between devices: 22.2 us -> 18.1 us
  Pallas kernels: 10.9 us -> 13.3 us
  waiting for transfers between devices: 17.8 us -> 18.8 us
    unnamed x32 -> x26, local copies, waits for them, and re-layouts: 7.65 us -> 2.82 us
    ppermute x23 -> x17, starting transfers between devices: 22.2 us -> 18.1 us  [swap(): return lax.ppermute(array, axis, [(i, i ^ bits) for i in range(size)])]
    pallas_call x1, Pallas kernels: 0.07 us -> 1.52 us  [local(): pl.pallas_call(functools.partial(pack_kernel, sizes), out_shape=shape((si...]
    ppermute x23 -> x17, waiting for transfers between devices: 17.8 us -> 18.8 us  [swap(): return lax.ppermute(array, axis, [(i, i ^ bits) for i in range(size)])]
    pallas_call x1, Pallas kernels: 8.31 us -> 9.19 us  [local(): pl.pallas_call(functools.partial(block_kernel, sizes, DAYS_PER_STEP), out...]
  transfers between devices with their start and end apart: 23 -> 17, of which waited for: 11 -> 11; matrix products, arithmetic and copies ran while one was open for 0% -> 0% of each run, Pallas kernels for 2% -> 2%
where the time goes in v4:
time: 54.2 us; the launch traced here: 53.9 us
  waiting for transfers between devices  18.8 us (35%)
  starting transfers between devices  18.1 us (33%)
  Pallas kernels  13.3 us (25%)
  local copies, waits for them, and re-layouts  2.82 us (5%)
  between operations  0.8 us (1%)
    ppermute x17, waiting for transfers between devices, swap(): return lax.ppermute(array, axis, [(i, i ^ bits) for i in range(size)])  18.8 us
    ppermute x17, starting transfers between devices, swap(): return lax.ppermute(array, axis, [(i, i ^ bits) for i in range(size)])  18.1 us
    pallas_call x1, Pallas kernels, local(): pl.pallas_call(functools.partial(block_kernel, sizes, DAYS_PER_STEP), out...  9.19 us
    unnamed x26, local copies, waits for them, and re-layouts  2.82 us
    pallas_call x1, Pallas kernels, local(): pl.pallas_call(functools.partial(pack_kernel, sizes), out_shape=shape((si...  1.52 us
    pallas_call x1, Pallas kernels, local(): pl.pallas_call(functools.partial(slot_kernel, sizes), out_shape=tuple([sh...  1.16 us
  transfers between devices with their start and end apart: 17, of which 11 were waited for; matrix products, arithmetic and copies ran while one was open for 0% of the time, Pallas kernels for 2%

profile of v4, /device:TPU:0, one launch (start us, length us, event | category | flops | bytes accessed | tf_op | source)
XLA Modules:
  0.0 53.9 jit_solution(6587280181140745251)
XLA Ops:
  0.7 1.5 %pack.1.refs_0_ = bf16[144,128]{1,0:T(8,128)(2,1)} custom-call(f32[64,128]{1,0:T(8,128)} %bitcast.13, f32[64,128]{1,0:T(8,128)} %bitcast.15, f32[32,64]{1,0:T(8,128)} %refs_10_.1), custom_call_target="tpu_custom_call" | custom-call | tf_op jit(solution)/shard_map/pack/pallas_call | solution.py:329
  2.2 5.1 %collective-permute-start.2 = (bf16[144,128]{1,0:T(8,128)(2,1)}, bf16[144,128]{1,0:T(8,128)(2,1)S(1)}, u32[]{:S(2)}, u32[]{:S(2)}) collective-permute-start(bf16[144,128]{1,0:T(8,128)(2,1)} %pack.1.refs_0_), channel_id=1, source_target_pairs={{0,3},{1,2},{2,1},{3,0},{4,7},{5,6},{6,5},{7,4},{8,11},{9,10},{10,... | collective-permute-start | bytes 110600 | tf_op jit(solution)/shard_map/ppermute | solution.py:301
  7.3 0.6 %collective-permute-start = (bf16[144,128]{1,0:T(8,128)(2,1)}, bf16[144,128]{1,0:T(8,128)(2,1)S(1)}, u32[]{:S(2)}, u32[]{:S(2)}) collective-permute-start(bf16[144,128]{1,0:T(8,128)(2,1)} %pack.1.refs_0_), channel_id=1, source_target_pairs={{0,1},{1,0},{2,3},{3,2},{4,5},{5,4},{6,7},{7,6},{8,9},{9,8},{10,11... | collective-permute-start | bytes 110600 | tf_op jit(solution)/shard_map/ppermute | solution.py:301
  8.0 0.7 %copy-done.10 = s32[1,256]{1,0:T(1,128)S(1)} copy-done((s32[1,256]{1,0:T(1,128)S(1)}, s32[1,256]{1,0:T(1,128)}, u32[]{:S(2)}) %copy-start.10) | copy-done | bytes 1048
  8.7 0.7 %copy-done.11 = s32[1,256]{1,0:T(1,128)S(1)} copy-done((s32[1,256]{1,0:T(1,128)S(1)}, s32[1,256]{1,0:T(1,128)}, u32[]{:S(2)}) %copy-start.11) | copy-done | bytes 1048
  9.3 0.7 %copy-done.12 = s32[1,32]{1,0:T(1,128)S(1)} copy-done((s32[1,32]{1,0:T(1,128)S(1)}, s32[1,32]{1,0:T(1,128)}, u32[]{:S(2)}) %copy-start.12) | copy-done | bytes 152
  10.0 1.2 %slots.1 = (bf16[1024,256]{1,0:T(8,128)(2,1)S(1)}, bf16[1024,256]{1,0:T(8,128)(2,1)S(1)}, bf16[256,32]{1,0:T(8,128)(2,1)S(1)}, bf16[384,256]{1,0:T(8,128)(2,1)S(...) custom-call(s32[1]{0:T(128)} %bitcast.2.me_ref, s32[1,256]{1,0:T(1,128)S(1)} %copy-done.10, ...), custom_call_target="tpu_custom_call" | custom-call | tf_op jit(solution)/shard_map/slots/pallas_call | solution.py:340
  11.2 1.2 %collective-permute-done.1.refs_2_ = bf16[144,128]{1,0:T(8,128)(2,1)S(1)} collective-permute-done((bf16[144,128]{1,0:T(8,128)(2,1)}, bf16[144,128]{1,0:T(8,128)(2,1)S(1)}, u32[]{:S(2)}, u32[]{:S(2)}) %collective-permute-start.1) | collective-permute-done | bytes 36896 | tf_op jit(solution)/shard_map/ppermute | solution.py:301
  12.4 0.8 %copy-done = bf16[144,128]{1,0:T(8,128)(2,1)S(1)} copy-done((bf16[144,128]{1,0:T(8,128)(2,1)S(1)}, bf16[144,128]{1,0:T(8,128)(2,1)}, u32[]{:S(2)}) %copy-start) | copy-done | bytes 36888
  13.3 2.5 %collective-permute-start.8 = (bf16[576,128]{1,0:T(8,128)(2,1)S(1)}, bf16[576,128]{1,0:T(8,128)(2,1)S(1)}, u32[]{:S(2)}, u32[]{:S(2)}) collective-permute-start(bf16[576,128]{1,0:T(8,128)(2,1)S(1)} %table.1.refs_0_), channel_id=1, source_target_pairs={{0,24},{4,28},{8,16},{12,20},{16,8},{20,12},{24,0},{28,4},{1,25},{... | collective-permute-start | bytes 442376 | tf_op jit(solution)/shard_map/ppermute | solution.py:301
  15.8 0.5 collective-permute-start.6
  16.3 0.5 collective-permute-start.4
  16.8 4.1 %collective-permute-done.8.refs_6_ = bf16[576,128]{1,0:T(8,128)(2,1)S(1)} collective-permute-done((bf16[576,128]{1,0:T(8,128)(2,1)S(1)}, bf16[576,128]{1,0:T(8,128)(2,1)S(1)}, u32[]{:S(2)}, u32[]{:S(2)}) %collective-permute-start.8) | collective-permute-done | bytes 147488 | tf_op jit(solution)/shard_map/ppermute | solution.py:301
  21.0 0.8 %collective-permute-done.6.refs_4_ = bf16[576,128]{1,0:T(8,128)(2,1)S(1)} collective-permute-done((bf16[576,128]{1,0:T(8,128)(2,1)S(1)}, bf16[576,128]{1,0:T(8,128)(2,1)S(1)}, u32[]{:S(2)}, u32[]{:S(2)}) %collective-permute-start.6) | collective-permute-done | bytes 147488 | tf_op jit(solution)/shard_map/ppermute | solution.py:301
  21.7 0.5 collective-permute-start.5
  22.3 0.8 %collective-permute-done.7.refs_5_ = bf16[576,128]{1,0:T(8,128)(2,1)S(1)} collective-permute-done((bf16[576,128]{1,0:T(8,128)(2,1)S(1)}, bf16[576,128]{1,0:T(8,128)(2,1)S(1)}, u32[]{:S(2)}, u32[]{:S(2)}) %collective-permute-start.7) | collective-permute-done | bytes 147488 | tf_op jit(solution)/shard_map/ppermute | solution.py:301
  23.1 0.2 collective-permute-done.5.refs_3_
  23.3 9.2 %block_gradients.1 = (bf16[448,256]{1,0:T(8,128)(2,1)S(1)}, bf16[448,256]{1,0:T(8,128)(2,1)S(1)}) custom-call(bf16[576,128]{1,0:T(8,128)(2,1)S(1)} %table.1.refs_0_, bf16[576,128]{1,0:T(8,128)(2,1)S(1)} %collective-permute-done.3.refs_1_, bf16[576,128]{1,0:T(8,128)(2,1)S(1)} %collective-permute-done.4.refs_2_, ...), custom_call_target="tpu_custom_call" | custom-call | tf_op jit(solution)/shard_map/block_gradients/pallas_call | solution.py:370
  32.5 0.4 collective-permute-start.10
  32.9 1.2 %collective-permute-done.10.crossed_ref.refs_1_ = bf16[448,256]{1,0:T(8,128)(2,1)S(1)} collective-permute-done((bf16[448,256]{1,0:T(8,128)(2,1)S(1)}, bf16[448,256]{1,0:T(8,128)(2,1)S(1)}, u32[]{:S(2)}, u32[]{:S(2)}) %collective-permute-start.10) | collective-permute-done | bytes 229408 | tf_op jit(solution)/shard_map/ppermute | solution.py:301
  34.1 1.4 %collective-permute-start.11 = (bf16[224,256]{1,0:T(8,128)(2,1)S(1)}, bf16[224,256]{1,0:T(8,128)(2,1)S(1)}, u32[]{:S(2)}, u32[]{:S(2)}) collective-permute-start(bf16[224,256]{1,0:T(8,128)(2,1)S(1)} %get-tuple-element.43), channel_id=1, source_target_pairs={{0,8},{4,12},{8,0},{12,4},{16,24},{20,28},{24,16},{28,20},{1,9},{5... | collective-permute-start | bytes 344072 | tf_op jit(solution)/shard_map/ppermute | solution.py:301
  35.5 0.8 %collective-permute-start.12 = (bf16[224,256]{1,0:T(8,128)(2,1)S(1)}, bf16[224,256]{1,0:T(8,128)(2,1)S(1)}, u32[]{:S(2)}, u32[]{:S(2)}) collective-permute-start(bf16[224,256]{1,0:T(8,128)(2,1)S(1)} %get-tuple-element.44), channel_id=1, source_target_pairs={{0,16},{4,20},{8,24},{12,28},{16,0},{20,4},{24,8},{28,12},{1,17},{... | collective-permute-start | bytes 344072 | tf_op jit(solution)/shard_map/ppermute | solution.py:301
  36.3 1.4 %collective-permute-start.13 = (bf16[224,256]{1,0:T(8,128)(2,1)S(1)}, bf16[224,256]{1,0:T(8,128)(2,1)S(1)}, u32[]{:S(2)}, u32[]{:S(2)}) collective-permute-start(bf16[224,256]{1,0:T(8,128)(2,1)S(1)} %get-tuple-element.45), channel_id=1, source_target_pairs={{0,24},{4,28},{8,16},{12,20},{16,8},{20,12},{24,0},{28,4},{1,25},{... | collective-permute-start | bytes 344072 | tf_op jit(solution)/shard_map/ppermute | solution.py:301
  37.6 2.0 %collective-permute-done.11.refs_2_ = bf16[224,256]{1,0:T(8,128)(2,1)S(1)} collective-permute-done((bf16[224,256]{1,0:T(8,128)(2,1)S(1)}, bf16[224,256]{1,0:T(8,128)(2,1)S(1)}, u32[]{:S(2)}, u32[]{:S(2)}) %collective-permute-start.11) | collective-permute-done | bytes 114720 | tf_op jit(solution)/shard_map/ppermute | solution.py:301
  39.7 3.3 %collective-permute-done.12.refs_3_ = bf16[224,256]{1,0:T(8,128)(2,1)S(1)} collective-permute-done((bf16[224,256]{1,0:T(8,128)(2,1)S(1)}, bf16[224,256]{1,0:T(8,128)(2,1)S(1)}, u32[]{:S(2)}, u32[]{:S(2)}) %collective-permute-start.12) | collective-permute-done | bytes 114720 | tf_op jit(solution)/shard_map/ppermute | solution.py:301
  43.0 0.6 %row_sums.1 = (bf16[144,128]{1,0:T(8,128)(2,1)S(1)}, bf16[144,128]{1,0:T(8,128)(2,1)S(1)}, bf16[144,128]{1,0:T(8,128)(2,1)S(1)}, bf16[144,128]{1,0:T(8,128)(2,1)S(1)}) custom-call(bf16[448,256]{1,0:T(8,128)(2,1)S(1)} %get-tuple-element.41.own_ref.refs_0_, bf16[448,256]{1,0:T(8,128)(2,1)S(1)} %collective-permute-done.10.crossed_ref.refs_1_, ...), custom_call_target="tpu_custom_call" | custom-call | tf_op jit(solution)/shard_map/row_sums/pallas_call | solution.py:399
  43.6 1.1 %collective-permute-start.14 = (bf16[144,128]{1,0:T(8,128)(2,1)S(1)}, bf16[144,128]{1,0:T(8,128)(2,1)S(1)}, u32[]{:S(2)}, u32[]{:S(2)}) collective-permute-start(bf16[144,128]{1,0:T(8,128)(2,1)S(1)} %get-tuple-element.47), channel_id=1, source_target_pairs={{0,1},{1,0},{2,3},{3,2},{4,5},{5,4},{6,7},{7,6},{8,9},{9,8},{10,11... | collective-permute-start | bytes 110600 | tf_op jit(solution)/shard_map/ppermute | solution.py:301
  44.7 2.6 %collective-permute-start.15 = (bf16[144,128]{1,0:T(8,128)(2,1)S(1)}, bf16[144,128]{1,0:T(8,128)(2,1)S(1)}, u32[]{:S(2)}, u32[]{:S(2)}) collective-permute-start(bf16[144,128]{1,0:T(8,128)(2,1)S(1)} %get-tuple-element.48), channel_id=1, source_target_pairs={{0,2},{1,3},{2,0},{3,1},{4,6},{5,7},{6,4},{7,5},{8,10},{9,11},{10,... | collective-permute-start | bytes 110600 | tf_op jit(solution)/shard_map/ppermute | solution.py:301
  47.3 0.7 %collective-permute-start.16 = (bf16[144,128]{1,0:T(8,128)(2,1)S(1)}, bf16[144,128]{1,0:T(8,128)(2,1)S(1)}, u32[]{:S(2)}, u32[]{:S(2)}) collective-permute-start(bf16[144,128]{1,0:T(8,128)(2,1)S(1)} %get-tuple-element.49), channel_id=1, source_target_pairs={{0,3},{1,2},{2,1},{3,0},{4,7},{5,6},{6,5},{7,4},{8,11},{9,10},{10,... | collective-permute-start | bytes 110600 | tf_op jit(solution)/shard_map/ppermute | solution.py:301
  48.0 1.5 %collective-permute-done.15.refs_2_ = bf16[144,128]{1,0:T(8,128)(2,1)S(1)} collective-permute-done((bf16[144,128]{1,0:T(8,128)(2,1)S(1)}, bf16[144,128]{1,0:T(8,128)(2,1)S(1)}, u32[]{:S(2)}, u32[]{:S(2)}) %collective-permute-start.15) | collective-permute-done | bytes 36896 | tf_op jit(solution)/shard_map/ppermute | solution.py:301
  49.5 3.5 %collective-permute-done.16.refs_3_ = bf16[144,128]{1,0:T(8,128)(2,1)S(1)} collective-permute-done((bf16[144,128]{1,0:T(8,128)(2,1)S(1)}, bf16[144,128]{1,0:T(8,128)(2,1)S(1)}, u32[]{:S(2)}, u32[]{:S(2)}) %collective-permute-start.16) | collective-permute-done | bytes 36896 | tf_op jit(solution)/shard_map/ppermute | solution.py:301
  53.1 0.7 %adam.1 = (f32[64,128]{1,0:T(8,128)}, f32[64,128]{1,0:T(8,128)}, f32[64,128]{1,0:T(8,128)}, f32[64,128]{1,0:T(8,128)}, f32[64,128]{1,0:T(8,128)}, /*index=5*/f32...) custom-call(bf16[144,128]{1,0:T(8,128)(2,1)S(1)} %get-tuple-element.46.refs_0_, ...), custom_call_target="tpu_custom_call" | custom-call | tf_op jit(solution)/shard_map/adam/pallas_call | solution.py:420
  (35 shorter events, 0.3 us)
Async XLA Ops:
  0.6 52.4 %copy-start.3 = (f32[32,64]{1,0:T(8,128)S(1)}, f32[32,64]{1,0:T(8,128)}, u32[]{:S(2)}) copy-start(f32[32,64]{1,0:T(8,128)} %refs_10_.1) | copy-start | bytes 24580
  0.7 52.4 %copy-start.2 = (f32[128,64]{0,1:T(8,128)S(1)}, f32[128,64]{0,1:T(8,128)}, u32[]{:S(2)}) copy-start(f32[128,64]{0,1:T(8,128)} %param.20) | copy-start | bytes 98308
  0.7 52.4 %copy-start.1 = (f32[128,64]{0,1:T(8,128)S(1)}, f32[128,64]{0,1:T(8,128)}, u32[]{:S(2)}) copy-start(f32[128,64]{0,1:T(8,128)} %param.17) | copy-start | bytes 98308
  0.7 52.4 %copy-start.8 = (f32[32,64]{1,0:T(8,128)S(1)}, f32[32,64]{1,0:T(8,128)}, u32[]{:S(2)}) copy-start(f32[32,64]{1,0:T(8,128)} %refs_11_.1) | copy-start | bytes 24580
  0.7 52.4 %copy-start.4 = (f32[128,64]{0,1:T(8,128)S(1)}, f32[128,64]{0,1:T(8,128)}, u32[]{:S(2)}) copy-start(f32[128,64]{0,1:T(8,128)} %param.18) | copy-start | bytes 98308
  2.2 8.9 %collective-permute-start.2 = (bf16[144,128]{1,0:T(8,128)(2,1)}, bf16[144,128]{1,0:T(8,128)(2,1)S(1)}, u32[]{:S(2)}, u32[]{:S(2)}) collective-permute-start(bf16[144,128]{1,0:T(8,128)(2,1)} %pack.1.refs_0_), channel_id=1, source_target_pairs={{0,3},{1,2},{2,1},{3,0},{4,7},{5,6},{6,5},{7,4},{8,11},{9,10},{10,... | collective-permute-start | bytes 110600 | tf_op jit(solution)/shard_map/ppermute | solution.py:301
  7.3 5.1 %collective-permute-start.1 = (bf16[144,128]{1,0:T(8,128)(2,1)}, bf16[144,128]{1,0:T(8,128)(2,1)S(1)}, u32[]{:S(2)}, u32[]{:S(2)}) collective-permute-start(bf16[144,128]{1,0:T(8,128)(2,1)} %pack.1.refs_0_), channel_id=1, source_target_pairs={{0,2},{1,3},{2,0},{3,1},{4,6},{5,7},{6,4},{7,5},{8,10},{9,11},{10,... | collective-permute-start | bytes 110600 | tf_op jit(solution)/shard_map/ppermute | solution.py:301
  7.3 5.1 %collective-permute-start = (bf16[144,128]{1,0:T(8,128)(2,1)}, bf16[144,128]{1,0:T(8,128)(2,1)S(1)}, u32[]{:S(2)}, u32[]{:S(2)}) collective-permute-start(bf16[144,128]{1,0:T(8,128)(2,1)} %pack.1.refs_0_), channel_id=1, source_target_pairs={{0,1},{1,0},{2,3},{3,2},{4,5},{5,4},{6,7},{7,6},{8,9},{9,8},{10,11... | collective-permute-start | bytes 110600 | tf_op jit(solution)/shard_map/ppermute | solution.py:301
  8.0 0.7 %copy-start.10 = (s32[1,256]{1,0:T(1,128)S(1)}, s32[1,256]{1,0:T(1,128)}, u32[]{:S(2)}) copy-start(s32[1,256]{1,0:T(1,128)} %refs_0_.1) | copy-start | bytes 3076
  8.7 0.7 %copy-start.11 = (s32[1,256]{1,0:T(1,128)S(1)}, s32[1,256]{1,0:T(1,128)}, u32[]{:S(2)}) copy-start(s32[1,256]{1,0:T(1,128)} %refs_1_.1) | copy-start | bytes 3076
  9.3 0.7 %copy-start.12 = (s32[1,32]{1,0:T(1,128)S(1)}, s32[1,32]{1,0:T(1,128)}, u32[]{:S(2)}) copy-start(s32[1,32]{1,0:T(1,128)} %refs_2_.1) | copy-start | bytes 388
  12.4 0.8 %copy-start = (bf16[144,128]{1,0:T(8,128)(2,1)S(1)}, bf16[144,128]{1,0:T(8,128)(2,1)}, u32[]{:S(2)}) copy-start(bf16[144,128]{1,0:T(8,128)(2,1)} %pack.1.refs_0_) | copy-start | bytes 110596
  13.2 39.9 %copy-start.5 = (f32[128,64]{0,1:T(8,128)S(1)}, f32[128,64]{0,1:T(8,128)}, u32[]{:S(2)}) copy-start(f32[128,64]{0,1:T(8,128)} %param.19) | copy-start | bytes 98308
  13.2 39.9 %copy-start.6 = (f32[128,64]{0,1:T(8,128)S(1)}, f32[128,64]{0,1:T(8,128)}, u32[]{:S(2)}) copy-start(f32[128,64]{0,1:T(8,128)} %param.21) | copy-start | bytes 98308
  13.2 39.9 %copy-start.7 = (f32[128,64]{0,1:T(8,128)S(1)}, f32[128,64]{0,1:T(8,128)}, u32[]{:S(2)}) copy-start(f32[128,64]{0,1:T(8,128)} %param.22) | copy-start | bytes 98308
  13.2 40.0 %copy-start.9 = (f32[32,64]{1,0:T(8,128)S(1)}, f32[32,64]{1,0:T(8,128)}, u32[]{:S(2)}) copy-start(f32[32,64]{1,0:T(8,128)} %refs_12_.1) | copy-start | bytes 24580
  13.3 7.6 %collective-permute-start.8 = (bf16[576,128]{1,0:T(8,128)(2,1)S(1)}, bf16[576,128]{1,0:T(8,128)(2,1)S(1)}, u32[]{:S(2)}, u32[]{:S(2)}) collective-permute-start(bf16[576,128]{1,0:T(8,128)(2,1)S(1)} %table.1.refs_0_), channel_id=1, source_target_pairs={{0,24},{4,28},{8,16},{12,20},{16,8},{20,12},{24,0},{28,4},{1,25},{... | collective-permute-start | bytes 442376 | tf_op jit(solution)/shard_map/ppermute | solution.py:301
  15.8 6.0 %collective-permute-start.6 = (bf16[576,128]{1,0:T(8,128)(2,1)S(1)}, bf16[576,128]{1,0:T(8,128)(2,1)S(1)}, u32[]{:S(2)}, u32[]{:S(2)}) collective-permute-start(bf16[576,128]{1,0:T(8,128)(2,1)S(1)} %table.1.refs_0_), channel_id=1, source_target_pairs={{0,16},{4,20},{8,24},{12,28},{16,0},{20,4},{24,8},{28,12},{1,17},{... | collective-permute-start | bytes 442376 | tf_op jit(solution)/shard_map/ppermute | solution.py:301
  16.3 5.4 %collective-permute-start.4 = (bf16[576,128]{1,0:T(8,128)(2,1)S(1)}, bf16[576,128]{1,0:T(8,128)(2,1)S(1)}, u32[]{:S(2)}, u32[]{:S(2)}) collective-permute-start(bf16[576,128]{1,0:T(8,128)(2,1)S(1)} %table.1.refs_0_), channel_id=1, source_target_pairs={{0,8},{4,12},{8,0},{12,4},{16,24},{20,28},{24,16},{28,20},{1,9},{5... | collective-permute-start | bytes 442376 | tf_op jit(solution)/shard_map/ppermute | solution.py:301
  16.8 5.4 %collective-permute-start.3 = (bf16[576,128]{1,0:T(8,128)(2,1)S(1)}, bf16[576,128]{1,0:T(8,128)(2,1)S(1)}, u32[]{:S(2)}, u32[]{:S(2)}) collective-permute-start(bf16[576,128]{1,0:T(8,128)(2,1)S(1)} %table.1.refs_0_), channel_id=1, source_target_pairs={{0,4},{4,0},{8,12},{12,8},{16,20},{20,16},{24,28},{28,24},{1,5},{5... | collective-permute-start | bytes 442376 | tf_op jit(solution)/shard_map/ppermute | solution.py:301
  21.0 1.4 %collective-permute-start.9 = (bf16[576,128]{1,0:T(8,128)(2,1)S(1)}, bf16[576,128]{1,0:T(8,128)(2,1)S(1)}, u32[]{:S(2)}, u32[]{:S(2)}) collective-permute-start(bf16[576,128]{1,0:T(8,128)(2,1)S(1)} %collective-permute-done.8.refs_6_), channel_id=1, source_target_pairs={{0,4},{4,0},{8,12},{12,8},{16,20},{20,16},{24,28},{28,24},{1,5},{5... | collective-permute-start | bytes 442376 | tf_op jit(solution)/shard_map/ppermute | solution.py:301
  21.7 1.4 %collective-permute-start.7 = (bf16[576,128]{1,0:T(8,128)(2,1)S(1)}, bf16[576,128]{1,0:T(8,128)(2,1)S(1)}, u32[]{:S(2)}, u32[]{:S(2)}) collective-permute-start(bf16[576,128]{1,0:T(8,128)(2,1)S(1)} %collective-permute-done.6.refs_4_), channel_id=1, source_target_pairs={{0,4},{4,0},{8,12},{12,8},{16,20},{20,16},{24,28},{28,24},{1,5},{5... | collective-permute-start | bytes 442376 | tf_op jit(solution)/shard_map/ppermute | solution.py:301
  21.7 1.6 %collective-permute-start.5 = (bf16[576,128]{1,0:T(8,128)(2,1)S(1)}, bf16[576,128]{1,0:T(8,128)(2,1)S(1)}, u32[]{:S(2)}, u32[]{:S(2)}) collective-permute-start(bf16[576,128]{1,0:T(8,128)(2,1)S(1)} %collective-permute-done.4.refs_2_), channel_id=1, source_target_pairs={{0,4},{4,0},{8,12},{12,8},{16,20},{20,16},{24,28},{28,24},{1,5},{5... | collective-permute-start | bytes 442376 | tf_op jit(solution)/shard_map/ppermute | solution.py:301
  32.5 1.6 %collective-permute-start.10 = (bf16[448,256]{1,0:T(8,128)(2,1)S(1)}, bf16[448,256]{1,0:T(8,128)(2,1)S(1)}, u32[]{:S(2)}, u32[]{:S(2)}) collective-permute-start(bf16[448,256]{1,0:T(8,128)(2,1)S(1)} %get-tuple-element.42), channel_id=1, source_target_pairs={{0,4},{4,0},{8,12},{12,8},{16,20},{20,16},{24,28},{28,24},{1,5},{5... | collective-permute-start | bytes 688136 | tf_op jit(solution)/shard_map/ppermute | solution.py:301
  34.1 5.6 %collective-permute-start.11 = (bf16[224,256]{1,0:T(8,128)(2,1)S(1)}, bf16[224,256]{1,0:T(8,128)(2,1)S(1)}, u32[]{:S(2)}, u32[]{:S(2)}) collective-permute-start(bf16[224,256]{1,0:T(8,128)(2,1)S(1)} %get-tuple-element.43), channel_id=1, source_target_pairs={{0,8},{4,12},{8,0},{12,4},{16,24},{20,28},{24,16},{28,20},{1,9},{5... | collective-permute-start | bytes 344072 | tf_op jit(solution)/shard_map/ppermute | solution.py:301
  35.5 7.5 %collective-permute-start.12 = (bf16[224,256]{1,0:T(8,128)(2,1)S(1)}, bf16[224,256]{1,0:T(8,128)(2,1)S(1)}, u32[]{:S(2)}, u32[]{:S(2)}) collective-permute-start(bf16[224,256]{1,0:T(8,128)(2,1)S(1)} %get-tuple-element.44), channel_id=1, source_target_pairs={{0,16},{4,20},{8,24},{12,28},{16,0},{20,4},{24,8},{28,12},{1,17},{... | collective-permute-start | bytes 344072 | tf_op jit(solution)/shard_map/ppermute | solution.py:301
  36.3 6.7 %collective-permute-start.13 = (bf16[224,256]{1,0:T(8,128)(2,1)S(1)}, bf16[224,256]{1,0:T(8,128)(2,1)S(1)}, u32[]{:S(2)}, u32[]{:S(2)}) collective-permute-start(bf16[224,256]{1,0:T(8,128)(2,1)S(1)} %get-tuple-element.45), channel_id=1, source_target_pairs={{0,24},{4,28},{8,16},{12,20},{16,8},{20,12},{24,0},{28,4},{1,25},{... | collective-permute-start | bytes 344072 | tf_op jit(solution)/shard_map/ppermute | solution.py:301
  43.6 4.5 %collective-permute-start.14 = (bf16[144,128]{1,0:T(8,128)(2,1)S(1)}, bf16[144,128]{1,0:T(8,128)(2,1)S(1)}, u32[]{:S(2)}, u32[]{:S(2)}) collective-permute-start(bf16[144,128]{1,0:T(8,128)(2,1)S(1)} %get-tuple-element.47), channel_id=1, source_target_pairs={{0,1},{1,0},{2,3},{3,2},{4,5},{5,4},{6,7},{7,6},{8,9},{9,8},{10,11... | collective-permute-start | bytes 110600 | tf_op jit(solution)/shard_map/ppermute | solution.py:301
  44.7 4.9 %collective-permute-start.15 = (bf16[144,128]{1,0:T(8,128)(2,1)S(1)}, bf16[144,128]{1,0:T(8,128)(2,1)S(1)}, u32[]{:S(2)}, u32[]{:S(2)}) collective-permute-start(bf16[144,128]{1,0:T(8,128)(2,1)S(1)} %get-tuple-element.48), channel_id=1, source_target_pairs={{0,2},{1,3},{2,0},{3,1},{4,6},{5,7},{6,4},{7,5},{8,10},{9,11},{10,... | collective-permute-start | bytes 110600 | tf_op jit(solution)/shard_map/ppermute | solution.py:301
  47.3 5.8 %collective-permute-start.16 = (bf16[144,128]{1,0:T(8,128)(2,1)S(1)}, bf16[144,128]{1,0:T(8,128)(2,1)S(1)}, u32[]{:S(2)}, u32[]{:S(2)}) collective-permute-start(bf16[144,128]{1,0:T(8,128)(2,1)S(1)} %get-tuple-element.49), channel_id=1, source_target_pairs={{0,3},{1,2},{2,1},{3,0},{4,7},{5,6},{6,5},{7,4},{8,11},{9,10},{10,... | collective-permute-start | bytes 110600 | tf_op jit(solution)/shard_map/ppermute | solution.py:301

commit v5 on v4

--- a/solution.py
+++ b/solution.py
@@ -16,7 +16,6 @@
 loss_scale = 0.0625
 
 LANES = 128
-DAYS_PER_STEP = 4
 SMALL_VMEM = 16 * 1024 * 1024
 BLOCK_VMEM = 48 * 1024 * 1024
 PACK_VMEM = 56 * 1024 * 1024
@@ -102,8 +101,8 @@
 
 def slot_kernel(sizes, me_ref, *refs):
     owners = sizes.owners
-    picks, places, note_ref, lists = refs[3:6], refs[6:9], refs[9], refs[10:13]
-    fetch(refs[:3], lists, refs[13])
+    picks, places, note_ref, lists = refs[4:7], refs[7:10], refs[10], refs[11:14]
+    fetch(refs[:3], lists, refs[14])
     me = me_ref[0]
     notes = [[] for _ in range(owners)]
     for t in range(3):
@@ -130,7 +129,7 @@
 
 
 def table_kernel(sizes, *refs):
-    pieces, out_ref = refs[:-2], refs[-1]
+    pieces, out_ref = refs[:-1], refs[-1]
     columns, rank, day_rows = sizes.columns, sizes.rank, sizes.row_counts[2]
     for j, ref in enumerate(pieces):
         for t in range(2):
@@ -145,39 +144,58 @@
         out_ref[start : start + day_rows, :] = days[:, chunk * LANES : (chunk + 1) * LANES]
 
 
-def block_kernel(sizes, days_per_step, *refs):
+def block_kernel(sizes, *refs):
     owners, rank, day_rows = sizes.owners, sizes.rank, sizes.row_counts[2]
-    tables = refs[:owners]
-    picks = refs[owners : owners + 3]
-    places = refs[owners + 3 : owners + 6]
-    note_ref, status_hbm, own_ref, other_ref = refs[owners + 6 : owners + 10]
+    own_table, own_crossed, tables_ref, tables_crossed = refs[:4]
+    picks, places = refs[4:7], refs[7:10]
+    note_ref, status_hbm, own_ref, other_ref = refs[10:14]
     (
         users,
+        users_low,
         items,
         items_half_t,
         days,
         user_gradient,
         item_gradient,
         day_gradient,
+        scaled_even,
+        scaled_odd,
+        residual_even,
+        residual_odd,
         status,
         semaphores,
-    ) = refs[owners + 10 :]
-    steps = status.shape[0] // days_per_step
-
-    def status_copy(step):
-        chunk = pl.ds(step * days_per_step, days_per_step)
+    ) = refs[14:]
+    pair = 2
+    pairs = status.shape[0] // pair
+    chunks = [(0, pair)]
+    chunks += [((2 * n - 1) * pair, 2 * pair) for n in range(1, pairs // 2)]
+    chunks += [((pairs - 1) * pair, pair)]
+
+    def status_copy(start, size, semaphore):
+        part = pl.ds(start, size)
         return pltpu.make_async_copy(
-            status_hbm.at[0, chunk], status.at[chunk], semaphores.at[step]
+            status_hbm.at[0, part], status.at[part], semaphores.at[semaphore]
         )
 
-    for step in range(steps):
-        status_copy(step).start()
+    for n, (start, size) in enumerate(chunks):
+        status_copy(start, size, n).start()
+
+    height = sizes.table_rows
+    tables = []
+    for n in range(owners // 2):
+        if n == 0:
+            tables += [own_table, own_crossed]
+        else:
+            part = slice((n - 1) * height, n * height)
+            tables += [tables_ref.at[part], tables_crossed.at[part]]
 
     def pick(t):
         table = jnp.concatenate([ref[t * rank : (t + 1) * rank, :] for ref in tables], axis=1)
         return jnp.dot(table, picks[t][...], preferred_element_type=f32)
 
-    users[...] = pick(0).T
+    user_values = pick(0).T
+    users[...] = user_values
+    users_low[...] = user_values.astype(bf16)
     items_t = pick(1)
     items[...] = items_t.T.astype(bf16)
     items_half_t[...] = (0.5 * items_t).astype(bf16)
@@ -194,32 +212,58 @@
     )
     user_gradient[...] = jnp.zeros_like(user_gradient)
     item_gradient[...] = jnp.zeros_like(item_gradient)
-
-    @pl.loop(0, steps)
-    def _(step):
-        status_copy(step).wait()
-        for j in range(days_per_step):
-            k = step * days_per_step + j
-            day = days[pl.ds(k, 1), :]
-            user_values = users[...]
-            scaled = (day * user_values).astype(bf16)
-            half_logits = jnp.dot(scaled, items_half_t[...], preferred_element_type=f32)
-            state = status[k]
-            residual = (
-                (0.5 * loss_scale)
-                * state.astype(f32)
-                * (jnp.tanh(half_logits) + jnp.where(state == 1, -1.0, 1.0))
+    count = users.shape[0]
+
+    def residuals(first, scaled, residual):
+        for j in range(pair):
+            rows = slice(j * count, (j + 1) * count)
+            day = days[pl.ds(first + j, 1), :].astype(bf16)
+            scaled_values = day * users_low[...]
+            scaled[rows, :] = scaled_values
+            half_logits = jnp.dot(scaled_values, items_half_t[...], preferred_element_type=f32)
+            state = status[first + j]
+            residual[rows, :] = (
+                state.astype(f32) * (jnp.tanh(half_logits) + jnp.where(state == 1, -1.0, 1.0))
             ).astype(bf16)
-            projected = jnp.dot(residual, items[...], preferred_element_type=f32)
-            user_gradient[...] += projected * day
-            day_gradient[pl.ds(k, 1), :] = jnp.sum(projected * user_values, axis=0, keepdims=True)
-            item_gradient[...] += lax.dot_general(
-                residual, scaled, (((0,), (0,)), ((), ())), preferred_element_type=f32
+
+    def gradients(first, scaled, residual):
+        total = 0.0
+        for j in range(pair):
+            rows = slice(j * count, (j + 1) * count)
+            day = days[pl.ds(first + j, 1), :]
+            projected = jnp.dot(residual[rows, :], items[...], preferred_element_type=f32)
+            total = total + projected * day
+            day_gradient[pl.ds(first + j, 1), :] = jnp.sum(
+                projected * users[...], axis=0, keepdims=True
             )
+        user_gradient[...] += total
+        item_gradient[...] += lax.dot_general(
+            residual[...], scaled[...], (((0,), (0,)), ((), ())), preferred_element_type=f32
+        )
+
+    even, odd = (scaled_even, residual_even), (scaled_odd, residual_odd)
+    status_copy(*chunks[0], 0).wait()
+    residuals(0, *even)
+
+    @pl.loop(0, pairs // 2 - 1)
+    def _(n):
+        first = 2 * n * pair
+        status_copy(first + pair, 2 * pair, n + 1).wait()
+        residuals(first + pair, *odd)
+        gradients(first, *even)
+        residuals(first + 2 * pair, *even)
+        gradients(first + pair, *odd)
+
+    last = (pairs - 1) * pair
+    status_copy(*chunks[-1], len(chunks) - 1).wait()
+    residuals(last, *odd)
+    gradients(last - pair, *even)
+    gradients(last, *odd)
 
     for t, gradient in enumerate((user_gradient, item_gradient, day_gradient)):
         start, slots = sizes.slot_starts[t], sizes.slots[t]
-        placed = jnp.dot(places[t][...], gradient[...].astype(bf16), preferred_element_type=f32)
+        values = (0.5 * loss_scale * gradient[...]).astype(bf16)
+        placed = jnp.dot(places[t][...], values, preferred_element_type=f32)
         for s in range(owners):
             rows = placed[s * slots : (s + 1) * slots]
             if t == 2:
@@ -228,6 +272,12 @@
             out = (own_ref, other_ref)[s % 2]
             first = (s // 2) * sizes.slot_rows + start
             out[first : first + slots, :] = rows.astype(bf16)
+
+
+def join_kernel(sizes, *refs):
+    arrived, out_ref = refs[:-2], refs[-1]
+    for n, ref in enumerate(arrived):
+        out_ref[n * sizes.table_rows : (n + 1) * sizes.table_rows, :] = ref[...]
 
 
 def merge_kernel(sizes, own_ref, crossed_ref, *outs):
@@ -337,6 +387,14 @@
     )(*tables_in)
     pieces = [piece] + [swap(piece, "mp", holders, bits) for bits in range(1, holders)]
 
+    table = pl.pallas_call(
+        functools.partial(table_kernel, sizes),
+        out_shape=shape((sizes.table_rows, LANES), bf16),
+        compiler_params=small,
+        name="table",
+    )(*pieces)
+    arrived = [swap(table, "dp", owners, bits) for bits in range(2, owners, 2)]
+    own_crossed = swap(table, "dp", owners, 1)
     picks_places_notes = pl.pallas_call(
         functools.partial(slot_kernel, sizes),
         out_shape=tuple(
@@ -344,43 +402,43 @@
             + [shape((owners * sizes.slots[t], list_counts[t]), bf16) for t in range(3)]
             + [shape((owners, sizes.rank), f32)]
         ),
-        in_specs=[pl.BlockSpec(memory_space=pltpu.SMEM)] + [hbm] * 3,
+        in_specs=[pl.BlockSpec(memory_space=pltpu.SMEM)] + [hbm] * 4,
         scratch_shapes=[pltpu.VMEM((1, count), jnp.int32) for count in list_counts]
         + [pltpu.SemaphoreType.DMA((3,))],
         compiler_params=small,
         name="slots",
-    )(lax.axis_index("dp").astype(jnp.int32).reshape(1), users_list, items_list, days_list)
-
-    table = pl.pallas_call(
-        functools.partial(table_kernel, sizes),
-        out_shape=shape((sizes.table_rows, LANES), bf16),
-        compiler_params=small,
-        name="table",
-    )(*pieces, picks_places_notes[6])
-    tables = {0: table}
-    for bits in range(2, owners, 2):
-        tables[bits] = swap(table, "dp", owners, bits)
-    for bits in range(0, owners, 2):
-        tables[bits + 1] = swap(tables[bits], "dp", owners, 1)
-
-    inputs = [*[tables[bits] for bits in range(owners)], *picks_places_notes]
+    )(lax.axis_index("dp").astype(jnp.int32).reshape(1), users_list, items_list, days_list, table)
+
+    joined = pl.pallas_call(
+        functools.partial(join_kernel, sizes),
+        out_shape=shape((len(arrived) * sizes.table_rows, LANES), bf16),
+        compiler_params=small,
+        name="join",
+    )(*arrived, picks_places_notes[6])
+    joined_crossed = swap(joined, "dp", owners, 1)
+
+    inputs = [table, own_crossed, joined, joined_crossed, *picks_places_notes]
     users, items, days = list_counts
-    steps = days // DAYS_PER_STEP
     half = shape((owners // 2 * sizes.slot_rows, sizes.rank), bf16)
     own, other = pl.pallas_call(
-        functools.partial(block_kernel, sizes, DAYS_PER_STEP),
+        functools.partial(block_kernel, sizes),
         out_shape=(half, half),
         in_specs=[pl.BlockSpec(memory_space=pltpu.VMEM)] * len(inputs) + [hbm],
         scratch_shapes=[
             pltpu.VMEM((users, sizes.rank), f32),
+            pltpu.VMEM((users, sizes.rank), bf16),
             pltpu.VMEM((items, sizes.rank), bf16),
             pltpu.VMEM((sizes.rank, items), bf16),
             pltpu.VMEM((days, sizes.rank), f32),
             pltpu.VMEM((users, sizes.rank), f32),
             pltpu.VMEM((items, sizes.rank), f32),
             pltpu.VMEM((days, sizes.rank), f32),
+            pltpu.VMEM((2 * users, sizes.rank), bf16),
+            pltpu.VMEM((2 * users, sizes.rank), bf16),
+            pltpu.VMEM((2 * users, items), bf16),
+            pltpu.VMEM((2 * users, items), bf16),
             pltpu.VMEM((days, users, items), jnp.int32),
-            pltpu.SemaphoreType.DMA((steps,)),
+            pltpu.SemaphoreType.DMA((days // 4 + 1,)),
         ],
         compiler_params=pltpu.CompilerParams(vmem_limit_bytes=BLOCK_VMEM),
         name="block_gradients",

time: 54.2 us -> 51.1 us (0.943)
  Pallas kernels: 13.3 us -> 11.1 us
  waiting for transfers between devices: 18.8 us -> 18.1 us
    pallas_call x1 -> x2, Pallas kernels: 9.19 us -> 6.93 us  [the longest x1 6.9 us: local(): pl.pallas_call(functools.partial(block_kernel, sizes), out_shape=(half, h...]
    ppermute x17 -> x15, waiting for transfers between devices: 18.8 us -> 18.1 us  [swap(): return lax.ppermute(array, axis, [(i, i ^ bits) for i in range(size)])]
    ppermute x17 -> x15, starting transfers between devices: 18.1 us -> 18 us  [swap(): return lax.ppermute(array, axis, [(i, i ^ bits) for i in range(size)])]
  transfers between devices with their start and end apart: 17 -> 15, of which waited for: 11 -> 10; matrix products, arithmetic and copies ran while one was open for 0% -> 0% of each run, Pallas kernels for 2% -> 2%
where the time goes in v5:
time: 51.1 us; the launch traced here: 50.8 us
  waiting for transfers between devices  18.1 us (35%)
  starting transfers between devices  18 us (35%)
  Pallas kernels  11.1 us (22%)
  local copies, waits for them, and re-layouts  2.82 us (6%)
  between operations  0.8 us (2%)
    ppermute x15, waiting for transfers between devices, swap(): return lax.ppermute(array, axis, [(i, i ^ bits) for i in range(size)])  18.1 us
    ppermute x15, starting transfers between devices, swap(): return lax.ppermute(array, axis, [(i, i ^ bits) for i in range(size)])  18 us
    pallas_call x1, Pallas kernels, local(): pl.pallas_call(functools.partial(block_kernel, sizes), out_shape=(half, h...  6.9 us
    unnamed x26, local copies, waits for them, and re-layouts  2.82 us
    pallas_call x1, Pallas kernels, local(): pl.pallas_call(functools.partial(pack_kernel, sizes), out_shape=shape((si...  1.52 us
    pallas_call x1, Pallas kernels, local(): pl.pallas_call(functools.partial(slot_kernel, sizes), out_shape=tuple([sh...  1.15 us
  transfers between devices with their start and end apart: 15, of which 10 were waited for; matrix products, arithmetic and copies ran while one was open for 0% of the time, Pallas kernels for 2%

profile of v5, /device:TPU:0, one launch (start us, length us, event | category | flops | bytes accessed | tf_op | source)
XLA Modules:
  0.0 50.8 jit_solution(12084106835453882007)
XLA Ops:
  0.7 1.5 %pack.1.refs_0_ = bf16[144,128]{1,0:T(8,128)(2,1)} custom-call(f32[64,128]{1,0:T(8,128)} %bitcast.13, f32[64,128]{1,0:T(8,128)} %bitcast.15, f32[32,64]{1,0:T(8,128)} %refs_10_.1), custom_call_target="tpu_custom_call" | custom-call | tf_op jit(solution)/shard_map/pack/pallas_call | solution.py:379
  2.2 5.1 %collective-permute-start.2 = (bf16[144,128]{1,0:T(8,128)(2,1)}, bf16[144,128]{1,0:T(8,128)(2,1)S(1)}, u32[]{:S(2)}, u32[]{:S(2)}) collective-permute-start(bf16[144,128]{1,0:T(8,128)(2,1)} %pack.1.refs_0_), channel_id=1, source_target_pairs={{0,3},{1,2},{2,1},{3,0},{4,7},{5,6},{6,5},{7,4},{8,11},{9,10},{10,... | collective-permute-start | bytes 110600 | tf_op jit(solution)/shard_map/ppermute | solution.py:351
  7.3 0.6 %collective-permute-start = (bf16[144,128]{1,0:T(8,128)(2,1)}, bf16[144,128]{1,0:T(8,128)(2,1)S(1)}, u32[]{:S(2)}, u32[]{:S(2)}) collective-permute-start(bf16[144,128]{1,0:T(8,128)(2,1)} %pack.1.refs_0_), channel_id=1, source_target_pairs={{0,1},{1,0},{2,3},{3,2},{4,5},{5,4},{6,7},{7,6},{8,9},{9,8},{10,11... | collective-permute-start | bytes 110600 | tf_op jit(solution)/shard_map/ppermute | solution.py:351
  8.0 1.5 %collective-permute-done.2.refs_3_ = bf16[144,128]{1,0:T(8,128)(2,1)S(1)} collective-permute-done((bf16[144,128]{1,0:T(8,128)(2,1)}, bf16[144,128]{1,0:T(8,128)(2,1)S(1)}, u32[]{:S(2)}, u32[]{:S(2)}) %collective-permute-start.2) | collective-permute-done | bytes 36896 | tf_op jit(solution)/shard_map/ppermute | solution.py:351
  9.5 2.9 %collective-permute-done.1.refs_2_ = bf16[144,128]{1,0:T(8,128)(2,1)S(1)} collective-permute-done((bf16[144,128]{1,0:T(8,128)(2,1)}, bf16[144,128]{1,0:T(8,128)(2,1)S(1)}, u32[]{:S(2)}, u32[]{:S(2)}) %collective-permute-start.1) | collective-permute-done | bytes 36896 | tf_op jit(solution)/shard_map/ppermute | solution.py:351
  12.4 0.8 %copy-done = bf16[144,128]{1,0:T(8,128)(2,1)S(1)} copy-done((bf16[144,128]{1,0:T(8,128)(2,1)S(1)}, bf16[144,128]{1,0:T(8,128)(2,1)}, u32[]{:S(2)}) %copy-start) | copy-done | bytes 36888
  13.3 2.5 %collective-permute-start.6 = (bf16[576,128]{1,0:T(8,128)(2,1)S(1)}, bf16[576,128]{1,0:T(8,128)(2,1)S(1)}, u32[]{:S(2)}, u32[]{:S(2)}) collective-permute-start(bf16[576,128]{1,0:T(8,128)(2,1)S(1)} %table.1.refs_3_.refs_0_), channel_id=1, source_target_pairs={{0,24},{4,28},{8,16},{12,20},{16,8},{20,12},{24,0},{28,4},{1,25},{... | collective-permute-start | bytes 442376 | tf_op jit(solution)/shard_map/ppermute | solution.py:351
  15.8 0.5 collective-permute-start.5
  16.3 0.5 %collective-permute-start.4 = (bf16[576,128]{1,0:T(8,128)(2,1)S(1)}, bf16[576,128]{1,0:T(8,128)(2,1)S(1)}, u32[]{:S(2)}, u32[]{:S(2)}) collective-permute-start(bf16[576,128]{1,0:T(8,128)(2,1)S(1)} %table.1.refs_3_.refs_0_), channel_id=1, source_target_pairs={{0,8},{4,12},{8,0},{12,4},{16,24},{20,28},{24,16},{28,20},{1,9},{5... | collective-permute-start | bytes 442376 | tf_op jit(solution)/shard_map/ppermute | solution.py:351
  16.8 0.7 %copy-done.10 = s32[1,256]{1,0:T(1,128)S(1)} copy-done((s32[1,256]{1,0:T(1,128)S(1)}, s32[1,256]{1,0:T(1,128)}, u32[]{:S(2)}) %copy-start.10) | copy-done | bytes 1048
  17.5 0.7 %copy-done.11 = s32[1,256]{1,0:T(1,128)S(1)} copy-done((s32[1,256]{1,0:T(1,128)S(1)}, s32[1,256]{1,0:T(1,128)}, u32[]{:S(2)}) %copy-start.11) | copy-done | bytes 1048
  18.2 0.7 %copy-done.12 = s32[1,32]{1,0:T(1,128)S(1)} copy-done((s32[1,32]{1,0:T(1,128)S(1)}, s32[1,32]{1,0:T(1,128)}, u32[]{:S(2)}) %copy-start.12) | copy-done | bytes 152
  18.9 1.2 %slots.1 = (bf16[1024,256]{1,0:T(8,128)(2,1)S(1)}, bf16[1024,256]{1,0:T(8,128)(2,1)S(1)}, bf16[256,32]{1,0:T(8,128)(2,1)S(1)}, bf16[384,256]{1,0:T(8,128)(2,1)S(...) custom-call(s32[1]{0:T(128)} %bitcast.2.me_ref, s32[1,256]{1,0:T(1,128)S(1)} %copy-done.10, ...), custom_call_target="tpu_custom_call" | custom-call | tf_op jit(solution)/shard_map/slots/pallas_call | solution.py:398
  20.0 1.0 %collective-permute-done.6.refs_2_ = bf16[576,128]{1,0:T(8,128)(2,1)S(1)} collective-permute-done((bf16[576,128]{1,0:T(8,128)(2,1)S(1)}, bf16[576,128]{1,0:T(8,128)(2,1)S(1)}, u32[]{:S(2)}, u32[]{:S(2)}) %collective-permute-start.6) | collective-permute-done | bytes 147488 | tf_op jit(solution)/shard_map/ppermute | solution.py:351
  21.0 0.8 %collective-permute-done.5.refs_1_ = bf16[576,128]{1,0:T(8,128)(2,1)S(1)} collective-permute-done((bf16[576,128]{1,0:T(8,128)(2,1)S(1)}, bf16[576,128]{1,0:T(8,128)(2,1)S(1)}, u32[]{:S(2)}, u32[]{:S(2)}) %collective-permute-start.5) | collective-permute-done | bytes 147488 | tf_op jit(solution)/shard_map/ppermute | solution.py:351
  21.9 0.5 collective-permute-start.3
  22.4 1.5 %collective-permute-done.3.refs_1_ = bf16[576,128]{1,0:T(8,128)(2,1)S(1)} collective-permute-done((bf16[576,128]{1,0:T(8,128)(2,1)S(1)}, bf16[576,128]{1,0:T(8,128)(2,1)S(1)}, u32[]{:S(2)}, u32[]{:S(2)}) %collective-permute-start.3) | collective-permute-done | bytes 147488 | tf_op jit(solution)/shard_map/ppermute | solution.py:351
  23.9 6.9 %block_gradients.1 = (bf16[448,256]{1,0:T(8,128)(2,1)S(1)}, bf16[448,256]{1,0:T(8,128)(2,1)S(1)}) custom-call(bf16[576,128]{1,0:T(8,128)(2,1)S(1)} %table.1.refs_3_.refs_0_, bf16[576,128]{1,0:T(8,128)(2,1)S(1)} %collective-permute-done.3.refs_1_, bf16[1728,128]{1,0:T(8,128)(2,1)S(1)} %join.1.refs_2_, bf16[1728,128]{1,0:T(8,128)(2,1)S(1)} %collective-permute-done.7.refs_3_, ...), custom_call_target="tpu_custom_call" | custom-call | tf_op jit(solution)/shard_map/block_gradients/pallas_call | solution.py:423
  30.8 0.2 collective-permute-start.8
  31.0 1.4 %collective-permute-done.8.crossed_ref.refs_1_ = bf16[448,256]{1,0:T(8,128)(2,1)S(1)} collective-permute-done((bf16[448,256]{1,0:T(8,128)(2,1)S(1)}, bf16[448,256]{1,0:T(8,128)(2,1)S(1)}, u32[]{:S(2)}, u32[]{:S(2)}) %collective-permute-start.8) | collective-permute-done | bytes 229408 | tf_op jit(solution)/shard_map/ppermute | solution.py:351
  32.3 1.5 %collective-permute-start.9 = (bf16[224,256]{1,0:T(8,128)(2,1)S(1)}, bf16[224,256]{1,0:T(8,128)(2,1)S(1)}, u32[]{:S(2)}, u32[]{:S(2)}) collective-permute-start(bf16[224,256]{1,0:T(8,128)(2,1)S(1)} %get-tuple-element.43), channel_id=1, source_target_pairs={{0,8},{4,12},{8,0},{12,4},{16,24},{20,28},{24,16},{28,20},{1,9},{5... | collective-permute-start | bytes 344072 | tf_op jit(solution)/shard_map/ppermute | solution.py:351
  33.9 0.7 %collective-permute-start.10 = (bf16[224,256]{1,0:T(8,128)(2,1)S(1)}, bf16[224,256]{1,0:T(8,128)(2,1)S(1)}, u32[]{:S(2)}, u32[]{:S(2)}) collective-permute-start(bf16[224,256]{1,0:T(8,128)(2,1)S(1)} %get-tuple-element.44), channel_id=1, source_target_pairs={{0,16},{4,20},{8,24},{12,28},{16,0},{20,4},{24,8},{28,12},{1,17},{... | collective-permute-start | bytes 344072 | tf_op jit(solution)/shard_map/ppermute | solution.py:351
  34.5 1.4 %collective-permute-start.11 = (bf16[224,256]{1,0:T(8,128)(2,1)S(1)}, bf16[224,256]{1,0:T(8,128)(2,1)S(1)}, u32[]{:S(2)}, u32[]{:S(2)}) collective-permute-start(bf16[224,256]{1,0:T(8,128)(2,1)S(1)} %get-tuple-element.45), channel_id=1, source_target_pairs={{0,24},{4,28},{8,16},{12,20},{16,8},{20,12},{24,0},{28,4},{1,25},{... | collective-permute-start | bytes 344072 | tf_op jit(solution)/shard_map/ppermute | solution.py:351
  35.9 1.7 %collective-permute-done.9.refs_2_ = bf16[224,256]{1,0:T(8,128)(2,1)S(1)} collective-permute-done((bf16[224,256]{1,0:T(8,128)(2,1)S(1)}, bf16[224,256]{1,0:T(8,128)(2,1)S(1)}, u32[]{:S(2)}, u32[]{:S(2)}) %collective-permute-start.9) | collective-permute-done | bytes 114720 | tf_op jit(solution)/shard_map/ppermute | solution.py:351
  37.6 3.6 %collective-permute-done.10.refs_3_ = bf16[224,256]{1,0:T(8,128)(2,1)S(1)} collective-permute-done((bf16[224,256]{1,0:T(8,128)(2,1)S(1)}, bf16[224,256]{1,0:T(8,128)(2,1)S(1)}, u32[]{:S(2)}, u32[]{:S(2)}) %collective-permute-start.10) | collective-permute-done | bytes 114720 | tf_op jit(solution)/shard_map/ppermute | solution.py:351
  41.2 0.6 %row_sums.1 = (bf16[144,128]{1,0:T(8,128)(2,1)S(1)}, bf16[144,128]{1,0:T(8,128)(2,1)S(1)}, bf16[144,128]{1,0:T(8,128)(2,1)S(1)}, bf16[144,128]{1,0:T(8,128)(2,1)S(1)}) custom-call(bf16[448,256]{1,0:T(8,128)(2,1)S(1)} %get-tuple-element.41.own_ref.refs_0_, bf16[448,256]{1,0:T(8,128)(2,1)S(1)} %collective-permute-done.8.crossed_ref.refs_1_, ...), custom_call_target="tpu_custom_call" | custom-call | tf_op jit(solution)/shard_map/row_sums/pallas_call | solution.py:457
  41.8 0.2 collective-permute-start.12
  42.0 2.3 %collective-permute-start.13 = (bf16[144,128]{1,0:T(8,128)(2,1)S(1)}, bf16[144,128]{1,0:T(8,128)(2,1)S(1)}, u32[]{:S(2)}, u32[]{:S(2)}) collective-permute-start(bf16[144,128]{1,0:T(8,128)(2,1)S(1)} %get-tuple-element.48), channel_id=1, source_target_pairs={{0,2},{1,3},{2,0},{3,1},{4,6},{5,7},{6,4},{7,5},{8,10},{9,11},{10,... | collective-permute-start | bytes 110600 | tf_op jit(solution)/shard_map/ppermute | solution.py:351
  44.3 2.0 %collective-permute-start.14 = (bf16[144,128]{1,0:T(8,128)(2,1)S(1)}, bf16[144,128]{1,0:T(8,128)(2,1)S(1)}, u32[]{:S(2)}, u32[]{:S(2)}) collective-permute-start(bf16[144,128]{1,0:T(8,128)(2,1)S(1)} %get-tuple-element.49), channel_id=1, source_target_pairs={{0,3},{1,2},{2,1},{3,0},{4,7},{5,6},{6,5},{7,4},{8,11},{9,10},{10,... | collective-permute-start | bytes 110600 | tf_op jit(solution)/shard_map/ppermute | solution.py:351
  46.2 0.9 %collective-permute-done.13.refs_2_ = bf16[144,128]{1,0:T(8,128)(2,1)S(1)} collective-permute-done((bf16[144,128]{1,0:T(8,128)(2,1)S(1)}, bf16[144,128]{1,0:T(8,128)(2,1)S(1)}, u32[]{:S(2)}, u32[]{:S(2)}) %collective-permute-start.13) | collective-permute-done | bytes 36896 | tf_op jit(solution)/shard_map/ppermute | solution.py:351
  47.1 2.9 %collective-permute-done.14.refs_3_ = bf16[144,128]{1,0:T(8,128)(2,1)S(1)} collective-permute-done((bf16[144,128]{1,0:T(8,128)(2,1)S(1)}, bf16[144,128]{1,0:T(8,128)(2,1)S(1)}, u32[]{:S(2)}, u32[]{:S(2)}) %collective-permute-start.14) | collective-permute-done | bytes 36896 | tf_op jit(solution)/shard_map/ppermute | solution.py:351
  50.1 0.7 %adam.1 = (f32[64,128]{1,0:T(8,128)}, f32[64,128]{1,0:T(8,128)}, f32[64,128]{1,0:T(8,128)}, f32[64,128]{1,0:T(8,128)}, f32[64,128]{1,0:T(8,128)}, /*index=5*/f32...) custom-call(bf16[144,128]{1,0:T(8,128)(2,1)S(1)} %get-tuple-element.46.refs_0_, ...), custom_call_target="tpu_custom_call" | custom-call | tf_op jit(solution)/shard_map/adam/pallas_call | solution.py:478
  (32 shorter events, 0.3 us)
Async XLA Ops:
  0.6 49.4 %copy-start.3 = (f32[32,64]{1,0:T(8,128)S(1)}, f32[32,64]{1,0:T(8,128)}, u32[]{:S(2)}) copy-start(f32[32,64]{1,0:T(8,128)} %refs_10_.1) | copy-start | bytes 24580
  0.7 49.4 %copy-start.2 = (f32[128,64]{0,1:T(8,128)S(1)}, f32[128,64]{0,1:T(8,128)}, u32[]{:S(2)}) copy-start(f32[128,64]{0,1:T(8,128)} %param.20) | copy-start | bytes 98308
  0.7 49.4 %copy-start.1 = (f32[128,64]{0,1:T(8,128)S(1)}, f32[128,64]{0,1:T(8,128)}, u32[]{:S(2)}) copy-start(f32[128,64]{0,1:T(8,128)} %param.17) | copy-start | bytes 98308
  0.7 49.4 %copy-start.4 = (f32[128,64]{0,1:T(8,128)S(1)}, f32[128,64]{0,1:T(8,128)}, u32[]{:S(2)}) copy-start(f32[128,64]{0,1:T(8,128)} %param.18) | copy-start | bytes 98308
  2.2 7.3 %collective-permute-start.2 = (bf16[144,128]{1,0:T(8,128)(2,1)}, bf16[144,128]{1,0:T(8,128)(2,1)S(1)}, u32[]{:S(2)}, u32[]{:S(2)}) collective-permute-start(bf16[144,128]{1,0:T(8,128)(2,1)} %pack.1.refs_0_), channel_id=1, source_target_pairs={{0,3},{1,2},{2,1},{3,0},{4,7},{5,6},{6,5},{7,4},{8,11},{9,10},{10,... | collective-permute-start | bytes 110600 | tf_op jit(solution)/shard_map/ppermute | solution.py:351
  7.3 5.1 %collective-permute-start.1 = (bf16[144,128]{1,0:T(8,128)(2,1)}, bf16[144,128]{1,0:T(8,128)(2,1)S(1)}, u32[]{:S(2)}, u32[]{:S(2)}) collective-permute-start(bf16[144,128]{1,0:T(8,128)(2,1)} %pack.1.refs_0_), channel_id=1, source_target_pairs={{0,2},{1,3},{2,0},{3,1},{4,6},{5,7},{6,4},{7,5},{8,10},{9,11},{10,... | collective-permute-start | bytes 110600 | tf_op jit(solution)/shard_map/ppermute | solution.py:351
  7.3 5.1 %collective-permute-start = (bf16[144,128]{1,0:T(8,128)(2,1)}, bf16[144,128]{1,0:T(8,128)(2,1)S(1)}, u32[]{:S(2)}, u32[]{:S(2)}) collective-permute-start(bf16[144,128]{1,0:T(8,128)(2,1)} %pack.1.refs_0_), channel_id=1, source_target_pairs={{0,1},{1,0},{2,3},{3,2},{4,5},{5,4},{6,7},{7,6},{8,9},{9,8},{10,11... | collective-permute-start | bytes 110600 | tf_op jit(solution)/shard_map/ppermute | solution.py:351
  12.4 0.8 %copy-start = (bf16[144,128]{1,0:T(8,128)(2,1)S(1)}, bf16[144,128]{1,0:T(8,128)(2,1)}, u32[]{:S(2)}) copy-start(bf16[144,128]{1,0:T(8,128)(2,1)} %pack.1.refs_0_) | copy-start | bytes 110596
  13.2 36.9 %copy-start.5 = (f32[128,64]{0,1:T(8,128)S(1)}, f32[128,64]{0,1:T(8,128)}, u32[]{:S(2)}) copy-start(f32[128,64]{0,1:T(8,128)} %param.19) | copy-start | bytes 98308
  13.2 36.9 %copy-start.6 = (f32[128,64]{0,1:T(8,128)S(1)}, f32[128,64]{0,1:T(8,128)}, u32[]{:S(2)}) copy-start(f32[128,64]{0,1:T(8,128)} %param.21) | copy-start | bytes 98308
  13.2 36.9 %copy-start.7 = (f32[128,64]{0,1:T(8,128)S(1)}, f32[128,64]{0,1:T(8,128)}, u32[]{:S(2)}) copy-start(f32[128,64]{0,1:T(8,128)} %param.22) | copy-start | bytes 98308
  13.2 36.9 %copy-start.8 = (f32[32,64]{1,0:T(8,128)S(1)}, f32[32,64]{1,0:T(8,128)}, u32[]{:S(2)}) copy-start(f32[32,64]{1,0:T(8,128)} %refs_11_.3) | copy-start | bytes 24580
  13.2 36.9 %copy-start.9 = (f32[32,64]{1,0:T(8,128)S(1)}, f32[32,64]{1,0:T(8,128)}, u32[]{:S(2)}) copy-start(f32[32,64]{1,0:T(8,128)} %refs_12_.1) | copy-start | bytes 24580
  13.3 7.6 %collective-permute-start.6 = (bf16[576,128]{1,0:T(8,128)(2,1)S(1)}, bf16[576,128]{1,0:T(8,128)(2,1)S(1)}, u32[]{:S(2)}, u32[]{:S(2)}) collective-permute-start(bf16[576,128]{1,0:T(8,128)(2,1)S(1)} %table.1.refs_3_.refs_0_), channel_id=1, source_target_pairs={{0,24},{4,28},{8,16},{12,20},{16,8},{20,12},{24,0},{28,4},{1,25},{... | collective-permute-start | bytes 442376 | tf_op jit(solution)/shard_map/ppermute | solution.py:351
  15.8 6.0 %collective-permute-start.5 = (bf16[576,128]{1,0:T(8,128)(2,1)S(1)}, bf16[576,128]{1,0:T(8,128)(2,1)S(1)}, u32[]{:S(2)}, u32[]{:S(2)}) collective-permute-start(bf16[576,128]{1,0:T(8,128)(2,1)S(1)} %table.1.refs_3_.refs_0_), channel_id=1, source_target_pairs={{0,16},{4,20},{8,24},{12,28},{16,0},{20,4},{24,8},{28,12},{1,17},{... | collective-permute-start | bytes 442376 | tf_op jit(solution)/shard_map/ppermute | solution.py:351
  16.3 5.4 %collective-permute-start.4 = (bf16[576,128]{1,0:T(8,128)(2,1)S(1)}, bf16[576,128]{1,0:T(8,128)(2,1)S(1)}, u32[]{:S(2)}, u32[]{:S(2)}) collective-permute-start(bf16[576,128]{1,0:T(8,128)(2,1)S(1)} %table.1.refs_3_.refs_0_), channel_id=1, source_target_pairs={{0,8},{4,12},{8,0},{12,4},{16,24},{20,28},{24,16},{28,20},{1,9},{5... | collective-permute-start | bytes 442376 | tf_op jit(solution)/shard_map/ppermute | solution.py:351
  16.8 0.7 %copy-start.10 = (s32[1,256]{1,0:T(1,128)S(1)}, s32[1,256]{1,0:T(1,128)}, u32[]{:S(2)}) copy-start(s32[1,256]{1,0:T(1,128)} %refs_0_.1) | copy-start | bytes 3076
  17.5 0.7 %copy-start.11 = (s32[1,256]{1,0:T(1,128)S(1)}, s32[1,256]{1,0:T(1,128)}, u32[]{:S(2)}) copy-start(s32[1,256]{1,0:T(1,128)} %refs_1_.1) | copy-start | bytes 3076
  18.2 0.7 %copy-start.12 = (s32[1,32]{1,0:T(1,128)S(1)}, s32[1,32]{1,0:T(1,128)}, u32[]{:S(2)}) copy-start(s32[1,32]{1,0:T(1,128)} %refs_2_.1) | copy-start | bytes 388
  21.8 2.1 %collective-permute-start.7 = (bf16[1728,128]{1,0:T(8,128)(2,1)S(1)}, bf16[1728,128]{1,0:T(8,128)(2,1)S(1)}, u32[]{:S(2)}, u32[]{:S(2)}) collective-permute-start(bf16[1728,128]{1,0:T(8,128)(2,1)S(1)} %join.1.refs_2_), channel_id=1, source_target_pairs={{0,4},{4,0},{8,12},{12,8},{16,20},{20,16},{24,28},{28,24},{1,5},{5... | collective-permute-start | bytes 1327112 | tf_op jit(solution)/shard_map/ppermute | solution.py:351
  21.9 2.0 %collective-permute-start.3 = (bf16[576,128]{1,0:T(8,128)(2,1)S(1)}, bf16[576,128]{1,0:T(8,128)(2,1)S(1)}, u32[]{:S(2)}, u32[]{:S(2)}) collective-permute-start(bf16[576,128]{1,0:T(8,128)(2,1)S(1)} %table.1.refs_3_.refs_0_), channel_id=1, source_target_pairs={{0,4},{4,0},{8,12},{12,8},{16,20},{20,16},{24,28},{28,24},{1,5},{5... | collective-permute-start | bytes 442376 | tf_op jit(solution)/shard_map/ppermute | solution.py:351
  30.8 1.6 %collective-permute-start.8 = (bf16[448,256]{1,0:T(8,128)(2,1)S(1)}, bf16[448,256]{1,0:T(8,128)(2,1)S(1)}, u32[]{:S(2)}, u32[]{:S(2)}) collective-permute-start(bf16[448,256]{1,0:T(8,128)(2,1)S(1)} %get-tuple-element.42), channel_id=1, source_target_pairs={{0,4},{4,0},{8,12},{12,8},{16,20},{20,16},{24,28},{28,24},{1,5},{5... | collective-permute-start | bytes 688136 | tf_op jit(solution)/shard_map/ppermute | solution.py:351
  32.3 5.3 %collective-permute-start.9 = (bf16[224,256]{1,0:T(8,128)(2,1)S(1)}, bf16[224,256]{1,0:T(8,128)(2,1)S(1)}, u32[]{:S(2)}, u32[]{:S(2)}) collective-permute-start(bf16[224,256]{1,0:T(8,128)(2,1)S(1)} %get-tuple-element.43), channel_id=1, source_target_pairs={{0,8},{4,12},{8,0},{12,4},{16,24},{20,28},{24,16},{28,20},{1,9},{5... | collective-permute-start | bytes 344072 | tf_op jit(solution)/shard_map/ppermute | solution.py:351
  33.9 7.4 %collective-permute-start.10 = (bf16[224,256]{1,0:T(8,128)(2,1)S(1)}, bf16[224,256]{1,0:T(8,128)(2,1)S(1)}, u32[]{:S(2)}, u32[]{:S(2)}) collective-permute-start(bf16[224,256]{1,0:T(8,128)(2,1)S(1)} %get-tuple-element.44), channel_id=1, source_target_pairs={{0,16},{4,20},{8,24},{12,28},{16,0},{20,4},{24,8},{28,12},{1,17},{... | collective-permute-start | bytes 344072 | tf_op jit(solution)/shard_map/ppermute | solution.py:351
  34.5 6.7 %collective-permute-start.11 = (bf16[224,256]{1,0:T(8,128)(2,1)S(1)}, bf16[224,256]{1,0:T(8,128)(2,1)S(1)}, u32[]{:S(2)}, u32[]{:S(2)}) collective-permute-start(bf16[224,256]{1,0:T(8,128)(2,1)S(1)} %get-tuple-element.45), channel_id=1, source_target_pairs={{0,24},{4,28},{8,16},{12,20},{16,8},{20,12},{24,0},{28,4},{1,25},{... | collective-permute-start | bytes 344072 | tf_op jit(solution)/shard_map/ppermute | solution.py:351
  41.8 4.5 %collective-permute-start.12 = (bf16[144,128]{1,0:T(8,128)(2,1)S(1)}, bf16[144,128]{1,0:T(8,128)(2,1)S(1)}, u32[]{:S(2)}, u32[]{:S(2)}) collective-permute-start(bf16[144,128]{1,0:T(8,128)(2,1)S(1)} %get-tuple-element.47), channel_id=1, source_target_pairs={{0,1},{1,0},{2,3},{3,2},{4,5},{5,4},{6,7},{7,6},{8,9},{9,8},{10,11... | collective-permute-start | bytes 110600 | tf_op jit(solution)/shard_map/ppermute | solution.py:351
  42.0 5.1 %collective-permute-start.13 = (bf16[144,128]{1,0:T(8,128)(2,1)S(1)}, bf16[144,128]{1,0:T(8,128)(2,1)S(1)}, u32[]{:S(2)}, u32[]{:S(2)}) collective-permute-start(bf16[144,128]{1,0:T(8,128)(2,1)S(1)} %get-tuple-element.48), channel_id=1, source_target_pairs={{0,2},{1,3},{2,0},{3,1},{4,6},{5,7},{6,4},{7,5},{8,10},{9,11},{10,... | collective-permute-start | bytes 110600 | tf_op jit(solution)/shard_map/ppermute | solution.py:351
  44.3 5.8 %collective-permute-start.14 = (bf16[144,128]{1,0:T(8,128)(2,1)S(1)}, bf16[144,128]{1,0:T(8,128)(2,1)S(1)}, u32[]{:S(2)}, u32[]{:S(2)}) collective-permute-start(bf16[144,128]{1,0:T(8,128)(2,1)S(1)} %get-tuple-element.49), channel_id=1, source_target_pairs={{0,3},{1,2},{2,1},{3,0},{4,7},{5,6},{6,5},{7,4},{8,11},{9,10},{10,... | collective-permute-start | bytes 110600 | tf_op jit(solution)/shard_map/ppermute | solution.py:351

commit v6 on v5

--- a/solution.py
+++ b/solution.py
@@ -18,7 +18,6 @@
 LANES = 128
 SMALL_VMEM = 16 * 1024 * 1024
 BLOCK_VMEM = 48 * 1024 * 1024
-PACK_VMEM = 56 * 1024 * 1024
 
 f32 = jnp.float32
 bf16 = jnp.bfloat16
@@ -129,7 +128,7 @@
 
 
 def table_kernel(sizes, *refs):
-    pieces, out_ref = refs[:-1], refs[-1]
+    pieces, out_ref = refs[-2::-1], refs[-1]
     columns, rank, day_rows = sizes.columns, sizes.rank, sizes.row_counts[2]
     for j, ref in enumerate(pieces):
         for t in range(2):
@@ -276,7 +275,7 @@
 
 def join_kernel(sizes, *refs):
     arrived, out_ref = refs[:-2], refs[-1]
-    for n, ref in enumerate(arrived):
+    for n, ref in enumerate(arrived[::-1]):
         out_ref[n * sizes.table_rows : (n + 1) * sizes.table_rows, :] = ref[...]
 
 
@@ -375,6 +374,7 @@
     small = pltpu.CompilerParams(vmem_limit_bytes=SMALL_VMEM)
 
     hbm = pl.BlockSpec(memory_space=pltpu.HBM)
+    in_hbm = lambda a: pltpu.with_memory_space_constraint(a, pltpu.HBM)
     tables_in = (user_factor.T, item_factor.T, day_factor)
     piece = pl.pallas_call(
         functools.partial(pack_kernel, sizes),
@@ -382,10 +382,10 @@
         in_specs=[hbm] * 3,
         scratch_shapes=[pltpu.VMEM(a.shape, f32) for a in tables_in]
         + [pltpu.SemaphoreType.DMA((3,))],
-        compiler_params=pltpu.CompilerParams(vmem_limit_bytes=PACK_VMEM),
+        compiler_params=small,
         name="pack",
-    )(*tables_in)
-    pieces = [piece] + [swap(piece, "mp", holders, bits) for bits in range(1, holders)]
+    )(*[in_hbm(a) for a in tables_in])
+    pieces = [swap(piece, "mp", holders, bits) for bits in range(holders - 1, 0, -1)] + [piece]
 
     table = pl.pallas_call(
         functools.partial(table_kernel, sizes),
@@ -393,7 +393,7 @@
         compiler_params=small,
         name="table",
     )(*pieces)
-    arrived = [swap(table, "dp", owners, bits) for bits in range(2, owners, 2)]
+    arrived = [swap(table, "dp", owners, bits) for bits in range(owners - 2, 0, -2)]
     own_crossed = swap(table, "dp", owners, 1)
     picks_places_notes = pl.pallas_call(
         functools.partial(slot_kernel, sizes),
@@ -402,12 +402,18 @@
             + [shape((owners * sizes.slots[t], list_counts[t]), bf16) for t in range(3)]
             + [shape((owners, sizes.rank), f32)]
         ),
-        in_specs=[pl.BlockSpec(memory_space=pltpu.SMEM)] + [hbm] * 4,
+        in_specs=[pl.BlockSpec(memory_space=pltpu.SMEM)]
+        + [hbm] * 3
+        + [pl.BlockSpec(memory_space=pl.ANY)],
         scratch_shapes=[pltpu.VMEM((1, count), jnp.int32) for count in list_counts]
         + [pltpu.SemaphoreType.DMA((3,))],
         compiler_params=small,
         name="slots",
-    )(lax.axis_index("dp").astype(jnp.int32).reshape(1), users_list, items_list, days_list, table)
+    )(
+        lax.axis_index("dp").astype(jnp.int32).reshape(1),
+        *[in_hbm(a) for a in (users_list, items_list, days_list)],
+        table,
+    )
 
     joined = pl.pallas_call(
         functools.partial(join_kernel, sizes),
@@ -442,7 +448,7 @@
         ],
         compiler_params=pltpu.CompilerParams(vmem_limit_bytes=BLOCK_VMEM),
         name="block_gradients",
-    )(*inputs, status)
+    )(*inputs, in_hbm(status))
     crossed = swap(other, "dp", owners, 1)
     message = shape((2 * sizes.slot_rows, sizes.rank), bf16)
     merged = pl.pallas_call(

time: 51.1 us -> 49.8 us (0.975)
  local copies, waits for them, and re-layouts: 2.82 us -> 0.04 us
  waiting for transfers between devices: 18.1 us -> 19.6 us
    unnamed x26 -> x18, local copies, waits for them, and re-layouts: 2.82 us -> 0.04 us
    ppermute x15, waiting for transfers between devices: 18.1 us -> 19.6 us  [swap(): return lax.ppermute(array, axis, [(i, i ^ bits) for i in range(size)])]
    pallas_call x1, Pallas kernels: 1.15 us -> 1.84 us  [local(): pl.pallas_call(functools.partial(slot_kernel, sizes), out_shape=tuple([sh...]
    pallas_call x1, Pallas kernels: 1.52 us -> 0.93 us  [local(): pl.pallas_call(functools.partial(pack_kernel, sizes), out_shape=shape((si...]
  transfers between devices with their start and end apart: 15 -> 15, of which waited for: 10 -> 10; matrix products, arithmetic and copies ran while one was open for 0% -> 0% of each run, Pallas kernels for 2% -> 4%
where the time goes in v6:
time: 49.8 us; the launch traced here: 49.6 us
  waiting for transfers between devices  19.6 us (39%)
  starting transfers between devices  17.9 us (36%)
  Pallas kernels  11.2 us (22%)
  between operations  0.83 us (2%)
    ppermute x15, waiting for transfers between devices, swap(): return lax.ppermute(array, axis, [(i, i ^ bits) for i in range(size)])  19.6 us
    ppermute x15, starting transfers between devices, swap(): return lax.ppermute(array, axis, [(i, i ^ bits) for i in range(size)])  17.9 us
    pallas_call x1, Pallas kernels, local(): pl.pallas_call(functools.partial(block_kernel, sizes), out_shape=(half, h...  6.91 us
    pallas_call x1, Pallas kernels, local(): pl.pallas_call(functools.partial(slot_kernel, sizes), out_shape=tuple([sh...  1.84 us
  transfers between devices with their start and end apart: 15, of which 10 were waited for; matrix products, arithmetic and copies ran while one was open for 0% of the time, Pallas kernels for 4%

profile of v6, /device:TPU:0, one launch (start us, length us, event | category | flops | bytes accessed | tf_op | source)
XLA Modules:
  0.0 49.6 jit_solution(12150980300808224464)
XLA Ops:
  0.7 0.9 %pack.1.refs_3_ = bf16[144,128]{1,0:T(8,128)(2,1)S(1)} custom-call(f32[64,128]{1,0:T(8,128)} %bitcast.13, f32[64,128]{1,0:T(8,128)} %bitcast.15, f32[32,64]{1,0:T(8,128)} %refs_10_.1), custom_call_target="tpu_custom_call" | custom-call | tf_op jit(solution)/shard_map/pack/pallas_call | solution.py:379
  1.7 3.1 %collective-permute-start.2 = (bf16[144,128]{1,0:T(8,128)(2,1)S(1)}, bf16[144,128]{1,0:T(8,128)(2,1)S(1)}, u32[]{:S(2)}, u32[]{:S(2)}) collective-permute-start(bf16[144,128]{1,0:T(8,128)(2,1)S(1)} %pack.1.refs_3_), channel_id=1, source_target_pairs={{0,1},{1,0},{2,3},{3,2},{4,5},{5,4},{6,7},{7,6},{8,9},{9,8},{10,11... | collective-permute-start | bytes 110600 | tf_op jit(solution)/shard_map/ppermute | solution.py:350
  4.8 2.6 %collective-permute-start.1 = (bf16[144,128]{1,0:T(8,128)(2,1)S(1)}, bf16[144,128]{1,0:T(8,128)(2,1)S(1)}, u32[]{:S(2)}, u32[]{:S(2)}) collective-permute-start(bf16[144,128]{1,0:T(8,128)(2,1)S(1)} %pack.1.refs_3_), channel_id=1, source_target_pairs={{0,2},{1,3},{2,0},{3,1},{4,6},{5,7},{6,4},{7,5},{8,10},{9,11},{10,... | collective-permute-start | bytes 110600 | tf_op jit(solution)/shard_map/ppermute | solution.py:350
  7.4 0.0 collective-permute-start
  7.4 0.0 collective-permute-done.2.refs_2_
  7.4 2.9 %collective-permute-done.1.refs_1_ = bf16[144,128]{1,0:T(8,128)(2,1)S(1)} collective-permute-done((bf16[144,128]{1,0:T(8,128)(2,1)S(1)}, bf16[144,128]{1,0:T(8,128)(2,1)S(1)}, u32[]{:S(2)}, u32[]{:S(2)}) %collective-permute-start.1) | collective-permute-done | bytes 36896 | tf_op jit(solution)/shard_map/ppermute | solution.py:350
  10.3 2.8 %collective-permute-done.refs_0_ = bf16[144,128]{1,0:T(8,128)(2,1)S(1)} collective-permute-done((bf16[144,128]{1,0:T(8,128)(2,1)S(1)}, bf16[144,128]{1,0:T(8,128)(2,1)S(1)}, u32[]{:S(2)}, u32[]{:S(2)}) %collective-permute-start) | collective-permute-done | bytes 36896 | tf_op jit(solution)/shard_map/ppermute | solution.py:350
  13.1 0.1 table.1.refs_3_.refs_0_
  13.3 1.5 %collective-permute-start.6 = (bf16[576,128]{1,0:T(8,128)(2,1)S(1)}, bf16[576,128]{1,0:T(8,128)(2,1)S(1)}, u32[]{:S(2)}, u32[]{:S(2)}) collective-permute-start(bf16[576,128]{1,0:T(8,128)(2,1)S(1)} %table.1.refs_3_.refs_0_), channel_id=1, source_target_pairs={{0,8},{4,12},{8,0},{12,4},{16,24},{20,28},{24,16},{28,20},{1,9},{5... | collective-permute-start | bytes 442376 | tf_op jit(solution)/shard_map/ppermute | solution.py:350
  14.8 1.5 %collective-permute-start.5 = (bf16[576,128]{1,0:T(8,128)(2,1)S(1)}, bf16[576,128]{1,0:T(8,128)(2,1)S(1)}, u32[]{:S(2)}, u32[]{:S(2)}) collective-permute-start(bf16[576,128]{1,0:T(8,128)(2,1)S(1)} %table.1.refs_3_.refs_0_), channel_id=1, source_target_pairs={{0,16},{4,20},{8,24},{12,28},{16,0},{20,4},{24,8},{28,12},{1,17},{... | collective-permute-start | bytes 442376 | tf_op jit(solution)/shard_map/ppermute | solution.py:350
  16.3 0.5 collective-permute-start.4
  16.7 1.8 %slots.1 = (bf16[1024,256]{1,0:T(8,128)(2,1)S(1)}, bf16[1024,256]{1,0:T(8,128)(2,1)S(1)}, bf16[256,32]{1,0:T(8,128)(2,1)S(1)}, bf16[384,256]{1,0:T(8,128)(2,1)S(...) custom-call(s32[1]{0:T(128)} %bitcast.2.me_ref, s32[1,256]{1,0:T(1,128)} %refs_0_.1, ...), custom_call_target="tpu_custom_call" | custom-call | tf_op jit(solution)/shard_map/slots/pallas_call | solution.py:398
  18.6 1.0 %collective-permute-done.6.refs_2_ = bf16[576,128]{1,0:T(8,128)(2,1)S(1)} collective-permute-done((bf16[576,128]{1,0:T(8,128)(2,1)S(1)}, bf16[576,128]{1,0:T(8,128)(2,1)S(1)}, u32[]{:S(2)}, u32[]{:S(2)}) %collective-permute-start.6) | collective-permute-done | bytes 147488 | tf_op jit(solution)/shard_map/ppermute | solution.py:350
  19.6 2.8 %collective-permute-done.5.refs_1_ = bf16[576,128]{1,0:T(8,128)(2,1)S(1)} collective-permute-done((bf16[576,128]{1,0:T(8,128)(2,1)S(1)}, bf16[576,128]{1,0:T(8,128)(2,1)S(1)}, u32[]{:S(2)}, u32[]{:S(2)}) %collective-permute-start.5) | collective-permute-done | bytes 147488 | tf_op jit(solution)/shard_map/ppermute | solution.py:350
  22.5 0.1 collective-permute-start.7
  22.6 0.5 %collective-permute-start.3 = (bf16[576,128]{1,0:T(8,128)(2,1)S(1)}, bf16[576,128]{1,0:T(8,128)(2,1)S(1)}, u32[]{:S(2)}, u32[]{:S(2)}) collective-permute-start(bf16[576,128]{1,0:T(8,128)(2,1)S(1)} %table.1.refs_3_.refs_0_), channel_id=1, source_target_pairs={{0,4},{4,0},{8,12},{12,8},{16,20},{20,16},{24,28},{28,24},{1,5},{5... | collective-permute-start | bytes 442376 | tf_op jit(solution)/shard_map/ppermute | solution.py:350
  23.1 1.5 %collective-permute-done.3.refs_1_ = bf16[576,128]{1,0:T(8,128)(2,1)S(1)} collective-permute-done((bf16[576,128]{1,0:T(8,128)(2,1)S(1)}, bf16[576,128]{1,0:T(8,128)(2,1)S(1)}, u32[]{:S(2)}, u32[]{:S(2)}) %collective-permute-start.3) | collective-permute-done | bytes 147488 | tf_op jit(solution)/shard_map/ppermute | solution.py:350
  24.6 6.9 %block_gradients.1 = (bf16[448,256]{1,0:T(8,128)(2,1)S(1)}, bf16[448,256]{1,0:T(8,128)(2,1)S(1)}) custom-call(bf16[576,128]{1,0:T(8,128)(2,1)S(1)} %table.1.refs_3_.refs_0_, bf16[576,128]{1,0:T(8,128)(2,1)S(1)} %collective-permute-done.3.refs_1_, bf16[1728,128]{1,0:T(8,128)(2,1)S(1)} %join.1.refs_2_, bf16[1728,128]{1,0:T(8,128)(2,1)S(1)} %collective-permute-done.7.refs_3_, ...), custom_call_target="tpu_custom_call" | custom-call | tf_op jit(solution)/shard_map/block_gradients/pallas_call | solution.py:429
  31.5 0.2 collective-permute-start.8
  31.7 1.4 %collective-permute-done.8.crossed_ref.refs_1_ = bf16[448,256]{1,0:T(8,128)(2,1)S(1)} collective-permute-done((bf16[448,256]{1,0:T(8,128)(2,1)S(1)}, bf16[448,256]{1,0:T(8,128)(2,1)S(1)}, u32[]{:S(2)}, u32[]{:S(2)}) %collective-permute-start.8) | collective-permute-done | bytes 229408 | tf_op jit(solution)/shard_map/ppermute | solution.py:350
  33.1 0.5 collective-permute-start.9
  33.5 0.8 %collective-permute-start.10 = (bf16[224,256]{1,0:T(8,128)(2,1)S(1)}, bf16[224,256]{1,0:T(8,128)(2,1)S(1)}, u32[]{:S(2)}, u32[]{:S(2)}) collective-permute-start(bf16[224,256]{1,0:T(8,128)(2,1)S(1)} %get-tuple-element.44), channel_id=1, source_target_pairs={{0,16},{4,20},{8,24},{12,28},{16,0},{20,4},{24,8},{28,12},{1,17},{... | collective-permute-start | bytes 344072 | tf_op jit(solution)/shard_map/ppermute | solution.py:350
  34.3 2.3 %collective-permute-start.11 = (bf16[224,256]{1,0:T(8,128)(2,1)S(1)}, bf16[224,256]{1,0:T(8,128)(2,1)S(1)}, u32[]{:S(2)}, u32[]{:S(2)}) collective-permute-start(bf16[224,256]{1,0:T(8,128)(2,1)S(1)} %get-tuple-element.45), channel_id=1, source_target_pairs={{0,24},{4,28},{8,16},{12,20},{16,8},{20,12},{24,0},{28,4},{1,25},{... | collective-permute-start | bytes 344072 | tf_op jit(solution)/shard_map/ppermute | solution.py:350
  36.6 2.5 %collective-permute-done.9.refs_2_ = bf16[224,256]{1,0:T(8,128)(2,1)S(1)} collective-permute-done((bf16[224,256]{1,0:T(8,128)(2,1)S(1)}, bf16[224,256]{1,0:T(8,128)(2,1)S(1)}, u32[]{:S(2)}, u32[]{:S(2)}) %collective-permute-start.9) | collective-permute-done | bytes 114720 | tf_op jit(solution)/shard_map/ppermute | solution.py:350
  39.1 2.1 %collective-permute-done.11.refs_4_ = bf16[224,256]{1,0:T(8,128)(2,1)S(1)} collective-permute-done((bf16[224,256]{1,0:T(8,128)(2,1)S(1)}, bf16[224,256]{1,0:T(8,128)(2,1)S(1)}, u32[]{:S(2)}, u32[]{:S(2)}) %collective-permute-start.11) | collective-permute-done | bytes 114720 | tf_op jit(solution)/shard_map/ppermute | solution.py:350
  41.2 0.6 %row_sums.1 = (bf16[144,128]{1,0:T(8,128)(2,1)S(1)}, bf16[144,128]{1,0:T(8,128)(2,1)S(1)}, bf16[144,128]{1,0:T(8,128)(2,1)S(1)}, bf16[144,128]{1,0:T(8,128)(2,1)S(1)}) custom-call(bf16[448,256]{1,0:T(8,128)(2,1)S(1)} %get-tuple-element.41.own_ref.refs_0_, bf16[448,256]{1,0:T(8,128)(2,1)S(1)} %collective-permute-done.8.crossed_ref.refs_1_, ...), custom_call_target="tpu_custom_call" | custom-call | tf_op jit(solution)/shard_map/row_sums/pallas_call | solution.py:463
  41.8 0.1 collective-permute-start.12
  41.8 1.2 %collective-permute-start.13 = (bf16[144,128]{1,0:T(8,128)(2,1)S(1)}, bf16[144,128]{1,0:T(8,128)(2,1)S(1)}, u32[]{:S(2)}, u32[]{:S(2)}) collective-permute-start(bf16[144,128]{1,0:T(8,128)(2,1)S(1)} %get-tuple-element.48), channel_id=1, source_target_pairs={{0,2},{1,3},{2,0},{3,1},{4,6},{5,7},{6,4},{7,5},{8,10},{9,11},{10,... | collective-permute-start | bytes 110600 | tf_op jit(solution)/shard_map/ppermute | solution.py:350
  43.0 3.2 %collective-permute-start.14 = (bf16[144,128]{1,0:T(8,128)(2,1)S(1)}, bf16[144,128]{1,0:T(8,128)(2,1)S(1)}, u32[]{:S(2)}, u32[]{:S(2)}) collective-permute-start(bf16[144,128]{1,0:T(8,128)(2,1)S(1)} %get-tuple-element.49), channel_id=1, source_target_pairs={{0,3},{1,2},{2,1},{3,0},{4,7},{5,6},{6,5},{7,4},{8,11},{9,10},{10,... | collective-permute-start | bytes 110600 | tf_op jit(solution)/shard_map/ppermute | solution.py:350
  46.2 0.8 %collective-permute-done.13.refs_2_ = bf16[144,128]{1,0:T(8,128)(2,1)S(1)} collective-permute-done((bf16[144,128]{1,0:T(8,128)(2,1)S(1)}, bf16[144,128]{1,0:T(8,128)(2,1)S(1)}, u32[]{:S(2)}, u32[]{:S(2)}) %collective-permute-start.13) | collective-permute-done | bytes 36896 | tf_op jit(solution)/shard_map/ppermute | solution.py:350
  47.0 1.8 %collective-permute-done.14.refs_3_ = bf16[144,128]{1,0:T(8,128)(2,1)S(1)} collective-permute-done((bf16[144,128]{1,0:T(8,128)(2,1)S(1)}, bf16[144,128]{1,0:T(8,128)(2,1)S(1)}, u32[]{:S(2)}, u32[]{:S(2)}) %collective-permute-start.14) | collective-permute-done | bytes 36896 | tf_op jit(solution)/shard_map/ppermute | solution.py:350
  48.8 0.7 %adam.1 = (f32[64,128]{1,0:T(8,128)}, f32[64,128]{1,0:T(8,128)}, f32[64,128]{1,0:T(8,128)}, f32[64,128]{1,0:T(8,128)}, f32[64,128]{1,0:T(8,128)}, /*index=5*/f32...) custom-call(bf16[144,128]{1,0:T(8,128)(2,1)S(1)} %get-tuple-element.46.refs_0_, ...), custom_call_target="tpu_custom_call" | custom-call | tf_op jit(solution)/shard_map/adam/pallas_call | solution.py:484
  (24 shorter events, 0.1 us)
Async XLA Ops:
  0.6 48.1 %copy-start.2 = (f32[32,64]{1,0:T(8,128)S(1)}, f32[32,64]{1,0:T(8,128)}, u32[]{:S(2)}) copy-start(f32[32,64]{1,0:T(8,128)} %refs_10_.1) | copy-start | bytes 24580
  0.7 48.1 %copy-start.1 = (f32[128,64]{0,1:T(8,128)S(1)}, f32[128,64]{0,1:T(8,128)}, u32[]{:S(2)}) copy-start(f32[128,64]{0,1:T(8,128)} %param.20) | copy-start | bytes 98308
  0.7 48.1 %copy-start = (f32[128,64]{0,1:T(8,128)S(1)}, f32[128,64]{0,1:T(8,128)}, u32[]{:S(2)}) copy-start(f32[128,64]{0,1:T(8,128)} %param.17) | copy-start | bytes 98308
  0.7 48.1 %copy-start.8 = (f32[32,64]{1,0:T(8,128)S(1)}, f32[32,64]{1,0:T(8,128)}, u32[]{:S(2)}) copy-start(f32[32,64]{1,0:T(8,128)} %refs_12_.1) | copy-start | bytes 24580
  0.7 48.1 %copy-start.7 = (f32[32,64]{1,0:T(8,128)S(1)}, f32[32,64]{1,0:T(8,128)}, u32[]{:S(2)}) copy-start(f32[32,64]{1,0:T(8,128)} %refs_11_.3) | copy-start | bytes 24580
  0.7 48.1 %copy-start.6 = (f32[128,64]{0,1:T(8,128)S(1)}, f32[128,64]{0,1:T(8,128)}, u32[]{:S(2)}) copy-start(f32[128,64]{0,1:T(8,128)} %param.22) | copy-start | bytes 98308
  0.7 48.1 %copy-start.5 = (f32[128,64]{0,1:T(8,128)S(1)}, f32[128,64]{0,1:T(8,128)}, u32[]{:S(2)}) copy-start(f32[128,64]{0,1:T(8,128)} %param.21) | copy-start | bytes 98308
  0.7 48.1 %copy-start.4 = (f32[128,64]{0,1:T(8,128)S(1)}, f32[128,64]{0,1:T(8,128)}, u32[]{:S(2)}) copy-start(f32[128,64]{0,1:T(8,128)} %param.19) | copy-start | bytes 98308
  0.7 48.1 %copy-start.3 = (f32[128,64]{0,1:T(8,128)S(1)}, f32[128,64]{0,1:T(8,128)}, u32[]{:S(2)}) copy-start(f32[128,64]{0,1:T(8,128)} %param.18) | copy-start | bytes 98308
  1.7 5.7 %collective-permute-start.2 = (bf16[144,128]{1,0:T(8,128)(2,1)S(1)}, bf16[144,128]{1,0:T(8,128)(2,1)S(1)}, u32[]{:S(2)}, u32[]{:S(2)}) collective-permute-start(bf16[144,128]{1,0:T(8,128)(2,1)S(1)} %pack.1.refs_3_), channel_id=1, source_target_pairs={{0,1},{1,0},{2,3},{3,2},{4,5},{5,4},{6,7},{7,6},{8,9},{9,8},{10,11... | collective-permute-start | bytes 110600 | tf_op jit(solution)/shard_map/ppermute | solution.py:350
  4.8 5.5 %collective-permute-start.1 = (bf16[144,128]{1,0:T(8,128)(2,1)S(1)}, bf16[144,128]{1,0:T(8,128)(2,1)S(1)}, u32[]{:S(2)}, u32[]{:S(2)}) collective-permute-start(bf16[144,128]{1,0:T(8,128)(2,1)S(1)} %pack.1.refs_3_), channel_id=1, source_target_pairs={{0,2},{1,3},{2,0},{3,1},{4,6},{5,7},{6,4},{7,5},{8,10},{9,11},{10,... | collective-permute-start | bytes 110600 | tf_op jit(solution)/shard_map/ppermute | solution.py:350
  7.4 5.8 %collective-permute-start = (bf16[144,128]{1,0:T(8,128)(2,1)S(1)}, bf16[144,128]{1,0:T(8,128)(2,1)S(1)}, u32[]{:S(2)}, u32[]{:S(2)}) collective-permute-start(bf16[144,128]{1,0:T(8,128)(2,1)S(1)} %pack.1.refs_3_), channel_id=1, source_target_pairs={{0,3},{1,2},{2,1},{3,0},{4,7},{5,6},{6,5},{7,4},{8,11},{9,10},{10,... | collective-permute-start | bytes 110600 | tf_op jit(solution)/shard_map/ppermute | solution.py:350
  13.3 6.4 %collective-permute-start.6 = (bf16[576,128]{1,0:T(8,128)(2,1)S(1)}, bf16[576,128]{1,0:T(8,128)(2,1)S(1)}, u32[]{:S(2)}, u32[]{:S(2)}) collective-permute-start(bf16[576,128]{1,0:T(8,128)(2,1)S(1)} %table.1.refs_3_.refs_0_), channel_id=1, source_target_pairs={{0,8},{4,12},{8,0},{12,4},{16,24},{20,28},{24,16},{28,20},{1,9},{5... | collective-permute-start | bytes 442376 | tf_op jit(solution)/shard_map/ppermute | solution.py:350
  14.8 7.7 %collective-permute-start.5 = (bf16[576,128]{1,0:T(8,128)(2,1)S(1)}, bf16[576,128]{1,0:T(8,128)(2,1)S(1)}, u32[]{:S(2)}, u32[]{:S(2)}) collective-permute-start(bf16[576,128]{1,0:T(8,128)(2,1)S(1)} %table.1.refs_3_.refs_0_), channel_id=1, source_target_pairs={{0,16},{4,20},{8,24},{12,28},{16,0},{20,4},{24,8},{28,12},{1,17},{... | collective-permute-start | bytes 442376 | tf_op jit(solution)/shard_map/ppermute | solution.py:350
  16.3 6.2 %collective-permute-start.4 = (bf16[576,128]{1,0:T(8,128)(2,1)S(1)}, bf16[576,128]{1,0:T(8,128)(2,1)S(1)}, u32[]{:S(2)}, u32[]{:S(2)}) collective-permute-start(bf16[576,128]{1,0:T(8,128)(2,1)S(1)} %table.1.refs_3_.refs_0_), channel_id=1, source_target_pairs={{0,24},{4,28},{8,16},{12,20},{16,8},{20,12},{24,0},{28,4},{1,25},{... | collective-permute-start | bytes 442376 | tf_op jit(solution)/shard_map/ppermute | solution.py:350
  22.5 2.1 %collective-permute-start.7 = (bf16[1728,128]{1,0:T(8,128)(2,1)S(1)}, bf16[1728,128]{1,0:T(8,128)(2,1)S(1)}, u32[]{:S(2)}, u32[]{:S(2)}) collective-permute-start(bf16[1728,128]{1,0:T(8,128)(2,1)S(1)} %join.1.refs_2_), channel_id=1, source_target_pairs={{0,4},{4,0},{8,12},{12,8},{16,20},{20,16},{24,28},{28,24},{1,5},{5... | collective-permute-start | bytes 1327112 | tf_op jit(solution)/shard_map/ppermute | solution.py:350
  22.6 2.0 %collective-permute-start.3 = (bf16[576,128]{1,0:T(8,128)(2,1)S(1)}, bf16[576,128]{1,0:T(8,128)(2,1)S(1)}, u32[]{:S(2)}, u32[]{:S(2)}) collective-permute-start(bf16[576,128]{1,0:T(8,128)(2,1)S(1)} %table.1.refs_3_.refs_0_), channel_id=1, source_target_pairs={{0,4},{4,0},{8,12},{12,8},{16,20},{20,16},{24,28},{28,24},{1,5},{5... | collective-permute-start | bytes 442376 | tf_op jit(solution)/shard_map/ppermute | solution.py:350
  31.5 1.6 %collective-permute-start.8 = (bf16[448,256]{1,0:T(8,128)(2,1)S(1)}, bf16[448,256]{1,0:T(8,128)(2,1)S(1)}, u32[]{:S(2)}, u32[]{:S(2)}) collective-permute-start(bf16[448,256]{1,0:T(8,128)(2,1)S(1)} %get-tuple-element.42), channel_id=1, source_target_pairs={{0,4},{4,0},{8,12},{12,8},{16,20},{20,16},{24,28},{28,24},{1,5},{5... | collective-permute-start | bytes 688136 | tf_op jit(solution)/shard_map/ppermute | solution.py:350
  33.1 6.1 %collective-permute-start.9 = (bf16[224,256]{1,0:T(8,128)(2,1)S(1)}, bf16[224,256]{1,0:T(8,128)(2,1)S(1)}, u32[]{:S(2)}, u32[]{:S(2)}) collective-permute-start(bf16[224,256]{1,0:T(8,128)(2,1)S(1)} %get-tuple-element.43), channel_id=1, source_target_pairs={{0,8},{4,12},{8,0},{12,4},{16,24},{20,28},{24,16},{28,20},{1,9},{5... | collective-permute-start | bytes 344072 | tf_op jit(solution)/shard_map/ppermute | solution.py:350
  33.5 5.6 %collective-permute-start.10 = (bf16[224,256]{1,0:T(8,128)(2,1)S(1)}, bf16[224,256]{1,0:T(8,128)(2,1)S(1)}, u32[]{:S(2)}, u32[]{:S(2)}) collective-permute-start(bf16[224,256]{1,0:T(8,128)(2,1)S(1)} %get-tuple-element.44), channel_id=1, source_target_pairs={{0,16},{4,20},{8,24},{12,28},{16,0},{20,4},{24,8},{28,12},{1,17},{... | collective-permute-start | bytes 344072 | tf_op jit(solution)/shard_map/ppermute | solution.py:350
  34.3 6.9 %collective-permute-start.11 = (bf16[224,256]{1,0:T(8,128)(2,1)S(1)}, bf16[224,256]{1,0:T(8,128)(2,1)S(1)}, u32[]{:S(2)}, u32[]{:S(2)}) collective-permute-start(bf16[224,256]{1,0:T(8,128)(2,1)S(1)} %get-tuple-element.45), channel_id=1, source_target_pairs={{0,24},{4,28},{8,16},{12,20},{16,8},{20,12},{24,0},{28,4},{1,25},{... | collective-permute-start | bytes 344072 | tf_op jit(solution)/shard_map/ppermute | solution.py:350
  41.8 4.5 %collective-permute-start.12 = (bf16[144,128]{1,0:T(8,128)(2,1)S(1)}, bf16[144,128]{1,0:T(8,128)(2,1)S(1)}, u32[]{:S(2)}, u32[]{:S(2)}) collective-permute-start(bf16[144,128]{1,0:T(8,128)(2,1)S(1)} %get-tuple-element.47), channel_id=1, source_target_pairs={{0,1},{1,0},{2,3},{3,2},{4,5},{5,4},{6,7},{7,6},{8,9},{9,8},{10,11... | collective-permute-start | bytes 110600 | tf_op jit(solution)/shard_map/ppermute | solution.py:350
  41.8 5.2 %collective-permute-start.13 = (bf16[144,128]{1,0:T(8,128)(2,1)S(1)}, bf16[144,128]{1,0:T(8,128)(2,1)S(1)}, u32[]{:S(2)}, u32[]{:S(2)}) collective-permute-start(bf16[144,128]{1,0:T(8,128)(2,1)S(1)} %get-tuple-element.48), channel_id=1, source_target_pairs={{0,2},{1,3},{2,0},{3,1},{4,6},{5,7},{6,4},{7,5},{8,10},{9,11},{10,... | collective-permute-start | bytes 110600 | tf_op jit(solution)/shard_map/ppermute | solution.py:350
  43.0 5.8 %collective-permute-start.14 = (bf16[144,128]{1,0:T(8,128)(2,1)S(1)}, bf16[144,128]{1,0:T(8,128)(2,1)S(1)}, u32[]{:S(2)}, u32[]{:S(2)}) collective-permute-start(bf16[144,128]{1,0:T(8,128)(2,1)S(1)} %get-tuple-element.49), channel_id=1, source_target_pairs={{0,3},{1,2},{2,1},{3,0},{4,7},{5,6},{6,5},{7,4},{8,11},{9,10},{10,... | collective-permute-start | bytes 110600 | tf_op jit(solution)/shard_map/ppermute | solution.py:350

commit v7 on v6

--- a/solution.py
+++ b/solution.py
@@ -26,6 +26,7 @@
 class Sizes:
     def __init__(self, owners, holders, columns, row_counts, list_counts):
         self.owners = owners
+        self.folded = owners == 8
         self.holders = holders
         self.columns = columns
         self.rank = columns * holders
@@ -98,6 +99,17 @@
     out_ref[2 * columns :, :] = pack_days(sizes, day[...]).astype(bf16)
 
 
+def place_of(sizes, owner, me):
+    apart = lax.bitwise_xor(owner, jnp.full_like(owner, me))
+    other_core = apart % 2
+    chip = apart // 2
+    if sizes.folded:
+        core = (other_core + me) % 2
+        along_x = jnp.where(core == 0, 2, 1)
+        chip = jnp.where(chip == 1, along_x, jnp.where(chip == 2, 3 - along_x, chip))
+    return other_core * (sizes.owners // 2) + chip
+
+
 def slot_kernel(sizes, me_ref, *refs):
     owners = sizes.owners
     picks, places, note_ref, lists = refs[4:7], refs[7:10], refs[10], refs[11:14]
@@ -109,7 +121,7 @@
         number = lists[t][...]
         owner = number // rows
         row = number % rows
-        partner = lax.bitwise_xor(owner, jnp.full_like(owner, me))
+        partner = place_of(sizes, owner, me)
         picks[t][...] = onehot(iota((owners * rows, count), 0) == partner * rows + row)
         earlier = onehot(iota((count, count), 0) < iota((count, count), 1))
         owner_hot = iota((owners, count), 0) == owner
@@ -145,9 +157,9 @@
 
 def block_kernel(sizes, *refs):
     owners, rank, day_rows = sizes.owners, sizes.rank, sizes.row_counts[2]
-    own_table, own_crossed, tables_ref, tables_crossed = refs[:4]
-    picks, places = refs[4:7], refs[7:10]
-    note_ref, status_hbm, own_ref, other_ref = refs[10:14]
+    tables, refs = refs[:owners], refs[owners:]
+    picks, places = refs[:3], refs[3:6]
+    note_ref, status_hbm, own_ref, other_ref = refs[6:10]
     (
         users,
         users_low,
@@ -163,7 +175,7 @@
         residual_odd,
         status,
         semaphores,
-    ) = refs[14:]
+    ) = refs[10:]
     pair = 2
     pairs = status.shape[0] // pair
     chunks = [(0, pair)]
@@ -178,15 +190,6 @@
 
     for n, (start, size) in enumerate(chunks):
         status_copy(start, size, n).start()
-
-    height = sizes.table_rows
-    tables = []
-    for n in range(owners // 2):
-        if n == 0:
-            tables += [own_table, own_crossed]
-        else:
-            part = slice((n - 1) * height, n * height)
-            tables += [tables_ref.at[part], tables_crossed.at[part]]
 
     def pick(t):
         table = jnp.concatenate([ref[t * rank : (t + 1) * rank, :] for ref in tables], axis=1)
@@ -268,33 +271,26 @@
             if t == 2:
                 note = iota(rows.shape, 0) == sizes.note_row
                 rows = jnp.where(note, note_ref[s : s + 1, :], rows)
-            out = (own_ref, other_ref)[s % 2]
-            first = (s // 2) * sizes.slot_rows + start
+            out = (own_ref, other_ref)[2 * s // owners]
+            first = (s % (owners // 2)) * sizes.slot_rows + start
             out[first : first + slots, :] = rows.astype(bf16)
 
 
-def join_kernel(sizes, *refs):
-    arrived, out_ref = refs[:-2], refs[-1]
-    for n, ref in enumerate(arrived[::-1]):
-        out_ref[n * sizes.table_rows : (n + 1) * sizes.table_rows, :] = ref[...]
-
-
-def merge_kernel(sizes, own_ref, crossed_ref, *outs):
+def hold_kernel(arrived_ref, note_ref, out_ref):
+    out_ref[...] = arrived_ref[...]
+
+
+def merge_kernel(sizes, parts, own_ref, crossed_ref, *outs):
     rows = sizes.slot_rows
-    for n, out in enumerate(outs):
-        start = (n + 1) * rows
+    for part, out in zip(parts, outs):
+        start = part * rows
         out[:rows, :] = own_ref[start : start + rows, :]
         out[rows:, :] = crossed_ref[start : start + rows, :]
 
 
-def sum_kernel(sizes, *refs):
-    holders, columns = sizes.holders, sizes.columns
-    inputs = sizes.owners // 2 + 1
-    arrived, outs = refs[:inputs], refs[inputs:]
+def sum_messages(sizes, messages):
     day_start = sizes.slot_starts[2]
     totals = [0.0, 0.0, 0.0]
-    messages = [ref.at[: sizes.slot_rows] for ref in arrived]
-    messages += [ref.at[sizes.slot_rows :] for ref in arrived[2:]]
     for ref in messages:
         notes = ref[day_start : day_start + sizes.slots[2], :].astype(f32)
         rows = notes[sizes.note_row : sizes.note_row + 1, : sizes.slot_rows].astype(jnp.int32)
@@ -305,18 +301,44 @@
             mine = (slot >= start) & (slot < start + slots)
             selector = onehot((iota(shape, 0) == rows) & mine)
             totals[t] = totals[t] + jnp.dot(selector, ref[...], preferred_element_type=f32)
-    for t in range(3):
-        if t < 2:
-            turned = totals[t].T.astype(bf16)
-            for j in range(holders):
-                outs[j][t * columns : (t + 1) * columns, :] = turned[
-                    j * columns : (j + 1) * columns
-                ]
-        else:
-            for j in range(holders):
-                outs[j][2 * columns :, :] = pack_days(
-                    sizes, totals[t][:, j * columns : (j + 1) * columns]
-                ).astype(bf16)
+    columns = sizes.columns
+    users, items = totals[0].T, totals[1].T
+    pieces = []
+    for j in range(sizes.holders):
+        part = slice(j * columns, (j + 1) * columns)
+        pieces.append((users[part], items[part], pack_days(sizes, totals[2][:, part])))
+    return pieces
+
+
+def fold_kernel(sizes, start, own_ref, crossed_ref, arrived_ref, *outs):
+    rows, columns = sizes.slot_rows, sizes.columns
+    messages = [own_ref.at[start : start + rows], crossed_ref.at[start : start + rows]]
+    messages += [arrived_ref.at[:rows], arrived_ref.at[rows:]]
+    for j, (users, items, days) in enumerate(sum_messages(sizes, messages)):
+        out_ref = outs[j * len(outs) // sizes.holders]
+        first = j % (sizes.holders // len(outs)) * sizes.piece_rows
+        out_ref[first : first + columns, :] = users.astype(bf16)
+        out_ref[first + columns : first + 2 * columns, :] = items.astype(bf16)
+        out_ref[first + 2 * columns : first + sizes.piece_rows, :] = days.astype(bf16)
+
+
+def sum_kernel(sizes, inputs, *refs):
+    rows, columns = sizes.slot_rows, sizes.columns
+    arrived, outs = refs[:inputs], refs[inputs:]
+    folded = ()
+    if sizes.folded:
+        arrived, folded = arrived[:-2], arrived[-2:]
+    messages = [ref.at[:rows] for ref in arrived]
+    messages += [ref.at[rows:] for ref in arrived[2:]]
+    for j, piece in enumerate(sum_messages(sizes, messages)):
+        starts = (0, columns, 2 * columns, sizes.piece_rows)
+        for t in range(3):
+            total = piece[t]
+            if folded:
+                ref = folded[j * len(folded) // sizes.holders]
+                first = j % (sizes.holders // len(folded)) * sizes.piece_rows
+                total = total + ref[first + starts[t] : first + starts[t + 1], :].astype(f32)
+            outs[j][starts[t] : starts[t + 1], :] = total.astype(bf16)
 
 
 def adam_kernel(sizes, *refs):
@@ -346,8 +368,8 @@
         new_second[...] = second_value
 
 
-def swap(array, axis, size, bits):
-    return lax.ppermute(array, axis, [(i, i ^ bits) for i in range(size)])
+def swap(array, axis, size, *bits):
+    return lax.ppermute(array, axis, [(i, i ^ bits[i % len(bits)]) for i in range(size)])
 
 
 def local(
@@ -393,7 +415,12 @@
         compiler_params=small,
         name="table",
     )(*pieces)
-    arrived = [swap(table, "dp", owners, bits) for bits in range(owners - 2, 0, -2)]
+    if sizes.folded:
+        across = swap(table, "dp", owners, 2, 4)
+        along = swap(table, "dp", owners, 4, 2)
+        arrived = [along, across]
+    else:
+        arrived = [swap(table, "dp", owners, bits) for bits in range(2, owners, 2)]
     own_crossed = swap(table, "dp", owners, 1)
     picks_places_notes = pl.pallas_call(
         functools.partial(slot_kernel, sizes),
@@ -415,15 +442,17 @@
         table,
     )
 
-    joined = pl.pallas_call(
-        functools.partial(join_kernel, sizes),
-        out_shape=shape((len(arrived) * sizes.table_rows, LANES), bf16),
-        compiler_params=small,
-        name="join",
-    )(*arrived, picks_places_notes[6])
-    joined_crossed = swap(joined, "dp", owners, 1)
-
-    inputs = [table, own_crossed, joined, joined_crossed, *picks_places_notes]
+    held = pl.pallas_call(
+        hold_kernel,
+        out_shape=shape(table.shape, bf16),
+        compiler_params=small,
+        name="hold",
+    )(arrived[0], picks_places_notes[6])
+    arrived[0] = held
+    if sizes.folded:
+        arrived.append(swap(held, "dp", owners, 2, 4))
+    crossed = [own_crossed] + [swap(a, "dp", owners, 1) for a in arrived]
+    inputs = [table, *arrived, *crossed, *picks_places_notes]
     users, items, days = list_counts
     half = shape((owners // 2 * sizes.slot_rows, sizes.rank), bf16)
     own, other = pl.pallas_call(
@@ -451,17 +480,37 @@
     )(*inputs, in_hbm(status))
     crossed = swap(other, "dp", owners, 1)
     message = shape((2 * sizes.slot_rows, sizes.rank), bf16)
+    if sizes.folded:
+        merges = (1, 3)
+    else:
+        merges = tuple(range(1, owners // 2))
     merged = pl.pallas_call(
-        functools.partial(merge_kernel, sizes),
-        out_shape=tuple([message] * (owners // 2 - 1)),
+        functools.partial(merge_kernel, sizes, merges),
+        out_shape=tuple([message] * len(merges)),
         compiler_params=small,
         name="merge",
     )(own, crossed)
     returned = [own, crossed]
-    returned += [swap(merged[bits // 2 - 1], "dp", owners, bits) for bits in range(2, owners, 2)]
+    if sizes.folded:
+        diagonal = swap(merged[1], "dp", owners, 4, 2)
+        returned.append(swap(merged[0], "dp", owners, 4, 2))
+        folded = pl.pallas_call(
+            functools.partial(fold_kernel, sizes, 2 * sizes.slot_rows),
+            out_shape=(shape((holders // 2 * sizes.piece_rows, LANES), bf16),) * 2,
+            compiler_params=small,
+            cost_estimate=pl.CostEstimate(
+                flops=4 * 10**9, bytes_accessed=4 * 10**6, transcendentals=0
+            ),
+            name="fold",
+        )(own, crossed, diagonal)
+        returned += [swap(a, "dp", owners, 2, 4) for a in folded]
+    else:
+        returned += [
+            swap(merged[bits // 2 - 1], "dp", owners, bits) for bits in range(2, owners, 2)
+        ]
 
     totals = pl.pallas_call(
-        functools.partial(sum_kernel, sizes),
+        functools.partial(sum_kernel, sizes, len(returned)),
         out_shape=tuple([shape(piece.shape, bf16)] * holders),
         compiler_params=small,
         name="row_sums",

time: 49.8 us -> 53.1 us (1.066)
  starting transfers between devices: 17.9 us -> 19.7 us
  waiting for transfers between devices: 19.6 us -> 20.9 us
    ppermute x15 -> x18, starting transfers between devices: 17.9 us -> 19.7 us  [swap(): lax.ppermute(array, axis, [(i, i ^ bits[i % len(bits)]) for i in range(si...]
    ppermute x15 -> x18, waiting for transfers between devices: 19.6 us -> 20.9 us  [swap(): lax.ppermute(array, axis, [(i, i ^ bits[i % len(bits)]) for i in range(si...]
  transfers between devices with their start and end apart: 15 -> 18, of which waited for: 10 -> 11; matrix products, arithmetic and copies ran while one was open for 0% -> 0% of each run, Pallas kernels for 4% -> 4%
where the time goes in v7:
time: 53.1 us; the launch traced here: 52.9 us
  waiting for transfers between devices  20.9 us (39%)
  starting transfers between devices  19.7 us (37%)
  Pallas kernels  11.4 us (21%)
  between operations  0.84 us (2%)
    ppermute x18, waiting for transfers between devices, swap(): lax.ppermute(array, axis, [(i, i ^ bits[i % len(bits)]) for i in range(si...  20.9 us
    ppermute x18, starting transfers between devices, swap(): lax.ppermute(array, axis, [(i, i ^ bits[i % len(bits)]) for i in range(si...  19.7 us
    pallas_call x1, Pallas kernels, local(): pl.pallas_call(functools.partial(block_kernel, sizes), out_shape=(half, h...  6.91 us
    pallas_call x1, Pallas kernels, local(): pl.pallas_call(functools.partial(slot_kernel, sizes), out_shape=tuple([sh...  1.82 us
  transfers between devices with their start and end apart: 18, of which 11 were waited for; matrix products, arithmetic and copies ran while one was open for 0% of the time, Pallas kernels for 4%

profile of v7, /device:TPU:0, one launch (start us, length us, event | category | flops | bytes accessed | tf_op | source)
XLA Modules:
  0.0 52.9 jit_solution(11908317051857164869)
XLA Ops:
  0.6 0.9 %pack.1.refs_3_ = bf16[144,128]{1,0:T(8,128)(2,1)S(1)} custom-call(f32[64,128]{1,0:T(8,128)} %bitcast.13, f32[64,128]{1,0:T(8,128)} %bitcast.15, f32[32,64]{1,0:T(8,128)} %refs_10_.1), custom_call_target="tpu_custom_call" | custom-call | tf_op jit(solution)/shard_map/pack/pallas_call | solution.py:401
  1.5 3.1 %collective-permute-start.2 = (bf16[144,128]{1,0:T(8,128)(2,1)S(1)}, bf16[144,128]{1,0:T(8,128)(2,1)S(1)}, u32[]{:S(2)}, u32[]{:S(2)}) collective-permute-start(bf16[144,128]{1,0:T(8,128)(2,1)S(1)} %pack.1.refs_3_), channel_id=1, source_target_pairs={{0,1},{1,0},{2,3},{3,2},{4,5},{5,4},{6,7},{7,6},{8,9},{9,8},{10,11... | collective-permute-start | bytes 110600 | tf_op jit(solution)/shard_map/ppermute | solution.py:372
  4.6 2.6 %collective-permute-start.1 = (bf16[144,128]{1,0:T(8,128)(2,1)S(1)}, bf16[144,128]{1,0:T(8,128)(2,1)S(1)}, u32[]{:S(2)}, u32[]{:S(2)}) collective-permute-start(bf16[144,128]{1,0:T(8,128)(2,1)S(1)} %pack.1.refs_3_), channel_id=1, source_target_pairs={{0,2},{1,3},{2,0},{3,1},{4,6},{5,7},{6,4},{7,5},{8,10},{9,11},{10,... | collective-permute-start | bytes 110600 | tf_op jit(solution)/shard_map/ppermute | solution.py:372
  7.2 2.9 %collective-permute-done.1.refs_1_ = bf16[144,128]{1,0:T(8,128)(2,1)S(1)} collective-permute-done((bf16[144,128]{1,0:T(8,128)(2,1)S(1)}, bf16[144,128]{1,0:T(8,128)(2,1)S(1)}, u32[]{:S(2)}, u32[]{:S(2)}) %collective-permute-start.1) | collective-permute-done | bytes 36896 | tf_op jit(solution)/shard_map/ppermute | solution.py:372
  10.1 2.8 %collective-permute-done.refs_0_ = bf16[144,128]{1,0:T(8,128)(2,1)S(1)} collective-permute-done((bf16[144,128]{1,0:T(8,128)(2,1)S(1)}, bf16[144,128]{1,0:T(8,128)(2,1)S(1)}, u32[]{:S(2)}, u32[]{:S(2)}) %collective-permute-start) | collective-permute-done | bytes 36896 | tf_op jit(solution)/shard_map/ppermute | solution.py:372
  13.0 0.1 table.1.refs_3_.refs_0_
  13.1 1.5 %collective-permute-start.3 = (bf16[576,128]{1,0:T(8,128)(2,1)S(1)}, bf16[576,128]{1,0:T(8,128)(2,1)S(1)}, u32[]{:S(2)}, u32[]{:S(2)}) collective-permute-start(bf16[576,128]{1,0:T(8,128)(2,1)S(1)} %table.1.refs_3_.refs_0_), channel_id=1, source_target_pairs={{0,16},{4,12},{8,24},{12,4},{16,0},{20,28},{24,8},{28,20},{1,17},{... | collective-permute-start | bytes 442376 | tf_op jit(solution)/shard_map/ppermute | solution.py:372
  14.6 1.5 %collective-permute-start.4 = (bf16[576,128]{1,0:T(8,128)(2,1)S(1)}, bf16[576,128]{1,0:T(8,128)(2,1)S(1)}, u32[]{:S(2)}, u32[]{:S(2)}) collective-permute-start(bf16[576,128]{1,0:T(8,128)(2,1)S(1)} %table.1.refs_3_.refs_0_), channel_id=1, source_target_pairs={{0,8},{4,20},{8,0},{12,28},{16,24},{20,4},{24,16},{28,12},{1,9},{5... | collective-permute-start | bytes 442376 | tf_op jit(solution)/shard_map/ppermute | solution.py:372
  16.1 1.8 %slots.1 = (bf16[1024,256]{1,0:T(8,128)(2,1)S(1)}, bf16[1024,256]{1,0:T(8,128)(2,1)S(1)}, bf16[256,32]{1,0:T(8,128)(2,1)S(1)}, bf16[384,256]{1,0:T(8,128)(2,1)S(...) custom-call(s32[1]{0:T(128)} %bitcast.2.me_ref, s32[1,256]{1,0:T(1,128)} %refs_0_.1, ...), custom_call_target="tpu_custom_call" | custom-call | tf_op jit(solution)/shard_map/slots/pallas_call | solution.py:425
  17.9 0.4 collective-permute-done.3.arrived_ref
  18.3 1.7 %collective-permute-start.5 = (bf16[576,128]{1,0:T(8,128)(2,1)S(1)}, bf16[576,128]{1,0:T(8,128)(2,1)S(1)}, u32[]{:S(2)}, u32[]{:S(2)}) collective-permute-start(bf16[576,128]{1,0:T(8,128)(2,1)S(1)} %hold.1.refs_1_), channel_id=1, source_target_pairs={{0,8},{4,20},{8,0},{12,28},{16,24},{20,4},{24,16},{28,12},{1,9},{5... | collective-permute-start | bytes 442376 | tf_op jit(solution)/shard_map/ppermute | solution.py:372
  20.0 0.5 collective-permute-start.7
  20.5 3.0 %collective-permute-done.5.refs_3_ = bf16[576,128]{1,0:T(8,128)(2,1)S(1)} collective-permute-done((bf16[576,128]{1,0:T(8,128)(2,1)S(1)}, bf16[576,128]{1,0:T(8,128)(2,1)S(1)}, u32[]{:S(2)}, u32[]{:S(2)}) %collective-permute-start.5) | collective-permute-done | bytes 147488 | tf_op jit(solution)/shard_map/ppermute | solution.py:372
  23.6 1.3 %collective-permute-done.9.refs_7_ = bf16[576,128]{1,0:T(8,128)(2,1)S(1)} collective-permute-done((bf16[576,128]{1,0:T(8,128)(2,1)S(1)}, bf16[576,128]{1,0:T(8,128)(2,1)S(1)}, u32[]{:S(2)}, u32[]{:S(2)}) %collective-permute-start.9) | collective-permute-done | bytes 147488 | tf_op jit(solution)/shard_map/ppermute | solution.py:372
  24.9 6.9 %block_gradients.1 = (bf16[448,256]{1,0:T(8,128)(2,1)S(1)}, bf16[448,256]{1,0:T(8,128)(2,1)S(1)}) custom-call(bf16[576,128]{1,0:T(8,128)(2,1)S(1)} %table.1.refs_3_.refs_0_, bf16[576,128]{1,0:T(8,128)(2,1)S(1)} %hold.1.refs_1_, bf16[576,128]{1,0:T(8,128)(2,1)S(1)} %collective-permute-done.4.refs_2_, bf16[576,128]{1,0:T(8,128)(2,1)S(1)} %collective-permute-done.5.refs_3_, ...), custom_call_target="tpu_custom_call" | custom-call | tf_op jit(solution)/shard_map/block_gradients/pallas_call | solution.py:458
  31.9 0.2 collective-permute-start.10
  32.1 1.3 %collective-permute-done.10.crossed_ref.refs_1_ = bf16[448,256]{1,0:T(8,128)(2,1)S(1)} collective-permute-done((bf16[448,256]{1,0:T(8,128)(2,1)S(1)}, bf16[448,256]{1,0:T(8,128)(2,1)S(1)}, u32[]{:S(2)}, u32[]{:S(2)}) %collective-permute-start.10) | collective-permute-done | bytes 229408 | tf_op jit(solution)/shard_map/ppermute | solution.py:372
  33.5 1.8 %collective-permute-start.12 = (bf16[224,256]{1,0:T(8,128)(2,1)S(1)}, bf16[224,256]{1,0:T(8,128)(2,1)S(1)}, u32[]{:S(2)}, u32[]{:S(2)}) collective-permute-start(bf16[224,256]{1,0:T(8,128)(2,1)S(1)} %get-tuple-element.45), channel_id=1, source_target_pairs={{0,16},{4,12},{8,24},{12,4},{16,0},{20,28},{24,8},{28,20},{1,17},{... | collective-permute-start | bytes 344072 | tf_op jit(solution)/shard_map/ppermute | solution.py:372
  35.3 0.3 collective-permute-start.11
  35.6 2.8 %collective-permute-done.12.arrived_ref = bf16[224,256]{1,0:T(8,128)(2,1)S(1)} collective-permute-done((bf16[224,256]{1,0:T(8,128)(2,1)S(1)}, bf16[224,256]{1,0:T(8,128)(2,1)S(1)}, u32[]{:S(2)}, u32[]{:S(2)}) %collective-permute-start.12) | collective-permute-done | bytes 114720 | tf_op jit(solution)/shard_map/ppermute | solution.py:372
  38.4 0.4 fold.1
  38.8 1.7 %collective-permute-start.13 = (bf16[288,128]{1,0:T(8,128)(2,1)S(1)}, bf16[288,128]{1,0:T(8,128)(2,1)S(1)}, u32[]{:S(2)}, u32[]{:S(2)}) collective-permute-start(bf16[288,128]{1,0:T(8,128)(2,1)S(1)} %get-tuple-element.46), channel_id=1, source_target_pairs={{0,8},{4,20},{8,0},{12,28},{16,24},{20,4},{24,16},{28,12},{1,9},{5... | collective-permute-start | bytes 221192 | tf_op jit(solution)/shard_map/ppermute | solution.py:372
  40.5 0.4 collective-permute-start.14
  40.9 2.3 %collective-permute-done.13.refs_3_ = bf16[288,128]{1,0:T(8,128)(2,1)S(1)} collective-permute-done((bf16[288,128]{1,0:T(8,128)(2,1)S(1)}, bf16[288,128]{1,0:T(8,128)(2,1)S(1)}, u32[]{:S(2)}, u32[]{:S(2)}) %collective-permute-start.13) | collective-permute-done | bytes 73760 | tf_op jit(solution)/shard_map/ppermute | solution.py:372
  43.2 1.6 %collective-permute-done.14.refs_4_ = bf16[288,128]{1,0:T(8,128)(2,1)S(1)} collective-permute-done((bf16[288,128]{1,0:T(8,128)(2,1)S(1)}, bf16[288,128]{1,0:T(8,128)(2,1)S(1)}, u32[]{:S(2)}, u32[]{:S(2)}) %collective-permute-start.14) | collective-permute-done | bytes 73760 | tf_op jit(solution)/shard_map/ppermute | solution.py:372
  44.8 0.5 row_sums.1
  45.3 0.1 collective-permute-start.15
  45.4 0.9 %collective-permute-start.16 = (bf16[144,128]{1,0:T(8,128)(2,1)S(1)}, bf16[144,128]{1,0:T(8,128)(2,1)S(1)}, u32[]{:S(2)}, u32[]{:S(2)}) collective-permute-start(bf16[144,128]{1,0:T(8,128)(2,1)S(1)} %get-tuple-element.50), channel_id=1, source_target_pairs={{0,2},{1,3},{2,0},{3,1},{4,6},{5,7},{6,4},{7,5},{8,10},{9,11},{10,... | collective-permute-start | bytes 110600 | tf_op jit(solution)/shard_map/ppermute | solution.py:372
  46.3 3.4 %collective-permute-start.17 = (bf16[144,128]{1,0:T(8,128)(2,1)S(1)}, bf16[144,128]{1,0:T(8,128)(2,1)S(1)}, u32[]{:S(2)}, u32[]{:S(2)}) collective-permute-start(bf16[144,128]{1,0:T(8,128)(2,1)S(1)} %get-tuple-element.51), channel_id=1, source_target_pairs={{0,3},{1,2},{2,1},{3,0},{4,7},{5,6},{6,5},{7,4},{8,11},{9,10},{10,... | collective-permute-start | bytes 110600 | tf_op jit(solution)/shard_map/ppermute | solution.py:372
  49.8 0.5 %collective-permute-done.16.refs_2_ = bf16[144,128]{1,0:T(8,128)(2,1)S(1)} collective-permute-done((bf16[144,128]{1,0:T(8,128)(2,1)S(1)}, bf16[144,128]{1,0:T(8,128)(2,1)S(1)}, u32[]{:S(2)}, u32[]{:S(2)}) %collective-permute-start.16) | collective-permute-done | bytes 36896 | tf_op jit(solution)/shard_map/ppermute | solution.py:372
  50.3 1.8 %collective-permute-done.17.refs_3_ = bf16[144,128]{1,0:T(8,128)(2,1)S(1)} collective-permute-done((bf16[144,128]{1,0:T(8,128)(2,1)S(1)}, bf16[144,128]{1,0:T(8,128)(2,1)S(1)}, u32[]{:S(2)}, u32[]{:S(2)}) %collective-permute-start.17) | collective-permute-done | bytes 36896 | tf_op jit(solution)/shard_map/ppermute | solution.py:372
  52.2 0.7 %adam.1 = (f32[64,128]{1,0:T(8,128)}, f32[64,128]{1,0:T(8,128)}, f32[64,128]{1,0:T(8,128)}, f32[64,128]{1,0:T(8,128)}, f32[64,128]{1,0:T(8,128)}, /*index=5*/f32...) custom-call(bf16[144,128]{1,0:T(8,128)(2,1)S(1)} %get-tuple-element.48.refs_0_, ...), custom_call_target="tpu_custom_call" | custom-call | tf_op jit(solution)/shard_map/adam/pallas_call | solution.py:533
  (31 shorter events, 0.1 us)
Async XLA Ops:
  1.5 5.7 %collective-permute-start.2 = (bf16[144,128]{1,0:T(8,128)(2,1)S(1)}, bf16[144,128]{1,0:T(8,128)(2,1)S(1)}, u32[]{:S(2)}, u32[]{:S(2)}) collective-permute-start(bf16[144,128]{1,0:T(8,128)(2,1)S(1)} %pack.1.refs_3_), channel_id=1, source_target_pairs={{0,1},{1,0},{2,3},{3,2},{4,5},{5,4},{6,7},{7,6},{8,9},{9,8},{10,11... | collective-permute-start | bytes 110600 | tf_op jit(solution)/shard_map/ppermute | solution.py:372
  4.6 5.5 %collective-permute-start.1 = (bf16[144,128]{1,0:T(8,128)(2,1)S(1)}, bf16[144,128]{1,0:T(8,128)(2,1)S(1)}, u32[]{:S(2)}, u32[]{:S(2)}) collective-permute-start(bf16[144,128]{1,0:T(8,128)(2,1)S(1)} %pack.1.refs_3_), channel_id=1, source_target_pairs={{0,2},{1,3},{2,0},{3,1},{4,6},{5,7},{6,4},{7,5},{8,10},{9,11},{10,... | collective-permute-start | bytes 110600 | tf_op jit(solution)/shard_map/ppermute | solution.py:372
  7.2 5.8 %collective-permute-start = (bf16[144,128]{1,0:T(8,128)(2,1)S(1)}, bf16[144,128]{1,0:T(8,128)(2,1)S(1)}, u32[]{:S(2)}, u32[]{:S(2)}) collective-permute-start(bf16[144,128]{1,0:T(8,128)(2,1)S(1)} %pack.1.refs_3_), channel_id=1, source_target_pairs={{0,3},{1,2},{2,1},{3,0},{4,7},{5,6},{6,5},{7,4},{8,11},{9,10},{10,... | collective-permute-start | bytes 110600 | tf_op jit(solution)/shard_map/ppermute | solution.py:372
  13.1 5.2 %collective-permute-start.3 = (bf16[576,128]{1,0:T(8,128)(2,1)S(1)}, bf16[576,128]{1,0:T(8,128)(2,1)S(1)}, u32[]{:S(2)}, u32[]{:S(2)}) collective-permute-start(bf16[576,128]{1,0:T(8,128)(2,1)S(1)} %table.1.refs_3_.refs_0_), channel_id=1, source_target_pairs={{0,16},{4,12},{8,24},{12,4},{16,0},{20,28},{24,8},{28,20},{1,17},{... | collective-permute-start | bytes 442376 | tf_op jit(solution)/shard_map/ppermute | solution.py:372
  14.6 5.9 %collective-permute-start.4 = (bf16[576,128]{1,0:T(8,128)(2,1)S(1)}, bf16[576,128]{1,0:T(8,128)(2,1)S(1)}, u32[]{:S(2)}, u32[]{:S(2)}) collective-permute-start(bf16[576,128]{1,0:T(8,128)(2,1)S(1)} %table.1.refs_3_.refs_0_), channel_id=1, source_target_pairs={{0,8},{4,20},{8,0},{12,28},{16,24},{20,4},{24,16},{28,12},{1,9},{5... | collective-permute-start | bytes 442376 | tf_op jit(solution)/shard_map/ppermute | solution.py:372
  18.3 5.2 %collective-permute-start.5 = (bf16[576,128]{1,0:T(8,128)(2,1)S(1)}, bf16[576,128]{1,0:T(8,128)(2,1)S(1)}, u32[]{:S(2)}, u32[]{:S(2)}) collective-permute-start(bf16[576,128]{1,0:T(8,128)(2,1)S(1)} %hold.1.refs_1_), channel_id=1, source_target_pairs={{0,8},{4,20},{8,0},{12,28},{16,24},{20,4},{24,16},{28,12},{1,9},{5... | collective-permute-start | bytes 442376 | tf_op jit(solution)/shard_map/ppermute | solution.py:372
  20.0 3.5 %collective-permute-start.6 = (bf16[576,128]{1,0:T(8,128)(2,1)S(1)}, bf16[576,128]{1,0:T(8,128)(2,1)S(1)}, u32[]{:S(2)}, u32[]{:S(2)}) collective-permute-start(bf16[576,128]{1,0:T(8,128)(2,1)S(1)} %table.1.refs_3_.refs_0_), channel_id=1, source_target_pairs={{0,4},{4,0},{8,12},{12,8},{16,20},{20,16},{24,28},{28,24},{1,5},{5... | collective-permute-start | bytes 442376 | tf_op jit(solution)/shard_map/ppermute | solution.py:372
  20.0 3.5 %collective-permute-start.7 = (bf16[576,128]{1,0:T(8,128)(2,1)S(1)}, bf16[576,128]{1,0:T(8,128)(2,1)S(1)}, u32[]{:S(2)}, u32[]{:S(2)}) collective-permute-start(bf16[576,128]{1,0:T(8,128)(2,1)S(1)} %hold.1.refs_1_), channel_id=1, source_target_pairs={{0,4},{4,0},{8,12},{12,8},{16,20},{20,16},{24,28},{28,24},{1,5},{5... | collective-permute-start | bytes 442376 | tf_op jit(solution)/shard_map/ppermute | solution.py:372
  20.5 3.0 %collective-permute-start.8 = (bf16[576,128]{1,0:T(8,128)(2,1)S(1)}, bf16[576,128]{1,0:T(8,128)(2,1)S(1)}, u32[]{:S(2)}, u32[]{:S(2)}) collective-permute-start(bf16[576,128]{1,0:T(8,128)(2,1)S(1)} %collective-permute-done.4.refs_2_), channel_id=1, source_target_pairs={{0,4},{4,0},{8,12},{12,8},{16,20},{20,16},{24,28},{28,24},{1,5},{5... | collective-permute-start | bytes 442376 | tf_op jit(solution)/shard_map/ppermute | solution.py:372
  23.5 1.4 %collective-permute-start.9 = (bf16[576,128]{1,0:T(8,128)(2,1)S(1)}, bf16[576,128]{1,0:T(8,128)(2,1)S(1)}, u32[]{:S(2)}, u32[]{:S(2)}) collective-permute-start(bf16[576,128]{1,0:T(8,128)(2,1)S(1)} %collective-permute-done.5.refs_3_), channel_id=1, source_target_pairs={{0,4},{4,0},{8,12},{12,8},{16,20},{20,16},{24,28},{28,24},{1,5},{5... | collective-permute-start | bytes 442376 | tf_op jit(solution)/shard_map/ppermute | solution.py:372
  31.8 20.3 %copy-start = (f32[128,64]{0,1:T(8,128)S(1)}, f32[128,64]{0,1:T(8,128)}, u32[]{:S(2)}) copy-start(f32[128,64]{0,1:T(8,128)} %param.17) | copy-start | bytes 98308
  31.8 20.3 %copy-start.1 = (f32[128,64]{0,1:T(8,128)S(1)}, f32[128,64]{0,1:T(8,128)}, u32[]{:S(2)}) copy-start(f32[128,64]{0,1:T(8,128)} %param.20) | copy-start | bytes 98308
  31.9 20.2 %copy-start.2 = (f32[32,64]{1,0:T(8,128)S(1)}, f32[32,64]{1,0:T(8,128)}, u32[]{:S(2)}) copy-start(f32[32,64]{1,0:T(8,128)} %refs_10_.1) | copy-start | bytes 24580
  31.9 20.2 %copy-start.3 = (f32[128,64]{0,1:T(8,128)S(1)}, f32[128,64]{0,1:T(8,128)}, u32[]{:S(2)}) copy-start(f32[128,64]{0,1:T(8,128)} %param.18) | copy-start | bytes 98308
  31.9 20.2 %copy-start.4 = (f32[128,64]{0,1:T(8,128)S(1)}, f32[128,64]{0,1:T(8,128)}, u32[]{:S(2)}) copy-start(f32[128,64]{0,1:T(8,128)} %param.19) | copy-start | bytes 98308
  31.9 20.2 %copy-start.5 = (f32[128,64]{0,1:T(8,128)S(1)}, f32[128,64]{0,1:T(8,128)}, u32[]{:S(2)}) copy-start(f32[128,64]{0,1:T(8,128)} %param.21) | copy-start | bytes 98308
  31.9 20.2 %copy-start.6 = (f32[128,64]{0,1:T(8,128)S(1)}, f32[128,64]{0,1:T(8,128)}, u32[]{:S(2)}) copy-start(f32[128,64]{0,1:T(8,128)} %param.22) | copy-start | bytes 98308
  31.9 20.2 %copy-start.7 = (f32[32,64]{1,0:T(8,128)S(1)}, f32[32,64]{1,0:T(8,128)}, u32[]{:S(2)}) copy-start(f32[32,64]{1,0:T(8,128)} %refs_11_.1) | copy-start | bytes 24580
  31.9 20.2 %copy-start.8 = (f32[32,64]{1,0:T(8,128)S(1)}, f32[32,64]{1,0:T(8,128)}, u32[]{:S(2)}) copy-start(f32[32,64]{1,0:T(8,128)} %refs_12_.1) | copy-start | bytes 24580
  31.9 1.6 %collective-permute-start.10 = (bf16[448,256]{1,0:T(8,128)(2,1)S(1)}, bf16[448,256]{1,0:T(8,128)(2,1)S(1)}, u32[]{:S(2)}, u32[]{:S(2)}) collective-permute-start(bf16[448,256]{1,0:T(8,128)(2,1)S(1)} %get-tuple-element.43), channel_id=1, source_target_pairs={{0,4},{4,0},{8,12},{12,8},{16,20},{20,16},{24,28},{28,24},{1,5},{5... | collective-permute-start | bytes 688136 | tf_op jit(solution)/shard_map/ppermute | solution.py:372
  33.5 4.9 %collective-permute-start.12 = (bf16[224,256]{1,0:T(8,128)(2,1)S(1)}, bf16[224,256]{1,0:T(8,128)(2,1)S(1)}, u32[]{:S(2)}, u32[]{:S(2)}) collective-permute-start(bf16[224,256]{1,0:T(8,128)(2,1)S(1)} %get-tuple-element.45), channel_id=1, source_target_pairs={{0,16},{4,12},{8,24},{12,4},{16,0},{20,28},{24,8},{28,20},{1,17},{... | collective-permute-start | bytes 344072 | tf_op jit(solution)/shard_map/ppermute | solution.py:372
  35.3 5.6 %collective-permute-start.11 = (bf16[224,256]{1,0:T(8,128)(2,1)S(1)}, bf16[224,256]{1,0:T(8,128)(2,1)S(1)}, u32[]{:S(2)}, u32[]{:S(2)}) collective-permute-start(bf16[224,256]{1,0:T(8,128)(2,1)S(1)} %get-tuple-element.44), channel_id=1, source_target_pairs={{0,16},{4,12},{8,24},{12,4},{16,0},{20,28},{24,8},{28,20},{1,17},{... | collective-permute-start | bytes 344072 | tf_op jit(solution)/shard_map/ppermute | solution.py:372
  38.8 4.4 %collective-permute-start.13 = (bf16[288,128]{1,0:T(8,128)(2,1)S(1)}, bf16[288,128]{1,0:T(8,128)(2,1)S(1)}, u32[]{:S(2)}, u32[]{:S(2)}) collective-permute-start(bf16[288,128]{1,0:T(8,128)(2,1)S(1)} %get-tuple-element.46), channel_id=1, source_target_pairs={{0,8},{4,20},{8,0},{12,28},{16,24},{20,4},{24,16},{28,12},{1,9},{5... | collective-permute-start | bytes 221192 | tf_op jit(solution)/shard_map/ppermute | solution.py:372
  40.5 4.4 %collective-permute-start.14 = (bf16[288,128]{1,0:T(8,128)(2,1)S(1)}, bf16[288,128]{1,0:T(8,128)(2,1)S(1)}, u32[]{:S(2)}, u32[]{:S(2)}) collective-permute-start(bf16[288,128]{1,0:T(8,128)(2,1)S(1)} %get-tuple-element.47), channel_id=1, source_target_pairs={{0,8},{4,20},{8,0},{12,28},{16,24},{20,4},{24,16},{28,12},{1,9},{5... | collective-permute-start | bytes 221192 | tf_op jit(solution)/shard_map/ppermute | solution.py:372
  45.3 4.5 %collective-permute-start.15 = (bf16[144,128]{1,0:T(8,128)(2,1)S(1)}, bf16[144,128]{1,0:T(8,128)(2,1)S(1)}, u32[]{:S(2)}, u32[]{:S(2)}) collective-permute-start(bf16[144,128]{1,0:T(8,128)(2,1)S(1)} %get-tuple-element.49), channel_id=1, source_target_pairs={{0,1},{1,0},{2,3},{3,2},{4,5},{5,4},{6,7},{7,6},{8,9},{9,8},{10,11... | collective-permute-start | bytes 110600 | tf_op jit(solution)/shard_map/ppermute | solution.py:372
  45.4 4.9 %collective-permute-start.16 = (bf16[144,128]{1,0:T(8,128)(2,1)S(1)}, bf16[144,128]{1,0:T(8,128)(2,1)S(1)}, u32[]{:S(2)}, u32[]{:S(2)}) collective-permute-start(bf16[144,128]{1,0:T(8,128)(2,1)S(1)} %get-tuple-element.50), channel_id=1, source_target_pairs={{0,2},{1,3},{2,0},{3,1},{4,6},{5,7},{6,4},{7,5},{8,10},{9,11},{10,... | collective-permute-start | bytes 110600 | tf_op jit(solution)/shard_map/ppermute | solution.py:372
  46.3 5.8 %collective-permute-start.17 = (bf16[144,128]{1,0:T(8,128)(2,1)S(1)}, bf16[144,128]{1,0:T(8,128)(2,1)S(1)}, u32[]{:S(2)}, u32[]{:S(2)}) collective-permute-start(bf16[144,128]{1,0:T(8,128)(2,1)S(1)} %get-tuple-element.51), channel_id=1, source_target_pairs={{0,3},{1,2},{2,1},{3,0},{4,7},{5,6},{6,5},{7,4},{8,11},{9,10},{10,... | collective-permute-start | bytes 110600 | tf_op jit(solution)/shard_map/ppermute | solution.py:372

commit v8 on v6

--- a/solution.py
+++ b/solution.py
@@ -38,8 +38,9 @@
         )
         self.slots = tuple(-(-(limit + t // 2) // 16) * 16 for t, limit in enumerate(limits))
         self.note_row = limits[2]
-        self.slot_starts = (0, self.slots[0], self.slots[0] + self.slots[1])
-        self.slot_rows = sum(self.slots)
+        self.slot_starts = (0, 0, self.slots[1])
+        self.message_rows = (self.slots[1] + self.slots[2], self.slots[0])
+        self.note_lanes = (0, LANES)
         self.day_parts = LANES // columns
         self.day_packed = -(-(row_counts[2] // self.day_parts) // 16) * 16
         self.piece_rows = 2 * columns + self.day_packed
@@ -121,9 +122,13 @@
         following = (row + 1).astype(bf16)
         for s in range(owners):
             notes[s].append(dot_nt(following, place[s * slots : (s + 1) * slots]) - 1.0)
-    blank = jnp.full((1, sizes.rank - sizes.slot_rows), -1.0, f32)
+    blanks = [jnp.full((1, LANES - rows), -1.0, f32) for rows in sizes.message_rows]
     note_ref[...] = jnp.concatenate(
-        [jnp.concatenate(note + [blank], axis=1) for note in notes], axis=0
+        [
+            jnp.concatenate([items, days, blanks[0], users, blanks[1]], axis=1)
+            for users, items, days in notes
+        ],
+        axis=0,
     )
 
 
@@ -145,9 +150,10 @@
 
 def block_kernel(sizes, *refs):
     owners, rank, day_rows = sizes.owners, sizes.rank, sizes.row_counts[2]
-    own_table, own_crossed, tables_ref, tables_crossed = refs[:4]
-    picks, places = refs[4:7], refs[7:10]
-    note_ref, status_hbm, own_ref, other_ref = refs[10:14]
+    tables, refs = refs[:owners], refs[owners:]
+    picks, places = refs[:3], refs[3:6]
+    note_ref, status_hbm = refs[6:8]
+    own_refs, other_refs = refs[8:10], refs[10:12]
     (
         users,
         users_low,
@@ -163,7 +169,7 @@
         residual_odd,
         status,
         semaphores,
-    ) = refs[14:]
+    ) = refs[12:]
     pair = 2
     pairs = status.shape[0] // pair
     chunks = [(0, pair)]
@@ -178,15 +184,6 @@
 
     for n, (start, size) in enumerate(chunks):
         status_copy(start, size, n).start()
-
-    height = sizes.table_rows
-    tables = []
-    for n in range(owners // 2):
-        if n == 0:
-            tables += [own_table, own_crossed]
-        else:
-            part = slice((n - 1) * height, n * height)
-            tables += [tables_ref.at[part], tables_crossed.at[part]]
 
     def pick(t):
         table = jnp.concatenate([ref[t * rank : (t + 1) * rank, :] for ref in tables], axis=1)
@@ -268,70 +265,71 @@
             if t == 2:
                 note = iota(rows.shape, 0) == sizes.note_row
                 rows = jnp.where(note, note_ref[s : s + 1, :], rows)
-            out = (own_ref, other_ref)[s % 2]
-            first = (s // 2) * sizes.slot_rows + start
+            part = int(t == 0)
+            out = (own_refs, other_refs)[s % 2][part]
+            first = (s // 2) * sizes.message_rows[part] + start
             out[first : first + slots, :] = rows.astype(bf16)
 
 
-def join_kernel(sizes, *refs):
-    arrived, out_ref = refs[:-2], refs[-1]
-    for n, ref in enumerate(arrived[::-1]):
-        out_ref[n * sizes.table_rows : (n + 1) * sizes.table_rows, :] = ref[...]
-
-
-def merge_kernel(sizes, own_ref, crossed_ref, *outs):
-    rows = sizes.slot_rows
+def hold_kernel(arrived_ref, note_ref, out_ref):
+    out_ref[...] = arrived_ref[...]
+
+
+def merge_kernel(rows, own_ref, crossed_ref, *outs):
     for n, out in enumerate(outs):
         start = (n + 1) * rows
         out[:rows, :] = own_ref[start : start + rows, :]
         out[rows:, :] = crossed_ref[start : start + rows, :]
 
 
-def sum_kernel(sizes, *refs):
+def split_messages(rows, refs):
+    messages = [ref.at[:rows] for ref in refs]
+    return messages + [ref.at[rows:] for ref in refs[2:]]
+
+
+def sum_kernel(sizes, part, *refs):
     holders, columns = sizes.holders, sizes.columns
-    inputs = sizes.owners // 2 + 1
-    arrived, outs = refs[:inputs], refs[inputs:]
+    count = sizes.owners // 2 + 1
+    outs = refs[-holders:]
+    firsts = split_messages(sizes.message_rows[0], refs[:count])
+    messages = split_messages(sizes.message_rows[part], refs[part * count : (part + 1) * count])
+    tables = ((1, 2), (0,))[part]
+    totals = [0.0] * len(tables)
     day_start = sizes.slot_starts[2]
-    totals = [0.0, 0.0, 0.0]
-    messages = [ref.at[: sizes.slot_rows] for ref in arrived]
-    messages += [ref.at[sizes.slot_rows :] for ref in arrived[2:]]
-    for ref in messages:
-        notes = ref[day_start : day_start + sizes.slots[2], :].astype(f32)
-        rows = notes[sizes.note_row : sizes.note_row + 1, : sizes.slot_rows].astype(jnp.int32)
-        for t in range(3):
+    width = sizes.message_rows[part]
+    for first, ref in zip(firsts, messages):
+        notes = first[day_start : day_start + sizes.slots[2], :].astype(f32)
+        lane = sizes.note_lanes[part]
+        rows = notes[sizes.note_row : sizes.note_row + 1, lane : lane + width].astype(jnp.int32)
+        for n, t in enumerate(tables):
             start, slots = sizes.slot_starts[t], sizes.slots[t]
-            shape = (sizes.row_counts[t], sizes.slot_rows)
+            shape = (sizes.row_counts[t], width)
             slot = iota(shape, 1)
             mine = (slot >= start) & (slot < start + slots)
             selector = onehot((iota(shape, 0) == rows) & mine)
-            totals[t] = totals[t] + jnp.dot(selector, ref[...], preferred_element_type=f32)
-    for t in range(3):
-        if t < 2:
-            turned = totals[t].T.astype(bf16)
-            for j in range(holders):
-                outs[j][t * columns : (t + 1) * columns, :] = turned[
-                    j * columns : (j + 1) * columns
-                ]
-        else:
-            for j in range(holders):
-                outs[j][2 * columns :, :] = pack_days(
-                    sizes, totals[t][:, j * columns : (j + 1) * columns]
-                ).astype(bf16)
-
-
-def adam_kernel(sizes, *refs):
+            totals[n] = totals[n] + jnp.dot(selector, ref[...], preferred_element_type=f32)
+    turned = totals[0].T.astype(bf16)
+    for j in range(holders):
+        outs[j][:columns, :] = turned[j * columns : (j + 1) * columns]
+        if part == 0:
+            days = totals[1][:, j * columns : (j + 1) * columns]
+            outs[j][columns:, :] = pack_days(sizes, days).astype(bf16)
+
+
+def adam_kernel(sizes, tables, *refs):
     holders, columns = sizes.holders, sizes.columns
+    count = 3 * len(tables)
     pieces = refs[:holders]
-    states = refs[holders : holders + 9]
-    outs = refs[holders + 9 :]
+    states = refs[holders : holders + count]
+    outs = refs[-count:]
     total = pieces[0][...].astype(f32)
     for ref in pieces[1:]:
         total = total + ref[...].astype(f32)
-    for t in range(3):
-        if t < 2:
-            gradient = total[t * columns : (t + 1) * columns]
+    for t, table in enumerate(tables):
+        if table < 2:
+            gradient = total[:columns]
         else:
-            gradient = unpack_days(sizes, total[2 * columns :])
+            gradient = unpack_days(sizes, total[columns:])
         factor, first, second = states[3 * t : 3 * t + 3]
         new_factor, new_first, new_second = outs[3 * t : 3 * t + 3]
         first_value = beta_one * first[...] + (1.0 - beta_one) * gradient
@@ -374,6 +372,8 @@
     small = pltpu.CompilerParams(vmem_limit_bytes=SMALL_VMEM)
 
     hbm = pl.BlockSpec(memory_space=pltpu.HBM)
+    vmem = pl.BlockSpec(memory_space=pltpu.VMEM)
+    anywhere = pl.BlockSpec(memory_space=pl.ANY)
     in_hbm = lambda a: pltpu.with_memory_space_constraint(a, pltpu.HBM)
     tables_in = (user_factor.T, item_factor.T, day_factor)
     piece = pl.pallas_call(
@@ -400,11 +400,11 @@
         out_shape=tuple(
             [shape((owners * row_counts[t], list_counts[t]), bf16) for t in range(3)]
             + [shape((owners * sizes.slots[t], list_counts[t]), bf16) for t in range(3)]
-            + [shape((owners, sizes.rank), f32)]
+            + [shape((owners, 2 * LANES), f32)]
         ),
         in_specs=[pl.BlockSpec(memory_space=pltpu.SMEM)]
         + [hbm] * 3
-        + [pl.BlockSpec(memory_space=pl.ANY)],
+        + [anywhere],
         scratch_shapes=[pltpu.VMEM((1, count), jnp.int32) for count in list_counts]
         + [pltpu.SemaphoreType.DMA((3,))],
         compiler_params=small,
@@ -415,21 +415,24 @@
         table,
     )
 
-    joined = pl.pallas_call(
-        functools.partial(join_kernel, sizes),
-        out_shape=shape((len(arrived) * sizes.table_rows, LANES), bf16),
+    arrived[0] = pl.pallas_call(
+        hold_kernel,
+        out_shape=shape(table.shape, bf16),
         compiler_params=small,
-        name="join",
-    )(*arrived, picks_places_notes[6])
-    joined_crossed = swap(joined, "dp", owners, 1)
-
-    inputs = [table, own_crossed, joined, joined_crossed, *picks_places_notes]
+        name="hold",
+    )(arrived[0], picks_places_notes[6])
+    tables = [table, own_crossed]
+    for a in arrived[::-1]:
+        tables += [a, swap(a, "dp", owners, 1)]
+    inputs = [*tables, *picks_places_notes]
     users, items, days = list_counts
-    half = shape((owners // 2 * sizes.slot_rows, sizes.rank), bf16)
-    own, other = pl.pallas_call(
+    halves = tuple(
+        shape((owners // 2 * rows, sizes.rank), bf16) for rows in sizes.message_rows
+    )
+    gradients = pl.pallas_call(
         functools.partial(block_kernel, sizes),
-        out_shape=(half, half),
-        in_specs=[pl.BlockSpec(memory_space=pltpu.VMEM)] * len(inputs) + [hbm],
+        out_shape=halves + halves,
+        in_specs=[vmem] * len(inputs) + [hbm],
         scratch_shapes=[
             pltpu.VMEM((users, sizes.rank), f32),
             pltpu.VMEM((users, sizes.rank), bf16),
@@ -449,27 +452,21 @@
         compiler_params=pltpu.CompilerParams(vmem_limit_bytes=BLOCK_VMEM),
         name="block_gradients",
     )(*inputs, in_hbm(status))
-    crossed = swap(other, "dp", owners, 1)
-    message = shape((2 * sizes.slot_rows, sizes.rank), bf16)
-    merged = pl.pallas_call(
-        functools.partial(merge_kernel, sizes),
-        out_shape=tuple([message] * (owners // 2 - 1)),
-        compiler_params=small,
-        name="merge",
-    )(own, crossed)
-    returned = [own, crossed]
-    returned += [swap(merged[bits // 2 - 1], "dp", owners, bits) for bits in range(2, owners, 2)]
-
-    totals = pl.pallas_call(
-        functools.partial(sum_kernel, sizes),
-        out_shape=tuple([shape(piece.shape, bf16)] * holders),
-        compiler_params=small,
-        name="row_sums",
-    )(*returned)
-    column_totals = [totals[0]] + [
-        swap(totals[bits], "mp", holders, bits) for bits in range(1, holders)
-    ]
-
+    returned, updated = [], {}
+    for part, rows in enumerate(sizes.message_rows):
+        own, other = gradients[part], gradients[2 + part]
+        crossed = swap(other, "dp", owners, 1)
+        message = shape((2 * rows, sizes.rank), bf16)
+        merged = pl.pallas_call(
+            functools.partial(merge_kernel, rows),
+            out_shape=tuple([message] * (owners // 2 - 1)),
+            compiler_params=small,
+            name="merge",
+        )(own, crossed)
+        returned += [own, crossed]
+        returned += [
+            swap(merged[bits // 2 - 1], "dp", owners, bits) for bits in range(2, owners, 2)
+        ]
     states = (
         user_factor.T,
         user_first.T,
@@ -481,13 +478,32 @@
         day_first,
         day_second,
     )
-    updated = pl.pallas_call(
-        functools.partial(adam_kernel, sizes),
-        out_shape=tuple(shape(a.shape, a.dtype) for a in states),
-        compiler_params=small,
-        name="adam",
-    )(*column_totals, *states)
-    return tuple(a.T for a in updated[:6]) + tuple(updated[6:])
+    behind_sums, behind_adam = [], []
+    for part, members in enumerate(((1, 2), (0,))):
+        rows = sizes.columns + (sizes.day_packed if part == 0 else 0)
+        totals = pl.pallas_call(
+            functools.partial(sum_kernel, sizes, part),
+            out_shape=tuple([shape((rows, LANES), bf16)] * holders),
+            in_specs=[vmem] * ((part + 1) * (owners // 2 + 1)) + [anywhere] * part,
+            compiler_params=small,
+            name="row_sums",
+        )(*returned[: (part + 1) * (owners // 2 + 1)], *behind_sums)
+        behind_sums = [totals[0]]
+        column_totals = [totals[0]] + [
+            swap(totals[bits], "mp", holders, bits) for bits in range(1, holders)
+        ]
+        held = [a for t in members for a in states[3 * t : 3 * t + 3]]
+        results = pl.pallas_call(
+            functools.partial(adam_kernel, sizes, members),
+            out_shape=tuple(shape(a.shape, a.dtype) for a in held),
+            in_specs=[vmem] * (holders + len(held)) + [anywhere] * part,
+            compiler_params=small,
+            name="adam",
+        )(*column_totals, *held, *behind_adam)
+        behind_adam = [results[0]]
+        for n, t in enumerate(members):
+            updated[t] = results[3 * n : 3 * n + 3]
+    return tuple(a.T for a in (*updated[0], *updated[1])) + tuple(updated[2])
 
 
 def solution(mesh):

time: 49.8 us -> 53.3 us (1.070)
  starting transfers between devices: 17.9 us -> 26.2 us
  waiting for transfers between devices: 19.6 us -> 13.3 us
  local copies, waits for them, and re-layouts: 0.04 us -> 0.79 us
  Pallas kernels: 11.2 us -> 11.9 us
    ppermute x15 -> x24, starting transfers between devices: 17.9 us -> 26.2 us  [swap(): return lax.ppermute(array, axis, [(i, i ^ bits) for i in range(size)])]
    ppermute x15 -> x24, waiting for transfers between devices: 19.6 us -> 13.3 us  [swap(): return lax.ppermute(array, axis, [(i, i ^ bits) for i in range(size)])]
    pallas_call x5 -> x8, Pallas kernels: 8.26 us -> 9.02 us  [the longest x1 6.89 us: local(): pl.pallas_call(functools.partial(block_kernel, sizes), out_shape=halves +...]
    unnamed x18 -> x20, local copies, waits for them, and re-layouts: 0.04 us -> 0.79 us
  transfers between devices with their start and end apart: 15 -> 24, of which waited for: 10 -> 9; matrix products, arithmetic and copies ran while one was open for 0% -> 0% of each run, Pallas kernels for 4% -> 6%
where the time goes in v8:
time: 53.3 us; the launch traced here: 53.1 us
  starting transfers between devices  26.2 us (49%)
  waiting for transfers between devices  13.3 us (25%)
  Pallas kernels  11.9 us (22%)
  between operations  0.89 us (2%)
  local copies, waits for them, and re-layouts  0.79 us (1%)
    ppermute x24, starting transfers between devices, swap(): return lax.ppermute(array, axis, [(i, i ^ bits) for i in range(size)])  26.2 us
    ppermute x24, waiting for transfers between devices, swap(): return lax.ppermute(array, axis, [(i, i ^ bits) for i in range(size)])  13.3 us
    pallas_call x1, Pallas kernels, local(): pl.pallas_call(functools.partial(block_kernel, sizes), out_shape=halves +...  6.89 us
    pallas_call x1, Pallas kernels, local(): pl.pallas_call(functools.partial(slot_kernel, sizes), out_shape=tuple([sh...  1.84 us
    pallas_call x2, Pallas kernels, local(): pl.pallas_call(functools.partial(adam_kernel, sizes, members), out_shape=...  1.37 us
  transfers between devices with their start and end apart: 24, of which 9 were waited for; matrix products, arithmetic and copies ran while one was open for 0% of the time, Pallas kernels for 6%

profile of v8, /device:TPU:0, one launch (start us, length us, event | category | flops | bytes accessed | tf_op | source)
XLA Modules:
  0.0 53.1 jit_solution(15547767408225386050)
XLA Ops:
  0.7 0.9 %pack.1.refs_3_ = bf16[144,128]{1,0:T(8,128)(2,1)S(1)} custom-call(f32[64,128]{1,0:T(8,128)} %bitcast.15, f32[64,128]{1,0:T(8,128)} %bitcast.13, f32[32,64]{1,0:T(8,128)} %refs_7_.1), custom_call_target="tpu_custom_call" | custom-call | tf_op jit(solution)/shard_map/pack/pallas_call | solution.py:379
  1.7 3.1 %collective-permute-start.2 = (bf16[144,128]{1,0:T(8,128)(2,1)S(1)}, bf16[144,128]{1,0:T(8,128)(2,1)S(1)}, u32[]{:S(2)}, u32[]{:S(2)}) collective-permute-start(bf16[144,128]{1,0:T(8,128)(2,1)S(1)} %pack.1.refs_3_), channel_id=1, source_target_pairs={{0,1},{1,0},{2,3},{3,2},{4,5},{5,4},{6,7},{7,6},{8,9},{9,8},{10,11... | collective-permute-start | bytes 110600 | tf_op jit(solution)/shard_map/ppermute | solution.py:348
  4.8 2.6 %collective-permute-start.1 = (bf16[144,128]{1,0:T(8,128)(2,1)S(1)}, bf16[144,128]{1,0:T(8,128)(2,1)S(1)}, u32[]{:S(2)}, u32[]{:S(2)}) collective-permute-start(bf16[144,128]{1,0:T(8,128)(2,1)S(1)} %pack.1.refs_3_), channel_id=1, source_target_pairs={{0,2},{1,3},{2,0},{3,1},{4,6},{5,7},{6,4},{7,5},{8,10},{9,11},{10,... | collective-permute-start | bytes 110600 | tf_op jit(solution)/shard_map/ppermute | solution.py:348
  7.4 2.9 %collective-permute-done.1.refs_1_ = bf16[144,128]{1,0:T(8,128)(2,1)S(1)} collective-permute-done((bf16[144,128]{1,0:T(8,128)(2,1)S(1)}, bf16[144,128]{1,0:T(8,128)(2,1)S(1)}, u32[]{:S(2)}, u32[]{:S(2)}) %collective-permute-start.1) | collective-permute-done | bytes 36896 | tf_op jit(solution)/shard_map/ppermute | solution.py:348
  10.3 2.8 %collective-permute-done.refs_0_ = bf16[144,128]{1,0:T(8,128)(2,1)S(1)} collective-permute-done((bf16[144,128]{1,0:T(8,128)(2,1)S(1)}, bf16[144,128]{1,0:T(8,128)(2,1)S(1)}, u32[]{:S(2)}, u32[]{:S(2)}) %collective-permute-start) | collective-permute-done | bytes 36896 | tf_op jit(solution)/shard_map/ppermute | solution.py:348
  13.3 1.5 %collective-permute-start.6 = (bf16[576,128]{1,0:T(8,128)(2,1)S(1)}, bf16[576,128]{1,0:T(8,128)(2,1)S(1)}, u32[]{:S(2)}, u32[]{:S(2)}) collective-permute-start(bf16[576,128]{1,0:T(8,128)(2,1)S(1)} %table.1.refs_3_.refs_0_), channel_id=1, source_target_pairs={{0,16},{4,20},{8,24},{12,28},{16,0},{20,4},{24,8},{28,12},{1,17},{... | collective-permute-start | bytes 442376 | tf_op jit(solution)/shard_map/ppermute | solution.py:348
  14.8 1.5 %collective-permute-start.4 = (bf16[576,128]{1,0:T(8,128)(2,1)S(1)}, bf16[576,128]{1,0:T(8,128)(2,1)S(1)}, u32[]{:S(2)}, u32[]{:S(2)}) collective-permute-start(bf16[576,128]{1,0:T(8,128)(2,1)S(1)} %table.1.refs_3_.refs_0_), channel_id=1, source_target_pairs={{0,8},{4,12},{8,0},{12,4},{16,24},{20,28},{24,16},{28,20},{1,9},{5... | collective-permute-start | bytes 442376 | tf_op jit(solution)/shard_map/ppermute | solution.py:348
  16.3 0.5 collective-permute-start.8
  16.8 1.8 %slots.1 = (bf16[1024,256]{1,0:T(8,128)(2,1)S(1)}, bf16[1024,256]{1,0:T(8,128)(2,1)S(1)}, bf16[256,32]{1,0:T(8,128)(2,1)S(1)}, bf16[384,256]{1,0:T(8,128)(2,1)S(...) custom-call(s32[1]{0:T(128)} %bitcast.2.me_ref, s32[1,256]{1,0:T(1,128)} %refs_0_.1, ...), custom_call_target="tpu_custom_call" | custom-call | tf_op jit(solution)/shard_map/slots/pallas_call | solution.py:398
  18.6 1.4 %collective-permute-done.6.refs_4_ = bf16[576,128]{1,0:T(8,128)(2,1)S(1)} collective-permute-done((bf16[576,128]{1,0:T(8,128)(2,1)S(1)}, bf16[576,128]{1,0:T(8,128)(2,1)S(1)}, u32[]{:S(2)}, u32[]{:S(2)}) %collective-permute-start.6) | collective-permute-done | bytes 147488 | tf_op jit(solution)/shard_map/ppermute | solution.py:348
  20.1 0.4 collective-permute-start.5
  20.5 1.8 %collective-permute-done.8.arrived_ref = bf16[576,128]{1,0:T(8,128)(2,1)S(1)} collective-permute-done((bf16[576,128]{1,0:T(8,128)(2,1)S(1)}, bf16[576,128]{1,0:T(8,128)(2,1)S(1)}, u32[]{:S(2)}, u32[]{:S(2)}) %collective-permute-start.8) | collective-permute-done | bytes 147488 | tf_op jit(solution)/shard_map/ppermute | solution.py:348
  22.4 1.3 %collective-permute-done.9.refs_7_ = bf16[576,128]{1,0:T(8,128)(2,1)S(1)} collective-permute-done((bf16[576,128]{1,0:T(8,128)(2,1)S(1)}, bf16[576,128]{1,0:T(8,128)(2,1)S(1)}, u32[]{:S(2)}, u32[]{:S(2)}) %collective-permute-start.9) | collective-permute-done | bytes 147488 | tf_op jit(solution)/shard_map/ppermute | solution.py:348
  23.8 6.9 %block_gradients.1 = (bf16[256,256]{1,0:T(8,128)(2,1)S(1)}, bf16[192,256]{1,0:T(8,128)(2,1)S(1)}, bf16[256,256]{1,0:T(8,128)(2,1)S(1)}, bf16[192,256]{1,0:T(8,128)(2,1)S(1)}) custom-call(bf16[576,128]{1,0:T(8,128)(2,1)S(1)} %table.1.refs_3_.refs_0_, bf16[576,128]{1,0:T(8,128)(2,1)S(1)} %collective-permute-done.3.refs_1_, ...), custom_call_target="tpu_custom_call" | custom-call | tf_op jit(solution)/shard_map/block_gradients/pallas_call | solution.py:432
  30.9 0.4 collective-permute-start.14
  31.2 0.8 %collective-permute-done.10.crossed_ref.refs_1_ = bf16[256,256]{1,0:T(8,128)(2,1)S(1)} collective-permute-done((bf16[256,256]{1,0:T(8,128)(2,1)S(1)}, bf16[256,256]{1,0:T(8,128)(2,1)S(1)}, u32[]{:S(2)}, u32[]{:S(2)}) %collective-permute-start.10) | collective-permute-done | bytes 131104 | tf_op jit(solution)/shard_map/ppermute | solution.py:348
  32.1 0.9 %collective-permute-start.11 = (bf16[128,256]{1,0:T(8,128)(2,1)S(1)}, bf16[128,256]{1,0:T(8,128)(2,1)S(1)}, u32[]{:S(2)}, u32[]{:S(2)}) collective-permute-start(bf16[128,256]{1,0:T(8,128)(2,1)S(1)} %get-tuple-element.52), channel_id=1, source_target_pairs={{0,8},{4,12},{8,0},{12,4},{16,24},{20,28},{24,16},{28,20},{1,9},{5... | collective-permute-start | bytes 196616 | tf_op jit(solution)/shard_map/ppermute | solution.py:348
  33.0 1.5 %collective-permute-start.12 = (bf16[128,256]{1,0:T(8,128)(2,1)S(1)}, bf16[128,256]{1,0:T(8,128)(2,1)S(1)}, u32[]{:S(2)}, u32[]{:S(2)}) collective-permute-start(bf16[128,256]{1,0:T(8,128)(2,1)S(1)} %get-tuple-element.53), channel_id=1, source_target_pairs={{0,16},{4,20},{8,24},{12,28},{16,0},{20,4},{24,8},{28,12},{1,17},{... | collective-permute-start | bytes 196616 | tf_op jit(solution)/shard_map/ppermute | solution.py:348
  34.5 1.1 %collective-permute-start.13 = (bf16[128,256]{1,0:T(8,128)(2,1)S(1)}, bf16[128,256]{1,0:T(8,128)(2,1)S(1)}, u32[]{:S(2)}, u32[]{:S(2)}) collective-permute-start(bf16[128,256]{1,0:T(8,128)(2,1)S(1)} %get-tuple-element.54), channel_id=1, source_target_pairs={{0,24},{4,28},{8,16},{12,20},{16,8},{20,12},{24,0},{28,4},{1,25},{... | collective-permute-start | bytes 196616 | tf_op jit(solution)/shard_map/ppermute | solution.py:348
  35.7 0.9 %collective-permute-start.15 = (bf16[96,256]{1,0:T(8,128)(2,1)S(1)}, bf16[96,256]{1,0:T(8,128)(2,1)S(1)}, u32[]{:S(2)}, u32[]{:S(2)}) collective-permute-start(bf16[96,256]{1,0:T(8,128)(2,1)S(1)} %get-tuple-element.57), channel_id=1, source_target_pairs={{0,8},{4,12},{8,0},{12,4},{16,24},{20,28},{24,16},{28,20},{1,9},{5... | collective-permute-start | bytes 147464 | tf_op jit(solution)/shard_map/ppermute | solution.py:348
  36.6 1.5 %collective-permute-start.16 = (bf16[96,256]{1,0:T(8,128)(2,1)S(1)}, bf16[96,256]{1,0:T(8,128)(2,1)S(1)}, u32[]{:S(2)}, u32[]{:S(2)}) collective-permute-start(bf16[96,256]{1,0:T(8,128)(2,1)S(1)} %get-tuple-element.58), channel_id=1, source_target_pairs={{0,16},{4,20},{8,24},{12,28},{16,0},{20,4},{24,8},{28,12},{1,17},{... | collective-permute-start | bytes 147464 | tf_op jit(solution)/shard_map/ppermute | solution.py:348
  38.1 1.1 %collective-permute-start.17 = (bf16[96,256]{1,0:T(8,128)(2,1)S(1)}, bf16[96,256]{1,0:T(8,128)(2,1)S(1)}, u32[]{:S(2)}, u32[]{:S(2)}) collective-permute-start(bf16[96,256]{1,0:T(8,128)(2,1)S(1)} %get-tuple-element.59), channel_id=1, source_target_pairs={{0,24},{4,28},{8,16},{12,20},{16,8},{20,12},{24,0},{28,4},{1,25},{... | collective-permute-start | bytes 147464 | tf_op jit(solution)/shard_map/ppermute | solution.py:348
  39.2 0.4 collective-permute-done.13.refs_4_
  39.7 0.4 row_sums.2
  40.1 1.2 %collective-permute-start.22 = (bf16[80,128]{1,0:T(8,128)(2,1)S(1)}, bf16[80,128]{1,0:T(8,128)(2,1)S(1)}, u32[]{:S(2)}, u32[]{:S(2)}) collective-permute-start(bf16[80,128]{1,0:T(8,128)(2,1)S(1)} %get-tuple-element.66), channel_id=1, source_target_pairs={{0,2},{1,3},{2,0},{3,1},{4,6},{5,7},{6,4},{7,5},{8,10},{9,11},{10,... | collective-permute-start | bytes 61448 | tf_op jit(solution)/shard_map/ppermute | solution.py:348
  41.3 3.2 %collective-permute-start.23 = (bf16[80,128]{1,0:T(8,128)(2,1)S(1)}, bf16[80,128]{1,0:T(8,128)(2,1)S(1)}, u32[]{:S(2)}, u32[]{:S(2)}) collective-permute-start(bf16[80,128]{1,0:T(8,128)(2,1)S(1)} %get-tuple-element.67), channel_id=1, source_target_pairs={{0,3},{1,2},{2,1},{3,0},{4,7},{5,6},{6,5},{7,4},{8,11},{9,10},{10,... | collective-permute-start | bytes 61448 | tf_op jit(solution)/shard_map/ppermute | solution.py:348
  44.9 1.2 %collective-permute-start.19 = (bf16[64,128]{1,0:T(8,128)(2,1)S(1)}, bf16[64,128]{1,0:T(8,128)(2,1)S(1)}, u32[]{:S(2)}, u32[]{:S(2)}) collective-permute-start(bf16[64,128]{1,0:T(8,128)(2,1)S(1)} %get-tuple-element.63), channel_id=1, source_target_pairs={{0,2},{1,3},{2,0},{3,1},{4,6},{5,7},{6,4},{7,5},{8,10},{9,11},{10,... | collective-permute-start | bytes 49160 | tf_op jit(solution)/shard_map/ppermute | solution.py:348
  46.1 3.2 %collective-permute-start.20 = (bf16[64,128]{1,0:T(8,128)(2,1)S(1)}, bf16[64,128]{1,0:T(8,128)(2,1)S(1)}, u32[]{:S(2)}, u32[]{:S(2)}) collective-permute-start(bf16[64,128]{1,0:T(8,128)(2,1)S(1)} %get-tuple-element.64), channel_id=1, source_target_pairs={{0,3},{1,2},{2,1},{3,0},{4,7},{5,6},{6,5},{7,4},{8,11},{9,10},{10,... | collective-permute-start | bytes 49160 | tf_op jit(solution)/shard_map/ppermute | solution.py:348
  49.4 0.7 %adam.2 = (f32[64,128]{1,0:T(8,128)}, f32[64,128]{1,0:T(8,128)}, f32[64,128]{1,0:T(8,128)}, f32[32,64]{1,0:T(8,128)}, f32[32,64]{1,0:T(8,128)}, /*index=5*/f32[32,64]{1,0:T(8,128)}) custom-call(bf16[80,128]{1,0:T(8,128)(2,1)S(1)} %get-tuple-element.60.refs_10_.refs_0_, bf16[80,128]{1,0:T(8,128)(2,1)S(1)} %collective-permute-done.21.refs_1_, ...), custom_call_target="tpu_custom_call" | custom-call | tf_op jit(solution)/shard_map/adam/pallas_call | solution.py:496
  50.1 1.5 %collective-permute-done.20.refs_3_ = bf16[64,128]{1,0:T(8,128)(2,1)S(1)} collective-permute-done((bf16[64,128]{1,0:T(8,128)(2,1)S(1)}, bf16[64,128]{1,0:T(8,128)(2,1)S(1)}, u32[]{:S(2)}, u32[]{:S(2)}) %collective-permute-start.20) | collective-permute-done | bytes 16416 | tf_op jit(solution)/shard_map/ppermute | solution.py:348
  51.7 0.7 %copy-done.7 = f32[64,128]{1,0:T(8,128)S(1)} copy-done((f32[64,128]{1,0:T(8,128)S(1)}, f32[64,128]{1,0:T(8,128)}, u32[]{:S(2)}) %copy-start.7) | copy-done | bytes 32792
  52.4 0.7 %adam.3 = (f32[64,128]{1,0:T(8,128)}, f32[64,128]{1,0:T(8,128)}, f32[64,128]{1,0:T(8,128)}) custom-call(bf16[64,128]{1,0:T(8,128)(2,1)S(1)} %get-tuple-element.61.refs_0_, bf16[64,128]{1,0:T(8,128)(2,1)S(1)} %collective-permute-done.18.refs_1_, bf16[64,128]{1,0:T(8,128)(2,1)S(1)} %collective-permute-done.19.refs_2_, ...), custom_call_target="tpu_custom_call" | custom-call | tf_op jit(solution)/shard_map/adam/pallas_call | solution.py:496
  (47 shorter events, 1.2 us)
Async XLA Ops:
  0.6 48.7 %copy-start.2 = (f32[32,64]{1,0:T(8,128)S(1)}, f32[32,64]{1,0:T(8,128)}, u32[]{:S(2)}) copy-start(f32[32,64]{1,0:T(8,128)} %refs_7_.1) | copy-start | bytes 24580
  0.7 48.7 %copy-start = (f32[128,64]{0,1:T(8,128)S(1)}, f32[128,64]{0,1:T(8,128)}, u32[]{:S(2)}) copy-start(f32[128,64]{0,1:T(8,128)} %param.20) | copy-start | bytes 98308
  0.7 51.0 %copy-start.1 = (f32[128,64]{0,1:T(8,128)S(1)}, f32[128,64]{0,1:T(8,128)}, u32[]{:S(2)}) copy-start(f32[128,64]{0,1:T(8,128)} %param.17) | copy-start | bytes 98308
  0.7 48.7 %copy-start.9 = (f32[32,64]{1,0:T(8,128)S(1)}, f32[32,64]{1,0:T(8,128)}, u32[]{:S(2)}) copy-start(f32[32,64]{1,0:T(8,128)} %refs_9_.1) | copy-start | bytes 24580
  0.7 48.7 %copy-start.8 = (f32[32,64]{1,0:T(8,128)S(1)}, f32[32,64]{1,0:T(8,128)}, u32[]{:S(2)}) copy-start(f32[32,64]{1,0:T(8,128)} %refs_8_.1) | copy-start | bytes 24580
  0.7 48.7 %copy-start.4 = (f32[128,64]{0,1:T(8,128)S(1)}, f32[128,64]{0,1:T(8,128)}, u32[]{:S(2)}) copy-start(f32[128,64]{0,1:T(8,128)} %param.22) | copy-start | bytes 98308
  0.7 50.9 %copy-start.6 = (f32[128,64]{0,1:T(8,128)S(1)}, f32[128,64]{0,1:T(8,128)}, u32[]{:S(2)}) copy-start(f32[128,64]{0,1:T(8,128)} %param.19) | copy-start | bytes 98308
  0.7 50.9 %copy-start.5 = (f32[128,64]{0,1:T(8,128)S(1)}, f32[128,64]{0,1:T(8,128)}, u32[]{:S(2)}) copy-start(f32[128,64]{0,1:T(8,128)} %param.18) | copy-start | bytes 98308
  1.7 5.7 %collective-permute-start.2 = (bf16[144,128]{1,0:T(8,128)(2,1)S(1)}, bf16[144,128]{1,0:T(8,128)(2,1)S(1)}, u32[]{:S(2)}, u32[]{:S(2)}) collective-permute-start(bf16[144,128]{1,0:T(8,128)(2,1)S(1)} %pack.1.refs_3_), channel_id=1, source_target_pairs={{0,1},{1,0},{2,3},{3,2},{4,5},{5,4},{6,7},{7,6},{8,9},{9,8},{10,11... | collective-permute-start | bytes 110600 | tf_op jit(solution)/shard_map/ppermute | solution.py:348
  4.8 5.5 %collective-permute-start.1 = (bf16[144,128]{1,0:T(8,128)(2,1)S(1)}, bf16[144,128]{1,0:T(8,128)(2,1)S(1)}, u32[]{:S(2)}, u32[]{:S(2)}) collective-permute-start(bf16[144,128]{1,0:T(8,128)(2,1)S(1)} %pack.1.refs_3_), channel_id=1, source_target_pairs={{0,2},{1,3},{2,0},{3,1},{4,6},{5,7},{6,4},{7,5},{8,10},{9,11},{10,... | collective-permute-start | bytes 110600 | tf_op jit(solution)/shard_map/ppermute | solution.py:348
  7.4 5.8 %collective-permute-start = (bf16[144,128]{1,0:T(8,128)(2,1)S(1)}, bf16[144,128]{1,0:T(8,128)(2,1)S(1)}, u32[]{:S(2)}, u32[]{:S(2)}) collective-permute-start(bf16[144,128]{1,0:T(8,128)(2,1)S(1)} %pack.1.refs_3_), channel_id=1, source_target_pairs={{0,3},{1,2},{2,1},{3,0},{4,7},{5,6},{6,5},{7,4},{8,11},{9,10},{10,... | collective-permute-start | bytes 110600 | tf_op jit(solution)/shard_map/ppermute | solution.py:348
  13.3 6.7 %collective-permute-start.6 = (bf16[576,128]{1,0:T(8,128)(2,1)S(1)}, bf16[576,128]{1,0:T(8,128)(2,1)S(1)}, u32[]{:S(2)}, u32[]{:S(2)}) collective-permute-start(bf16[576,128]{1,0:T(8,128)(2,1)S(1)} %table.1.refs_3_.refs_0_), channel_id=1, source_target_pairs={{0,16},{4,20},{8,24},{12,28},{16,0},{20,4},{24,8},{28,12},{1,17},{... | collective-permute-start | bytes 442376 | tf_op jit(solution)/shard_map/ppermute | solution.py:348
  14.8 5.3 %collective-permute-start.4 = (bf16[576,128]{1,0:T(8,128)(2,1)S(1)}, bf16[576,128]{1,0:T(8,128)(2,1)S(1)}, u32[]{:S(2)}, u32[]{:S(2)}) collective-permute-start(bf16[576,128]{1,0:T(8,128)(2,1)S(1)} %table.1.refs_3_.refs_0_), channel_id=1, source_target_pairs={{0,8},{4,12},{8,0},{12,4},{16,24},{20,28},{24,16},{28,20},{1,9},{5... | collective-permute-start | bytes 442376 | tf_op jit(solution)/shard_map/ppermute | solution.py:348
  16.3 6.0 %collective-permute-start.8 = (bf16[576,128]{1,0:T(8,128)(2,1)S(1)}, bf16[576,128]{1,0:T(8,128)(2,1)S(1)}, u32[]{:S(2)}, u32[]{:S(2)}) collective-permute-start(bf16[576,128]{1,0:T(8,128)(2,1)S(1)} %table.1.refs_3_.refs_0_), channel_id=1, source_target_pairs={{0,24},{4,28},{8,16},{12,20},{16,8},{20,12},{24,0},{28,4},{1,25},{... | collective-permute-start | bytes 442376 | tf_op jit(solution)/shard_map/ppermute | solution.py:348
  16.7 5.7 %collective-permute-start.3 = (bf16[576,128]{1,0:T(8,128)(2,1)S(1)}, bf16[576,128]{1,0:T(8,128)(2,1)S(1)}, u32[]{:S(2)}, u32[]{:S(2)}) collective-permute-start(bf16[576,128]{1,0:T(8,128)(2,1)S(1)} %table.1.refs_3_.refs_0_), channel_id=1, source_target_pairs={{0,4},{4,0},{8,12},{12,8},{16,20},{20,16},{24,28},{28,24},{1,5},{5... | collective-permute-start | bytes 442376 | tf_op jit(solution)/shard_map/ppermute | solution.py:348
  20.0 2.4 %collective-permute-start.7 = (bf16[576,128]{1,0:T(8,128)(2,1)S(1)}, bf16[576,128]{1,0:T(8,128)(2,1)S(1)}, u32[]{:S(2)}, u32[]{:S(2)}) collective-permute-start(bf16[576,128]{1,0:T(8,128)(2,1)S(1)} %collective-permute-done.6.refs_4_), channel_id=1, source_target_pairs={{0,4},{4,0},{8,12},{12,8},{16,20},{20,16},{24,28},{28,24},{1,5},{5... | collective-permute-start | bytes 442376 | tf_op jit(solution)/shard_map/ppermute | solution.py:348
  20.1 2.3 %collective-permute-start.5 = (bf16[576,128]{1,0:T(8,128)(2,1)S(1)}, bf16[576,128]{1,0:T(8,128)(2,1)S(1)}, u32[]{:S(2)}, u32[]{:S(2)}) collective-permute-start(bf16[576,128]{1,0:T(8,128)(2,1)S(1)} %collective-permute-done.4.refs_2_), channel_id=1, source_target_pairs={{0,4},{4,0},{8,12},{12,8},{16,20},{20,16},{24,28},{28,24},{1,5},{5... | collective-permute-start | bytes 442376 | tf_op jit(solution)/shard_map/ppermute | solution.py:348
  22.3 1.4 %collective-permute-start.9 = (bf16[576,128]{1,0:T(8,128)(2,1)S(1)}, bf16[576,128]{1,0:T(8,128)(2,1)S(1)}, u32[]{:S(2)}, u32[]{:S(2)}) collective-permute-start(bf16[576,128]{1,0:T(8,128)(2,1)S(1)} %hold.1.refs_6_), channel_id=1, source_target_pairs={{0,4},{4,0},{8,12},{12,8},{16,20},{20,16},{24,28},{28,24},{1,5},{5... | collective-permute-start | bytes 442376 | tf_op jit(solution)/shard_map/ppermute | solution.py:348
  30.7 1.4 %collective-permute-start.10 = (bf16[256,256]{1,0:T(8,128)(2,1)S(1)}, bf16[256,256]{1,0:T(8,128)(2,1)S(1)}, u32[]{:S(2)}, u32[]{:S(2)}) collective-permute-start(bf16[256,256]{1,0:T(8,128)(2,1)S(1)} %get-tuple-element.51), channel_id=1, source_target_pairs={{0,4},{4,0},{8,12},{12,8},{16,20},{20,16},{24,28},{28,24},{1,5},{5... | collective-permute-start | bytes 393224 | tf_op jit(solution)/shard_map/ppermute | solution.py:348
  30.9 4.8 %collective-permute-start.14 = (bf16[192,256]{1,0:T(8,128)(2,1)S(1)}, bf16[192,256]{1,0:T(8,128)(2,1)S(1)}, u32[]{:S(2)}, u32[]{:S(2)}) collective-permute-start(bf16[192,256]{1,0:T(8,128)(2,1)S(1)} %get-tuple-element.56), channel_id=1, source_target_pairs={{0,4},{4,0},{8,12},{12,8},{16,20},{20,16},{24,28},{28,24},{1,5},{5... | collective-permute-start | bytes 294920 | tf_op jit(solution)/shard_map/ppermute | solution.py:348
  32.1 6.0 %collective-permute-start.11 = (bf16[128,256]{1,0:T(8,128)(2,1)S(1)}, bf16[128,256]{1,0:T(8,128)(2,1)S(1)}, u32[]{:S(2)}, u32[]{:S(2)}) collective-permute-start(bf16[128,256]{1,0:T(8,128)(2,1)S(1)} %get-tuple-element.52), channel_id=1, source_target_pairs={{0,8},{4,12},{8,0},{12,4},{16,24},{20,28},{24,16},{28,20},{1,9},{5... | collective-permute-start | bytes 196616 | tf_op jit(solution)/shard_map/ppermute | solution.py:348
  33.0 6.2 %collective-permute-start.12 = (bf16[128,256]{1,0:T(8,128)(2,1)S(1)}, bf16[128,256]{1,0:T(8,128)(2,1)S(1)}, u32[]{:S(2)}, u32[]{:S(2)}) collective-permute-start(bf16[128,256]{1,0:T(8,128)(2,1)S(1)} %get-tuple-element.53), channel_id=1, source_target_pairs={{0,16},{4,20},{8,24},{12,28},{16,0},{20,4},{24,8},{28,12},{1,17},{... | collective-permute-start | bytes 196616 | tf_op jit(solution)/shard_map/ppermute | solution.py:348
  34.5 5.2 %collective-permute-start.13 = (bf16[128,256]{1,0:T(8,128)(2,1)S(1)}, bf16[128,256]{1,0:T(8,128)(2,1)S(1)}, u32[]{:S(2)}, u32[]{:S(2)}) collective-permute-start(bf16[128,256]{1,0:T(8,128)(2,1)S(1)} %get-tuple-element.54), channel_id=1, source_target_pairs={{0,24},{4,28},{8,16},{12,20},{16,8},{20,12},{24,0},{28,4},{1,25},{... | collective-permute-start | bytes 196616 | tf_op jit(solution)/shard_map/ppermute | solution.py:348
  35.7 5.6 %collective-permute-start.15 = (bf16[96,256]{1,0:T(8,128)(2,1)S(1)}, bf16[96,256]{1,0:T(8,128)(2,1)S(1)}, u32[]{:S(2)}, u32[]{:S(2)}) collective-permute-start(bf16[96,256]{1,0:T(8,128)(2,1)S(1)} %get-tuple-element.57), channel_id=1, source_target_pairs={{0,8},{4,12},{8,0},{12,4},{16,24},{20,28},{24,16},{28,20},{1,9},{5... | collective-permute-start | bytes 147464 | tf_op jit(solution)/shard_map/ppermute | solution.py:348
  36.6 8.0 %collective-permute-start.16 = (bf16[96,256]{1,0:T(8,128)(2,1)S(1)}, bf16[96,256]{1,0:T(8,128)(2,1)S(1)}, u32[]{:S(2)}, u32[]{:S(2)}) collective-permute-start(bf16[96,256]{1,0:T(8,128)(2,1)S(1)} %get-tuple-element.58), channel_id=1, source_target_pairs={{0,16},{4,20},{8,24},{12,28},{16,0},{20,4},{24,8},{28,12},{1,17},{... | collective-permute-start | bytes 147464 | tf_op jit(solution)/shard_map/ppermute | solution.py:348
  38.1 6.4 %collective-permute-start.17 = (bf16[96,256]{1,0:T(8,128)(2,1)S(1)}, bf16[96,256]{1,0:T(8,128)(2,1)S(1)}, u32[]{:S(2)}, u32[]{:S(2)}) collective-permute-start(bf16[96,256]{1,0:T(8,128)(2,1)S(1)} %get-tuple-element.59), channel_id=1, source_target_pairs={{0,24},{4,28},{8,16},{12,20},{16,8},{20,12},{24,0},{28,4},{1,25},{... | collective-permute-start | bytes 147464 | tf_op jit(solution)/shard_map/ppermute | solution.py:348
  40.1 6.1 %collective-permute-start.21 = (bf16[80,128]{1,0:T(8,128)(2,1)S(1)}, bf16[80,128]{1,0:T(8,128)(2,1)S(1)}, u32[]{:S(2)}, u32[]{:S(2)}) collective-permute-start(bf16[80,128]{1,0:T(8,128)(2,1)S(1)} %get-tuple-element.65), channel_id=1, source_target_pairs={{0,1},{1,0},{2,3},{3,2},{4,5},{5,4},{6,7},{7,6},{8,9},{9,8},{10,11... | collective-permute-start | bytes 61448 | tf_op jit(solution)/shard_map/ppermute | solution.py:348
  40.1 9.2 %collective-permute-start.22 = (bf16[80,128]{1,0:T(8,128)(2,1)S(1)}, bf16[80,128]{1,0:T(8,128)(2,1)S(1)}, u32[]{:S(2)}, u32[]{:S(2)}) collective-permute-start(bf16[80,128]{1,0:T(8,128)(2,1)S(1)} %get-tuple-element.66), channel_id=1, source_target_pairs={{0,2},{1,3},{2,0},{3,1},{4,6},{5,7},{6,4},{7,5},{8,10},{9,11},{10,... | collective-permute-start | bytes 61448 | tf_op jit(solution)/shard_map/ppermute | solution.py:348
  41.3 8.0 %collective-permute-start.23 = (bf16[80,128]{1,0:T(8,128)(2,1)S(1)}, bf16[80,128]{1,0:T(8,128)(2,1)S(1)}, u32[]{:S(2)}, u32[]{:S(2)}) collective-permute-start(bf16[80,128]{1,0:T(8,128)(2,1)S(1)} %get-tuple-element.67), channel_id=1, source_target_pairs={{0,3},{1,2},{2,1},{3,0},{4,7},{5,6},{6,5},{7,4},{8,11},{9,10},{10,... | collective-permute-start | bytes 61448 | tf_op jit(solution)/shard_map/ppermute | solution.py:348
  44.9 5.2 %collective-permute-start.18 = (bf16[64,128]{1,0:T(8,128)(2,1)S(1)}, bf16[64,128]{1,0:T(8,128)(2,1)S(1)}, u32[]{:S(2)}, u32[]{:S(2)}) collective-permute-start(bf16[64,128]{1,0:T(8,128)(2,1)S(1)} %get-tuple-element.62), channel_id=1, source_target_pairs={{0,1},{1,0},{2,3},{3,2},{4,5},{5,4},{6,7},{7,6},{8,9},{9,8},{10,11... | collective-permute-start | bytes 49160 | tf_op jit(solution)/shard_map/ppermute | solution.py:348
  44.9 5.2 %collective-permute-start.19 = (bf16[64,128]{1,0:T(8,128)(2,1)S(1)}, bf16[64,128]{1,0:T(8,128)(2,1)S(1)}, u32[]{:S(2)}, u32[]{:S(2)}) collective-permute-start(bf16[64,128]{1,0:T(8,128)(2,1)S(1)} %get-tuple-element.63), channel_id=1, source_target_pairs={{0,2},{1,3},{2,0},{3,1},{4,6},{5,7},{6,4},{7,5},{8,10},{9,11},{10,... | collective-permute-start | bytes 49160 | tf_op jit(solution)/shard_map/ppermute | solution.py:348
  46.1 5.5 %collective-permute-start.20 = (bf16[64,128]{1,0:T(8,128)(2,1)S(1)}, bf16[64,128]{1,0:T(8,128)(2,1)S(1)}, u32[]{:S(2)}, u32[]{:S(2)}) collective-permute-start(bf16[64,128]{1,0:T(8,128)(2,1)S(1)} %get-tuple-element.64), channel_id=1, source_target_pairs={{0,3},{1,2},{2,1},{3,0},{4,7},{5,6},{6,5},{7,4},{8,11},{9,10},{10,... | collective-permute-start | bytes 49160 | tf_op jit(solution)/shard_map/ppermute | solution.py:348
  (2 other events, 49.4 us)

commit v9 on v6

--- a/solution.py
+++ b/solution.py
@@ -16,6 +16,7 @@
 loss_scale = 0.0625
 
 LANES = 128
+HOLD = 2
 SMALL_VMEM = 16 * 1024 * 1024
 BLOCK_VMEM = 48 * 1024 * 1024
 
@@ -96,6 +97,11 @@
     out_ref[:columns, :] = user[...].astype(bf16)
     out_ref[columns : 2 * columns, :] = item[...].astype(bf16)
     out_ref[2 * columns :, :] = pack_days(sizes, day[...]).astype(bf16)
+
+
+def exchange_order(size):
+    order = list(range(1, size))
+    return [1] + order[:0:-1]
 
 
 def slot_kernel(sizes, me_ref, *refs):
@@ -128,7 +134,8 @@
 
 
 def table_kernel(sizes, *refs):
-    pieces, out_ref = refs[-2::-1], refs[-1]
+    order = exchange_order(sizes.holders) + [0]
+    pieces, out_ref = [refs[order.index(j)] for j in range(sizes.holders)], refs[-1]
     columns, rank, day_rows = sizes.columns, sizes.rank, sizes.row_counts[2]
     for j, ref in enumerate(pieces):
         for t in range(2):
@@ -145,9 +152,9 @@
 
 def block_kernel(sizes, *refs):
     owners, rank, day_rows = sizes.owners, sizes.rank, sizes.row_counts[2]
-    own_table, own_crossed, tables_ref, tables_crossed = refs[:4]
-    picks, places = refs[4:7], refs[7:10]
-    note_ref, status_hbm, own_ref, other_ref = refs[10:14]
+    tables, refs = refs[:owners], refs[owners:]
+    picks, places = refs[:3], refs[3:6]
+    note_ref, status_hbm, own_ref, other_ref = refs[6:10]
     (
         users,
         users_low,
@@ -163,7 +170,7 @@
         residual_odd,
         status,
         semaphores,
-    ) = refs[14:]
+    ) = refs[10:]
     pair = 2
     pairs = status.shape[0] // pair
     chunks = [(0, pair)]
@@ -178,15 +185,6 @@
 
     for n, (start, size) in enumerate(chunks):
         status_copy(start, size, n).start()
-
-    height = sizes.table_rows
-    tables = []
-    for n in range(owners // 2):
-        if n == 0:
-            tables += [own_table, own_crossed]
-        else:
-            part = slice((n - 1) * height, n * height)
-            tables += [tables_ref.at[part], tables_crossed.at[part]]
 
     def pick(t):
         table = jnp.concatenate([ref[t * rank : (t + 1) * rank, :] for ref in tables], axis=1)
@@ -273,10 +271,8 @@
             out[first : first + slots, :] = rows.astype(bf16)
 
 
-def join_kernel(sizes, *refs):
-    arrived, out_ref = refs[:-2], refs[-1]
-    for n, ref in enumerate(arrived[::-1]):
-        out_ref[n * sizes.table_rows : (n + 1) * sizes.table_rows, :] = ref[...]
+def hold_kernel(arrived_ref, note_ref, out_ref):
+    out_ref[...] = arrived_ref[...]
 
 
 def merge_kernel(sizes, own_ref, crossed_ref, *outs):
@@ -385,7 +381,8 @@
         compiler_params=small,
         name="pack",
     )(*[in_hbm(a) for a in tables_in])
-    pieces = [swap(piece, "mp", holders, bits) for bits in range(holders - 1, 0, -1)] + [piece]
+    distances = exchange_order(holders)
+    pieces = [swap(piece, "mp", holders, bits) for bits in distances] + [piece]
 
     table = pl.pallas_call(
         functools.partial(table_kernel, sizes),
@@ -393,7 +390,7 @@
         compiler_params=small,
         name="table",
     )(*pieces)
-    arrived = [swap(table, "dp", owners, bits) for bits in range(owners - 2, 0, -2)]
+    arrived = {bits: swap(table, "dp", owners, bits) for bits in range(2, owners, 2)}
     own_crossed = swap(table, "dp", owners, 1)
     picks_places_notes = pl.pallas_call(
         functools.partial(slot_kernel, sizes),
@@ -415,15 +412,16 @@
         table,
     )
 
-    joined = pl.pallas_call(
-        functools.partial(join_kernel, sizes),
-        out_shape=shape((len(arrived) * sizes.table_rows, LANES), bf16),
-        compiler_params=small,
-        name="join",
-    )(*arrived, picks_places_notes[6])
-    joined_crossed = swap(joined, "dp", owners, 1)
-
-    inputs = [table, own_crossed, joined, joined_crossed, *picks_places_notes]
+    arrived[HOLD] = pl.pallas_call(
+        hold_kernel,
+        out_shape=shape(table.shape, bf16),
+        compiler_params=small,
+        name="hold",
+    )(arrived[HOLD], picks_places_notes[6])
+    tables = [table, own_crossed]
+    for bits in range(2, owners, 2):
+        tables += [arrived[bits], swap(arrived[bits], "dp", owners, 1)]
+    inputs = [*tables, *picks_places_notes]
     users, items, days = list_counts
     half = shape((owners // 2 * sizes.slot_rows, sizes.rank), bf16)
     own, other = pl.pallas_call(
@@ -458,7 +456,9 @@
         name="merge",
     )(own, crossed)
     returned = [own, crossed]
-    returned += [swap(merged[bits // 2 - 1], "dp", owners, bits) for bits in range(2, owners, 2)]
+    returned += [
+        swap(merged[bits // 2 - 1], "dp", owners, bits) for bits in range(owners - 2, 0, -2)
+    ]
 
     totals = pl.pallas_call(
         functools.partial(sum_kernel, sizes),
@@ -467,7 +467,7 @@
         name="row_sums",
     )(*returned)
     column_totals = [totals[0]] + [
-        swap(totals[bits], "mp", holders, bits) for bits in range(1, holders)
+        swap(totals[bits], "mp", holders, bits) for bits in range(holders - 1, 0, -1)
     ]
 
     states = (

time: 49.8 us -> 48.1 us (0.966)
  waiting for transfers between devices: 19.6 us -> 17.7 us
    ppermute x15 -> x17, waiting for transfers between devices: 19.6 us -> 17.7 us  [swap(): return lax.ppermute(array, axis, [(i, i ^ bits) for i in range(size)])]
    ppermute x15 -> x17, starting transfers between devices: 17.9 us -> 18.2 us  [swap(): return lax.ppermute(array, axis, [(i, i ^ bits) for i in range(size)])]
  transfers between devices with their start and end apart: 15 -> 17, of which waited for: 10 -> 11; matrix products, arithmetic and copies ran while one was open for 0% -> 0% of each run, Pallas kernels for 4% -> 4%
where the time goes in v9:
time: 48.1 us; the launch traced here: 47.9 us
  starting transfers between devices  18.2 us (38%)
  waiting for transfers between devices  17.7 us (37%)
  Pallas kernels  11.1 us (23%)
  between operations  0.83 us (2%)
    ppermute x17, starting transfers between devices, swap(): return lax.ppermute(array, axis, [(i, i ^ bits) for i in range(size)])  18.2 us
    ppermute x17, waiting for transfers between devices, swap(): return lax.ppermute(array, axis, [(i, i ^ bits) for i in range(size)])  17.7 us
    pallas_call x1, Pallas kernels, local(): pl.pallas_call(functools.partial(block_kernel, sizes), out_shape=(half, h...  6.89 us
    pallas_call x1, Pallas kernels, local(): pl.pallas_call(functools.partial(slot_kernel, sizes), out_shape=tuple([sh...  1.85 us
  transfers between devices with their start and end apart: 17, of which 11 were waited for; matrix products, arithmetic and copies ran while one was open for 0% of the time, Pallas kernels for 4%

profile of v9, /device:TPU:0, one launch (start us, length us, event | category | flops | bytes accessed | tf_op | source)
XLA Modules:
  0.0 47.9 jit_solution(7244280181045793719)
XLA Ops:
  0.7 0.9 %pack.1.refs_3_ = bf16[144,128]{1,0:T(8,128)(2,1)S(1)} custom-call(f32[64,128]{1,0:T(8,128)} %bitcast.13, f32[64,128]{1,0:T(8,128)} %bitcast.15, f32[32,64]{1,0:T(8,128)} %refs_10_.1), custom_call_target="tpu_custom_call" | custom-call | tf_op jit(solution)/shard_map/pack/pallas_call | solution.py:375
  1.7 4.1 %collective-permute-start.2 = (bf16[144,128]{1,0:T(8,128)(2,1)S(1)}, bf16[144,128]{1,0:T(8,128)(2,1)S(1)}, u32[]{:S(2)}, u32[]{:S(2)}) collective-permute-start(bf16[144,128]{1,0:T(8,128)(2,1)S(1)} %pack.1.refs_3_), channel_id=1, source_target_pairs={{0,2},{1,3},{2,0},{3,1},{4,6},{5,7},{6,4},{7,5},{8,10},{9,11},{10,... | collective-permute-start | bytes 110600 | tf_op jit(solution)/shard_map/ppermute | solution.py:346
  5.8 1.3 %collective-permute-start.1 = (bf16[144,128]{1,0:T(8,128)(2,1)S(1)}, bf16[144,128]{1,0:T(8,128)(2,1)S(1)}, u32[]{:S(2)}, u32[]{:S(2)}) collective-permute-start(bf16[144,128]{1,0:T(8,128)(2,1)S(1)} %pack.1.refs_3_), channel_id=1, source_target_pairs={{0,3},{1,2},{2,1},{3,0},{4,7},{5,6},{6,5},{7,4},{8,11},{9,10},{10,... | collective-permute-start | bytes 110600 | tf_op jit(solution)/shard_map/ppermute | solution.py:346
  7.1 0.2 collective-permute-start
  7.4 0.8 %collective-permute-done.2.refs_2_ = bf16[144,128]{1,0:T(8,128)(2,1)S(1)} collective-permute-done((bf16[144,128]{1,0:T(8,128)(2,1)S(1)}, bf16[144,128]{1,0:T(8,128)(2,1)S(1)}, u32[]{:S(2)}, u32[]{:S(2)}) %collective-permute-start.2) | collective-permute-done | bytes 36896 | tf_op jit(solution)/shard_map/ppermute | solution.py:346
  8.1 3.4 %collective-permute-done.1.refs_1_ = bf16[144,128]{1,0:T(8,128)(2,1)S(1)} collective-permute-done((bf16[144,128]{1,0:T(8,128)(2,1)S(1)}, bf16[144,128]{1,0:T(8,128)(2,1)S(1)}, u32[]{:S(2)}, u32[]{:S(2)}) %collective-permute-start.1) | collective-permute-done | bytes 36896 | tf_op jit(solution)/shard_map/ppermute | solution.py:346
  11.5 0.0 collective-permute-done.refs_0_
  11.5 0.1 table.1.refs_3_.refs_0_
  11.7 2.5 %collective-permute-start.8 = (bf16[576,128]{1,0:T(8,128)(2,1)S(1)}, bf16[576,128]{1,0:T(8,128)(2,1)S(1)}, u32[]{:S(2)}, u32[]{:S(2)}) collective-permute-start(bf16[576,128]{1,0:T(8,128)(2,1)S(1)} %table.1.refs_3_.refs_0_), channel_id=1, source_target_pairs={{0,24},{4,28},{8,16},{12,20},{16,8},{20,12},{24,0},{28,4},{1,25},{... | collective-permute-start | bytes 442376 | tf_op jit(solution)/shard_map/ppermute | solution.py:346
  14.1 0.5 %collective-permute-start.6 = (bf16[576,128]{1,0:T(8,128)(2,1)S(1)}, bf16[576,128]{1,0:T(8,128)(2,1)S(1)}, u32[]{:S(2)}, u32[]{:S(2)}) collective-permute-start(bf16[576,128]{1,0:T(8,128)(2,1)S(1)} %table.1.refs_3_.refs_0_), channel_id=1, source_target_pairs={{0,16},{4,20},{8,24},{12,28},{16,0},{20,4},{24,8},{28,12},{1,17},{... | collective-permute-start | bytes 442376 | tf_op jit(solution)/shard_map/ppermute | solution.py:346
  14.6 0.5 %collective-permute-start.4 = (bf16[576,128]{1,0:T(8,128)(2,1)S(1)}, bf16[576,128]{1,0:T(8,128)(2,1)S(1)}, u32[]{:S(2)}, u32[]{:S(2)}) collective-permute-start(bf16[576,128]{1,0:T(8,128)(2,1)S(1)} %table.1.refs_3_.refs_0_), channel_id=1, source_target_pairs={{0,8},{4,12},{8,0},{12,4},{16,24},{20,28},{24,16},{28,20},{1,9},{5... | collective-permute-start | bytes 442376 | tf_op jit(solution)/shard_map/ppermute | solution.py:346
  15.2 0.0 collective-permute-start.3
  15.2 1.8 %slots.1 = (bf16[1024,256]{1,0:T(8,128)(2,1)S(1)}, bf16[1024,256]{1,0:T(8,128)(2,1)S(1)}, bf16[256,32]{1,0:T(8,128)(2,1)S(1)}, bf16[384,256]{1,0:T(8,128)(2,1)S(...) custom-call(s32[1]{0:T(128)} %bitcast.2.me_ref, s32[1,256]{1,0:T(1,128)} %refs_0_.1, ...), custom_call_target="tpu_custom_call" | custom-call | tf_op jit(solution)/shard_map/slots/pallas_call | solution.py:395
  17.0 2.3 %collective-permute-done.8.refs_6_ = bf16[576,128]{1,0:T(8,128)(2,1)S(1)} collective-permute-done((bf16[576,128]{1,0:T(8,128)(2,1)S(1)}, bf16[576,128]{1,0:T(8,128)(2,1)S(1)}, u32[]{:S(2)}, u32[]{:S(2)}) %collective-permute-start.8) | collective-permute-done | bytes 147488 | tf_op jit(solution)/shard_map/ppermute | solution.py:346
  19.3 0.8 %collective-permute-done.6.refs_4_ = bf16[576,128]{1,0:T(8,128)(2,1)S(1)} collective-permute-done((bf16[576,128]{1,0:T(8,128)(2,1)S(1)}, bf16[576,128]{1,0:T(8,128)(2,1)S(1)}, u32[]{:S(2)}, u32[]{:S(2)}) %collective-permute-start.6) | collective-permute-done | bytes 147488 | tf_op jit(solution)/shard_map/ppermute | solution.py:346
  20.1 0.6 %collective-permute-start.5 = (bf16[576,128]{1,0:T(8,128)(2,1)S(1)}, bf16[576,128]{1,0:T(8,128)(2,1)S(1)}, u32[]{:S(2)}, u32[]{:S(2)}) collective-permute-start(bf16[576,128]{1,0:T(8,128)(2,1)S(1)} %hold.1.refs_2_), channel_id=1, source_target_pairs={{0,4},{4,0},{8,12},{12,8},{16,20},{20,16},{24,28},{28,24},{1,5},{5... | collective-permute-start | bytes 442376 | tf_op jit(solution)/shard_map/ppermute | solution.py:346
  20.7 0.8 %collective-permute-done.7.refs_5_ = bf16[576,128]{1,0:T(8,128)(2,1)S(1)} collective-permute-done((bf16[576,128]{1,0:T(8,128)(2,1)S(1)}, bf16[576,128]{1,0:T(8,128)(2,1)S(1)}, u32[]{:S(2)}, u32[]{:S(2)}) %collective-permute-start.7) | collective-permute-done | bytes 147488 | tf_op jit(solution)/shard_map/ppermute | solution.py:346
  21.5 0.2 collective-permute-done.5.refs_3_
  21.7 6.9 %block_gradients.1 = (bf16[448,256]{1,0:T(8,128)(2,1)S(1)}, bf16[448,256]{1,0:T(8,128)(2,1)S(1)}) custom-call(bf16[576,128]{1,0:T(8,128)(2,1)S(1)} %table.1.refs_3_.refs_0_, bf16[576,128]{1,0:T(8,128)(2,1)S(1)} %collective-permute-done.3.refs_1_, bf16[576,128]{1,0:T(8,128)(2,1)S(1)} %hold.1.refs_2_, bf16[576,128]{1,0:T(8,128)(2,1)S(1)} %collective-permute-done.5.refs_3_, ...), custom_call_target="tpu_custom_call" | custom-call | tf_op jit(solution)/shard_map/block_gradients/pallas_call | solution.py:427
  28.6 0.4 collective-permute-start.10
  29.0 1.1 %collective-permute-done.10.crossed_ref.refs_1_ = bf16[448,256]{1,0:T(8,128)(2,1)S(1)} collective-permute-done((bf16[448,256]{1,0:T(8,128)(2,1)S(1)}, bf16[448,256]{1,0:T(8,128)(2,1)S(1)}, u32[]{:S(2)}, u32[]{:S(2)}) %collective-permute-start.10) | collective-permute-done | bytes 229408 | tf_op jit(solution)/shard_map/ppermute | solution.py:346
  30.2 1.6 %collective-permute-start.11 = (bf16[224,256]{1,0:T(8,128)(2,1)S(1)}, bf16[224,256]{1,0:T(8,128)(2,1)S(1)}, u32[]{:S(2)}, u32[]{:S(2)}) collective-permute-start(bf16[224,256]{1,0:T(8,128)(2,1)S(1)} %get-tuple-element.43), channel_id=1, source_target_pairs={{0,24},{4,28},{8,16},{12,20},{16,8},{20,12},{24,0},{28,4},{1,25},{... | collective-permute-start | bytes 344072 | tf_op jit(solution)/shard_map/ppermute | solution.py:346
  31.8 1.2 %collective-permute-start.12 = (bf16[224,256]{1,0:T(8,128)(2,1)S(1)}, bf16[224,256]{1,0:T(8,128)(2,1)S(1)}, u32[]{:S(2)}, u32[]{:S(2)}) collective-permute-start(bf16[224,256]{1,0:T(8,128)(2,1)S(1)} %get-tuple-element.44), channel_id=1, source_target_pairs={{0,16},{4,20},{8,24},{12,28},{16,0},{20,4},{24,8},{28,12},{1,17},{... | collective-permute-start | bytes 344072 | tf_op jit(solution)/shard_map/ppermute | solution.py:346
  33.0 0.7 %collective-permute-start.13 = (bf16[224,256]{1,0:T(8,128)(2,1)S(1)}, bf16[224,256]{1,0:T(8,128)(2,1)S(1)}, u32[]{:S(2)}, u32[]{:S(2)}) collective-permute-start(bf16[224,256]{1,0:T(8,128)(2,1)S(1)} %get-tuple-element.45), channel_id=1, source_target_pairs={{0,8},{4,12},{8,0},{12,4},{16,24},{20,28},{24,16},{28,20},{1,9},{5... | collective-permute-start | bytes 344072 | tf_op jit(solution)/shard_map/ppermute | solution.py:346
  33.7 3.4 %collective-permute-done.11.refs_2_ = bf16[224,256]{1,0:T(8,128)(2,1)S(1)} collective-permute-done((bf16[224,256]{1,0:T(8,128)(2,1)S(1)}, bf16[224,256]{1,0:T(8,128)(2,1)S(1)}, u32[]{:S(2)}, u32[]{:S(2)}) %collective-permute-start.11) | collective-permute-done | bytes 114720 | tf_op jit(solution)/shard_map/ppermute | solution.py:346
  37.1 1.9 %collective-permute-done.12.refs_3_ = bf16[224,256]{1,0:T(8,128)(2,1)S(1)} collective-permute-done((bf16[224,256]{1,0:T(8,128)(2,1)S(1)}, bf16[224,256]{1,0:T(8,128)(2,1)S(1)}, u32[]{:S(2)}, u32[]{:S(2)}) %collective-permute-start.12) | collective-permute-done | bytes 114720 | tf_op jit(solution)/shard_map/ppermute | solution.py:346
  39.0 0.6 %row_sums.1 = (bf16[144,128]{1,0:T(8,128)(2,1)S(1)}, bf16[144,128]{1,0:T(8,128)(2,1)S(1)}, bf16[144,128]{1,0:T(8,128)(2,1)S(1)}, bf16[144,128]{1,0:T(8,128)(2,1)S(1)}) custom-call(bf16[448,256]{1,0:T(8,128)(2,1)S(1)} %get-tuple-element.41.own_ref.refs_0_, bf16[448,256]{1,0:T(8,128)(2,1)S(1)} %collective-permute-done.10.crossed_ref.refs_1_, ...), custom_call_target="tpu_custom_call" | custom-call | tf_op jit(solution)/shard_map/row_sums/pallas_call | solution.py:463
  39.6 2.6 %collective-permute-start.14 = (bf16[144,128]{1,0:T(8,128)(2,1)S(1)}, bf16[144,128]{1,0:T(8,128)(2,1)S(1)}, u32[]{:S(2)}, u32[]{:S(2)}) collective-permute-start(bf16[144,128]{1,0:T(8,128)(2,1)S(1)} %get-tuple-element.47), channel_id=1, source_target_pairs={{0,3},{1,2},{2,1},{3,0},{4,7},{5,6},{6,5},{7,4},{8,11},{9,10},{10,... | collective-permute-start | bytes 110600 | tf_op jit(solution)/shard_map/ppermute | solution.py:346
  42.2 1.8 %collective-permute-start.16 = (bf16[144,128]{1,0:T(8,128)(2,1)S(1)}, bf16[144,128]{1,0:T(8,128)(2,1)S(1)}, u32[]{:S(2)}, u32[]{:S(2)}) collective-permute-start(bf16[144,128]{1,0:T(8,128)(2,1)S(1)} %get-tuple-element.49), channel_id=1, source_target_pairs={{0,1},{1,0},{2,3},{3,2},{4,5},{5,4},{6,7},{7,6},{8,9},{9,8},{10,11... | collective-permute-start | bytes 110600 | tf_op jit(solution)/shard_map/ppermute | solution.py:346
  44.0 1.4 %collective-permute-done.14.refs_1_ = bf16[144,128]{1,0:T(8,128)(2,1)S(1)} collective-permute-done((bf16[144,128]{1,0:T(8,128)(2,1)S(1)}, bf16[144,128]{1,0:T(8,128)(2,1)S(1)}, u32[]{:S(2)}, u32[]{:S(2)}) %collective-permute-start.14) | collective-permute-done | bytes 36896 | tf_op jit(solution)/shard_map/ppermute | solution.py:346
  45.4 1.7 %collective-permute-done.15.refs_2_ = bf16[144,128]{1,0:T(8,128)(2,1)S(1)} collective-permute-done((bf16[144,128]{1,0:T(8,128)(2,1)S(1)}, bf16[144,128]{1,0:T(8,128)(2,1)S(1)}, u32[]{:S(2)}, u32[]{:S(2)}) %collective-permute-start.15) | collective-permute-done | bytes 36896 | tf_op jit(solution)/shard_map/ppermute | solution.py:346
  47.1 0.7 %adam.1 = (f32[64,128]{1,0:T(8,128)}, f32[64,128]{1,0:T(8,128)}, f32[64,128]{1,0:T(8,128)}, f32[64,128]{1,0:T(8,128)}, f32[64,128]{1,0:T(8,128)}, /*index=5*/f32...) custom-call(bf16[144,128]{1,0:T(8,128)(2,1)S(1)} %get-tuple-element.46.refs_0_, ...), custom_call_target="tpu_custom_call" | custom-call | tf_op jit(solution)/shard_map/adam/pallas_call | solution.py:484
  (28 shorter events, 0.1 us)
Async XLA Ops:
  0.6 46.4 %copy-start.2 = (f32[32,64]{1,0:T(8,128)S(1)}, f32[32,64]{1,0:T(8,128)}, u32[]{:S(2)}) copy-start(f32[32,64]{1,0:T(8,128)} %refs_10_.1) | copy-start | bytes 24580
  0.7 46.4 %copy-start.1 = (f32[128,64]{0,1:T(8,128)S(1)}, f32[128,64]{0,1:T(8,128)}, u32[]{:S(2)}) copy-start(f32[128,64]{0,1:T(8,128)} %param.20) | copy-start | bytes 98308
  0.7 46.4 %copy-start = (f32[128,64]{0,1:T(8,128)S(1)}, f32[128,64]{0,1:T(8,128)}, u32[]{:S(2)}) copy-start(f32[128,64]{0,1:T(8,128)} %param.17) | copy-start | bytes 98308
  0.7 46.4 %copy-start.8 = (f32[32,64]{1,0:T(8,128)S(1)}, f32[32,64]{1,0:T(8,128)}, u32[]{:S(2)}) copy-start(f32[32,64]{1,0:T(8,128)} %refs_12_.1) | copy-start | bytes 24580
  0.7 46.4 %copy-start.7 = (f32[32,64]{1,0:T(8,128)S(1)}, f32[32,64]{1,0:T(8,128)}, u32[]{:S(2)}) copy-start(f32[32,64]{1,0:T(8,128)} %refs_11_.1) | copy-start | bytes 24580
  0.7 46.4 %copy-start.6 = (f32[128,64]{0,1:T(8,128)S(1)}, f32[128,64]{0,1:T(8,128)}, u32[]{:S(2)}) copy-start(f32[128,64]{0,1:T(8,128)} %param.22) | copy-start | bytes 98308
  0.7 46.4 %copy-start.5 = (f32[128,64]{0,1:T(8,128)S(1)}, f32[128,64]{0,1:T(8,128)}, u32[]{:S(2)}) copy-start(f32[128,64]{0,1:T(8,128)} %param.21) | copy-start | bytes 98308
  0.7 46.4 %copy-start.4 = (f32[128,64]{0,1:T(8,128)S(1)}, f32[128,64]{0,1:T(8,128)}, u32[]{:S(2)}) copy-start(f32[128,64]{0,1:T(8,128)} %param.19) | copy-start | bytes 98308
  0.7 46.4 %copy-start.3 = (f32[128,64]{0,1:T(8,128)S(1)}, f32[128,64]{0,1:T(8,128)}, u32[]{:S(2)}) copy-start(f32[128,64]{0,1:T(8,128)} %param.18) | copy-start | bytes 98308
  1.7 6.4 %collective-permute-start.2 = (bf16[144,128]{1,0:T(8,128)(2,1)S(1)}, bf16[144,128]{1,0:T(8,128)(2,1)S(1)}, u32[]{:S(2)}, u32[]{:S(2)}) collective-permute-start(bf16[144,128]{1,0:T(8,128)(2,1)S(1)} %pack.1.refs_3_), channel_id=1, source_target_pairs={{0,2},{1,3},{2,0},{3,1},{4,6},{5,7},{6,4},{7,5},{8,10},{9,11},{10,... | collective-permute-start | bytes 110600 | tf_op jit(solution)/shard_map/ppermute | solution.py:346
  5.8 5.8 %collective-permute-start.1 = (bf16[144,128]{1,0:T(8,128)(2,1)S(1)}, bf16[144,128]{1,0:T(8,128)(2,1)S(1)}, u32[]{:S(2)}, u32[]{:S(2)}) collective-permute-start(bf16[144,128]{1,0:T(8,128)(2,1)S(1)} %pack.1.refs_3_), channel_id=1, source_target_pairs={{0,3},{1,2},{2,1},{3,0},{4,7},{5,6},{6,5},{7,4},{8,11},{9,10},{10,... | collective-permute-start | bytes 110600 | tf_op jit(solution)/shard_map/ppermute | solution.py:346
  7.1 4.4 %collective-permute-start = (bf16[144,128]{1,0:T(8,128)(2,1)S(1)}, bf16[144,128]{1,0:T(8,128)(2,1)S(1)}, u32[]{:S(2)}, u32[]{:S(2)}) collective-permute-start(bf16[144,128]{1,0:T(8,128)(2,1)S(1)} %pack.1.refs_3_), channel_id=1, source_target_pairs={{0,1},{1,0},{2,3},{3,2},{4,5},{5,4},{6,7},{7,6},{8,9},{9,8},{10,11... | collective-permute-start | bytes 110600 | tf_op jit(solution)/shard_map/ppermute | solution.py:346
  11.7 7.6 %collective-permute-start.8 = (bf16[576,128]{1,0:T(8,128)(2,1)S(1)}, bf16[576,128]{1,0:T(8,128)(2,1)S(1)}, u32[]{:S(2)}, u32[]{:S(2)}) collective-permute-start(bf16[576,128]{1,0:T(8,128)(2,1)S(1)} %table.1.refs_3_.refs_0_), channel_id=1, source_target_pairs={{0,24},{4,28},{8,16},{12,20},{16,8},{20,12},{24,0},{28,4},{1,25},{... | collective-permute-start | bytes 442376 | tf_op jit(solution)/shard_map/ppermute | solution.py:346
  14.1 6.0 %collective-permute-start.6 = (bf16[576,128]{1,0:T(8,128)(2,1)S(1)}, bf16[576,128]{1,0:T(8,128)(2,1)S(1)}, u32[]{:S(2)}, u32[]{:S(2)}) collective-permute-start(bf16[576,128]{1,0:T(8,128)(2,1)S(1)} %table.1.refs_3_.refs_0_), channel_id=1, source_target_pairs={{0,16},{4,20},{8,24},{12,28},{16,0},{20,4},{24,8},{28,12},{1,17},{... | collective-permute-start | bytes 442376 | tf_op jit(solution)/shard_map/ppermute | solution.py:346
  14.6 5.4 %collective-permute-start.4 = (bf16[576,128]{1,0:T(8,128)(2,1)S(1)}, bf16[576,128]{1,0:T(8,128)(2,1)S(1)}, u32[]{:S(2)}, u32[]{:S(2)}) collective-permute-start(bf16[576,128]{1,0:T(8,128)(2,1)S(1)} %table.1.refs_3_.refs_0_), channel_id=1, source_target_pairs={{0,8},{4,12},{8,0},{12,4},{16,24},{20,28},{24,16},{28,20},{1,9},{5... | collective-permute-start | bytes 442376 | tf_op jit(solution)/shard_map/ppermute | solution.py:346
  15.2 5.5 %collective-permute-start.3 = (bf16[576,128]{1,0:T(8,128)(2,1)S(1)}, bf16[576,128]{1,0:T(8,128)(2,1)S(1)}, u32[]{:S(2)}, u32[]{:S(2)}) collective-permute-start(bf16[576,128]{1,0:T(8,128)(2,1)S(1)} %table.1.refs_3_.refs_0_), channel_id=1, source_target_pairs={{0,4},{4,0},{8,12},{12,8},{16,20},{20,16},{24,28},{28,24},{1,5},{5... | collective-permute-start | bytes 442376 | tf_op jit(solution)/shard_map/ppermute | solution.py:346
  19.3 1.4 %collective-permute-start.9 = (bf16[576,128]{1,0:T(8,128)(2,1)S(1)}, bf16[576,128]{1,0:T(8,128)(2,1)S(1)}, u32[]{:S(2)}, u32[]{:S(2)}) collective-permute-start(bf16[576,128]{1,0:T(8,128)(2,1)S(1)} %collective-permute-done.8.refs_6_), channel_id=1, source_target_pairs={{0,4},{4,0},{8,12},{12,8},{16,20},{20,16},{24,28},{28,24},{1,5},{5... | collective-permute-start | bytes 442376 | tf_op jit(solution)/shard_map/ppermute | solution.py:346
  20.1 1.4 %collective-permute-start.7 = (bf16[576,128]{1,0:T(8,128)(2,1)S(1)}, bf16[576,128]{1,0:T(8,128)(2,1)S(1)}, u32[]{:S(2)}, u32[]{:S(2)}) collective-permute-start(bf16[576,128]{1,0:T(8,128)(2,1)S(1)} %collective-permute-done.6.refs_4_), channel_id=1, source_target_pairs={{0,4},{4,0},{8,12},{12,8},{16,20},{20,16},{24,28},{28,24},{1,5},{5... | collective-permute-start | bytes 442376 | tf_op jit(solution)/shard_map/ppermute | solution.py:346
  20.1 1.6 %collective-permute-start.5 = (bf16[576,128]{1,0:T(8,128)(2,1)S(1)}, bf16[576,128]{1,0:T(8,128)(2,1)S(1)}, u32[]{:S(2)}, u32[]{:S(2)}) collective-permute-start(bf16[576,128]{1,0:T(8,128)(2,1)S(1)} %hold.1.refs_2_), channel_id=1, source_target_pairs={{0,4},{4,0},{8,12},{12,8},{16,20},{20,16},{24,28},{28,24},{1,5},{5... | collective-permute-start | bytes 442376 | tf_op jit(solution)/shard_map/ppermute | solution.py:346
  28.6 1.6 %collective-permute-start.10 = (bf16[448,256]{1,0:T(8,128)(2,1)S(1)}, bf16[448,256]{1,0:T(8,128)(2,1)S(1)}, u32[]{:S(2)}, u32[]{:S(2)}) collective-permute-start(bf16[448,256]{1,0:T(8,128)(2,1)S(1)} %get-tuple-element.42), channel_id=1, source_target_pairs={{0,4},{4,0},{8,12},{12,8},{16,20},{20,16},{24,28},{28,24},{1,5},{5... | collective-permute-start | bytes 688136 | tf_op jit(solution)/shard_map/ppermute | solution.py:346
  30.2 6.9 %collective-permute-start.11 = (bf16[224,256]{1,0:T(8,128)(2,1)S(1)}, bf16[224,256]{1,0:T(8,128)(2,1)S(1)}, u32[]{:S(2)}, u32[]{:S(2)}) collective-permute-start(bf16[224,256]{1,0:T(8,128)(2,1)S(1)} %get-tuple-element.43), channel_id=1, source_target_pairs={{0,24},{4,28},{8,16},{12,20},{16,8},{20,12},{24,0},{28,4},{1,25},{... | collective-permute-start | bytes 344072 | tf_op jit(solution)/shard_map/ppermute | solution.py:346
  31.8 7.2 %collective-permute-start.12 = (bf16[224,256]{1,0:T(8,128)(2,1)S(1)}, bf16[224,256]{1,0:T(8,128)(2,1)S(1)}, u32[]{:S(2)}, u32[]{:S(2)}) collective-permute-start(bf16[224,256]{1,0:T(8,128)(2,1)S(1)} %get-tuple-element.44), channel_id=1, source_target_pairs={{0,16},{4,20},{8,24},{12,28},{16,0},{20,4},{24,8},{28,12},{1,17},{... | collective-permute-start | bytes 344072 | tf_op jit(solution)/shard_map/ppermute | solution.py:346
  33.0 6.0 %collective-permute-start.13 = (bf16[224,256]{1,0:T(8,128)(2,1)S(1)}, bf16[224,256]{1,0:T(8,128)(2,1)S(1)}, u32[]{:S(2)}, u32[]{:S(2)}) collective-permute-start(bf16[224,256]{1,0:T(8,128)(2,1)S(1)} %get-tuple-element.45), channel_id=1, source_target_pairs={{0,8},{4,12},{8,0},{12,4},{16,24},{20,28},{24,16},{28,20},{1,9},{5... | collective-permute-start | bytes 344072 | tf_op jit(solution)/shard_map/ppermute | solution.py:346
  39.6 5.8 %collective-permute-start.14 = (bf16[144,128]{1,0:T(8,128)(2,1)S(1)}, bf16[144,128]{1,0:T(8,128)(2,1)S(1)}, u32[]{:S(2)}, u32[]{:S(2)}) collective-permute-start(bf16[144,128]{1,0:T(8,128)(2,1)S(1)} %get-tuple-element.47), channel_id=1, source_target_pairs={{0,3},{1,2},{2,1},{3,0},{4,7},{5,6},{6,5},{7,4},{8,11},{9,10},{10,... | collective-permute-start | bytes 110600 | tf_op jit(solution)/shard_map/ppermute | solution.py:346
  42.2 4.9 %collective-permute-start.15 = (bf16[144,128]{1,0:T(8,128)(2,1)S(1)}, bf16[144,128]{1,0:T(8,128)(2,1)S(1)}, u32[]{:S(2)}, u32[]{:S(2)}) collective-permute-start(bf16[144,128]{1,0:T(8,128)(2,1)S(1)} %get-tuple-element.48), channel_id=1, source_target_pairs={{0,2},{1,3},{2,0},{3,1},{4,6},{5,7},{6,4},{7,5},{8,10},{9,11},{10,... | collective-permute-start | bytes 110600 | tf_op jit(solution)/shard_map/ppermute | solution.py:346
  42.2 4.9 %collective-permute-start.16 = (bf16[144,128]{1,0:T(8,128)(2,1)S(1)}, bf16[144,128]{1,0:T(8,128)(2,1)S(1)}, u32[]{:S(2)}, u32[]{:S(2)}) collective-permute-start(bf16[144,128]{1,0:T(8,128)(2,1)S(1)} %get-tuple-element.49), channel_id=1, source_target_pairs={{0,1},{1,0},{2,3},{3,2},{4,5},{5,4},{6,7},{7,6},{8,9},{9,8},{10,11... | collective-permute-start | bytes 110600 | tf_op jit(solution)/shard_map/ppermute | solution.py:346

commit v10 on v9

--- a/solution.py
+++ b/solution.py
@@ -41,6 +41,8 @@
         self.note_row = limits[2]
         self.slot_starts = (0, self.slots[0], self.slots[0] + self.slots[1])
         self.slot_rows = sum(self.slots)
+        self.chunks = self.rank // LANES
+        self.message_rows = self.chunks * self.slot_rows
         self.day_parts = LANES // columns
         self.day_packed = -(-(row_counts[2] // self.day_parts) // 16) * 16
         self.piece_rows = 2 * columns + self.day_packed
@@ -267,8 +269,11 @@
                 note = iota(rows.shape, 0) == sizes.note_row
                 rows = jnp.where(note, note_ref[s : s + 1, :], rows)
             out = (own_ref, other_ref)[s % 2]
-            first = (s // 2) * sizes.slot_rows + start
-            out[first : first + slots, :] = rows.astype(bf16)
+            for chunk in range(sizes.chunks):
+                first = (s // 2) * sizes.message_rows + chunk * sizes.slot_rows + start
+                out[first : first + slots, :] = rows[
+                    :, chunk * LANES : (chunk + 1) * LANES
+                ].astype(bf16)
 
 
 def hold_kernel(arrived_ref, note_ref, out_ref):
@@ -276,7 +281,7 @@
 
 
 def merge_kernel(sizes, own_ref, crossed_ref, *outs):
-    rows = sizes.slot_rows
+    rows = sizes.message_rows
     for n, out in enumerate(outs):
         start = (n + 1) * rows
         out[:rows, :] = own_ref[start : start + rows, :]
@@ -289,9 +294,13 @@
     arrived, outs = refs[:inputs], refs[inputs:]
     day_start = sizes.slot_starts[2]
     totals = [0.0, 0.0, 0.0]
-    messages = [ref.at[: sizes.slot_rows] for ref in arrived]
-    messages += [ref.at[sizes.slot_rows :] for ref in arrived[2:]]
+    height = sizes.slot_rows
+    messages = [ref.at[: sizes.message_rows] for ref in arrived]
+    messages += [ref.at[sizes.message_rows :] for ref in arrived[2:]]
     for ref in messages:
+        values = jnp.concatenate(
+            [ref[c * height : (c + 1) * height, :] for c in range(sizes.chunks)], axis=1
+        )
         notes = ref[day_start : day_start + sizes.slots[2], :].astype(f32)
         rows = notes[sizes.note_row : sizes.note_row + 1, : sizes.slot_rows].astype(jnp.int32)
         for t in range(3):
@@ -300,7 +309,7 @@
             slot = iota(shape, 1)
             mine = (slot >= start) & (slot < start + slots)
             selector = onehot((iota(shape, 0) == rows) & mine)
-            totals[t] = totals[t] + jnp.dot(selector, ref[...], preferred_element_type=f32)
+            totals[t] = totals[t] + jnp.dot(selector, values, preferred_element_type=f32)
     for t in range(3):
         if t < 2:
             turned = totals[t].T.astype(bf16)
@@ -423,7 +432,7 @@
         tables += [arrived[bits], swap(arrived[bits], "dp", owners, 1)]
     inputs = [*tables, *picks_places_notes]
     users, items, days = list_counts
-    half = shape((owners // 2 * sizes.slot_rows, sizes.rank), bf16)
+    half = shape((owners // 2 * sizes.message_rows, LANES), bf16)
     own, other = pl.pallas_call(
         functools.partial(block_kernel, sizes),
         out_shape=(half, half),
@@ -448,7 +457,7 @@
         name="block_gradients",
     )(*inputs, in_hbm(status))
     crossed = swap(other, "dp", owners, 1)
-    message = shape((2 * sizes.slot_rows, sizes.rank), bf16)
+    message = shape((2 * sizes.message_rows, LANES), bf16)
     merged = pl.pallas_call(
         functools.partial(merge_kernel, sizes),
         out_shape=tuple([message] * (owners // 2 - 1)),

time: 48.1 us -> 48.1 us (level)
  no operation moved by 1% of the time
where the time goes in v10:
time: 48.1 us; the launch traced here: 47.9 us
  starting transfers between devices  18.2 us (38%)
  waiting for transfers between devices  17.7 us (37%)
  Pallas kernels  11.1 us (23%)
  between operations  0.83 us (2%)
    ppermute x17, starting transfers between devices, swap(): return lax.ppermute(array, axis, [(i, i ^ bits) for i in range(size)])  18.2 us
    ppermute x17, waiting for transfers between devices, swap(): return lax.ppermute(array, axis, [(i, i ^ bits) for i in range(size)])  17.7 us
    pallas_call x1, Pallas kernels, local(): pl.pallas_call(functools.partial(block_kernel, sizes), out_shape=(half, h...  6.89 us
    pallas_call x1, Pallas kernels, local(): pl.pallas_call(functools.partial(slot_kernel, sizes), out_shape=tuple([sh...  1.85 us
  transfers between devices with their start and end apart: 17, of which 11 were waited for; matrix products, arithmetic and copies ran while one was open for 0% of the time, Pallas kernels for 4%

profile of v10, /device:TPU:0, one launch (start us, length us, event | category | flops | bytes accessed | tf_op | source)
XLA Modules:
  0.0 47.9 jit_solution(8873740015952255846)
XLA Ops:
  0.7 0.9 %pack.1.refs_3_ = bf16[144,128]{1,0:T(8,128)(2,1)S(1)} custom-call(f32[64,128]{1,0:T(8,128)} %bitcast.13, f32[64,128]{1,0:T(8,128)} %bitcast.15, f32[32,64]{1,0:T(8,128)} %refs_10_.1), custom_call_target="tpu_custom_call" | custom-call | tf_op jit(solution)/shard_map/pack/pallas_call | solution.py:384
  1.7 4.1 %collective-permute-start.2 = (bf16[144,128]{1,0:T(8,128)(2,1)S(1)}, bf16[144,128]{1,0:T(8,128)(2,1)S(1)}, u32[]{:S(2)}, u32[]{:S(2)}) collective-permute-start(bf16[144,128]{1,0:T(8,128)(2,1)S(1)} %pack.1.refs_3_), channel_id=1, source_target_pairs={{0,2},{1,3},{2,0},{3,1},{4,6},{5,7},{6,4},{7,5},{8,10},{9,11},{10,... | collective-permute-start | bytes 110600 | tf_op jit(solution)/shard_map/ppermute | solution.py:355
  5.8 1.3 %collective-permute-start.1 = (bf16[144,128]{1,0:T(8,128)(2,1)S(1)}, bf16[144,128]{1,0:T(8,128)(2,1)S(1)}, u32[]{:S(2)}, u32[]{:S(2)}) collective-permute-start(bf16[144,128]{1,0:T(8,128)(2,1)S(1)} %pack.1.refs_3_), channel_id=1, source_target_pairs={{0,3},{1,2},{2,1},{3,0},{4,7},{5,6},{6,5},{7,4},{8,11},{9,10},{10,... | collective-permute-start | bytes 110600 | tf_op jit(solution)/shard_map/ppermute | solution.py:355
  7.1 0.2 collective-permute-start
  7.4 0.8 %collective-permute-done.2.refs_2_ = bf16[144,128]{1,0:T(8,128)(2,1)S(1)} collective-permute-done((bf16[144,128]{1,0:T(8,128)(2,1)S(1)}, bf16[144,128]{1,0:T(8,128)(2,1)S(1)}, u32[]{:S(2)}, u32[]{:S(2)}) %collective-permute-start.2) | collective-permute-done | bytes 36896 | tf_op jit(solution)/shard_map/ppermute | solution.py:355
  8.1 3.4 %collective-permute-done.1.refs_1_ = bf16[144,128]{1,0:T(8,128)(2,1)S(1)} collective-permute-done((bf16[144,128]{1,0:T(8,128)(2,1)S(1)}, bf16[144,128]{1,0:T(8,128)(2,1)S(1)}, u32[]{:S(2)}, u32[]{:S(2)}) %collective-permute-start.1) | collective-permute-done | bytes 36896 | tf_op jit(solution)/shard_map/ppermute | solution.py:355
  11.5 0.0 collective-permute-done.refs_0_
  11.5 0.1 table.1.refs_3_.refs_0_
  11.7 2.5 %collective-permute-start.8 = (bf16[576,128]{1,0:T(8,128)(2,1)S(1)}, bf16[576,128]{1,0:T(8,128)(2,1)S(1)}, u32[]{:S(2)}, u32[]{:S(2)}) collective-permute-start(bf16[576,128]{1,0:T(8,128)(2,1)S(1)} %table.1.refs_3_.refs_0_), channel_id=1, source_target_pairs={{0,24},{4,28},{8,16},{12,20},{16,8},{20,12},{24,0},{28,4},{1,25},{... | collective-permute-start | bytes 442376 | tf_op jit(solution)/shard_map/ppermute | solution.py:355
  14.1 0.5 %collective-permute-start.6 = (bf16[576,128]{1,0:T(8,128)(2,1)S(1)}, bf16[576,128]{1,0:T(8,128)(2,1)S(1)}, u32[]{:S(2)}, u32[]{:S(2)}) collective-permute-start(bf16[576,128]{1,0:T(8,128)(2,1)S(1)} %table.1.refs_3_.refs_0_), channel_id=1, source_target_pairs={{0,16},{4,20},{8,24},{12,28},{16,0},{20,4},{24,8},{28,12},{1,17},{... | collective-permute-start | bytes 442376 | tf_op jit(solution)/shard_map/ppermute | solution.py:355
  14.6 0.5 %collective-permute-start.4 = (bf16[576,128]{1,0:T(8,128)(2,1)S(1)}, bf16[576,128]{1,0:T(8,128)(2,1)S(1)}, u32[]{:S(2)}, u32[]{:S(2)}) collective-permute-start(bf16[576,128]{1,0:T(8,128)(2,1)S(1)} %table.1.refs_3_.refs_0_), channel_id=1, source_target_pairs={{0,8},{4,12},{8,0},{12,4},{16,24},{20,28},{24,16},{28,20},{1,9},{5... | collective-permute-start | bytes 442376 | tf_op jit(solution)/shard_map/ppermute | solution.py:355
  15.2 0.0 collective-permute-start.3
  15.2 1.8 %slots.1 = (bf16[1024,256]{1,0:T(8,128)(2,1)S(1)}, bf16[1024,256]{1,0:T(8,128)(2,1)S(1)}, bf16[256,32]{1,0:T(8,128)(2,1)S(1)}, bf16[384,256]{1,0:T(8,128)(2,1)S(...) custom-call(s32[1]{0:T(128)} %bitcast.2.me_ref, s32[1,256]{1,0:T(1,128)} %refs_0_.1, ...), custom_call_target="tpu_custom_call" | custom-call | tf_op jit(solution)/shard_map/slots/pallas_call | solution.py:404
  17.0 2.3 %collective-permute-done.8.refs_6_ = bf16[576,128]{1,0:T(8,128)(2,1)S(1)} collective-permute-done((bf16[576,128]{1,0:T(8,128)(2,1)S(1)}, bf16[576,128]{1,0:T(8,128)(2,1)S(1)}, u32[]{:S(2)}, u32[]{:S(2)}) %collective-permute-start.8) | collective-permute-done | bytes 147488 | tf_op jit(solution)/shard_map/ppermute | solution.py:355
  19.3 0.8 %collective-permute-done.6.refs_4_ = bf16[576,128]{1,0:T(8,128)(2,1)S(1)} collective-permute-done((bf16[576,128]{1,0:T(8,128)(2,1)S(1)}, bf16[576,128]{1,0:T(8,128)(2,1)S(1)}, u32[]{:S(2)}, u32[]{:S(2)}) %collective-permute-start.6) | collective-permute-done | bytes 147488 | tf_op jit(solution)/shard_map/ppermute | solution.py:355
  20.1 0.6 %collective-permute-start.5 = (bf16[576,128]{1,0:T(8,128)(2,1)S(1)}, bf16[576,128]{1,0:T(8,128)(2,1)S(1)}, u32[]{:S(2)}, u32[]{:S(2)}) collective-permute-start(bf16[576,128]{1,0:T(8,128)(2,1)S(1)} %hold.1.refs_2_), channel_id=1, source_target_pairs={{0,4},{4,0},{8,12},{12,8},{16,20},{20,16},{24,28},{28,24},{1,5},{5... | collective-permute-start | bytes 442376 | tf_op jit(solution)/shard_map/ppermute | solution.py:355
  20.7 0.8 %collective-permute-done.7.refs_5_ = bf16[576,128]{1,0:T(8,128)(2,1)S(1)} collective-permute-done((bf16[576,128]{1,0:T(8,128)(2,1)S(1)}, bf16[576,128]{1,0:T(8,128)(2,1)S(1)}, u32[]{:S(2)}, u32[]{:S(2)}) %collective-permute-start.7) | collective-permute-done | bytes 147488 | tf_op jit(solution)/shard_map/ppermute | solution.py:355
  21.5 0.2 collective-permute-done.5.refs_3_
  21.7 6.9 %block_gradients.1 = (bf16[896,128]{1,0:T(8,128)(2,1)S(1)}, bf16[896,128]{1,0:T(8,128)(2,1)S(1)}) custom-call(bf16[576,128]{1,0:T(8,128)(2,1)S(1)} %table.1.refs_3_.refs_0_, bf16[576,128]{1,0:T(8,128)(2,1)S(1)} %collective-permute-done.3.refs_1_, bf16[576,128]{1,0:T(8,128)(2,1)S(1)} %hold.1.refs_2_, bf16[576,128]{1,0:T(8,128)(2,1)S(1)} %collective-permute-done.5.refs_3_, ...), custom_call_target="tpu_custom_call" | custom-call | tf_op jit(solution)/shard_map/block_gradients/pallas_call | solution.py:436
  28.6 0.4 collective-permute-start.10
  29.0 1.1 %collective-permute-done.10.crossed_ref.refs_1_ = bf16[896,128]{1,0:T(8,128)(2,1)S(1)} collective-permute-done((bf16[896,128]{1,0:T(8,128)(2,1)S(1)}, bf16[896,128]{1,0:T(8,128)(2,1)S(1)}, u32[]{:S(2)}, u32[]{:S(2)}) %collective-permute-start.10) | collective-permute-done | bytes 229408 | tf_op jit(solution)/shard_map/ppermute | solution.py:355
  30.2 1.6 %collective-permute-start.11 = (bf16[448,128]{1,0:T(8,128)(2,1)S(1)}, bf16[448,128]{1,0:T(8,128)(2,1)S(1)}, u32[]{:S(2)}, u32[]{:S(2)}) collective-permute-start(bf16[448,128]{1,0:T(8,128)(2,1)S(1)} %get-tuple-element.43), channel_id=1, source_target_pairs={{0,24},{4,28},{8,16},{12,20},{16,8},{20,12},{24,0},{28,4},{1,25},{... | collective-permute-start | bytes 344072 | tf_op jit(solution)/shard_map/ppermute | solution.py:355
  31.8 1.2 %collective-permute-start.12 = (bf16[448,128]{1,0:T(8,128)(2,1)S(1)}, bf16[448,128]{1,0:T(8,128)(2,1)S(1)}, u32[]{:S(2)}, u32[]{:S(2)}) collective-permute-start(bf16[448,128]{1,0:T(8,128)(2,1)S(1)} %get-tuple-element.44), channel_id=1, source_target_pairs={{0,16},{4,20},{8,24},{12,28},{16,0},{20,4},{24,8},{28,12},{1,17},{... | collective-permute-start | bytes 344072 | tf_op jit(solution)/shard_map/ppermute | solution.py:355
  33.0 0.7 %collective-permute-start.13 = (bf16[448,128]{1,0:T(8,128)(2,1)S(1)}, bf16[448,128]{1,0:T(8,128)(2,1)S(1)}, u32[]{:S(2)}, u32[]{:S(2)}) collective-permute-start(bf16[448,128]{1,0:T(8,128)(2,1)S(1)} %get-tuple-element.45), channel_id=1, source_target_pairs={{0,8},{4,12},{8,0},{12,4},{16,24},{20,28},{24,16},{28,20},{1,9},{5... | collective-permute-start | bytes 344072 | tf_op jit(solution)/shard_map/ppermute | solution.py:355
  33.7 3.4 %collective-permute-done.11.refs_2_ = bf16[448,128]{1,0:T(8,128)(2,1)S(1)} collective-permute-done((bf16[448,128]{1,0:T(8,128)(2,1)S(1)}, bf16[448,128]{1,0:T(8,128)(2,1)S(1)}, u32[]{:S(2)}, u32[]{:S(2)}) %collective-permute-start.11) | collective-permute-done | bytes 114720 | tf_op jit(solution)/shard_map/ppermute | solution.py:355
  37.1 1.9 %collective-permute-done.12.refs_3_ = bf16[448,128]{1,0:T(8,128)(2,1)S(1)} collective-permute-done((bf16[448,128]{1,0:T(8,128)(2,1)S(1)}, bf16[448,128]{1,0:T(8,128)(2,1)S(1)}, u32[]{:S(2)}, u32[]{:S(2)}) %collective-permute-start.12) | collective-permute-done | bytes 114720 | tf_op jit(solution)/shard_map/ppermute | solution.py:355
  39.0 0.6 %row_sums.1 = (bf16[144,128]{1,0:T(8,128)(2,1)S(1)}, bf16[144,128]{1,0:T(8,128)(2,1)S(1)}, bf16[144,128]{1,0:T(8,128)(2,1)S(1)}, bf16[144,128]{1,0:T(8,128)(2,1)S(1)}) custom-call(bf16[896,128]{1,0:T(8,128)(2,1)S(1)} %get-tuple-element.41.own_ref.refs_0_, bf16[896,128]{1,0:T(8,128)(2,1)S(1)} %collective-permute-done.10.crossed_ref.refs_1_, ...), custom_call_target="tpu_custom_call" | custom-call | tf_op jit(solution)/shard_map/row_sums/pallas_call | solution.py:472
  39.6 2.6 %collective-permute-start.14 = (bf16[144,128]{1,0:T(8,128)(2,1)S(1)}, bf16[144,128]{1,0:T(8,128)(2,1)S(1)}, u32[]{:S(2)}, u32[]{:S(2)}) collective-permute-start(bf16[144,128]{1,0:T(8,128)(2,1)S(1)} %get-tuple-element.47), channel_id=1, source_target_pairs={{0,3},{1,2},{2,1},{3,0},{4,7},{5,6},{6,5},{7,4},{8,11},{9,10},{10,... | collective-permute-start | bytes 110600 | tf_op jit(solution)/shard_map/ppermute | solution.py:355
  42.2 1.8 %collective-permute-start.16 = (bf16[144,128]{1,0:T(8,128)(2,1)S(1)}, bf16[144,128]{1,0:T(8,128)(2,1)S(1)}, u32[]{:S(2)}, u32[]{:S(2)}) collective-permute-start(bf16[144,128]{1,0:T(8,128)(2,1)S(1)} %get-tuple-element.49), channel_id=1, source_target_pairs={{0,1},{1,0},{2,3},{3,2},{4,5},{5,4},{6,7},{7,6},{8,9},{9,8},{10,11... | collective-permute-start | bytes 110600 | tf_op jit(solution)/shard_map/ppermute | solution.py:355
  44.0 1.4 %collective-permute-done.14.refs_1_ = bf16[144,128]{1,0:T(8,128)(2,1)S(1)} collective-permute-done((bf16[144,128]{1,0:T(8,128)(2,1)S(1)}, bf16[144,128]{1,0:T(8,128)(2,1)S(1)}, u32[]{:S(2)}, u32[]{:S(2)}) %collective-permute-start.14) | collective-permute-done | bytes 36896 | tf_op jit(solution)/shard_map/ppermute | solution.py:355
  45.4 1.7 %collective-permute-done.15.refs_2_ = bf16[144,128]{1,0:T(8,128)(2,1)S(1)} collective-permute-done((bf16[144,128]{1,0:T(8,128)(2,1)S(1)}, bf16[144,128]{1,0:T(8,128)(2,1)S(1)}, u32[]{:S(2)}, u32[]{:S(2)}) %collective-permute-start.15) | collective-permute-done | bytes 36896 | tf_op jit(solution)/shard_map/ppermute | solution.py:355
  47.1 0.7 %adam.1 = (f32[64,128]{1,0:T(8,128)}, f32[64,128]{1,0:T(8,128)}, f32[64,128]{1,0:T(8,128)}, f32[64,128]{1,0:T(8,128)}, f32[64,128]{1,0:T(8,128)}, /*index=5*/f32...) custom-call(bf16[144,128]{1,0:T(8,128)(2,1)S(1)} %get-tuple-element.46.refs_0_, ...), custom_call_target="tpu_custom_call" | custom-call | tf_op jit(solution)/shard_map/adam/pallas_call | solution.py:493
  (28 shorter events, 0.1 us)
Async XLA Ops:
  0.6 46.4 %copy-start.2 = (f32[32,64]{1,0:T(8,128)S(1)}, f32[32,64]{1,0:T(8,128)}, u32[]{:S(2)}) copy-start(f32[32,64]{1,0:T(8,128)} %refs_10_.1) | copy-start | bytes 24580
  0.7 46.4 %copy-start.1 = (f32[128,64]{0,1:T(8,128)S(1)}, f32[128,64]{0,1:T(8,128)}, u32[]{:S(2)}) copy-start(f32[128,64]{0,1:T(8,128)} %param.20) | copy-start | bytes 98308
  0.7 46.4 %copy-start = (f32[128,64]{0,1:T(8,128)S(1)}, f32[128,64]{0,1:T(8,128)}, u32[]{:S(2)}) copy-start(f32[128,64]{0,1:T(8,128)} %param.17) | copy-start | bytes 98308
  0.7 46.4 %copy-start.8 = (f32[32,64]{1,0:T(8,128)S(1)}, f32[32,64]{1,0:T(8,128)}, u32[]{:S(2)}) copy-start(f32[32,64]{1,0:T(8,128)} %refs_12_.1) | copy-start | bytes 24580
  0.7 46.4 %copy-start.7 = (f32[32,64]{1,0:T(8,128)S(1)}, f32[32,64]{1,0:T(8,128)}, u32[]{:S(2)}) copy-start(f32[32,64]{1,0:T(8,128)} %refs_11_.1) | copy-start | bytes 24580
  0.7 46.4 %copy-start.6 = (f32[128,64]{0,1:T(8,128)S(1)}, f32[128,64]{0,1:T(8,128)}, u32[]{:S(2)}) copy-start(f32[128,64]{0,1:T(8,128)} %param.22) | copy-start | bytes 98308
  0.7 46.4 %copy-start.5 = (f32[128,64]{0,1:T(8,128)S(1)}, f32[128,64]{0,1:T(8,128)}, u32[]{:S(2)}) copy-start(f32[128,64]{0,1:T(8,128)} %param.21) | copy-start | bytes 98308
  0.7 46.4 %copy-start.4 = (f32[128,64]{0,1:T(8,128)S(1)}, f32[128,64]{0,1:T(8,128)}, u32[]{:S(2)}) copy-start(f32[128,64]{0,1:T(8,128)} %param.19) | copy-start | bytes 98308
  0.7 46.4 %copy-start.3 = (f32[128,64]{0,1:T(8,128)S(1)}, f32[128,64]{0,1:T(8,128)}, u32[]{:S(2)}) copy-start(f32[128,64]{0,1:T(8,128)} %param.18) | copy-start | bytes 98308
  1.7 6.4 %collective-permute-start.2 = (bf16[144,128]{1,0:T(8,128)(2,1)S(1)}, bf16[144,128]{1,0:T(8,128)(2,1)S(1)}, u32[]{:S(2)}, u32[]{:S(2)}) collective-permute-start(bf16[144,128]{1,0:T(8,128)(2,1)S(1)} %pack.1.refs_3_), channel_id=1, source_target_pairs={{0,2},{1,3},{2,0},{3,1},{4,6},{5,7},{6,4},{7,5},{8,10},{9,11},{10,... | collective-permute-start | bytes 110600 | tf_op jit(solution)/shard_map/ppermute | solution.py:355
  5.8 5.8 %collective-permute-start.1 = (bf16[144,128]{1,0:T(8,128)(2,1)S(1)}, bf16[144,128]{1,0:T(8,128)(2,1)S(1)}, u32[]{:S(2)}, u32[]{:S(2)}) collective-permute-start(bf16[144,128]{1,0:T(8,128)(2,1)S(1)} %pack.1.refs_3_), channel_id=1, source_target_pairs={{0,3},{1,2},{2,1},{3,0},{4,7},{5,6},{6,5},{7,4},{8,11},{9,10},{10,... | collective-permute-start | bytes 110600 | tf_op jit(solution)/shard_map/ppermute | solution.py:355
  7.1 4.4 %collective-permute-start = (bf16[144,128]{1,0:T(8,128)(2,1)S(1)}, bf16[144,128]{1,0:T(8,128)(2,1)S(1)}, u32[]{:S(2)}, u32[]{:S(2)}) collective-permute-start(bf16[144,128]{1,0:T(8,128)(2,1)S(1)} %pack.1.refs_3_), channel_id=1, source_target_pairs={{0,1},{1,0},{2,3},{3,2},{4,5},{5,4},{6,7},{7,6},{8,9},{9,8},{10,11... | collective-permute-start | bytes 110600 | tf_op jit(solution)/shard_map/ppermute | solution.py:355
  11.7 7.6 %collective-permute-start.8 = (bf16[576,128]{1,0:T(8,128)(2,1)S(1)}, bf16[576,128]{1,0:T(8,128)(2,1)S(1)}, u32[]{:S(2)}, u32[]{:S(2)}) collective-permute-start(bf16[576,128]{1,0:T(8,128)(2,1)S(1)} %table.1.refs_3_.refs_0_), channel_id=1, source_target_pairs={{0,24},{4,28},{8,16},{12,20},{16,8},{20,12},{24,0},{28,4},{1,25},{... | collective-permute-start | bytes 442376 | tf_op jit(solution)/shard_map/ppermute | solution.py:355
  14.1 6.0 %collective-permute-start.6 = (bf16[576,128]{1,0:T(8,128)(2,1)S(1)}, bf16[576,128]{1,0:T(8,128)(2,1)S(1)}, u32[]{:S(2)}, u32[]{:S(2)}) collective-permute-start(bf16[576,128]{1,0:T(8,128)(2,1)S(1)} %table.1.refs_3_.refs_0_), channel_id=1, source_target_pairs={{0,16},{4,20},{8,24},{12,28},{16,0},{20,4},{24,8},{28,12},{1,17},{... | collective-permute-start | bytes 442376 | tf_op jit(solution)/shard_map/ppermute | solution.py:355
  14.6 5.4 %collective-permute-start.4 = (bf16[576,128]{1,0:T(8,128)(2,1)S(1)}, bf16[576,128]{1,0:T(8,128)(2,1)S(1)}, u32[]{:S(2)}, u32[]{:S(2)}) collective-permute-start(bf16[576,128]{1,0:T(8,128)(2,1)S(1)} %table.1.refs_3_.refs_0_), channel_id=1, source_target_pairs={{0,8},{4,12},{8,0},{12,4},{16,24},{20,28},{24,16},{28,20},{1,9},{5... | collective-permute-start | bytes 442376 | tf_op jit(solution)/shard_map/ppermute | solution.py:355
  15.2 5.5 %collective-permute-start.3 = (bf16[576,128]{1,0:T(8,128)(2,1)S(1)}, bf16[576,128]{1,0:T(8,128)(2,1)S(1)}, u32[]{:S(2)}, u32[]{:S(2)}) collective-permute-start(bf16[576,128]{1,0:T(8,128)(2,1)S(1)} %table.1.refs_3_.refs_0_), channel_id=1, source_target_pairs={{0,4},{4,0},{8,12},{12,8},{16,20},{20,16},{24,28},{28,24},{1,5},{5... | collective-permute-start | bytes 442376 | tf_op jit(solution)/shard_map/ppermute | solution.py:355
  19.3 1.4 %collective-permute-start.9 = (bf16[576,128]{1,0:T(8,128)(2,1)S(1)}, bf16[576,128]{1,0:T(8,128)(2,1)S(1)}, u32[]{:S(2)}, u32[]{:S(2)}) collective-permute-start(bf16[576,128]{1,0:T(8,128)(2,1)S(1)} %collective-permute-done.8.refs_6_), channel_id=1, source_target_pairs={{0,4},{4,0},{8,12},{12,8},{16,20},{20,16},{24,28},{28,24},{1,5},{5... | collective-permute-start | bytes 442376 | tf_op jit(solution)/shard_map/ppermute | solution.py:355
  20.1 1.4 %collective-permute-start.7 = (bf16[576,128]{1,0:T(8,128)(2,1)S(1)}, bf16[576,128]{1,0:T(8,128)(2,1)S(1)}, u32[]{:S(2)}, u32[]{:S(2)}) collective-permute-start(bf16[576,128]{1,0:T(8,128)(2,1)S(1)} %collective-permute-done.6.refs_4_), channel_id=1, source_target_pairs={{0,4},{4,0},{8,12},{12,8},{16,20},{20,16},{24,28},{28,24},{1,5},{5... | collective-permute-start | bytes 442376 | tf_op jit(solution)/shard_map/ppermute | solution.py:355
  20.1 1.6 %collective-permute-start.5 = (bf16[576,128]{1,0:T(8,128)(2,1)S(1)}, bf16[576,128]{1,0:T(8,128)(2,1)S(1)}, u32[]{:S(2)}, u32[]{:S(2)}) collective-permute-start(bf16[576,128]{1,0:T(8,128)(2,1)S(1)} %hold.1.refs_2_), channel_id=1, source_target_pairs={{0,4},{4,0},{8,12},{12,8},{16,20},{20,16},{24,28},{28,24},{1,5},{5... | collective-permute-start | bytes 442376 | tf_op jit(solution)/shard_map/ppermute | solution.py:355
  28.6 1.6 %collective-permute-start.10 = (bf16[896,128]{1,0:T(8,128)(2,1)S(1)}, bf16[896,128]{1,0:T(8,128)(2,1)S(1)}, u32[]{:S(2)}, u32[]{:S(2)}) collective-permute-start(bf16[896,128]{1,0:T(8,128)(2,1)S(1)} %get-tuple-element.42), channel_id=1, source_target_pairs={{0,4},{4,0},{8,12},{12,8},{16,20},{20,16},{24,28},{28,24},{1,5},{5... | collective-permute-start | bytes 688136 | tf_op jit(solution)/shard_map/ppermute | solution.py:355
  30.2 6.9 %collective-permute-start.11 = (bf16[448,128]{1,0:T(8,128)(2,1)S(1)}, bf16[448,128]{1,0:T(8,128)(2,1)S(1)}, u32[]{:S(2)}, u32[]{:S(2)}) collective-permute-start(bf16[448,128]{1,0:T(8,128)(2,1)S(1)} %get-tuple-element.43), channel_id=1, source_target_pairs={{0,24},{4,28},{8,16},{12,20},{16,8},{20,12},{24,0},{28,4},{1,25},{... | collective-permute-start | bytes 344072 | tf_op jit(solution)/shard_map/ppermute | solution.py:355
  31.8 7.2 %collective-permute-start.12 = (bf16[448,128]{1,0:T(8,128)(2,1)S(1)}, bf16[448,128]{1,0:T(8,128)(2,1)S(1)}, u32[]{:S(2)}, u32[]{:S(2)}) collective-permute-start(bf16[448,128]{1,0:T(8,128)(2,1)S(1)} %get-tuple-element.44), channel_id=1, source_target_pairs={{0,16},{4,20},{8,24},{12,28},{16,0},{20,4},{24,8},{28,12},{1,17},{... | collective-permute-start | bytes 344072 | tf_op jit(solution)/shard_map/ppermute | solution.py:355
  33.0 6.0 %collective-permute-start.13 = (bf16[448,128]{1,0:T(8,128)(2,1)S(1)}, bf16[448,128]{1,0:T(8,128)(2,1)S(1)}, u32[]{:S(2)}, u32[]{:S(2)}) collective-permute-start(bf16[448,128]{1,0:T(8,128)(2,1)S(1)} %get-tuple-element.45), channel_id=1, source_target_pairs={{0,8},{4,12},{8,0},{12,4},{16,24},{20,28},{24,16},{28,20},{1,9},{5... | collective-permute-start | bytes 344072 | tf_op jit(solution)/shard_map/ppermute | solution.py:355
  39.6 5.8 %collective-permute-start.14 = (bf16[144,128]{1,0:T(8,128)(2,1)S(1)}, bf16[144,128]{1,0:T(8,128)(2,1)S(1)}, u32[]{:S(2)}, u32[]{:S(2)}) collective-permute-start(bf16[144,128]{1,0:T(8,128)(2,1)S(1)} %get-tuple-element.47), channel_id=1, source_target_pairs={{0,3},{1,2},{2,1},{3,0},{4,7},{5,6},{6,5},{7,4},{8,11},{9,10},{10,... | collective-permute-start | bytes 110600 | tf_op jit(solution)/shard_map/ppermute | solution.py:355
  42.2 4.9 %collective-permute-start.15 = (bf16[144,128]{1,0:T(8,128)(2,1)S(1)}, bf16[144,128]{1,0:T(8,128)(2,1)S(1)}, u32[]{:S(2)}, u32[]{:S(2)}) collective-permute-start(bf16[144,128]{1,0:T(8,128)(2,1)S(1)} %get-tuple-element.48), channel_id=1, source_target_pairs={{0,2},{1,3},{2,0},{3,1},{4,6},{5,7},{6,4},{7,5},{8,10},{9,11},{10,... | collective-permute-start | bytes 110600 | tf_op jit(solution)/shard_map/ppermute | solution.py:355
  42.2 4.9 %collective-permute-start.16 = (bf16[144,128]{1,0:T(8,128)(2,1)S(1)}, bf16[144,128]{1,0:T(8,128)(2,1)S(1)}, u32[]{:S(2)}, u32[]{:S(2)}) collective-permute-start(bf16[144,128]{1,0:T(8,128)(2,1)S(1)} %get-tuple-element.49), channel_id=1, source_target_pairs={{0,1},{1,0},{2,3},{3,2},{4,5},{5,4},{6,7},{7,6},{8,9},{9,8},{10,11... | collective-permute-start | bytes 110600 | tf_op jit(solution)/shard_map/ppermute | solution.py:355

commit v11 on v9

--- a/solution.py
+++ b/solution.py
@@ -171,7 +171,7 @@
         status,
         semaphores,
     ) = refs[10:]
-    pair = 2
+    pair = 4
     pairs = status.shape[0] // pair
     chunks = [(0, pair)]
     chunks += [((2 * n - 1) * pair, 2 * pair) for n in range(1, pairs // 2)]
@@ -437,12 +437,12 @@
             pltpu.VMEM((users, sizes.rank), f32),
             pltpu.VMEM((items, sizes.rank), f32),
             pltpu.VMEM((days, sizes.rank), f32),
-            pltpu.VMEM((2 * users, sizes.rank), bf16),
-            pltpu.VMEM((2 * users, sizes.rank), bf16),
-            pltpu.VMEM((2 * users, items), bf16),
-            pltpu.VMEM((2 * users, items), bf16),
+            pltpu.VMEM((4 * users, sizes.rank), bf16),
+            pltpu.VMEM((4 * users, sizes.rank), bf16),
+            pltpu.VMEM((4 * users, items), bf16),
+            pltpu.VMEM((4 * users, items), bf16),
             pltpu.VMEM((days, users, items), jnp.int32),
-            pltpu.SemaphoreType.DMA((days // 4 + 1,)),
+            pltpu.SemaphoreType.DMA((days // 8 + 1,)),
         ],
         compiler_params=pltpu.CompilerParams(vmem_limit_bytes=BLOCK_VMEM),
         name="block_gradients",

time: 48.1 us -> 48.1 us (level)
  no operation moved by 1% of the time
where the time goes in v11:
time: 48.1 us; the launch traced here: 47.9 us
  starting transfers between devices  18.2 us (38%)
  waiting for transfers between devices  17.7 us (37%)
  Pallas kernels  11.1 us (23%)
  between operations  0.83 us (2%)
    ppermute x17, starting transfers between devices, swap(): return lax.ppermute(array, axis, [(i, i ^ bits) for i in range(size)])  18.2 us
    ppermute x17, waiting for transfers between devices, swap(): return lax.ppermute(array, axis, [(i, i ^ bits) for i in range(size)])  17.7 us
    pallas_call x1, Pallas kernels, local(): pl.pallas_call(functools.partial(block_kernel, sizes), out_shape=(half, h...  6.9 us
    pallas_call x1, Pallas kernels, local(): pl.pallas_call(functools.partial(slot_kernel, sizes), out_shape=tuple([sh...  1.85 us
  transfers between devices with their start and end apart: 17, of which 11 were waited for; matrix products, arithmetic and copies ran while one was open for 0% of the time, Pallas kernels for 4%

profile of v11, /device:TPU:0, one launch (start us, length us, event | category | flops | bytes accessed | tf_op | source)
XLA Modules:
  0.0 47.9 jit_solution(11337510112702483454)
XLA Ops:
  0.7 0.9 %pack.1.refs_3_ = bf16[144,128]{1,0:T(8,128)(2,1)S(1)} custom-call(f32[64,128]{1,0:T(8,128)} %bitcast.13, f32[64,128]{1,0:T(8,128)} %bitcast.15, f32[32,64]{1,0:T(8,128)} %refs_10_.1), custom_call_target="tpu_custom_call" | custom-call | tf_op jit(solution)/shard_map/pack/pallas_call | solution.py:375
  1.7 4.1 %collective-permute-start.2 = (bf16[144,128]{1,0:T(8,128)(2,1)S(1)}, bf16[144,128]{1,0:T(8,128)(2,1)S(1)}, u32[]{:S(2)}, u32[]{:S(2)}) collective-permute-start(bf16[144,128]{1,0:T(8,128)(2,1)S(1)} %pack.1.refs_3_), channel_id=1, source_target_pairs={{0,2},{1,3},{2,0},{3,1},{4,6},{5,7},{6,4},{7,5},{8,10},{9,11},{10,... | collective-permute-start | bytes 110600 | tf_op jit(solution)/shard_map/ppermute | solution.py:346
  5.8 1.3 %collective-permute-start.1 = (bf16[144,128]{1,0:T(8,128)(2,1)S(1)}, bf16[144,128]{1,0:T(8,128)(2,1)S(1)}, u32[]{:S(2)}, u32[]{:S(2)}) collective-permute-start(bf16[144,128]{1,0:T(8,128)(2,1)S(1)} %pack.1.refs_3_), channel_id=1, source_target_pairs={{0,3},{1,2},{2,1},{3,0},{4,7},{5,6},{6,5},{7,4},{8,11},{9,10},{10,... | collective-permute-start | bytes 110600 | tf_op jit(solution)/shard_map/ppermute | solution.py:346
  7.1 0.2 collective-permute-start
  7.4 0.8 %collective-permute-done.2.refs_2_ = bf16[144,128]{1,0:T(8,128)(2,1)S(1)} collective-permute-done((bf16[144,128]{1,0:T(8,128)(2,1)S(1)}, bf16[144,128]{1,0:T(8,128)(2,1)S(1)}, u32[]{:S(2)}, u32[]{:S(2)}) %collective-permute-start.2) | collective-permute-done | bytes 36896 | tf_op jit(solution)/shard_map/ppermute | solution.py:346
  8.1 3.4 %collective-permute-done.1.refs_1_ = bf16[144,128]{1,0:T(8,128)(2,1)S(1)} collective-permute-done((bf16[144,128]{1,0:T(8,128)(2,1)S(1)}, bf16[144,128]{1,0:T(8,128)(2,1)S(1)}, u32[]{:S(2)}, u32[]{:S(2)}) %collective-permute-start.1) | collective-permute-done | bytes 36896 | tf_op jit(solution)/shard_map/ppermute | solution.py:346
  11.5 0.0 collective-permute-done.refs_0_
  11.5 0.1 table.1.refs_3_.refs_0_
  11.7 2.5 %collective-permute-start.8 = (bf16[576,128]{1,0:T(8,128)(2,1)S(1)}, bf16[576,128]{1,0:T(8,128)(2,1)S(1)}, u32[]{:S(2)}, u32[]{:S(2)}) collective-permute-start(bf16[576,128]{1,0:T(8,128)(2,1)S(1)} %table.1.refs_3_.refs_0_), channel_id=1, source_target_pairs={{0,24},{4,28},{8,16},{12,20},{16,8},{20,12},{24,0},{28,4},{1,25},{... | collective-permute-start | bytes 442376 | tf_op jit(solution)/shard_map/ppermute | solution.py:346
  14.1 0.5 %collective-permute-start.6 = (bf16[576,128]{1,0:T(8,128)(2,1)S(1)}, bf16[576,128]{1,0:T(8,128)(2,1)S(1)}, u32[]{:S(2)}, u32[]{:S(2)}) collective-permute-start(bf16[576,128]{1,0:T(8,128)(2,1)S(1)} %table.1.refs_3_.refs_0_), channel_id=1, source_target_pairs={{0,16},{4,20},{8,24},{12,28},{16,0},{20,4},{24,8},{28,12},{1,17},{... | collective-permute-start | bytes 442376 | tf_op jit(solution)/shard_map/ppermute | solution.py:346
  14.6 0.5 %collective-permute-start.4 = (bf16[576,128]{1,0:T(8,128)(2,1)S(1)}, bf16[576,128]{1,0:T(8,128)(2,1)S(1)}, u32[]{:S(2)}, u32[]{:S(2)}) collective-permute-start(bf16[576,128]{1,0:T(8,128)(2,1)S(1)} %table.1.refs_3_.refs_0_), channel_id=1, source_target_pairs={{0,8},{4,12},{8,0},{12,4},{16,24},{20,28},{24,16},{28,20},{1,9},{5... | collective-permute-start | bytes 442376 | tf_op jit(solution)/shard_map/ppermute | solution.py:346
  15.2 0.0 collective-permute-start.3
  15.2 1.8 %slots.1 = (bf16[1024,256]{1,0:T(8,128)(2,1)S(1)}, bf16[1024,256]{1,0:T(8,128)(2,1)S(1)}, bf16[256,32]{1,0:T(8,128)(2,1)S(1)}, bf16[384,256]{1,0:T(8,128)(2,1)S(...) custom-call(s32[1]{0:T(128)} %bitcast.2.me_ref, s32[1,256]{1,0:T(1,128)} %refs_0_.1, ...), custom_call_target="tpu_custom_call" | custom-call | tf_op jit(solution)/shard_map/slots/pallas_call | solution.py:395
  17.0 2.3 %collective-permute-done.8.refs_6_ = bf16[576,128]{1,0:T(8,128)(2,1)S(1)} collective-permute-done((bf16[576,128]{1,0:T(8,128)(2,1)S(1)}, bf16[576,128]{1,0:T(8,128)(2,1)S(1)}, u32[]{:S(2)}, u32[]{:S(2)}) %collective-permute-start.8) | collective-permute-done | bytes 147488 | tf_op jit(solution)/shard_map/ppermute | solution.py:346
  19.3 0.8 %collective-permute-done.6.refs_4_ = bf16[576,128]{1,0:T(8,128)(2,1)S(1)} collective-permute-done((bf16[576,128]{1,0:T(8,128)(2,1)S(1)}, bf16[576,128]{1,0:T(8,128)(2,1)S(1)}, u32[]{:S(2)}, u32[]{:S(2)}) %collective-permute-start.6) | collective-permute-done | bytes 147488 | tf_op jit(solution)/shard_map/ppermute | solution.py:346
  20.1 0.6 %collective-permute-start.5 = (bf16[576,128]{1,0:T(8,128)(2,1)S(1)}, bf16[576,128]{1,0:T(8,128)(2,1)S(1)}, u32[]{:S(2)}, u32[]{:S(2)}) collective-permute-start(bf16[576,128]{1,0:T(8,128)(2,1)S(1)} %hold.1.refs_2_), channel_id=1, source_target_pairs={{0,4},{4,0},{8,12},{12,8},{16,20},{20,16},{24,28},{28,24},{1,5},{5... | collective-permute-start | bytes 442376 | tf_op jit(solution)/shard_map/ppermute | solution.py:346
  20.7 0.8 %collective-permute-done.7.refs_5_ = bf16[576,128]{1,0:T(8,128)(2,1)S(1)} collective-permute-done((bf16[576,128]{1,0:T(8,128)(2,1)S(1)}, bf16[576,128]{1,0:T(8,128)(2,1)S(1)}, u32[]{:S(2)}, u32[]{:S(2)}) %collective-permute-start.7) | collective-permute-done | bytes 147488 | tf_op jit(solution)/shard_map/ppermute | solution.py:346
  21.5 0.2 collective-permute-done.5.refs_3_
  21.7 6.9 %block_gradients.1 = (bf16[448,256]{1,0:T(8,128)(2,1)S(1)}, bf16[448,256]{1,0:T(8,128)(2,1)S(1)}) custom-call(bf16[576,128]{1,0:T(8,128)(2,1)S(1)} %table.1.refs_3_.refs_0_, bf16[576,128]{1,0:T(8,128)(2,1)S(1)} %collective-permute-done.3.refs_1_, bf16[576,128]{1,0:T(8,128)(2,1)S(1)} %hold.1.refs_2_, bf16[576,128]{1,0:T(8,128)(2,1)S(1)} %collective-permute-done.5.refs_3_, ...), custom_call_target="tpu_custom_call" | custom-call | tf_op jit(solution)/shard_map/block_gradients/pallas_call | solution.py:427
  28.6 0.4 collective-permute-start.10
  29.0 1.1 %collective-permute-done.10.crossed_ref.refs_1_ = bf16[448,256]{1,0:T(8,128)(2,1)S(1)} collective-permute-done((bf16[448,256]{1,0:T(8,128)(2,1)S(1)}, bf16[448,256]{1,0:T(8,128)(2,1)S(1)}, u32[]{:S(2)}, u32[]{:S(2)}) %collective-permute-start.10) | collective-permute-done | bytes 229408 | tf_op jit(solution)/shard_map/ppermute | solution.py:346
  30.2 1.6 %collective-permute-start.11 = (bf16[224,256]{1,0:T(8,128)(2,1)S(1)}, bf16[224,256]{1,0:T(8,128)(2,1)S(1)}, u32[]{:S(2)}, u32[]{:S(2)}) collective-permute-start(bf16[224,256]{1,0:T(8,128)(2,1)S(1)} %get-tuple-element.43), channel_id=1, source_target_pairs={{0,24},{4,28},{8,16},{12,20},{16,8},{20,12},{24,0},{28,4},{1,25},{... | collective-permute-start | bytes 344072 | tf_op jit(solution)/shard_map/ppermute | solution.py:346
  31.8 1.2 %collective-permute-start.12 = (bf16[224,256]{1,0:T(8,128)(2,1)S(1)}, bf16[224,256]{1,0:T(8,128)(2,1)S(1)}, u32[]{:S(2)}, u32[]{:S(2)}) collective-permute-start(bf16[224,256]{1,0:T(8,128)(2,1)S(1)} %get-tuple-element.44), channel_id=1, source_target_pairs={{0,16},{4,20},{8,24},{12,28},{16,0},{20,4},{24,8},{28,12},{1,17},{... | collective-permute-start | bytes 344072 | tf_op jit(solution)/shard_map/ppermute | solution.py:346
  33.0 0.7 %collective-permute-start.13 = (bf16[224,256]{1,0:T(8,128)(2,1)S(1)}, bf16[224,256]{1,0:T(8,128)(2,1)S(1)}, u32[]{:S(2)}, u32[]{:S(2)}) collective-permute-start(bf16[224,256]{1,0:T(8,128)(2,1)S(1)} %get-tuple-element.45), channel_id=1, source_target_pairs={{0,8},{4,12},{8,0},{12,4},{16,24},{20,28},{24,16},{28,20},{1,9},{5... | collective-permute-start | bytes 344072 | tf_op jit(solution)/shard_map/ppermute | solution.py:346
  33.7 3.4 %collective-permute-done.11.refs_2_ = bf16[224,256]{1,0:T(8,128)(2,1)S(1)} collective-permute-done((bf16[224,256]{1,0:T(8,128)(2,1)S(1)}, bf16[224,256]{1,0:T(8,128)(2,1)S(1)}, u32[]{:S(2)}, u32[]{:S(2)}) %collective-permute-start.11) | collective-permute-done | bytes 114720 | tf_op jit(solution)/shard_map/ppermute | solution.py:346
  37.1 1.9 %collective-permute-done.12.refs_3_ = bf16[224,256]{1,0:T(8,128)(2,1)S(1)} collective-permute-done((bf16[224,256]{1,0:T(8,128)(2,1)S(1)}, bf16[224,256]{1,0:T(8,128)(2,1)S(1)}, u32[]{:S(2)}, u32[]{:S(2)}) %collective-permute-start.12) | collective-permute-done | bytes 114720 | tf_op jit(solution)/shard_map/ppermute | solution.py:346
  39.0 0.6 %row_sums.1 = (bf16[144,128]{1,0:T(8,128)(2,1)S(1)}, bf16[144,128]{1,0:T(8,128)(2,1)S(1)}, bf16[144,128]{1,0:T(8,128)(2,1)S(1)}, bf16[144,128]{1,0:T(8,128)(2,1)S(1)}) custom-call(bf16[448,256]{1,0:T(8,128)(2,1)S(1)} %get-tuple-element.41.own_ref.refs_0_, bf16[448,256]{1,0:T(8,128)(2,1)S(1)} %collective-permute-done.10.crossed_ref.refs_1_, ...), custom_call_target="tpu_custom_call" | custom-call | tf_op jit(solution)/shard_map/row_sums/pallas_call | solution.py:463
  39.6 2.6 %collective-permute-start.14 = (bf16[144,128]{1,0:T(8,128)(2,1)S(1)}, bf16[144,128]{1,0:T(8,128)(2,1)S(1)}, u32[]{:S(2)}, u32[]{:S(2)}) collective-permute-start(bf16[144,128]{1,0:T(8,128)(2,1)S(1)} %get-tuple-element.47), channel_id=1, source_target_pairs={{0,3},{1,2},{2,1},{3,0},{4,7},{5,6},{6,5},{7,4},{8,11},{9,10},{10,... | collective-permute-start | bytes 110600 | tf_op jit(solution)/shard_map/ppermute | solution.py:346
  42.2 1.8 %collective-permute-start.16 = (bf16[144,128]{1,0:T(8,128)(2,1)S(1)}, bf16[144,128]{1,0:T(8,128)(2,1)S(1)}, u32[]{:S(2)}, u32[]{:S(2)}) collective-permute-start(bf16[144,128]{1,0:T(8,128)(2,1)S(1)} %get-tuple-element.49), channel_id=1, source_target_pairs={{0,1},{1,0},{2,3},{3,2},{4,5},{5,4},{6,7},{7,6},{8,9},{9,8},{10,11... | collective-permute-start | bytes 110600 | tf_op jit(solution)/shard_map/ppermute | solution.py:346
  44.0 1.4 %collective-permute-done.14.refs_1_ = bf16[144,128]{1,0:T(8,128)(2,1)S(1)} collective-permute-done((bf16[144,128]{1,0:T(8,128)(2,1)S(1)}, bf16[144,128]{1,0:T(8,128)(2,1)S(1)}, u32[]{:S(2)}, u32[]{:S(2)}) %collective-permute-start.14) | collective-permute-done | bytes 36896 | tf_op jit(solution)/shard_map/ppermute | solution.py:346
  45.4 1.7 %collective-permute-done.15.refs_2_ = bf16[144,128]{1,0:T(8,128)(2,1)S(1)} collective-permute-done((bf16[144,128]{1,0:T(8,128)(2,1)S(1)}, bf16[144,128]{1,0:T(8,128)(2,1)S(1)}, u32[]{:S(2)}, u32[]{:S(2)}) %collective-permute-start.15) | collective-permute-done | bytes 36896 | tf_op jit(solution)/shard_map/ppermute | solution.py:346
  47.1 0.7 %adam.1 = (f32[64,128]{1,0:T(8,128)}, f32[64,128]{1,0:T(8,128)}, f32[64,128]{1,0:T(8,128)}, f32[64,128]{1,0:T(8,128)}, f32[64,128]{1,0:T(8,128)}, /*index=5*/f32...) custom-call(bf16[144,128]{1,0:T(8,128)(2,1)S(1)} %get-tuple-element.46.refs_0_, ...), custom_call_target="tpu_custom_call" | custom-call | tf_op jit(solution)/shard_map/adam/pallas_call | solution.py:484
  (28 shorter events, 0.1 us)
Async XLA Ops:
  0.6 46.4 %copy-start.2 = (f32[32,64]{1,0:T(8,128)S(1)}, f32[32,64]{1,0:T(8,128)}, u32[]{:S(2)}) copy-start(f32[32,64]{1,0:T(8,128)} %refs_10_.1) | copy-start | bytes 24580
  0.7 46.4 %copy-start.1 = (f32[128,64]{0,1:T(8,128)S(1)}, f32[128,64]{0,1:T(8,128)}, u32[]{:S(2)}) copy-start(f32[128,64]{0,1:T(8,128)} %param.20) | copy-start | bytes 98308
  0.7 46.4 %copy-start = (f32[128,64]{0,1:T(8,128)S(1)}, f32[128,64]{0,1:T(8,128)}, u32[]{:S(2)}) copy-start(f32[128,64]{0,1:T(8,128)} %param.17) | copy-start | bytes 98308
  0.7 46.4 %copy-start.8 = (f32[32,64]{1,0:T(8,128)S(1)}, f32[32,64]{1,0:T(8,128)}, u32[]{:S(2)}) copy-start(f32[32,64]{1,0:T(8,128)} %refs_12_.1) | copy-start | bytes 24580
  0.7 46.4 %copy-start.7 = (f32[32,64]{1,0:T(8,128)S(1)}, f32[32,64]{1,0:T(8,128)}, u32[]{:S(2)}) copy-start(f32[32,64]{1,0:T(8,128)} %refs_11_.1) | copy-start | bytes 24580
  0.7 46.4 %copy-start.6 = (f32[128,64]{0,1:T(8,128)S(1)}, f32[128,64]{0,1:T(8,128)}, u32[]{:S(2)}) copy-start(f32[128,64]{0,1:T(8,128)} %param.22) | copy-start | bytes 98308
  0.7 46.4 %copy-start.5 = (f32[128,64]{0,1:T(8,128)S(1)}, f32[128,64]{0,1:T(8,128)}, u32[]{:S(2)}) copy-start(f32[128,64]{0,1:T(8,128)} %param.21) | copy-start | bytes 98308
  0.7 46.4 %copy-start.4 = (f32[128,64]{0,1:T(8,128)S(1)}, f32[128,64]{0,1:T(8,128)}, u32[]{:S(2)}) copy-start(f32[128,64]{0,1:T(8,128)} %param.19) | copy-start | bytes 98308
  0.7 46.4 %copy-start.3 = (f32[128,64]{0,1:T(8,128)S(1)}, f32[128,64]{0,1:T(8,128)}, u32[]{:S(2)}) copy-start(f32[128,64]{0,1:T(8,128)} %param.18) | copy-start | bytes 98308
  1.7 6.4 %collective-permute-start.2 = (bf16[144,128]{1,0:T(8,128)(2,1)S(1)}, bf16[144,128]{1,0:T(8,128)(2,1)S(1)}, u32[]{:S(2)}, u32[]{:S(2)}) collective-permute-start(bf16[144,128]{1,0:T(8,128)(2,1)S(1)} %pack.1.refs_3_), channel_id=1, source_target_pairs={{0,2},{1,3},{2,0},{3,1},{4,6},{5,7},{6,4},{7,5},{8,10},{9,11},{10,... | collective-permute-start | bytes 110600 | tf_op jit(solution)/shard_map/ppermute | solution.py:346
  5.8 5.8 %collective-permute-start.1 = (bf16[144,128]{1,0:T(8,128)(2,1)S(1)}, bf16[144,128]{1,0:T(8,128)(2,1)S(1)}, u32[]{:S(2)}, u32[]{:S(2)}) collective-permute-start(bf16[144,128]{1,0:T(8,128)(2,1)S(1)} %pack.1.refs_3_), channel_id=1, source_target_pairs={{0,3},{1,2},{2,1},{3,0},{4,7},{5,6},{6,5},{7,4},{8,11},{9,10},{10,... | collective-permute-start | bytes 110600 | tf_op jit(solution)/shard_map/ppermute | solution.py:346
  7.1 4.4 %collective-permute-start = (bf16[144,128]{1,0:T(8,128)(2,1)S(1)}, bf16[144,128]{1,0:T(8,128)(2,1)S(1)}, u32[]{:S(2)}, u32[]{:S(2)}) collective-permute-start(bf16[144,128]{1,0:T(8,128)(2,1)S(1)} %pack.1.refs_3_), channel_id=1, source_target_pairs={{0,1},{1,0},{2,3},{3,2},{4,5},{5,4},{6,7},{7,6},{8,9},{9,8},{10,11... | collective-permute-start | bytes 110600 | tf_op jit(solution)/shard_map/ppermute | solution.py:346
  11.7 7.6 %collective-permute-start.8 = (bf16[576,128]{1,0:T(8,128)(2,1)S(1)}, bf16[576,128]{1,0:T(8,128)(2,1)S(1)}, u32[]{:S(2)}, u32[]{:S(2)}) collective-permute-start(bf16[576,128]{1,0:T(8,128)(2,1)S(1)} %table.1.refs_3_.refs_0_), channel_id=1, source_target_pairs={{0,24},{4,28},{8,16},{12,20},{16,8},{20,12},{24,0},{28,4},{1,25},{... | collective-permute-start | bytes 442376 | tf_op jit(solution)/shard_map/ppermute | solution.py:346
  14.1 6.0 %collective-permute-start.6 = (bf16[576,128]{1,0:T(8,128)(2,1)S(1)}, bf16[576,128]{1,0:T(8,128)(2,1)S(1)}, u32[]{:S(2)}, u32[]{:S(2)}) collective-permute-start(bf16[576,128]{1,0:T(8,128)(2,1)S(1)} %table.1.refs_3_.refs_0_), channel_id=1, source_target_pairs={{0,16},{4,20},{8,24},{12,28},{16,0},{20,4},{24,8},{28,12},{1,17},{... | collective-permute-start | bytes 442376 | tf_op jit(solution)/shard_map/ppermute | solution.py:346
  14.6 5.4 %collective-permute-start.4 = (bf16[576,128]{1,0:T(8,128)(2,1)S(1)}, bf16[576,128]{1,0:T(8,128)(2,1)S(1)}, u32[]{:S(2)}, u32[]{:S(2)}) collective-permute-start(bf16[576,128]{1,0:T(8,128)(2,1)S(1)} %table.1.refs_3_.refs_0_), channel_id=1, source_target_pairs={{0,8},{4,12},{8,0},{12,4},{16,24},{20,28},{24,16},{28,20},{1,9},{5... | collective-permute-start | bytes 442376 | tf_op jit(solution)/shard_map/ppermute | solution.py:346
  15.2 5.5 %collective-permute-start.3 = (bf16[576,128]{1,0:T(8,128)(2,1)S(1)}, bf16[576,128]{1,0:T(8,128)(2,1)S(1)}, u32[]{:S(2)}, u32[]{:S(2)}) collective-permute-start(bf16[576,128]{1,0:T(8,128)(2,1)S(1)} %table.1.refs_3_.refs_0_), channel_id=1, source_target_pairs={{0,4},{4,0},{8,12},{12,8},{16,20},{20,16},{24,28},{28,24},{1,5},{5... | collective-permute-start | bytes 442376 | tf_op jit(solution)/shard_map/ppermute | solution.py:346
  19.3 1.4 %collective-permute-start.9 = (bf16[576,128]{1,0:T(8,128)(2,1)S(1)}, bf16[576,128]{1,0:T(8,128)(2,1)S(1)}, u32[]{:S(2)}, u32[]{:S(2)}) collective-permute-start(bf16[576,128]{1,0:T(8,128)(2,1)S(1)} %collective-permute-done.8.refs_6_), channel_id=1, source_target_pairs={{0,4},{4,0},{8,12},{12,8},{16,20},{20,16},{24,28},{28,24},{1,5},{5... | collective-permute-start | bytes 442376 | tf_op jit(solution)/shard_map/ppermute | solution.py:346
  20.1 1.4 %collective-permute-start.7 = (bf16[576,128]{1,0:T(8,128)(2,1)S(1)}, bf16[576,128]{1,0:T(8,128)(2,1)S(1)}, u32[]{:S(2)}, u32[]{:S(2)}) collective-permute-start(bf16[576,128]{1,0:T(8,128)(2,1)S(1)} %collective-permute-done.6.refs_4_), channel_id=1, source_target_pairs={{0,4},{4,0},{8,12},{12,8},{16,20},{20,16},{24,28},{28,24},{1,5},{5... | collective-permute-start | bytes 442376 | tf_op jit(solution)/shard_map/ppermute | solution.py:346
  20.1 1.6 %collective-permute-start.5 = (bf16[576,128]{1,0:T(8,128)(2,1)S(1)}, bf16[576,128]{1,0:T(8,128)(2,1)S(1)}, u32[]{:S(2)}, u32[]{:S(2)}) collective-permute-start(bf16[576,128]{1,0:T(8,128)(2,1)S(1)} %hold.1.refs_2_), channel_id=1, source_target_pairs={{0,4},{4,0},{8,12},{12,8},{16,20},{20,16},{24,28},{28,24},{1,5},{5... | collective-permute-start | bytes 442376 | tf_op jit(solution)/shard_map/ppermute | solution.py:346
  28.6 1.6 %collective-permute-start.10 = (bf16[448,256]{1,0:T(8,128)(2,1)S(1)}, bf16[448,256]{1,0:T(8,128)(2,1)S(1)}, u32[]{:S(2)}, u32[]{:S(2)}) collective-permute-start(bf16[448,256]{1,0:T(8,128)(2,1)S(1)} %get-tuple-element.42), channel_id=1, source_target_pairs={{0,4},{4,0},{8,12},{12,8},{16,20},{20,16},{24,28},{28,24},{1,5},{5... | collective-permute-start | bytes 688136 | tf_op jit(solution)/shard_map/ppermute | solution.py:346
  30.2 6.9 %collective-permute-start.11 = (bf16[224,256]{1,0:T(8,128)(2,1)S(1)}, bf16[224,256]{1,0:T(8,128)(2,1)S(1)}, u32[]{:S(2)}, u32[]{:S(2)}) collective-permute-start(bf16[224,256]{1,0:T(8,128)(2,1)S(1)} %get-tuple-element.43), channel_id=1, source_target_pairs={{0,24},{4,28},{8,16},{12,20},{16,8},{20,12},{24,0},{28,4},{1,25},{... | collective-permute-start | bytes 344072 | tf_op jit(solution)/shard_map/ppermute | solution.py:346
  31.8 7.2 %collective-permute-start.12 = (bf16[224,256]{1,0:T(8,128)(2,1)S(1)}, bf16[224,256]{1,0:T(8,128)(2,1)S(1)}, u32[]{:S(2)}, u32[]{:S(2)}) collective-permute-start(bf16[224,256]{1,0:T(8,128)(2,1)S(1)} %get-tuple-element.44), channel_id=1, source_target_pairs={{0,16},{4,20},{8,24},{12,28},{16,0},{20,4},{24,8},{28,12},{1,17},{... | collective-permute-start | bytes 344072 | tf_op jit(solution)/shard_map/ppermute | solution.py:346
  33.0 6.0 %collective-permute-start.13 = (bf16[224,256]{1,0:T(8,128)(2,1)S(1)}, bf16[224,256]{1,0:T(8,128)(2,1)S(1)}, u32[]{:S(2)}, u32[]{:S(2)}) collective-permute-start(bf16[224,256]{1,0:T(8,128)(2,1)S(1)} %get-tuple-element.45), channel_id=1, source_target_pairs={{0,8},{4,12},{8,0},{12,4},{16,24},{20,28},{24,16},{28,20},{1,9},{5... | collective-permute-start | bytes 344072 | tf_op jit(solution)/shard_map/ppermute | solution.py:346
  39.6 5.8 %collective-permute-start.14 = (bf16[144,128]{1,0:T(8,128)(2,1)S(1)}, bf16[144,128]{1,0:T(8,128)(2,1)S(1)}, u32[]{:S(2)}, u32[]{:S(2)}) collective-permute-start(bf16[144,128]{1,0:T(8,128)(2,1)S(1)} %get-tuple-element.47), channel_id=1, source_target_pairs={{0,3},{1,2},{2,1},{3,0},{4,7},{5,6},{6,5},{7,4},{8,11},{9,10},{10,... | collective-permute-start | bytes 110600 | tf_op jit(solution)/shard_map/ppermute | solution.py:346
  42.2 4.9 %collective-permute-start.15 = (bf16[144,128]{1,0:T(8,128)(2,1)S(1)}, bf16[144,128]{1,0:T(8,128)(2,1)S(1)}, u32[]{:S(2)}, u32[]{:S(2)}) collective-permute-start(bf16[144,128]{1,0:T(8,128)(2,1)S(1)} %get-tuple-element.48), channel_id=1, source_target_pairs={{0,2},{1,3},{2,0},{3,1},{4,6},{5,7},{6,4},{7,5},{8,10},{9,11},{10,... | collective-permute-start | bytes 110600 | tf_op jit(solution)/shard_map/ppermute | solution.py:346
  42.2 4.9 %collective-permute-start.16 = (bf16[144,128]{1,0:T(8,128)(2,1)S(1)}, bf16[144,128]{1,0:T(8,128)(2,1)S(1)}, u32[]{:S(2)}, u32[]{:S(2)}) collective-permute-start(bf16[144,128]{1,0:T(8,128)(2,1)S(1)} %get-tuple-element.49), channel_id=1, source_target_pairs={{0,1},{1,0},{2,3},{3,2},{4,5},{5,4},{6,7},{7,6},{8,9},{9,8},{10,11... | collective-permute-start | bytes 110600 | tf_op jit(solution)/shard_map/ppermute | solution.py:346

commit v12 on v11

--- a/solution.py
+++ b/solution.py
@@ -213,25 +213,26 @@
 
     def residuals(first, scaled, residual):
         for j in range(pair):
+            day = days[pl.ds(first + j, 1), :].astype(bf16)
+            scaled[j * count : (j + 1) * count, :] = day * users_low[...]
+        half_logits = jnp.dot(scaled[...], items_half_t[...], preferred_element_type=f32)
+        for j in range(pair):
             rows = slice(j * count, (j + 1) * count)
-            day = days[pl.ds(first + j, 1), :].astype(bf16)
-            scaled_values = day * users_low[...]
-            scaled[rows, :] = scaled_values
-            half_logits = jnp.dot(scaled_values, items_half_t[...], preferred_element_type=f32)
             state = status[first + j]
             residual[rows, :] = (
-                state.astype(f32) * (jnp.tanh(half_logits) + jnp.where(state == 1, -1.0, 1.0))
+                state.astype(f32)
+                * (jnp.tanh(half_logits[rows]) + jnp.where(state == 1, -1.0, 1.0))
             ).astype(bf16)
 
     def gradients(first, scaled, residual):
+        projected = jnp.dot(residual[...], items[...], preferred_element_type=f32)
         total = 0.0
         for j in range(pair):
-            rows = slice(j * count, (j + 1) * count)
+            part = projected[j * count : (j + 1) * count]
             day = days[pl.ds(first + j, 1), :]
-            projected = jnp.dot(residual[rows, :], items[...], preferred_element_type=f32)
-            total = total + projected * day
+            total = total + part * day
             day_gradient[pl.ds(first + j, 1), :] = jnp.sum(
-                projected * users[...], axis=0, keepdims=True
+                part * users[...], axis=0, keepdims=True
             )
         user_gradient[...] += total
         item_gradient[...] += lax.dot_general(

time: 48.1 us -> 47.9 us (level)
  no operation moved by 1% of the time
where the time goes in v12:
time: 47.9 us; the launch traced here: 47.7 us
  starting transfers between devices  18.2 us (38%)
  waiting for transfers between devices  17.7 us (37%)
  Pallas kernels  11 us (23%)
  between operations  0.83 us (2%)
    ppermute x17, starting transfers between devices, swap(): return lax.ppermute(array, axis, [(i, i ^ bits) for i in range(size)])  18.2 us
    ppermute x17, waiting for transfers between devices, swap(): return lax.ppermute(array, axis, [(i, i ^ bits) for i in range(size)])  17.7 us
    pallas_call x1, Pallas kernels, local(): pl.pallas_call(functools.partial(block_kernel, sizes), out_shape=(half, h...  6.73 us
    pallas_call x1, Pallas kernels, local(): pl.pallas_call(functools.partial(slot_kernel, sizes), out_shape=tuple([sh...  1.85 us
  transfers between devices with their start and end apart: 17, of which 11 were waited for; matrix products, arithmetic and copies ran while one was open for 0% of the time, Pallas kernels for 4%

profile of v12, /device:TPU:0, one launch (start us, length us, event | category | flops | bytes accessed | tf_op | source)
XLA Modules:
  0.0 47.7 jit_solution(7545251225796606499)
XLA Ops:
  0.7 0.9 %pack.1.refs_3_ = bf16[144,128]{1,0:T(8,128)(2,1)S(1)} custom-call(f32[64,128]{1,0:T(8,128)} %bitcast.13, f32[64,128]{1,0:T(8,128)} %bitcast.15, f32[32,64]{1,0:T(8,128)} %refs_10_.1), custom_call_target="tpu_custom_call" | custom-call | tf_op jit(solution)/shard_map/pack/pallas_call | solution.py:376
  1.7 4.1 %collective-permute-start.2 = (bf16[144,128]{1,0:T(8,128)(2,1)S(1)}, bf16[144,128]{1,0:T(8,128)(2,1)S(1)}, u32[]{:S(2)}, u32[]{:S(2)}) collective-permute-start(bf16[144,128]{1,0:T(8,128)(2,1)S(1)} %pack.1.refs_3_), channel_id=1, source_target_pairs={{0,2},{1,3},{2,0},{3,1},{4,6},{5,7},{6,4},{7,5},{8,10},{9,11},{10,... | collective-permute-start | bytes 110600 | tf_op jit(solution)/shard_map/ppermute | solution.py:347
  5.8 1.3 %collective-permute-start.1 = (bf16[144,128]{1,0:T(8,128)(2,1)S(1)}, bf16[144,128]{1,0:T(8,128)(2,1)S(1)}, u32[]{:S(2)}, u32[]{:S(2)}) collective-permute-start(bf16[144,128]{1,0:T(8,128)(2,1)S(1)} %pack.1.refs_3_), channel_id=1, source_target_pairs={{0,3},{1,2},{2,1},{3,0},{4,7},{5,6},{6,5},{7,4},{8,11},{9,10},{10,... | collective-permute-start | bytes 110600 | tf_op jit(solution)/shard_map/ppermute | solution.py:347
  7.1 0.2 collective-permute-start
  7.4 0.8 %collective-permute-done.2.refs_2_ = bf16[144,128]{1,0:T(8,128)(2,1)S(1)} collective-permute-done((bf16[144,128]{1,0:T(8,128)(2,1)S(1)}, bf16[144,128]{1,0:T(8,128)(2,1)S(1)}, u32[]{:S(2)}, u32[]{:S(2)}) %collective-permute-start.2) | collective-permute-done | bytes 36896 | tf_op jit(solution)/shard_map/ppermute | solution.py:347
  8.1 3.4 %collective-permute-done.1.refs_1_ = bf16[144,128]{1,0:T(8,128)(2,1)S(1)} collective-permute-done((bf16[144,128]{1,0:T(8,128)(2,1)S(1)}, bf16[144,128]{1,0:T(8,128)(2,1)S(1)}, u32[]{:S(2)}, u32[]{:S(2)}) %collective-permute-start.1) | collective-permute-done | bytes 36896 | tf_op jit(solution)/shard_map/ppermute | solution.py:347
  11.5 0.1 table.1.refs_3_.refs_0_
  11.7 2.5 %collective-permute-start.8 = (bf16[576,128]{1,0:T(8,128)(2,1)S(1)}, bf16[576,128]{1,0:T(8,128)(2,1)S(1)}, u32[]{:S(2)}, u32[]{:S(2)}) collective-permute-start(bf16[576,128]{1,0:T(8,128)(2,1)S(1)} %table.1.refs_3_.refs_0_), channel_id=1, source_target_pairs={{0,24},{4,28},{8,16},{12,20},{16,8},{20,12},{24,0},{28,4},{1,25},{... | collective-permute-start | bytes 442376 | tf_op jit(solution)/shard_map/ppermute | solution.py:347
  14.1 0.5 %collective-permute-start.6 = (bf16[576,128]{1,0:T(8,128)(2,1)S(1)}, bf16[576,128]{1,0:T(8,128)(2,1)S(1)}, u32[]{:S(2)}, u32[]{:S(2)}) collective-permute-start(bf16[576,128]{1,0:T(8,128)(2,1)S(1)} %table.1.refs_3_.refs_0_), channel_id=1, source_target_pairs={{0,16},{4,20},{8,24},{12,28},{16,0},{20,4},{24,8},{28,12},{1,17},{... | collective-permute-start | bytes 442376 | tf_op jit(solution)/shard_map/ppermute | solution.py:347
  14.6 0.5 %collective-permute-start.4 = (bf16[576,128]{1,0:T(8,128)(2,1)S(1)}, bf16[576,128]{1,0:T(8,128)(2,1)S(1)}, u32[]{:S(2)}, u32[]{:S(2)}) collective-permute-start(bf16[576,128]{1,0:T(8,128)(2,1)S(1)} %table.1.refs_3_.refs_0_), channel_id=1, source_target_pairs={{0,8},{4,12},{8,0},{12,4},{16,24},{20,28},{24,16},{28,20},{1,9},{5... | collective-permute-start | bytes 442376 | tf_op jit(solution)/shard_map/ppermute | solution.py:347
  15.2 1.8 %slots.1 = (bf16[1024,256]{1,0:T(8,128)(2,1)S(1)}, bf16[1024,256]{1,0:T(8,128)(2,1)S(1)}, bf16[256,32]{1,0:T(8,128)(2,1)S(1)}, bf16[384,256]{1,0:T(8,128)(2,1)S(...) custom-call(s32[1]{0:T(128)} %bitcast.2.me_ref, s32[1,256]{1,0:T(1,128)} %refs_0_.1, ...), custom_call_target="tpu_custom_call" | custom-call | tf_op jit(solution)/shard_map/slots/pallas_call | solution.py:396
  17.0 2.3 %collective-permute-done.8.refs_6_ = bf16[576,128]{1,0:T(8,128)(2,1)S(1)} collective-permute-done((bf16[576,128]{1,0:T(8,128)(2,1)S(1)}, bf16[576,128]{1,0:T(8,128)(2,1)S(1)}, u32[]{:S(2)}, u32[]{:S(2)}) %collective-permute-start.8) | collective-permute-done | bytes 147488 | tf_op jit(solution)/shard_map/ppermute | solution.py:347
  19.3 0.0 collective-permute-start.9
  19.3 0.8 %collective-permute-done.6.refs_4_ = bf16[576,128]{1,0:T(8,128)(2,1)S(1)} collective-permute-done((bf16[576,128]{1,0:T(8,128)(2,1)S(1)}, bf16[576,128]{1,0:T(8,128)(2,1)S(1)}, u32[]{:S(2)}, u32[]{:S(2)}) %collective-permute-start.6) | collective-permute-done | bytes 147488 | tf_op jit(solution)/shard_map/ppermute | solution.py:347
  20.1 0.0 collective-permute-start.7
  20.1 0.6 %collective-permute-start.5 = (bf16[576,128]{1,0:T(8,128)(2,1)S(1)}, bf16[576,128]{1,0:T(8,128)(2,1)S(1)}, u32[]{:S(2)}, u32[]{:S(2)}) collective-permute-start(bf16[576,128]{1,0:T(8,128)(2,1)S(1)} %hold.1.refs_2_), channel_id=1, source_target_pairs={{0,4},{4,0},{8,12},{12,8},{16,20},{20,16},{24,28},{28,24},{1,5},{5... | collective-permute-start | bytes 442376 | tf_op jit(solution)/shard_map/ppermute | solution.py:347
  20.7 0.8 %collective-permute-done.7.refs_5_ = bf16[576,128]{1,0:T(8,128)(2,1)S(1)} collective-permute-done((bf16[576,128]{1,0:T(8,128)(2,1)S(1)}, bf16[576,128]{1,0:T(8,128)(2,1)S(1)}, u32[]{:S(2)}, u32[]{:S(2)}) %collective-permute-start.7) | collective-permute-done | bytes 147488 | tf_op jit(solution)/shard_map/ppermute | solution.py:347
  21.5 0.2 collective-permute-done.5.refs_3_
  21.7 6.7 %block_gradients.1 = (bf16[448,256]{1,0:T(8,128)(2,1)S(1)}, bf16[448,256]{1,0:T(8,128)(2,1)S(1)}) custom-call(bf16[576,128]{1,0:T(8,128)(2,1)S(1)} %table.1.refs_3_.refs_0_, bf16[576,128]{1,0:T(8,128)(2,1)S(1)} %collective-permute-done.3.refs_1_, bf16[576,128]{1,0:T(8,128)(2,1)S(1)} %hold.1.refs_2_, bf16[576,128]{1,0:T(8,128)(2,1)S(1)} %collective-permute-done.5.refs_3_, ...), custom_call_target="tpu_custom_call" | custom-call | tf_op jit(solution)/shard_map/block_gradients/pallas_call | solution.py:428
  28.4 0.4 collective-permute-start.10
  28.8 1.1 %collective-permute-done.10.crossed_ref.refs_1_ = bf16[448,256]{1,0:T(8,128)(2,1)S(1)} collective-permute-done((bf16[448,256]{1,0:T(8,128)(2,1)S(1)}, bf16[448,256]{1,0:T(8,128)(2,1)S(1)}, u32[]{:S(2)}, u32[]{:S(2)}) %collective-permute-start.10) | collective-permute-done | bytes 229408 | tf_op jit(solution)/shard_map/ppermute | solution.py:347
  30.0 1.6 %collective-permute-start.11 = (bf16[224,256]{1,0:T(8,128)(2,1)S(1)}, bf16[224,256]{1,0:T(8,128)(2,1)S(1)}, u32[]{:S(2)}, u32[]{:S(2)}) collective-permute-start(bf16[224,256]{1,0:T(8,128)(2,1)S(1)} %get-tuple-element.43), channel_id=1, source_target_pairs={{0,24},{4,28},{8,16},{12,20},{16,8},{20,12},{24,0},{28,4},{1,25},{... | collective-permute-start | bytes 344072 | tf_op jit(solution)/shard_map/ppermute | solution.py:347
  31.7 1.2 %collective-permute-start.12 = (bf16[224,256]{1,0:T(8,128)(2,1)S(1)}, bf16[224,256]{1,0:T(8,128)(2,1)S(1)}, u32[]{:S(2)}, u32[]{:S(2)}) collective-permute-start(bf16[224,256]{1,0:T(8,128)(2,1)S(1)} %get-tuple-element.44), channel_id=1, source_target_pairs={{0,16},{4,20},{8,24},{12,28},{16,0},{20,4},{24,8},{28,12},{1,17},{... | collective-permute-start | bytes 344072 | tf_op jit(solution)/shard_map/ppermute | solution.py:347
  32.9 0.7 %collective-permute-start.13 = (bf16[224,256]{1,0:T(8,128)(2,1)S(1)}, bf16[224,256]{1,0:T(8,128)(2,1)S(1)}, u32[]{:S(2)}, u32[]{:S(2)}) collective-permute-start(bf16[224,256]{1,0:T(8,128)(2,1)S(1)} %get-tuple-element.45), channel_id=1, source_target_pairs={{0,8},{4,12},{8,0},{12,4},{16,24},{20,28},{24,16},{28,20},{1,9},{5... | collective-permute-start | bytes 344072 | tf_op jit(solution)/shard_map/ppermute | solution.py:347
  33.6 3.4 %collective-permute-done.11.refs_2_ = bf16[224,256]{1,0:T(8,128)(2,1)S(1)} collective-permute-done((bf16[224,256]{1,0:T(8,128)(2,1)S(1)}, bf16[224,256]{1,0:T(8,128)(2,1)S(1)}, u32[]{:S(2)}, u32[]{:S(2)}) %collective-permute-start.11) | collective-permute-done | bytes 114720 | tf_op jit(solution)/shard_map/ppermute | solution.py:347
  36.9 1.9 %collective-permute-done.12.refs_3_ = bf16[224,256]{1,0:T(8,128)(2,1)S(1)} collective-permute-done((bf16[224,256]{1,0:T(8,128)(2,1)S(1)}, bf16[224,256]{1,0:T(8,128)(2,1)S(1)}, u32[]{:S(2)}, u32[]{:S(2)}) %collective-permute-start.12) | collective-permute-done | bytes 114720 | tf_op jit(solution)/shard_map/ppermute | solution.py:347
  38.8 0.6 %row_sums.1 = (bf16[144,128]{1,0:T(8,128)(2,1)S(1)}, bf16[144,128]{1,0:T(8,128)(2,1)S(1)}, bf16[144,128]{1,0:T(8,128)(2,1)S(1)}, bf16[144,128]{1,0:T(8,128)(2,1)S(1)}) custom-call(bf16[448,256]{1,0:T(8,128)(2,1)S(1)} %get-tuple-element.41.own_ref.refs_0_, bf16[448,256]{1,0:T(8,128)(2,1)S(1)} %collective-permute-done.10.crossed_ref.refs_1_, ...), custom_call_target="tpu_custom_call" | custom-call | tf_op jit(solution)/shard_map/row_sums/pallas_call | solution.py:464
  39.4 2.6 %collective-permute-start.14 = (bf16[144,128]{1,0:T(8,128)(2,1)S(1)}, bf16[144,128]{1,0:T(8,128)(2,1)S(1)}, u32[]{:S(2)}, u32[]{:S(2)}) collective-permute-start(bf16[144,128]{1,0:T(8,128)(2,1)S(1)} %get-tuple-element.47), channel_id=1, source_target_pairs={{0,3},{1,2},{2,1},{3,0},{4,7},{5,6},{6,5},{7,4},{8,11},{9,10},{10,... | collective-permute-start | bytes 110600 | tf_op jit(solution)/shard_map/ppermute | solution.py:347
  42.0 1.8 %collective-permute-start.16 = (bf16[144,128]{1,0:T(8,128)(2,1)S(1)}, bf16[144,128]{1,0:T(8,128)(2,1)S(1)}, u32[]{:S(2)}, u32[]{:S(2)}) collective-permute-start(bf16[144,128]{1,0:T(8,128)(2,1)S(1)} %get-tuple-element.49), channel_id=1, source_target_pairs={{0,1},{1,0},{2,3},{3,2},{4,5},{5,4},{6,7},{7,6},{8,9},{9,8},{10,11... | collective-permute-start | bytes 110600 | tf_op jit(solution)/shard_map/ppermute | solution.py:347
  43.9 1.4 %collective-permute-done.14.refs_1_ = bf16[144,128]{1,0:T(8,128)(2,1)S(1)} collective-permute-done((bf16[144,128]{1,0:T(8,128)(2,1)S(1)}, bf16[144,128]{1,0:T(8,128)(2,1)S(1)}, u32[]{:S(2)}, u32[]{:S(2)}) %collective-permute-start.14) | collective-permute-done | bytes 36896 | tf_op jit(solution)/shard_map/ppermute | solution.py:347
  45.2 1.7 %collective-permute-done.15.refs_2_ = bf16[144,128]{1,0:T(8,128)(2,1)S(1)} collective-permute-done((bf16[144,128]{1,0:T(8,128)(2,1)S(1)}, bf16[144,128]{1,0:T(8,128)(2,1)S(1)}, u32[]{:S(2)}, u32[]{:S(2)}) %collective-permute-start.15) | collective-permute-done | bytes 36896 | tf_op jit(solution)/shard_map/ppermute | solution.py:347
  47.0 0.7 %adam.1 = (f32[64,128]{1,0:T(8,128)}, f32[64,128]{1,0:T(8,128)}, f32[64,128]{1,0:T(8,128)}, f32[64,128]{1,0:T(8,128)}, f32[64,128]{1,0:T(8,128)}, /*index=5*/f32...) custom-call(bf16[144,128]{1,0:T(8,128)(2,1)S(1)} %get-tuple-element.46.refs_0_, ...), custom_call_target="tpu_custom_call" | custom-call | tf_op jit(solution)/shard_map/adam/pallas_call | solution.py:485
  (28 shorter events, 0.1 us)
Async XLA Ops:
  0.6 46.2 %copy-start.2 = (f32[32,64]{1,0:T(8,128)S(1)}, f32[32,64]{1,0:T(8,128)}, u32[]{:S(2)}) copy-start(f32[32,64]{1,0:T(8,128)} %refs_10_.1) | copy-start | bytes 24580
  0.7 46.2 %copy-start.1 = (f32[128,64]{0,1:T(8,128)S(1)}, f32[128,64]{0,1:T(8,128)}, u32[]{:S(2)}) copy-start(f32[128,64]{0,1:T(8,128)} %param.20) | copy-start | bytes 98308
  0.7 46.2 %copy-start = (f32[128,64]{0,1:T(8,128)S(1)}, f32[128,64]{0,1:T(8,128)}, u32[]{:S(2)}) copy-start(f32[128,64]{0,1:T(8,128)} %param.17) | copy-start | bytes 98308
  0.7 46.2 %copy-start.8 = (f32[32,64]{1,0:T(8,128)S(1)}, f32[32,64]{1,0:T(8,128)}, u32[]{:S(2)}) copy-start(f32[32,64]{1,0:T(8,128)} %refs_12_.1) | copy-start | bytes 24580
  0.7 46.2 %copy-start.7 = (f32[32,64]{1,0:T(8,128)S(1)}, f32[32,64]{1,0:T(8,128)}, u32[]{:S(2)}) copy-start(f32[32,64]{1,0:T(8,128)} %refs_11_.1) | copy-start | bytes 24580
  0.7 46.2 %copy-start.6 = (f32[128,64]{0,1:T(8,128)S(1)}, f32[128,64]{0,1:T(8,128)}, u32[]{:S(2)}) copy-start(f32[128,64]{0,1:T(8,128)} %param.22) | copy-start | bytes 98308
  0.7 46.2 %copy-start.5 = (f32[128,64]{0,1:T(8,128)S(1)}, f32[128,64]{0,1:T(8,128)}, u32[]{:S(2)}) copy-start(f32[128,64]{0,1:T(8,128)} %param.21) | copy-start | bytes 98308
  0.7 46.2 %copy-start.4 = (f32[128,64]{0,1:T(8,128)S(1)}, f32[128,64]{0,1:T(8,128)}, u32[]{:S(2)}) copy-start(f32[128,64]{0,1:T(8,128)} %param.19) | copy-start | bytes 98308
  0.7 46.2 %copy-start.3 = (f32[128,64]{0,1:T(8,128)S(1)}, f32[128,64]{0,1:T(8,128)}, u32[]{:S(2)}) copy-start(f32[128,64]{0,1:T(8,128)} %param.18) | copy-start | bytes 98308
  1.7 6.4 %collective-permute-start.2 = (bf16[144,128]{1,0:T(8,128)(2,1)S(1)}, bf16[144,128]{1,0:T(8,128)(2,1)S(1)}, u32[]{:S(2)}, u32[]{:S(2)}) collective-permute-start(bf16[144,128]{1,0:T(8,128)(2,1)S(1)} %pack.1.refs_3_), channel_id=1, source_target_pairs={{0,2},{1,3},{2,0},{3,1},{4,6},{5,7},{6,4},{7,5},{8,10},{9,11},{10,... | collective-permute-start | bytes 110600 | tf_op jit(solution)/shard_map/ppermute | solution.py:347
  5.8 5.8 %collective-permute-start.1 = (bf16[144,128]{1,0:T(8,128)(2,1)S(1)}, bf16[144,128]{1,0:T(8,128)(2,1)S(1)}, u32[]{:S(2)}, u32[]{:S(2)}) collective-permute-start(bf16[144,128]{1,0:T(8,128)(2,1)S(1)} %pack.1.refs_3_), channel_id=1, source_target_pairs={{0,3},{1,2},{2,1},{3,0},{4,7},{5,6},{6,5},{7,4},{8,11},{9,10},{10,... | collective-permute-start | bytes 110600 | tf_op jit(solution)/shard_map/ppermute | solution.py:347
  7.1 4.4 %collective-permute-start = (bf16[144,128]{1,0:T(8,128)(2,1)S(1)}, bf16[144,128]{1,0:T(8,128)(2,1)S(1)}, u32[]{:S(2)}, u32[]{:S(2)}) collective-permute-start(bf16[144,128]{1,0:T(8,128)(2,1)S(1)} %pack.1.refs_3_), channel_id=1, source_target_pairs={{0,1},{1,0},{2,3},{3,2},{4,5},{5,4},{6,7},{7,6},{8,9},{9,8},{10,11... | collective-permute-start | bytes 110600 | tf_op jit(solution)/shard_map/ppermute | solution.py:347
  11.7 7.6 %collective-permute-start.8 = (bf16[576,128]{1,0:T(8,128)(2,1)S(1)}, bf16[576,128]{1,0:T(8,128)(2,1)S(1)}, u32[]{:S(2)}, u32[]{:S(2)}) collective-permute-start(bf16[576,128]{1,0:T(8,128)(2,1)S(1)} %table.1.refs_3_.refs_0_), channel_id=1, source_target_pairs={{0,24},{4,28},{8,16},{12,20},{16,8},{20,12},{24,0},{28,4},{1,25},{... | collective-permute-start | bytes 442376 | tf_op jit(solution)/shard_map/ppermute | solution.py:347
  14.1 6.0 %collective-permute-start.6 = (bf16[576,128]{1,0:T(8,128)(2,1)S(1)}, bf16[576,128]{1,0:T(8,128)(2,1)S(1)}, u32[]{:S(2)}, u32[]{:S(2)}) collective-permute-start(bf16[576,128]{1,0:T(8,128)(2,1)S(1)} %table.1.refs_3_.refs_0_), channel_id=1, source_target_pairs={{0,16},{4,20},{8,24},{12,28},{16,0},{20,4},{24,8},{28,12},{1,17},{... | collective-permute-start | bytes 442376 | tf_op jit(solution)/shard_map/ppermute | solution.py:347
  14.6 5.4 %collective-permute-start.4 = (bf16[576,128]{1,0:T(8,128)(2,1)S(1)}, bf16[576,128]{1,0:T(8,128)(2,1)S(1)}, u32[]{:S(2)}, u32[]{:S(2)}) collective-permute-start(bf16[576,128]{1,0:T(8,128)(2,1)S(1)} %table.1.refs_3_.refs_0_), channel_id=1, source_target_pairs={{0,8},{4,12},{8,0},{12,4},{16,24},{20,28},{24,16},{28,20},{1,9},{5... | collective-permute-start | bytes 442376 | tf_op jit(solution)/shard_map/ppermute | solution.py:347
  15.2 5.5 %collective-permute-start.3 = (bf16[576,128]{1,0:T(8,128)(2,1)S(1)}, bf16[576,128]{1,0:T(8,128)(2,1)S(1)}, u32[]{:S(2)}, u32[]{:S(2)}) collective-permute-start(bf16[576,128]{1,0:T(8,128)(2,1)S(1)} %table.1.refs_3_.refs_0_), channel_id=1, source_target_pairs={{0,4},{4,0},{8,12},{12,8},{16,20},{20,16},{24,28},{28,24},{1,5},{5... | collective-permute-start | bytes 442376 | tf_op jit(solution)/shard_map/ppermute | solution.py:347
  19.3 1.4 %collective-permute-start.9 = (bf16[576,128]{1,0:T(8,128)(2,1)S(1)}, bf16[576,128]{1,0:T(8,128)(2,1)S(1)}, u32[]{:S(2)}, u32[]{:S(2)}) collective-permute-start(bf16[576,128]{1,0:T(8,128)(2,1)S(1)} %collective-permute-done.8.refs_6_), channel_id=1, source_target_pairs={{0,4},{4,0},{8,12},{12,8},{16,20},{20,16},{24,28},{28,24},{1,5},{5... | collective-permute-start | bytes 442376 | tf_op jit(solution)/shard_map/ppermute | solution.py:347
  20.1 1.4 %collective-permute-start.7 = (bf16[576,128]{1,0:T(8,128)(2,1)S(1)}, bf16[576,128]{1,0:T(8,128)(2,1)S(1)}, u32[]{:S(2)}, u32[]{:S(2)}) collective-permute-start(bf16[576,128]{1,0:T(8,128)(2,1)S(1)} %collective-permute-done.6.refs_4_), channel_id=1, source_target_pairs={{0,4},{4,0},{8,12},{12,8},{16,20},{20,16},{24,28},{28,24},{1,5},{5... | collective-permute-start | bytes 442376 | tf_op jit(solution)/shard_map/ppermute | solution.py:347
  20.1 1.6 %collective-permute-start.5 = (bf16[576,128]{1,0:T(8,128)(2,1)S(1)}, bf16[576,128]{1,0:T(8,128)(2,1)S(1)}, u32[]{:S(2)}, u32[]{:S(2)}) collective-permute-start(bf16[576,128]{1,0:T(8,128)(2,1)S(1)} %hold.1.refs_2_), channel_id=1, source_target_pairs={{0,4},{4,0},{8,12},{12,8},{16,20},{20,16},{24,28},{28,24},{1,5},{5... | collective-permute-start | bytes 442376 | tf_op jit(solution)/shard_map/ppermute | solution.py:347
  28.4 1.6 %collective-permute-start.10 = (bf16[448,256]{1,0:T(8,128)(2,1)S(1)}, bf16[448,256]{1,0:T(8,128)(2,1)S(1)}, u32[]{:S(2)}, u32[]{:S(2)}) collective-permute-start(bf16[448,256]{1,0:T(8,128)(2,1)S(1)} %get-tuple-element.42), channel_id=1, source_target_pairs={{0,4},{4,0},{8,12},{12,8},{16,20},{20,16},{24,28},{28,24},{1,5},{5... | collective-permute-start | bytes 688136 | tf_op jit(solution)/shard_map/ppermute | solution.py:347
  30.0 6.9 %collective-permute-start.11 = (bf16[224,256]{1,0:T(8,128)(2,1)S(1)}, bf16[224,256]{1,0:T(8,128)(2,1)S(1)}, u32[]{:S(2)}, u32[]{:S(2)}) collective-permute-start(bf16[224,256]{1,0:T(8,128)(2,1)S(1)} %get-tuple-element.43), channel_id=1, source_target_pairs={{0,24},{4,28},{8,16},{12,20},{16,8},{20,12},{24,0},{28,4},{1,25},{... | collective-permute-start | bytes 344072 | tf_op jit(solution)/shard_map/ppermute | solution.py:347
  31.7 7.2 %collective-permute-start.12 = (bf16[224,256]{1,0:T(8,128)(2,1)S(1)}, bf16[224,256]{1,0:T(8,128)(2,1)S(1)}, u32[]{:S(2)}, u32[]{:S(2)}) collective-permute-start(bf16[224,256]{1,0:T(8,128)(2,1)S(1)} %get-tuple-element.44), channel_id=1, source_target_pairs={{0,16},{4,20},{8,24},{12,28},{16,0},{20,4},{24,8},{28,12},{1,17},{... | collective-permute-start | bytes 344072 | tf_op jit(solution)/shard_map/ppermute | solution.py:347
  32.9 6.0 %collective-permute-start.13 = (bf16[224,256]{1,0:T(8,128)(2,1)S(1)}, bf16[224,256]{1,0:T(8,128)(2,1)S(1)}, u32[]{:S(2)}, u32[]{:S(2)}) collective-permute-start(bf16[224,256]{1,0:T(8,128)(2,1)S(1)} %get-tuple-element.45), channel_id=1, source_target_pairs={{0,8},{4,12},{8,0},{12,4},{16,24},{20,28},{24,16},{28,20},{1,9},{5... | collective-permute-start | bytes 344072 | tf_op jit(solution)/shard_map/ppermute | solution.py:347
  39.4 5.8 %collective-permute-start.14 = (bf16[144,128]{1,0:T(8,128)(2,1)S(1)}, bf16[144,128]{1,0:T(8,128)(2,1)S(1)}, u32[]{:S(2)}, u32[]{:S(2)}) collective-permute-start(bf16[144,128]{1,0:T(8,128)(2,1)S(1)} %get-tuple-element.47), channel_id=1, source_target_pairs={{0,3},{1,2},{2,1},{3,0},{4,7},{5,6},{6,5},{7,4},{8,11},{9,10},{10,... | collective-permute-start | bytes 110600 | tf_op jit(solution)/shard_map/ppermute | solution.py:347
  42.0 4.9 %collective-permute-start.15 = (bf16[144,128]{1,0:T(8,128)(2,1)S(1)}, bf16[144,128]{1,0:T(8,128)(2,1)S(1)}, u32[]{:S(2)}, u32[]{:S(2)}) collective-permute-start(bf16[144,128]{1,0:T(8,128)(2,1)S(1)} %get-tuple-element.48), channel_id=1, source_target_pairs={{0,2},{1,3},{2,0},{3,1},{4,6},{5,7},{6,4},{7,5},{8,10},{9,11},{10,... | collective-permute-start | bytes 110600 | tf_op jit(solution)/shard_map/ppermute | solution.py:347
  42.0 4.9 %collective-permute-start.16 = (bf16[144,128]{1,0:T(8,128)(2,1)S(1)}, bf16[144,128]{1,0:T(8,128)(2,1)S(1)}, u32[]{:S(2)}, u32[]{:S(2)}) collective-permute-start(bf16[144,128]{1,0:T(8,128)(2,1)S(1)} %get-tuple-element.49), channel_id=1, source_target_pairs={{0,1},{1,0},{2,3},{3,2},{4,5},{5,4},{6,7},{7,6},{8,9},{9,8},{10,11... | collective-permute-start | bytes 110600 | tf_op jit(solution)/shard_map/ppermute | solution.py:347

commit v13 on v12

--- a/solution.py
+++ b/solution.py
@@ -18,7 +18,7 @@
 LANES = 128
 HOLD = 2
 SMALL_VMEM = 16 * 1024 * 1024
-BLOCK_VMEM = 48 * 1024 * 1024
+BLOCK_VMEM = 24 * 1024 * 1024
 
 f32 = jnp.float32
 bf16 = jnp.bfloat16
@@ -106,8 +106,11 @@
 
 def slot_kernel(sizes, me_ref, *refs):
     owners = sizes.owners
-    picks, places, note_ref, lists = refs[4:7], refs[7:10], refs[10], refs[11:14]
-    fetch(refs[:3], lists, refs[14])
+    picks, places, note_ref, status_ref = refs[5:8], refs[8:11], refs[11], refs[12]
+    lists, semaphores, status_semaphore = refs[13:16], refs[16], refs[17]
+    status_copy = pltpu.make_async_copy(refs[4].at[0], status_ref, status_semaphore.at[0])
+    fetch(refs[:3], lists, semaphores)
+    status_copy.start()
     me = me_ref[0]
     notes = [[] for _ in range(owners)]
     for t in range(3):
@@ -131,6 +134,7 @@
     note_ref[...] = jnp.concatenate(
         [jnp.concatenate(note + [blank], axis=1) for note in notes], axis=0
     )
+    status_copy.wait()
 
 
 def table_kernel(sizes, *refs):
@@ -154,7 +158,7 @@
     owners, rank, day_rows = sizes.owners, sizes.rank, sizes.row_counts[2]
     tables, refs = refs[:owners], refs[owners:]
     picks, places = refs[:3], refs[3:6]
-    note_ref, status_hbm, own_ref, other_ref = refs[6:10]
+    note_ref, status, own_ref, other_ref = refs[6:10]
     (
         users,
         users_low,
@@ -168,24 +172,9 @@
         scaled_odd,
         residual_even,
         residual_odd,
-        status,
-        semaphores,
     ) = refs[10:]
     pair = 4
     pairs = status.shape[0] // pair
-    chunks = [(0, pair)]
-    chunks += [((2 * n - 1) * pair, 2 * pair) for n in range(1, pairs // 2)]
-    chunks += [((pairs - 1) * pair, pair)]
-
-    def status_copy(start, size, semaphore):
-        part = pl.ds(start, size)
-        return pltpu.make_async_copy(
-            status_hbm.at[0, part], status.at[part], semaphores.at[semaphore]
-        )
-
-    for n, (start, size) in enumerate(chunks):
-        status_copy(start, size, n).start()
-
     def pick(t):
         table = jnp.concatenate([ref[t * rank : (t + 1) * rank, :] for ref in tables], axis=1)
         return jnp.dot(table, picks[t][...], preferred_element_type=f32)
@@ -240,20 +229,17 @@
         )
 
     even, odd = (scaled_even, residual_even), (scaled_odd, residual_odd)
-    status_copy(*chunks[0], 0).wait()
     residuals(0, *even)
 
     @pl.loop(0, pairs // 2 - 1)
     def _(n):
         first = 2 * n * pair
-        status_copy(first + pair, 2 * pair, n + 1).wait()
         residuals(first + pair, *odd)
         gradients(first, *even)
         residuals(first + 2 * pair, *even)
         gradients(first + pair, *odd)
 
     last = (pairs - 1) * pair
-    status_copy(*chunks[-1], len(chunks) - 1).wait()
     residuals(last, *odd)
     gradients(last - pair, *even)
     gradients(last, *odd)
@@ -398,19 +384,20 @@
         out_shape=tuple(
             [shape((owners * row_counts[t], list_counts[t]), bf16) for t in range(3)]
             + [shape((owners * sizes.slots[t], list_counts[t]), bf16) for t in range(3)]
-            + [shape((owners, sizes.rank), f32)]
+            + [shape((owners, sizes.rank), f32), shape(status.shape[1:], jnp.int32)]
         ),
         in_specs=[pl.BlockSpec(memory_space=pltpu.SMEM)]
         + [hbm] * 3
-        + [pl.BlockSpec(memory_space=pl.ANY)],
+        + [pl.BlockSpec(memory_space=pl.ANY), hbm],
         scratch_shapes=[pltpu.VMEM((1, count), jnp.int32) for count in list_counts]
-        + [pltpu.SemaphoreType.DMA((3,))],
+        + [pltpu.SemaphoreType.DMA((3,)), pltpu.SemaphoreType.DMA((1,))],
         compiler_params=small,
         name="slots",
     )(
         lax.axis_index("dp").astype(jnp.int32).reshape(1),
         *[in_hbm(a) for a in (users_list, items_list, days_list)],
         table,
+        in_hbm(status),
     )
 
     arrived[HOLD] = pl.pallas_call(
@@ -428,7 +415,7 @@
     own, other = pl.pallas_call(
         functools.partial(block_kernel, sizes),
         out_shape=(half, half),
-        in_specs=[pl.BlockSpec(memory_space=pltpu.VMEM)] * len(inputs) + [hbm],
+        in_specs=[pl.BlockSpec(memory_space=pltpu.VMEM)] * len(inputs),
         scratch_shapes=[
             pltpu.VMEM((users, sizes.rank), f32),
             pltpu.VMEM((users, sizes.rank), bf16),
@@ -442,12 +429,10 @@
             pltpu.VMEM((4 * users, sizes.rank), bf16),
             pltpu.VMEM((4 * users, items), bf16),
             pltpu.VMEM((4 * users, items), bf16),
-            pltpu.VMEM((days, users, items), jnp.int32),
-            pltpu.SemaphoreType.DMA((days // 8 + 1,)),
         ],
         compiler_params=pltpu.CompilerParams(vmem_limit_bytes=BLOCK_VMEM),
         name="block_gradients",
-    )(*inputs, in_hbm(status))
+    )(*inputs)
     crossed = swap(other, "dp", owners, 1)
     message = shape((2 * sizes.slot_rows, sizes.rank), bf16)
     merged = pl.pallas_call(

time: 47.9 us -> 46.6 us (0.973)
  waiting for transfers between devices: 17.7 us -> 14.7 us
  Pallas kernels: 11 us -> 12 us
  starting transfers between devices: 18.2 us -> 18.7 us
    ppermute x17, waiting for transfers between devices: 17.7 us -> 14.7 us  [swap(): return lax.ppermute(array, axis, [(i, i ^ bits) for i in range(size)])]
    pallas_call x1, Pallas kernels: 1.85 us -> 4.11 us  [local(): pl.pallas_call(functools.partial(slot_kernel, sizes), out_shape=tuple([sh...]
    pallas_call x1, Pallas kernels: 6.73 us -> 5.56 us  [local(): pl.pallas_call(functools.partial(block_kernel, sizes), out_shape=(half, h...]
    ppermute x17, starting transfers between devices: 18.2 us -> 18.7 us  [swap(): return lax.ppermute(array, axis, [(i, i ^ bits) for i in range(size)])]
  transfers between devices with their start and end apart: 17 -> 17, of which waited for: 11 -> 11; matrix products, arithmetic and copies ran while one was open for 0% -> 0% of each run, Pallas kernels for 4% -> 9%
where the time goes in v13:
time: 46.6 us; the launch traced here: 46.4 us
  starting transfers between devices  18.7 us (40%)
  waiting for transfers between devices  14.7 us (32%)
  Pallas kernels  12 us (26%)
  between operations  0.83 us (2%)
    ppermute x17, starting transfers between devices, swap(): return lax.ppermute(array, axis, [(i, i ^ bits) for i in range(size)])  18.7 us
    ppermute x17, waiting for transfers between devices, swap(): return lax.ppermute(array, axis, [(i, i ^ bits) for i in range(size)])  14.7 us
    pallas_call x1, Pallas kernels, local(): pl.pallas_call(functools.partial(block_kernel, sizes), out_shape=(half, h...  5.56 us
    pallas_call x1, Pallas kernels, local(): pl.pallas_call(functools.partial(slot_kernel, sizes), out_shape=tuple([sh...  4.11 us
  transfers between devices with their start and end apart: 17, of which 11 were waited for; matrix products, arithmetic and copies ran while one was open for 0% of the time, Pallas kernels for 9%

profile of v13, /device:TPU:0, one launch (start us, length us, event | category | flops | bytes accessed | tf_op | source)
XLA Modules:
  0.0 46.4 jit_solution(5396085833503120254)
XLA Ops:
  0.6 0.9 %pack.1.refs_3_ = bf16[144,128]{1,0:T(8,128)(2,1)S(1)} custom-call(f32[64,128]{1,0:T(8,128)} %bitcast.13, f32[64,128]{1,0:T(8,128)} %bitcast.15, f32[32,64]{1,0:T(8,128)} %refs_10_.1), custom_call_target="tpu_custom_call" | custom-call | tf_op jit(solution)/shard_map/pack/pallas_call | solution.py:362
  1.5 4.1 %collective-permute-start.2 = (bf16[144,128]{1,0:T(8,128)(2,1)S(1)}, bf16[144,128]{1,0:T(8,128)(2,1)S(1)}, u32[]{:S(2)}, u32[]{:S(2)}) collective-permute-start(bf16[144,128]{1,0:T(8,128)(2,1)S(1)} %pack.1.refs_3_), channel_id=1, source_target_pairs={{0,2},{1,3},{2,0},{3,1},{4,6},{5,7},{6,4},{7,5},{8,10},{9,11},{10,... | collective-permute-start | bytes 110600 | tf_op jit(solution)/shard_map/ppermute | solution.py:333
  5.6 1.3 %collective-permute-start.1 = (bf16[144,128]{1,0:T(8,128)(2,1)S(1)}, bf16[144,128]{1,0:T(8,128)(2,1)S(1)}, u32[]{:S(2)}, u32[]{:S(2)}) collective-permute-start(bf16[144,128]{1,0:T(8,128)(2,1)S(1)} %pack.1.refs_3_), channel_id=1, source_target_pairs={{0,3},{1,2},{2,1},{3,0},{4,7},{5,6},{6,5},{7,4},{8,11},{9,10},{10,... | collective-permute-start | bytes 110600 | tf_op jit(solution)/shard_map/ppermute | solution.py:333
  7.0 0.2 collective-permute-start
  7.2 0.8 %collective-permute-done.2.refs_2_ = bf16[144,128]{1,0:T(8,128)(2,1)S(1)} collective-permute-done((bf16[144,128]{1,0:T(8,128)(2,1)S(1)}, bf16[144,128]{1,0:T(8,128)(2,1)S(1)}, u32[]{:S(2)}, u32[]{:S(2)}) %collective-permute-start.2) | collective-permute-done | bytes 36896 | tf_op jit(solution)/shard_map/ppermute | solution.py:333
  8.0 3.4 %collective-permute-done.1.refs_1_ = bf16[144,128]{1,0:T(8,128)(2,1)S(1)} collective-permute-done((bf16[144,128]{1,0:T(8,128)(2,1)S(1)}, bf16[144,128]{1,0:T(8,128)(2,1)S(1)}, u32[]{:S(2)}, u32[]{:S(2)}) %collective-permute-start.1) | collective-permute-done | bytes 36896 | tf_op jit(solution)/shard_map/ppermute | solution.py:333
  11.4 0.1 table.1.refs_3_.refs_0_
  11.5 2.5 %collective-permute-start.8 = (bf16[576,128]{1,0:T(8,128)(2,1)S(1)}, bf16[576,128]{1,0:T(8,128)(2,1)S(1)}, u32[]{:S(2)}, u32[]{:S(2)}) collective-permute-start(bf16[576,128]{1,0:T(8,128)(2,1)S(1)} %table.1.refs_3_.refs_0_), channel_id=1, source_target_pairs={{0,24},{4,28},{8,16},{12,20},{16,8},{20,12},{24,0},{28,4},{1,25},{... | collective-permute-start | bytes 442376 | tf_op jit(solution)/shard_map/ppermute | solution.py:333
  14.0 0.5 %collective-permute-start.6 = (bf16[576,128]{1,0:T(8,128)(2,1)S(1)}, bf16[576,128]{1,0:T(8,128)(2,1)S(1)}, u32[]{:S(2)}, u32[]{:S(2)}) collective-permute-start(bf16[576,128]{1,0:T(8,128)(2,1)S(1)} %table.1.refs_3_.refs_0_), channel_id=1, source_target_pairs={{0,16},{4,20},{8,24},{12,28},{16,0},{20,4},{24,8},{28,12},{1,17},{... | collective-permute-start | bytes 442376 | tf_op jit(solution)/shard_map/ppermute | solution.py:333
  14.5 0.5 %collective-permute-start.4 = (bf16[576,128]{1,0:T(8,128)(2,1)S(1)}, bf16[576,128]{1,0:T(8,128)(2,1)S(1)}, u32[]{:S(2)}, u32[]{:S(2)}) collective-permute-start(bf16[576,128]{1,0:T(8,128)(2,1)S(1)} %table.1.refs_3_.refs_0_), channel_id=1, source_target_pairs={{0,8},{4,12},{8,0},{12,4},{16,24},{20,28},{24,16},{28,20},{1,9},{5... | collective-permute-start | bytes 442376 | tf_op jit(solution)/shard_map/ppermute | solution.py:333
  15.0 4.1 %slots.1 = (bf16[1024,256]{1,0:T(8,128)(2,1)S(1)}, bf16[1024,256]{1,0:T(8,128)(2,1)S(1)}, bf16[256,32]{1,0:T(8,128)(2,1)S(1)}, bf16[384,256]{1,0:T(8,128)(2,1)S(...) custom-call(s32[1]{0:T(128)} %bitcast.2.me_ref, ...), custom_call_target="tpu_custom_call" | custom-call | tf_op jit(solution)/shard_map/slots/pallas_call | solution.py:382
  19.2 0.0 copy-start
  19.3 0.6 %collective-permute-start.9 = (bf16[576,128]{1,0:T(8,128)(2,1)S(1)}, bf16[576,128]{1,0:T(8,128)(2,1)S(1)}, u32[]{:S(2)}, u32[]{:S(2)}) collective-permute-start(bf16[576,128]{1,0:T(8,128)(2,1)S(1)} %collective-permute-done.8.refs_6_), channel_id=1, source_target_pairs={{0,4},{4,0},{8,12},{12,8},{16,20},{20,16},{24,28},{28,24},{1,5},{5... | collective-permute-start | bytes 442376 | tf_op jit(solution)/shard_map/ppermute | solution.py:333
  19.8 0.1 collective-permute-done.6.refs_4_
  20.0 0.6 %collective-permute-start.5 = (bf16[576,128]{1,0:T(8,128)(2,1)S(1)}, bf16[576,128]{1,0:T(8,128)(2,1)S(1)}, u32[]{:S(2)}, u32[]{:S(2)}) collective-permute-start(bf16[576,128]{1,0:T(8,128)(2,1)S(1)} %hold.1.refs_2_), channel_id=1, source_target_pairs={{0,4},{4,0},{8,12},{12,8},{16,20},{20,16},{24,28},{28,24},{1,5},{5... | collective-permute-start | bytes 442376 | tf_op jit(solution)/shard_map/ppermute | solution.py:333
  20.5 0.3 collective-permute-done.9.refs_7_
  20.9 0.5 collective-permute-done.7.refs_5_
  21.3 0.2 collective-permute-done.5.refs_3_
  21.5 5.6 %block_gradients.1 = (bf16[448,256]{1,0:T(8,128)(2,1)S(1)}, bf16[448,256]{1,0:T(8,128)(2,1)S(1)}) custom-call(bf16[576,128]{1,0:T(8,128)(2,1)S(1)} %table.1.refs_3_.refs_0_, bf16[576,128]{1,0:T(8,128)(2,1)S(1)} %collective-permute-done.3.refs_1_, bf16[576,128]{1,0:T(8,128)(2,1)S(1)} %hold.1.refs_2_, bf16[576,128]{1,0:T(8,128)(2,1)S(1)} %collective-permute-done.5.refs_3_, ...), custom_call_target="tpu_custom_call" | custom-call | tf_op jit(solution)/shard_map/block_gradients/pallas_call | solution.py:415
  27.1 0.4 collective-permute-start.10
  27.5 1.1 %collective-permute-done.10.crossed_ref.refs_1_ = bf16[448,256]{1,0:T(8,128)(2,1)S(1)} collective-permute-done((bf16[448,256]{1,0:T(8,128)(2,1)S(1)}, bf16[448,256]{1,0:T(8,128)(2,1)S(1)}, u32[]{:S(2)}, u32[]{:S(2)}) %collective-permute-start.10) | collective-permute-done | bytes 229408 | tf_op jit(solution)/shard_map/ppermute | solution.py:333
  28.7 2.4 %collective-permute-start.11 = (bf16[224,256]{1,0:T(8,128)(2,1)S(1)}, bf16[224,256]{1,0:T(8,128)(2,1)S(1)}, u32[]{:S(2)}, u32[]{:S(2)}) collective-permute-start(bf16[224,256]{1,0:T(8,128)(2,1)S(1)} %get-tuple-element.45), channel_id=1, source_target_pairs={{0,24},{4,28},{8,16},{12,20},{16,8},{20,12},{24,0},{28,4},{1,25},{... | collective-permute-start | bytes 344072 | tf_op jit(solution)/shard_map/ppermute | solution.py:333
  31.1 0.5 %collective-permute-start.12 = (bf16[224,256]{1,0:T(8,128)(2,1)S(1)}, bf16[224,256]{1,0:T(8,128)(2,1)S(1)}, u32[]{:S(2)}, u32[]{:S(2)}) collective-permute-start(bf16[224,256]{1,0:T(8,128)(2,1)S(1)} %get-tuple-element.46), channel_id=1, source_target_pairs={{0,16},{4,20},{8,24},{12,28},{16,0},{20,4},{24,8},{28,12},{1,17},{... | collective-permute-start | bytes 344072 | tf_op jit(solution)/shard_map/ppermute | solution.py:333
  31.6 0.6 %collective-permute-start.13 = (bf16[224,256]{1,0:T(8,128)(2,1)S(1)}, bf16[224,256]{1,0:T(8,128)(2,1)S(1)}, u32[]{:S(2)}, u32[]{:S(2)}) collective-permute-start(bf16[224,256]{1,0:T(8,128)(2,1)S(1)} %get-tuple-element.47), channel_id=1, source_target_pairs={{0,8},{4,12},{8,0},{12,4},{16,24},{20,28},{24,16},{28,20},{1,9},{5... | collective-permute-start | bytes 344072 | tf_op jit(solution)/shard_map/ppermute | solution.py:333
  32.2 2.9 %collective-permute-done.11.refs_2_ = bf16[224,256]{1,0:T(8,128)(2,1)S(1)} collective-permute-done((bf16[224,256]{1,0:T(8,128)(2,1)S(1)}, bf16[224,256]{1,0:T(8,128)(2,1)S(1)}, u32[]{:S(2)}, u32[]{:S(2)}) %collective-permute-start.11) | collective-permute-done | bytes 114720 | tf_op jit(solution)/shard_map/ppermute | solution.py:333
  35.2 2.4 %collective-permute-done.12.refs_3_ = bf16[224,256]{1,0:T(8,128)(2,1)S(1)} collective-permute-done((bf16[224,256]{1,0:T(8,128)(2,1)S(1)}, bf16[224,256]{1,0:T(8,128)(2,1)S(1)}, u32[]{:S(2)}, u32[]{:S(2)}) %collective-permute-start.12) | collective-permute-done | bytes 114720 | tf_op jit(solution)/shard_map/ppermute | solution.py:333
  37.5 0.6 %row_sums.1 = (bf16[144,128]{1,0:T(8,128)(2,1)S(1)}, bf16[144,128]{1,0:T(8,128)(2,1)S(1)}, bf16[144,128]{1,0:T(8,128)(2,1)S(1)}, bf16[144,128]{1,0:T(8,128)(2,1)S(1)}) custom-call(bf16[448,256]{1,0:T(8,128)(2,1)S(1)} %get-tuple-element.43.own_ref.refs_0_, bf16[448,256]{1,0:T(8,128)(2,1)S(1)} %collective-permute-done.10.crossed_ref.refs_1_, ...), custom_call_target="tpu_custom_call" | custom-call | tf_op jit(solution)/shard_map/row_sums/pallas_call | solution.py:449
  38.1 2.6 %collective-permute-start.14 = (bf16[144,128]{1,0:T(8,128)(2,1)S(1)}, bf16[144,128]{1,0:T(8,128)(2,1)S(1)}, u32[]{:S(2)}, u32[]{:S(2)}) collective-permute-start(bf16[144,128]{1,0:T(8,128)(2,1)S(1)} %get-tuple-element.49), channel_id=1, source_target_pairs={{0,3},{1,2},{2,1},{3,0},{4,7},{5,6},{6,5},{7,4},{8,11},{9,10},{10,... | collective-permute-start | bytes 110600 | tf_op jit(solution)/shard_map/ppermute | solution.py:333
  40.7 1.8 %collective-permute-start.16 = (bf16[144,128]{1,0:T(8,128)(2,1)S(1)}, bf16[144,128]{1,0:T(8,128)(2,1)S(1)}, u32[]{:S(2)}, u32[]{:S(2)}) collective-permute-start(bf16[144,128]{1,0:T(8,128)(2,1)S(1)} %get-tuple-element.51), channel_id=1, source_target_pairs={{0,1},{1,0},{2,3},{3,2},{4,5},{5,4},{6,7},{7,6},{8,9},{9,8},{10,11... | collective-permute-start | bytes 110600 | tf_op jit(solution)/shard_map/ppermute | solution.py:333
  42.5 1.4 %collective-permute-done.14.refs_1_ = bf16[144,128]{1,0:T(8,128)(2,1)S(1)} collective-permute-done((bf16[144,128]{1,0:T(8,128)(2,1)S(1)}, bf16[144,128]{1,0:T(8,128)(2,1)S(1)}, u32[]{:S(2)}, u32[]{:S(2)}) %collective-permute-start.14) | collective-permute-done | bytes 36896 | tf_op jit(solution)/shard_map/ppermute | solution.py:333
  43.9 1.7 %collective-permute-done.15.refs_2_ = bf16[144,128]{1,0:T(8,128)(2,1)S(1)} collective-permute-done((bf16[144,128]{1,0:T(8,128)(2,1)S(1)}, bf16[144,128]{1,0:T(8,128)(2,1)S(1)}, u32[]{:S(2)}, u32[]{:S(2)}) %collective-permute-start.15) | collective-permute-done | bytes 36896 | tf_op jit(solution)/shard_map/ppermute | solution.py:333
  45.6 0.7 %adam.1 = (f32[64,128]{1,0:T(8,128)}, f32[64,128]{1,0:T(8,128)}, f32[64,128]{1,0:T(8,128)}, f32[64,128]{1,0:T(8,128)}, f32[64,128]{1,0:T(8,128)}, /*index=5*/f32...) custom-call(bf16[144,128]{1,0:T(8,128)(2,1)S(1)} %get-tuple-element.48.refs_0_, ...), custom_call_target="tpu_custom_call" | custom-call | tf_op jit(solution)/shard_map/adam/pallas_call | solution.py:470
  (28 shorter events, 0.1 us)
Async XLA Ops:
  1.5 6.4 %collective-permute-start.2 = (bf16[144,128]{1,0:T(8,128)(2,1)S(1)}, bf16[144,128]{1,0:T(8,128)(2,1)S(1)}, u32[]{:S(2)}, u32[]{:S(2)}) collective-permute-start(bf16[144,128]{1,0:T(8,128)(2,1)S(1)} %pack.1.refs_3_), channel_id=1, source_target_pairs={{0,2},{1,3},{2,0},{3,1},{4,6},{5,7},{6,4},{7,5},{8,10},{9,11},{10,... | collective-permute-start | bytes 110600 | tf_op jit(solution)/shard_map/ppermute | solution.py:333
  5.6 5.8 %collective-permute-start.1 = (bf16[144,128]{1,0:T(8,128)(2,1)S(1)}, bf16[144,128]{1,0:T(8,128)(2,1)S(1)}, u32[]{:S(2)}, u32[]{:S(2)}) collective-permute-start(bf16[144,128]{1,0:T(8,128)(2,1)S(1)} %pack.1.refs_3_), channel_id=1, source_target_pairs={{0,3},{1,2},{2,1},{3,0},{4,7},{5,6},{6,5},{7,4},{8,11},{9,10},{10,... | collective-permute-start | bytes 110600 | tf_op jit(solution)/shard_map/ppermute | solution.py:333
  7.0 4.4 %collective-permute-start = (bf16[144,128]{1,0:T(8,128)(2,1)S(1)}, bf16[144,128]{1,0:T(8,128)(2,1)S(1)}, u32[]{:S(2)}, u32[]{:S(2)}) collective-permute-start(bf16[144,128]{1,0:T(8,128)(2,1)S(1)} %pack.1.refs_3_), channel_id=1, source_target_pairs={{0,1},{1,0},{2,3},{3,2},{4,5},{5,4},{6,7},{7,6},{8,9},{9,8},{10,11... | collective-permute-start | bytes 110600 | tf_op jit(solution)/shard_map/ppermute | solution.py:333
  11.5 7.7 %collective-permute-start.8 = (bf16[576,128]{1,0:T(8,128)(2,1)S(1)}, bf16[576,128]{1,0:T(8,128)(2,1)S(1)}, u32[]{:S(2)}, u32[]{:S(2)}) collective-permute-start(bf16[576,128]{1,0:T(8,128)(2,1)S(1)} %table.1.refs_3_.refs_0_), channel_id=1, source_target_pairs={{0,24},{4,28},{8,16},{12,20},{16,8},{20,12},{24,0},{28,4},{1,25},{... | collective-permute-start | bytes 442376 | tf_op jit(solution)/shard_map/ppermute | solution.py:333
  14.0 6.0 %collective-permute-start.6 = (bf16[576,128]{1,0:T(8,128)(2,1)S(1)}, bf16[576,128]{1,0:T(8,128)(2,1)S(1)}, u32[]{:S(2)}, u32[]{:S(2)}) collective-permute-start(bf16[576,128]{1,0:T(8,128)(2,1)S(1)} %table.1.refs_3_.refs_0_), channel_id=1, source_target_pairs={{0,16},{4,20},{8,24},{12,28},{16,0},{20,4},{24,8},{28,12},{1,17},{... | collective-permute-start | bytes 442376 | tf_op jit(solution)/shard_map/ppermute | solution.py:333
  14.5 5.4 %collective-permute-start.4 = (bf16[576,128]{1,0:T(8,128)(2,1)S(1)}, bf16[576,128]{1,0:T(8,128)(2,1)S(1)}, u32[]{:S(2)}, u32[]{:S(2)}) collective-permute-start(bf16[576,128]{1,0:T(8,128)(2,1)S(1)} %table.1.refs_3_.refs_0_), channel_id=1, source_target_pairs={{0,8},{4,12},{8,0},{12,4},{16,24},{20,28},{24,16},{28,20},{1,9},{5... | collective-permute-start | bytes 442376 | tf_op jit(solution)/shard_map/ppermute | solution.py:333
  15.0 5.5 %collective-permute-start.3 = (bf16[576,128]{1,0:T(8,128)(2,1)S(1)}, bf16[576,128]{1,0:T(8,128)(2,1)S(1)}, u32[]{:S(2)}, u32[]{:S(2)}) collective-permute-start(bf16[576,128]{1,0:T(8,128)(2,1)S(1)} %table.1.refs_3_.refs_0_), channel_id=1, source_target_pairs={{0,4},{4,0},{8,12},{12,8},{16,20},{20,16},{24,28},{28,24},{1,5},{5... | collective-permute-start | bytes 442376 | tf_op jit(solution)/shard_map/ppermute | solution.py:333
  19.2 26.4 %copy-start = (f32[128,64]{0,1:T(8,128)S(1)}, f32[128,64]{0,1:T(8,128)}, u32[]{:S(2)}) copy-start(f32[128,64]{0,1:T(8,128)} %param.17) | copy-start | bytes 98308
  19.2 26.4 %copy-start.1 = (f32[128,64]{0,1:T(8,128)S(1)}, f32[128,64]{0,1:T(8,128)}, u32[]{:S(2)}) copy-start(f32[128,64]{0,1:T(8,128)} %param.20) | copy-start | bytes 98308
  19.2 26.4 %copy-start.2 = (f32[32,64]{1,0:T(8,128)S(1)}, f32[32,64]{1,0:T(8,128)}, u32[]{:S(2)}) copy-start(f32[32,64]{1,0:T(8,128)} %refs_10_.1) | copy-start | bytes 24580
  19.2 26.4 %copy-start.3 = (f32[128,64]{0,1:T(8,128)S(1)}, f32[128,64]{0,1:T(8,128)}, u32[]{:S(2)}) copy-start(f32[128,64]{0,1:T(8,128)} %param.18) | copy-start | bytes 98308
  19.2 26.4 %copy-start.4 = (f32[128,64]{0,1:T(8,128)S(1)}, f32[128,64]{0,1:T(8,128)}, u32[]{:S(2)}) copy-start(f32[128,64]{0,1:T(8,128)} %param.19) | copy-start | bytes 98308
  19.2 26.4 %copy-start.5 = (f32[128,64]{0,1:T(8,128)S(1)}, f32[128,64]{0,1:T(8,128)}, u32[]{:S(2)}) copy-start(f32[128,64]{0,1:T(8,128)} %param.21) | copy-start | bytes 98308
  19.2 26.4 %copy-start.6 = (f32[128,64]{0,1:T(8,128)S(1)}, f32[128,64]{0,1:T(8,128)}, u32[]{:S(2)}) copy-start(f32[128,64]{0,1:T(8,128)} %param.22) | copy-start | bytes 98308
  19.2 26.4 %copy-start.7 = (f32[32,64]{1,0:T(8,128)S(1)}, f32[32,64]{1,0:T(8,128)}, u32[]{:S(2)}) copy-start(f32[32,64]{1,0:T(8,128)} %refs_11_.1) | copy-start | bytes 24580
  19.3 26.4 %copy-start.8 = (f32[32,64]{1,0:T(8,128)S(1)}, f32[32,64]{1,0:T(8,128)}, u32[]{:S(2)}) copy-start(f32[32,64]{1,0:T(8,128)} %refs_12_.1) | copy-start | bytes 24580
  19.3 1.6 %collective-permute-start.9 = (bf16[576,128]{1,0:T(8,128)(2,1)S(1)}, bf16[576,128]{1,0:T(8,128)(2,1)S(1)}, u32[]{:S(2)}, u32[]{:S(2)}) collective-permute-start(bf16[576,128]{1,0:T(8,128)(2,1)S(1)} %collective-permute-done.8.refs_6_), channel_id=1, source_target_pairs={{0,4},{4,0},{8,12},{12,8},{16,20},{20,16},{24,28},{28,24},{1,5},{5... | collective-permute-start | bytes 442376 | tf_op jit(solution)/shard_map/ppermute | solution.py:333
  19.9 1.4 %collective-permute-start.7 = (bf16[576,128]{1,0:T(8,128)(2,1)S(1)}, bf16[576,128]{1,0:T(8,128)(2,1)S(1)}, u32[]{:S(2)}, u32[]{:S(2)}) collective-permute-start(bf16[576,128]{1,0:T(8,128)(2,1)S(1)} %collective-permute-done.6.refs_4_), channel_id=1, source_target_pairs={{0,4},{4,0},{8,12},{12,8},{16,20},{20,16},{24,28},{28,24},{1,5},{5... | collective-permute-start | bytes 442376 | tf_op jit(solution)/shard_map/ppermute | solution.py:333
  20.0 1.6 %collective-permute-start.5 = (bf16[576,128]{1,0:T(8,128)(2,1)S(1)}, bf16[576,128]{1,0:T(8,128)(2,1)S(1)}, u32[]{:S(2)}, u32[]{:S(2)}) collective-permute-start(bf16[576,128]{1,0:T(8,128)(2,1)S(1)} %hold.1.refs_2_), channel_id=1, source_target_pairs={{0,4},{4,0},{8,12},{12,8},{16,20},{20,16},{24,28},{28,24},{1,5},{5... | collective-permute-start | bytes 442376 | tf_op jit(solution)/shard_map/ppermute | solution.py:333
  27.1 1.6 %collective-permute-start.10 = (bf16[448,256]{1,0:T(8,128)(2,1)S(1)}, bf16[448,256]{1,0:T(8,128)(2,1)S(1)}, u32[]{:S(2)}, u32[]{:S(2)}) collective-permute-start(bf16[448,256]{1,0:T(8,128)(2,1)S(1)} %get-tuple-element.44), channel_id=1, source_target_pairs={{0,4},{4,0},{8,12},{12,8},{16,20},{20,16},{24,28},{28,24},{1,5},{5... | collective-permute-start | bytes 688136 | tf_op jit(solution)/shard_map/ppermute | solution.py:333
  28.7 6.5 %collective-permute-start.11 = (bf16[224,256]{1,0:T(8,128)(2,1)S(1)}, bf16[224,256]{1,0:T(8,128)(2,1)S(1)}, u32[]{:S(2)}, u32[]{:S(2)}) collective-permute-start(bf16[224,256]{1,0:T(8,128)(2,1)S(1)} %get-tuple-element.45), channel_id=1, source_target_pairs={{0,24},{4,28},{8,16},{12,20},{16,8},{20,12},{24,0},{28,4},{1,25},{... | collective-permute-start | bytes 344072 | tf_op jit(solution)/shard_map/ppermute | solution.py:333
  31.1 6.4 %collective-permute-start.12 = (bf16[224,256]{1,0:T(8,128)(2,1)S(1)}, bf16[224,256]{1,0:T(8,128)(2,1)S(1)}, u32[]{:S(2)}, u32[]{:S(2)}) collective-permute-start(bf16[224,256]{1,0:T(8,128)(2,1)S(1)} %get-tuple-element.46), channel_id=1, source_target_pairs={{0,16},{4,20},{8,24},{12,28},{16,0},{20,4},{24,8},{28,12},{1,17},{... | collective-permute-start | bytes 344072 | tf_op jit(solution)/shard_map/ppermute | solution.py:333
  31.6 5.9 %collective-permute-start.13 = (bf16[224,256]{1,0:T(8,128)(2,1)S(1)}, bf16[224,256]{1,0:T(8,128)(2,1)S(1)}, u32[]{:S(2)}, u32[]{:S(2)}) collective-permute-start(bf16[224,256]{1,0:T(8,128)(2,1)S(1)} %get-tuple-element.47), channel_id=1, source_target_pairs={{0,8},{4,12},{8,0},{12,4},{16,24},{20,28},{24,16},{28,20},{1,9},{5... | collective-permute-start | bytes 344072 | tf_op jit(solution)/shard_map/ppermute | solution.py:333
  38.1 5.8 %collective-permute-start.14 = (bf16[144,128]{1,0:T(8,128)(2,1)S(1)}, bf16[144,128]{1,0:T(8,128)(2,1)S(1)}, u32[]{:S(2)}, u32[]{:S(2)}) collective-permute-start(bf16[144,128]{1,0:T(8,128)(2,1)S(1)} %get-tuple-element.49), channel_id=1, source_target_pairs={{0,3},{1,2},{2,1},{3,0},{4,7},{5,6},{6,5},{7,4},{8,11},{9,10},{10,... | collective-permute-start | bytes 110600 | tf_op jit(solution)/shard_map/ppermute | solution.py:333
  40.7 4.9 %collective-permute-start.15 = (bf16[144,128]{1,0:T(8,128)(2,1)S(1)}, bf16[144,128]{1,0:T(8,128)(2,1)S(1)}, u32[]{:S(2)}, u32[]{:S(2)}) collective-permute-start(bf16[144,128]{1,0:T(8,128)(2,1)S(1)} %get-tuple-element.50), channel_id=1, source_target_pairs={{0,2},{1,3},{2,0},{3,1},{4,6},{5,7},{6,4},{7,5},{8,10},{9,11},{10,... | collective-permute-start | bytes 110600 | tf_op jit(solution)/shard_map/ppermute | solution.py:333
  40.7 4.9 %collective-permute-start.16 = (bf16[144,128]{1,0:T(8,128)(2,1)S(1)}, bf16[144,128]{1,0:T(8,128)(2,1)S(1)}, u32[]{:S(2)}, u32[]{:S(2)}) collective-permute-start(bf16[144,128]{1,0:T(8,128)(2,1)S(1)} %get-tuple-element.51), channel_id=1, source_target_pairs={{0,1},{1,0},{2,3},{3,2},{4,5},{5,4},{6,7},{7,6},{8,9},{9,8},{10,11... | collective-permute-start | bytes 110600 | tf_op jit(solution)/shard_map/ppermute | solution.py:333

commit v14 on v13

--- a/solution.py
+++ b/solution.py
@@ -18,7 +18,8 @@
 LANES = 128
 HOLD = 2
 SMALL_VMEM = 16 * 1024 * 1024
-BLOCK_VMEM = 24 * 1024 * 1024
+LARGE_VMEM = 32 * 1024 * 1024
+STATUS_PARTS = 4
 
 f32 = jnp.float32
 bf16 = jnp.bfloat16
@@ -106,11 +107,19 @@
 
 def slot_kernel(sizes, me_ref, *refs):
     owners = sizes.owners
-    picks, places, note_ref, status_ref = refs[5:8], refs[8:11], refs[11], refs[12]
-    lists, semaphores, status_semaphore = refs[13:16], refs[16], refs[17]
-    status_copy = pltpu.make_async_copy(refs[4].at[0], status_ref, status_semaphore.at[0])
+    picks, places, note_ref, weight_ref, shift_ref = refs[5:8], refs[8:11], *refs[11:14]
+    lists, semaphores, status, status_semaphores = refs[14:17], *refs[17:20]
+    size = status.shape[0] // STATUS_PARTS
+
+    def status_copy(n):
+        part = pl.ds(n * size, size)
+        return pltpu.make_async_copy(
+            refs[4].at[0, part], status.at[part], status_semaphores.at[n]
+        )
+
     fetch(refs[:3], lists, semaphores)
-    status_copy.start()
+    for n in range(STATUS_PARTS):
+        status_copy(n).start()
     me = me_ref[0]
     notes = [[] for _ in range(owners)]
     for t in range(3):
@@ -134,7 +143,15 @@
     note_ref[...] = jnp.concatenate(
         [jnp.concatenate(note + [blank], axis=1) for note in notes], axis=0
     )
-    status_copy.wait()
+    for n in range(STATUS_PARTS):
+        status_copy(n).wait()
+
+        @pl.loop(n * size, (n + 1) * size)
+        def _(k):
+            state = status[k]
+            weight = state.astype(f32)
+            weight_ref[k] = weight
+            shift_ref[k] = jnp.where(state == 1, -weight, weight)
 
 
 def table_kernel(sizes, *refs):
@@ -158,7 +175,7 @@
     owners, rank, day_rows = sizes.owners, sizes.rank, sizes.row_counts[2]
     tables, refs = refs[:owners], refs[owners:]
     picks, places = refs[:3], refs[3:6]
-    note_ref, status, own_ref, other_ref = refs[6:10]
+    note_ref, weights, shifts, own_ref, other_ref = refs[6:11]
     (
         users,
         users_low,
@@ -172,9 +189,9 @@
         scaled_odd,
         residual_even,
         residual_odd,
-    ) = refs[10:]
+    ) = refs[11:]
     pair = 4
-    pairs = status.shape[0] // pair
+    pairs = weights.shape[0] // pair
     def pick(t):
         table = jnp.concatenate([ref[t * rank : (t + 1) * rank, :] for ref in tables], axis=1)
         return jnp.dot(table, picks[t][...], preferred_element_type=f32)
@@ -207,10 +224,8 @@
         half_logits = jnp.dot(scaled[...], items_half_t[...], preferred_element_type=f32)
         for j in range(pair):
             rows = slice(j * count, (j + 1) * count)
-            state = status[first + j]
             residual[rows, :] = (
-                state.astype(f32)
-                * (jnp.tanh(half_logits[rows]) + jnp.where(state == 1, -1.0, 1.0))
+                weights[first + j] * jnp.tanh(half_logits[rows]) + shifts[first + j]
             ).astype(bf16)
 
     def gradients(first, scaled, residual):
@@ -355,6 +370,7 @@
     sizes = Sizes(owners, holders, user_factor.shape[1], row_counts, list_counts)
     shape = jax.ShapeDtypeStruct
     small = pltpu.CompilerParams(vmem_limit_bytes=SMALL_VMEM)
+    large = pltpu.CompilerParams(vmem_limit_bytes=LARGE_VMEM)
 
     hbm = pl.BlockSpec(memory_space=pltpu.HBM)
     in_hbm = lambda a: pltpu.with_memory_space_constraint(a, pltpu.HBM)
@@ -384,14 +400,19 @@
         out_shape=tuple(
             [shape((owners * row_counts[t], list_counts[t]), bf16) for t in range(3)]
             + [shape((owners * sizes.slots[t], list_counts[t]), bf16) for t in range(3)]
-            + [shape((owners, sizes.rank), f32), shape(status.shape[1:], jnp.int32)]
+            + [shape((owners, sizes.rank), f32)]
+            + [shape(status.shape[1:], f32)] * 2
         ),
         in_specs=[pl.BlockSpec(memory_space=pltpu.SMEM)]
         + [hbm] * 3
         + [pl.BlockSpec(memory_space=pl.ANY), hbm],
         scratch_shapes=[pltpu.VMEM((1, count), jnp.int32) for count in list_counts]
-        + [pltpu.SemaphoreType.DMA((3,)), pltpu.SemaphoreType.DMA((1,))],
-        compiler_params=small,
+        + [
+            pltpu.SemaphoreType.DMA((3,)),
+            pltpu.VMEM(status.shape[1:], jnp.int32),
+            pltpu.SemaphoreType.DMA((STATUS_PARTS,)),
+        ],
+        compiler_params=large,
         name="slots",
     )(
         lax.axis_index("dp").astype(jnp.int32).reshape(1),
@@ -430,7 +451,7 @@
             pltpu.VMEM((4 * users, items), bf16),
             pltpu.VMEM((4 * users, items), bf16),
         ],
-        compiler_params=pltpu.CompilerParams(vmem_limit_bytes=BLOCK_VMEM),
+        compiler_params=large,
         name="block_gradients",
     )(*inputs)
     crossed = swap(other, "dp", owners, 1)
@@ -442,9 +463,7 @@
         name="merge",
     )(own, crossed)
     returned = [own, crossed]
-    returned += [
-        swap(merged[bits // 2 - 1], "dp", owners, bits) for bits in range(owners - 2, 0, -2)
-    ]
+    returned += [swap(merged[bits // 2 - 1], "dp", owners, bits) for bits in range(2, owners, 2)]
 
     totals = pl.pallas_call(
         functools.partial(sum_kernel, sizes),

time: 46.6 us -> 47.1 us (1.011)
  Pallas kernels: 12 us -> 12.9 us
    pallas_call x1, Pallas kernels: 4.11 us -> 4.76 us  [local(): pl.pallas_call(functools.partial(slot_kernel, sizes), out_shape=tuple([sh...]
  transfers between devices with their start and end apart: 17 -> 17, of which waited for: 11 -> 10; matrix products, arithmetic and copies ran while one was open for 0% -> 0% of each run, Pallas kernels for 9% -> 10%
where the time goes in v14:
time: 47.1 us; the launch traced here: 46.9 us
  starting transfers between devices  18.8 us (40%)
  waiting for transfers between devices  14.4 us (31%)
  Pallas kernels  12.9 us (27%)
  between operations  0.8 us (2%)
    ppermute x17, starting transfers between devices, swap(): return lax.ppermute(array, axis, [(i, i ^ bits) for i in range(size)])  18.8 us
    ppermute x17, waiting for transfers between devices, swap(): return lax.ppermute(array, axis, [(i, i ^ bits) for i in range(size)])  14.4 us
    pallas_call x1, Pallas kernels, local(): pl.pallas_call(functools.partial(block_kernel, sizes), out_shape=(half, h...  5.77 us
    pallas_call x1, Pallas kernels, local(): pl.pallas_call(functools.partial(slot_kernel, sizes), out_shape=tuple([sh...  4.76 us
  transfers between devices with their start and end apart: 17, of which 10 were waited for; matrix products, arithmetic and copies ran while one was open for 0% of the time, Pallas kernels for 10%

profile of v14, /device:TPU:0, one launch (start us, length us, event | category | flops | bytes accessed | tf_op | source)
XLA Modules:
  0.0 46.9 jit_solution(2659496718851224131)
XLA Ops:
  0.6 0.9 %pack.1.refs_3_ = bf16[144,128]{1,0:T(8,128)(2,1)S(1)} custom-call(f32[64,128]{1,0:T(8,128)} %bitcast.13, f32[64,128]{1,0:T(8,128)} %bitcast.15, f32[32,64]{1,0:T(8,128)} %refs_10_.1), custom_call_target="tpu_custom_call" | custom-call | tf_op jit(solution)/shard_map/pack/pallas_call | solution.py:378
  1.5 4.1 %collective-permute-start.2 = (bf16[144,128]{1,0:T(8,128)(2,1)S(1)}, bf16[144,128]{1,0:T(8,128)(2,1)S(1)}, u32[]{:S(2)}, u32[]{:S(2)}) collective-permute-start(bf16[144,128]{1,0:T(8,128)(2,1)S(1)} %pack.1.refs_3_), channel_id=1, source_target_pairs={{0,2},{1,3},{2,0},{3,1},{4,6},{5,7},{6,4},{7,5},{8,10},{9,11},{10,... | collective-permute-start | bytes 110600 | tf_op jit(solution)/shard_map/ppermute | solution.py:348
  5.6 1.3 %collective-permute-start.1 = (bf16[144,128]{1,0:T(8,128)(2,1)S(1)}, bf16[144,128]{1,0:T(8,128)(2,1)S(1)}, u32[]{:S(2)}, u32[]{:S(2)}) collective-permute-start(bf16[144,128]{1,0:T(8,128)(2,1)S(1)} %pack.1.refs_3_), channel_id=1, source_target_pairs={{0,3},{1,2},{2,1},{3,0},{4,7},{5,6},{6,5},{7,4},{8,11},{9,10},{10,... | collective-permute-start | bytes 110600 | tf_op jit(solution)/shard_map/ppermute | solution.py:348
  7.0 0.2 collective-permute-start
  7.2 0.8 %collective-permute-done.2.refs_2_ = bf16[144,128]{1,0:T(8,128)(2,1)S(1)} collective-permute-done((bf16[144,128]{1,0:T(8,128)(2,1)S(1)}, bf16[144,128]{1,0:T(8,128)(2,1)S(1)}, u32[]{:S(2)}, u32[]{:S(2)}) %collective-permute-start.2) | collective-permute-done | bytes 36896 | tf_op jit(solution)/shard_map/ppermute | solution.py:348
  8.0 3.4 %collective-permute-done.1.refs_1_ = bf16[144,128]{1,0:T(8,128)(2,1)S(1)} collective-permute-done((bf16[144,128]{1,0:T(8,128)(2,1)S(1)}, bf16[144,128]{1,0:T(8,128)(2,1)S(1)}, u32[]{:S(2)}, u32[]{:S(2)}) %collective-permute-start.1) | collective-permute-done | bytes 36896 | tf_op jit(solution)/shard_map/ppermute | solution.py:348
  11.4 0.1 table.1.refs_3_.refs_0_
  11.5 2.5 %collective-permute-start.8 = (bf16[576,128]{1,0:T(8,128)(2,1)S(1)}, bf16[576,128]{1,0:T(8,128)(2,1)S(1)}, u32[]{:S(2)}, u32[]{:S(2)}) collective-permute-start(bf16[576,128]{1,0:T(8,128)(2,1)S(1)} %table.1.refs_3_.refs_0_), channel_id=1, source_target_pairs={{0,24},{4,28},{8,16},{12,20},{16,8},{20,12},{24,0},{28,4},{1,25},{... | collective-permute-start | bytes 442376 | tf_op jit(solution)/shard_map/ppermute | solution.py:348
  14.0 0.5 %collective-permute-start.6 = (bf16[576,128]{1,0:T(8,128)(2,1)S(1)}, bf16[576,128]{1,0:T(8,128)(2,1)S(1)}, u32[]{:S(2)}, u32[]{:S(2)}) collective-permute-start(bf16[576,128]{1,0:T(8,128)(2,1)S(1)} %table.1.refs_3_.refs_0_), channel_id=1, source_target_pairs={{0,16},{4,20},{8,24},{12,28},{16,0},{20,4},{24,8},{28,12},{1,17},{... | collective-permute-start | bytes 442376 | tf_op jit(solution)/shard_map/ppermute | solution.py:348
  14.5 0.5 %collective-permute-start.4 = (bf16[576,128]{1,0:T(8,128)(2,1)S(1)}, bf16[576,128]{1,0:T(8,128)(2,1)S(1)}, u32[]{:S(2)}, u32[]{:S(2)}) collective-permute-start(bf16[576,128]{1,0:T(8,128)(2,1)S(1)} %table.1.refs_3_.refs_0_), channel_id=1, source_target_pairs={{0,8},{4,12},{8,0},{12,4},{16,24},{20,28},{24,16},{28,20},{1,9},{5... | collective-permute-start | bytes 442376 | tf_op jit(solution)/shard_map/ppermute | solution.py:348
  15.0 4.8 %slots.1 = (bf16[1024,256]{1,0:T(8,128)(2,1)S(1)}, bf16[1024,256]{1,0:T(8,128)(2,1)S(1)}, bf16[256,32]{1,0:T(8,128)(2,1)S(1)}, bf16[384,256]{1,0:T(8,128)(2,1)S(...) custom-call(s32[1]{0:T(128)} %bitcast.2.me_ref, ...), custom_call_target="tpu_custom_call" | custom-call | tf_op jit(solution)/shard_map/slots/pallas_call | solution.py:398
  19.8 0.6 %collective-permute-start.9 = (bf16[576,128]{1,0:T(8,128)(2,1)S(1)}, bf16[576,128]{1,0:T(8,128)(2,1)S(1)}, u32[]{:S(2)}, u32[]{:S(2)}) collective-permute-start(bf16[576,128]{1,0:T(8,128)(2,1)S(1)} %collective-permute-done.8.refs_6_), channel_id=1, source_target_pairs={{0,4},{4,0},{8,12},{12,8},{16,20},{20,16},{24,28},{28,24},{1,5},{5... | collective-permute-start | bytes 442376 | tf_op jit(solution)/shard_map/ppermute | solution.py:348
  20.4 0.1 collective-permute-start.7
  20.5 0.5 %collective-permute-start.5 = (bf16[576,128]{1,0:T(8,128)(2,1)S(1)}, bf16[576,128]{1,0:T(8,128)(2,1)S(1)}, u32[]{:S(2)}, u32[]{:S(2)}) collective-permute-start(bf16[576,128]{1,0:T(8,128)(2,1)S(1)} %hold.1.refs_2_), channel_id=1, source_target_pairs={{0,4},{4,0},{8,12},{12,8},{16,20},{20,16},{24,28},{28,24},{1,5},{5... | collective-permute-start | bytes 442376 | tf_op jit(solution)/shard_map/ppermute | solution.py:348
  21.0 0.4 collective-permute-done.9.refs_7_
  21.4 0.4 collective-permute-done.7.refs_5_
  21.8 0.2 collective-permute-done.5.refs_3_
  22.0 0.0 copy-start.7
  22.1 5.8 %block_gradients.1 = (bf16[448,256]{1,0:T(8,128)(2,1)S(1)}, bf16[448,256]{1,0:T(8,128)(2,1)S(1)}) custom-call(bf16[576,128]{1,0:T(8,128)(2,1)S(1)} %table.1.refs_3_.refs_0_, bf16[576,128]{1,0:T(8,128)(2,1)S(1)} %collective-permute-done.3.refs_1_, bf16[576,128]{1,0:T(8,128)(2,1)S(1)} %hold.1.refs_2_, bf16[576,128]{1,0:T(8,128)(2,1)S(1)} %collective-permute-done.5.refs_3_, ...), custom_call_target="tpu_custom_call" | custom-call | tf_op jit(solution)/shard_map/block_gradients/pallas_call | solution.py:436
  27.8 0.4 collective-permute-start.10
  28.3 1.1 %collective-permute-done.10.crossed_ref.refs_1_ = bf16[448,256]{1,0:T(8,128)(2,1)S(1)} collective-permute-done((bf16[448,256]{1,0:T(8,128)(2,1)S(1)}, bf16[448,256]{1,0:T(8,128)(2,1)S(1)}, u32[]{:S(2)}, u32[]{:S(2)}) %collective-permute-start.10) | collective-permute-done | bytes 229408 | tf_op jit(solution)/shard_map/ppermute | solution.py:348
  29.4 1.6 %collective-permute-start.11 = (bf16[224,256]{1,0:T(8,128)(2,1)S(1)}, bf16[224,256]{1,0:T(8,128)(2,1)S(1)}, u32[]{:S(2)}, u32[]{:S(2)}) collective-permute-start(bf16[224,256]{1,0:T(8,128)(2,1)S(1)} %get-tuple-element.47), channel_id=1, source_target_pairs={{0,8},{4,12},{8,0},{12,4},{16,24},{20,28},{24,16},{28,20},{1,9},{5... | collective-permute-start | bytes 344072 | tf_op jit(solution)/shard_map/ppermute | solution.py:348
  31.0 1.5 %collective-permute-start.12 = (bf16[224,256]{1,0:T(8,128)(2,1)S(1)}, bf16[224,256]{1,0:T(8,128)(2,1)S(1)}, u32[]{:S(2)}, u32[]{:S(2)}) collective-permute-start(bf16[224,256]{1,0:T(8,128)(2,1)S(1)} %get-tuple-element.48), channel_id=1, source_target_pairs={{0,16},{4,20},{8,24},{12,28},{16,0},{20,4},{24,8},{28,12},{1,17},{... | collective-permute-start | bytes 344072 | tf_op jit(solution)/shard_map/ppermute | solution.py:348
  32.5 0.5 %collective-permute-start.13 = (bf16[224,256]{1,0:T(8,128)(2,1)S(1)}, bf16[224,256]{1,0:T(8,128)(2,1)S(1)}, u32[]{:S(2)}, u32[]{:S(2)}) collective-permute-start(bf16[224,256]{1,0:T(8,128)(2,1)S(1)} %get-tuple-element.49), channel_id=1, source_target_pairs={{0,24},{4,28},{8,16},{12,20},{16,8},{20,12},{24,0},{28,4},{1,25},{... | collective-permute-start | bytes 344072 | tf_op jit(solution)/shard_map/ppermute | solution.py:348
  33.0 1.9 %collective-permute-done.11.refs_2_ = bf16[224,256]{1,0:T(8,128)(2,1)S(1)} collective-permute-done((bf16[224,256]{1,0:T(8,128)(2,1)S(1)}, bf16[224,256]{1,0:T(8,128)(2,1)S(1)}, u32[]{:S(2)}, u32[]{:S(2)}) %collective-permute-start.11) | collective-permute-done | bytes 114720 | tf_op jit(solution)/shard_map/ppermute | solution.py:348
  34.9 3.7 %collective-permute-done.12.refs_3_ = bf16[224,256]{1,0:T(8,128)(2,1)S(1)} collective-permute-done((bf16[224,256]{1,0:T(8,128)(2,1)S(1)}, bf16[224,256]{1,0:T(8,128)(2,1)S(1)}, u32[]{:S(2)}, u32[]{:S(2)}) %collective-permute-start.12) | collective-permute-done | bytes 114720 | tf_op jit(solution)/shard_map/ppermute | solution.py:348
  38.6 0.6 %row_sums.1 = (bf16[144,128]{1,0:T(8,128)(2,1)S(1)}, bf16[144,128]{1,0:T(8,128)(2,1)S(1)}, bf16[144,128]{1,0:T(8,128)(2,1)S(1)}, bf16[144,128]{1,0:T(8,128)(2,1)S(1)}) custom-call(bf16[448,256]{1,0:T(8,128)(2,1)S(1)} %get-tuple-element.45.own_ref.refs_0_, bf16[448,256]{1,0:T(8,128)(2,1)S(1)} %collective-permute-done.10.crossed_ref.refs_1_, ...), custom_call_target="tpu_custom_call" | custom-call | tf_op jit(solution)/shard_map/row_sums/pallas_call | solution.py:468
  39.2 2.1 %collective-permute-start.14 = (bf16[144,128]{1,0:T(8,128)(2,1)S(1)}, bf16[144,128]{1,0:T(8,128)(2,1)S(1)}, u32[]{:S(2)}, u32[]{:S(2)}) collective-permute-start(bf16[144,128]{1,0:T(8,128)(2,1)S(1)} %get-tuple-element.51), channel_id=1, source_target_pairs={{0,3},{1,2},{2,1},{3,0},{4,7},{5,6},{6,5},{7,4},{8,11},{9,10},{10,... | collective-permute-start | bytes 110600 | tf_op jit(solution)/shard_map/ppermute | solution.py:348
  41.2 2.4 %collective-permute-start.16 = (bf16[144,128]{1,0:T(8,128)(2,1)S(1)}, bf16[144,128]{1,0:T(8,128)(2,1)S(1)}, u32[]{:S(2)}, u32[]{:S(2)}) collective-permute-start(bf16[144,128]{1,0:T(8,128)(2,1)S(1)} %get-tuple-element.53), channel_id=1, source_target_pairs={{0,1},{1,0},{2,3},{3,2},{4,5},{5,4},{6,7},{7,6},{8,9},{9,8},{10,11... | collective-permute-start | bytes 110600 | tf_op jit(solution)/shard_map/ppermute | solution.py:348
  43.6 1.6 %collective-permute-done.14.refs_1_ = bf16[144,128]{1,0:T(8,128)(2,1)S(1)} collective-permute-done((bf16[144,128]{1,0:T(8,128)(2,1)S(1)}, bf16[144,128]{1,0:T(8,128)(2,1)S(1)}, u32[]{:S(2)}, u32[]{:S(2)}) %collective-permute-start.14) | collective-permute-done | bytes 36896 | tf_op jit(solution)/shard_map/ppermute | solution.py:348
  45.2 0.8 %collective-permute-done.15.refs_2_ = bf16[144,128]{1,0:T(8,128)(2,1)S(1)} collective-permute-done((bf16[144,128]{1,0:T(8,128)(2,1)S(1)}, bf16[144,128]{1,0:T(8,128)(2,1)S(1)}, u32[]{:S(2)}, u32[]{:S(2)}) %collective-permute-start.15) | collective-permute-done | bytes 36896 | tf_op jit(solution)/shard_map/ppermute | solution.py:348
  46.2 0.7 %adam.1 = (f32[64,128]{1,0:T(8,128)}, f32[64,128]{1,0:T(8,128)}, f32[64,128]{1,0:T(8,128)}, f32[64,128]{1,0:T(8,128)}, f32[64,128]{1,0:T(8,128)}, /*index=5*/f32...) custom-call(bf16[144,128]{1,0:T(8,128)(2,1)S(1)} %get-tuple-element.50.refs_0_, ...), custom_call_target="tpu_custom_call" | custom-call | tf_op jit(solution)/shard_map/adam/pallas_call | solution.py:489
  (28 shorter events, 0.1 us)
Async XLA Ops:
  1.5 6.4 %collective-permute-start.2 = (bf16[144,128]{1,0:T(8,128)(2,1)S(1)}, bf16[144,128]{1,0:T(8,128)(2,1)S(1)}, u32[]{:S(2)}, u32[]{:S(2)}) collective-permute-start(bf16[144,128]{1,0:T(8,128)(2,1)S(1)} %pack.1.refs_3_), channel_id=1, source_target_pairs={{0,2},{1,3},{2,0},{3,1},{4,6},{5,7},{6,4},{7,5},{8,10},{9,11},{10,... | collective-permute-start | bytes 110600 | tf_op jit(solution)/shard_map/ppermute | solution.py:348
  5.6 5.8 %collective-permute-start.1 = (bf16[144,128]{1,0:T(8,128)(2,1)S(1)}, bf16[144,128]{1,0:T(8,128)(2,1)S(1)}, u32[]{:S(2)}, u32[]{:S(2)}) collective-permute-start(bf16[144,128]{1,0:T(8,128)(2,1)S(1)} %pack.1.refs_3_), channel_id=1, source_target_pairs={{0,3},{1,2},{2,1},{3,0},{4,7},{5,6},{6,5},{7,4},{8,11},{9,10},{10,... | collective-permute-start | bytes 110600 | tf_op jit(solution)/shard_map/ppermute | solution.py:348
  7.0 4.4 %collective-permute-start = (bf16[144,128]{1,0:T(8,128)(2,1)S(1)}, bf16[144,128]{1,0:T(8,128)(2,1)S(1)}, u32[]{:S(2)}, u32[]{:S(2)}) collective-permute-start(bf16[144,128]{1,0:T(8,128)(2,1)S(1)} %pack.1.refs_3_), channel_id=1, source_target_pairs={{0,1},{1,0},{2,3},{3,2},{4,5},{5,4},{6,7},{7,6},{8,9},{9,8},{10,11... | collective-permute-start | bytes 110600 | tf_op jit(solution)/shard_map/ppermute | solution.py:348
  11.5 8.3 %collective-permute-start.8 = (bf16[576,128]{1,0:T(8,128)(2,1)S(1)}, bf16[576,128]{1,0:T(8,128)(2,1)S(1)}, u32[]{:S(2)}, u32[]{:S(2)}) collective-permute-start(bf16[576,128]{1,0:T(8,128)(2,1)S(1)} %table.1.refs_3_.refs_0_), channel_id=1, source_target_pairs={{0,24},{4,28},{8,16},{12,20},{16,8},{20,12},{24,0},{28,4},{1,25},{... | collective-permute-start | bytes 442376 | tf_op jit(solution)/shard_map/ppermute | solution.py:348
  14.0 6.4 %collective-permute-start.6 = (bf16[576,128]{1,0:T(8,128)(2,1)S(1)}, bf16[576,128]{1,0:T(8,128)(2,1)S(1)}, u32[]{:S(2)}, u32[]{:S(2)}) collective-permute-start(bf16[576,128]{1,0:T(8,128)(2,1)S(1)} %table.1.refs_3_.refs_0_), channel_id=1, source_target_pairs={{0,16},{4,20},{8,24},{12,28},{16,0},{20,4},{24,8},{28,12},{1,17},{... | collective-permute-start | bytes 442376 | tf_op jit(solution)/shard_map/ppermute | solution.py:348
  14.5 6.0 %collective-permute-start.4 = (bf16[576,128]{1,0:T(8,128)(2,1)S(1)}, bf16[576,128]{1,0:T(8,128)(2,1)S(1)}, u32[]{:S(2)}, u32[]{:S(2)}) collective-permute-start(bf16[576,128]{1,0:T(8,128)(2,1)S(1)} %table.1.refs_3_.refs_0_), channel_id=1, source_target_pairs={{0,8},{4,12},{8,0},{12,4},{16,24},{20,28},{24,16},{28,20},{1,9},{5... | collective-permute-start | bytes 442376 | tf_op jit(solution)/shard_map/ppermute | solution.py:348
  15.0 6.0 %collective-permute-start.3 = (bf16[576,128]{1,0:T(8,128)(2,1)S(1)}, bf16[576,128]{1,0:T(8,128)(2,1)S(1)}, u32[]{:S(2)}, u32[]{:S(2)}) collective-permute-start(bf16[576,128]{1,0:T(8,128)(2,1)S(1)} %table.1.refs_3_.refs_0_), channel_id=1, source_target_pairs={{0,4},{4,0},{8,12},{12,8},{16,20},{20,16},{24,28},{28,24},{1,5},{5... | collective-permute-start | bytes 442376 | tf_op jit(solution)/shard_map/ppermute | solution.py:348
  19.8 1.6 %collective-permute-start.9 = (bf16[576,128]{1,0:T(8,128)(2,1)S(1)}, bf16[576,128]{1,0:T(8,128)(2,1)S(1)}, u32[]{:S(2)}, u32[]{:S(2)}) collective-permute-start(bf16[576,128]{1,0:T(8,128)(2,1)S(1)} %collective-permute-done.8.refs_6_), channel_id=1, source_target_pairs={{0,4},{4,0},{8,12},{12,8},{16,20},{20,16},{24,28},{28,24},{1,5},{5... | collective-permute-start | bytes 442376 | tf_op jit(solution)/shard_map/ppermute | solution.py:348
  20.4 1.4 %collective-permute-start.7 = (bf16[576,128]{1,0:T(8,128)(2,1)S(1)}, bf16[576,128]{1,0:T(8,128)(2,1)S(1)}, u32[]{:S(2)}, u32[]{:S(2)}) collective-permute-start(bf16[576,128]{1,0:T(8,128)(2,1)S(1)} %collective-permute-done.6.refs_4_), channel_id=1, source_target_pairs={{0,4},{4,0},{8,12},{12,8},{16,20},{20,16},{24,28},{28,24},{1,5},{5... | collective-permute-start | bytes 442376 | tf_op jit(solution)/shard_map/ppermute | solution.py:348
  20.5 1.5 %collective-permute-start.5 = (bf16[576,128]{1,0:T(8,128)(2,1)S(1)}, bf16[576,128]{1,0:T(8,128)(2,1)S(1)}, u32[]{:S(2)}, u32[]{:S(2)}) collective-permute-start(bf16[576,128]{1,0:T(8,128)(2,1)S(1)} %hold.1.refs_2_), channel_id=1, source_target_pairs={{0,4},{4,0},{8,12},{12,8},{16,20},{20,16},{24,28},{28,24},{1,5},{5... | collective-permute-start | bytes 442376 | tf_op jit(solution)/shard_map/ppermute | solution.py:348
  22.0 24.1 %copy-start = (f32[128,64]{0,1:T(8,128)S(1)}, f32[128,64]{0,1:T(8,128)}, u32[]{:S(2)}) copy-start(f32[128,64]{0,1:T(8,128)} %param.17) | copy-start | bytes 98308
  22.0 24.1 %copy-start.1 = (f32[128,64]{0,1:T(8,128)S(1)}, f32[128,64]{0,1:T(8,128)}, u32[]{:S(2)}) copy-start(f32[128,64]{0,1:T(8,128)} %param.20) | copy-start | bytes 98308
  22.0 24.1 %copy-start.2 = (f32[32,64]{1,0:T(8,128)S(1)}, f32[32,64]{1,0:T(8,128)}, u32[]{:S(2)}) copy-start(f32[32,64]{1,0:T(8,128)} %refs_10_.1) | copy-start | bytes 24580
  22.0 24.1 %copy-start.3 = (f32[128,64]{0,1:T(8,128)S(1)}, f32[128,64]{0,1:T(8,128)}, u32[]{:S(2)}) copy-start(f32[128,64]{0,1:T(8,128)} %param.18) | copy-start | bytes 98308
  22.0 24.1 %copy-start.4 = (f32[128,64]{0,1:T(8,128)S(1)}, f32[128,64]{0,1:T(8,128)}, u32[]{:S(2)}) copy-start(f32[128,64]{0,1:T(8,128)} %param.19) | copy-start | bytes 98308
  22.0 24.1 %copy-start.5 = (f32[128,64]{0,1:T(8,128)S(1)}, f32[128,64]{0,1:T(8,128)}, u32[]{:S(2)}) copy-start(f32[128,64]{0,1:T(8,128)} %param.21) | copy-start | bytes 98308
  22.0 24.1 %copy-start.6 = (f32[128,64]{0,1:T(8,128)S(1)}, f32[128,64]{0,1:T(8,128)}, u32[]{:S(2)}) copy-start(f32[128,64]{0,1:T(8,128)} %param.22) | copy-start | bytes 98308
  22.0 24.1 %copy-start.7 = (f32[32,64]{1,0:T(8,128)S(1)}, f32[32,64]{1,0:T(8,128)}, u32[]{:S(2)}) copy-start(f32[32,64]{1,0:T(8,128)} %refs_11_.1) | copy-start | bytes 24580
  22.0 24.1 %copy-start.8 = (f32[32,64]{1,0:T(8,128)S(1)}, f32[32,64]{1,0:T(8,128)}, u32[]{:S(2)}) copy-start(f32[32,64]{1,0:T(8,128)} %refs_12_.1) | copy-start | bytes 24580
  27.8 1.6 %collective-permute-start.10 = (bf16[448,256]{1,0:T(8,128)(2,1)S(1)}, bf16[448,256]{1,0:T(8,128)(2,1)S(1)}, u32[]{:S(2)}, u32[]{:S(2)}) collective-permute-start(bf16[448,256]{1,0:T(8,128)(2,1)S(1)} %get-tuple-element.46), channel_id=1, source_target_pairs={{0,4},{4,0},{8,12},{12,8},{16,20},{20,16},{24,28},{28,24},{1,5},{5... | collective-permute-start | bytes 688136 | tf_op jit(solution)/shard_map/ppermute | solution.py:348
  29.4 5.5 %collective-permute-start.11 = (bf16[224,256]{1,0:T(8,128)(2,1)S(1)}, bf16[224,256]{1,0:T(8,128)(2,1)S(1)}, u32[]{:S(2)}, u32[]{:S(2)}) collective-permute-start(bf16[224,256]{1,0:T(8,128)(2,1)S(1)} %get-tuple-element.47), channel_id=1, source_target_pairs={{0,8},{4,12},{8,0},{12,4},{16,24},{20,28},{24,16},{28,20},{1,9},{5... | collective-permute-start | bytes 344072 | tf_op jit(solution)/shard_map/ppermute | solution.py:348
  31.0 7.6 %collective-permute-start.12 = (bf16[224,256]{1,0:T(8,128)(2,1)S(1)}, bf16[224,256]{1,0:T(8,128)(2,1)S(1)}, u32[]{:S(2)}, u32[]{:S(2)}) collective-permute-start(bf16[224,256]{1,0:T(8,128)(2,1)S(1)} %get-tuple-element.48), channel_id=1, source_target_pairs={{0,16},{4,20},{8,24},{12,28},{16,0},{20,4},{24,8},{28,12},{1,17},{... | collective-permute-start | bytes 344072 | tf_op jit(solution)/shard_map/ppermute | solution.py:348
  32.5 6.1 %collective-permute-start.13 = (bf16[224,256]{1,0:T(8,128)(2,1)S(1)}, bf16[224,256]{1,0:T(8,128)(2,1)S(1)}, u32[]{:S(2)}, u32[]{:S(2)}) collective-permute-start(bf16[224,256]{1,0:T(8,128)(2,1)S(1)} %get-tuple-element.49), channel_id=1, source_target_pairs={{0,24},{4,28},{8,16},{12,20},{16,8},{20,12},{24,0},{28,4},{1,25},{... | collective-permute-start | bytes 344072 | tf_op jit(solution)/shard_map/ppermute | solution.py:348
  39.2 6.1 %collective-permute-start.14 = (bf16[144,128]{1,0:T(8,128)(2,1)S(1)}, bf16[144,128]{1,0:T(8,128)(2,1)S(1)}, u32[]{:S(2)}, u32[]{:S(2)}) collective-permute-start(bf16[144,128]{1,0:T(8,128)(2,1)S(1)} %get-tuple-element.51), channel_id=1, source_target_pairs={{0,3},{1,2},{2,1},{3,0},{4,7},{5,6},{6,5},{7,4},{8,11},{9,10},{10,... | collective-permute-start | bytes 110600 | tf_op jit(solution)/shard_map/ppermute | solution.py:348
  41.2 4.9 %collective-permute-start.15 = (bf16[144,128]{1,0:T(8,128)(2,1)S(1)}, bf16[144,128]{1,0:T(8,128)(2,1)S(1)}, u32[]{:S(2)}, u32[]{:S(2)}) collective-permute-start(bf16[144,128]{1,0:T(8,128)(2,1)S(1)} %get-tuple-element.52), channel_id=1, source_target_pairs={{0,2},{1,3},{2,0},{3,1},{4,6},{5,7},{6,4},{7,5},{8,10},{9,11},{10,... | collective-permute-start | bytes 110600 | tf_op jit(solution)/shard_map/ppermute | solution.py:348
  41.2 4.9 %collective-permute-start.16 = (bf16[144,128]{1,0:T(8,128)(2,1)S(1)}, bf16[144,128]{1,0:T(8,128)(2,1)S(1)}, u32[]{:S(2)}, u32[]{:S(2)}) collective-permute-start(bf16[144,128]{1,0:T(8,128)(2,1)S(1)} %get-tuple-element.53), channel_id=1, source_target_pairs={{0,1},{1,0},{2,3},{3,2},{4,5},{5,4},{6,7},{7,6},{8,9},{9,8},{10,11... | collective-permute-start | bytes 110600 | tf_op jit(solution)/shard_map/ppermute | solution.py:348

commit v15 on v13

--- a/solution.py
+++ b/solution.py
@@ -173,7 +173,7 @@
         residual_even,
         residual_odd,
     ) = refs[10:]
-    pair = 4
+    pair = 2
     pairs = status.shape[0] // pair
     def pick(t):
         table = jnp.concatenate([ref[t * rank : (t + 1) * rank, :] for ref in tables], axis=1)
@@ -425,10 +425,10 @@
             pltpu.VMEM((users, sizes.rank), f32),
             pltpu.VMEM((items, sizes.rank), f32),
             pltpu.VMEM((days, sizes.rank), f32),
-            pltpu.VMEM((4 * users, sizes.rank), bf16),
-            pltpu.VMEM((4 * users, sizes.rank), bf16),
-            pltpu.VMEM((4 * users, items), bf16),
-            pltpu.VMEM((4 * users, items), bf16),
+            pltpu.VMEM((2 * users, sizes.rank), bf16),
+            pltpu.VMEM((2 * users, sizes.rank), bf16),
+            pltpu.VMEM((2 * users, items), bf16),
+            pltpu.VMEM((2 * users, items), bf16),
         ],
         compiler_params=pltpu.CompilerParams(vmem_limit_bytes=BLOCK_VMEM),
         name="block_gradients",

time: 46.6 us -> 47 us (level)
  no operation moved by 1% of the time
where the time goes in v15:
time: 47 us; the launch traced here: 46.8 us
  starting transfers between devices  18.8 us (40%)
  waiting for transfers between devices  14.7 us (31%)
  Pallas kernels  12.4 us (26%)
  between operations  0.83 us (2%)
    ppermute x17, starting transfers between devices, swap(): return lax.ppermute(array, axis, [(i, i ^ bits) for i in range(size)])  18.8 us
    ppermute x17, waiting for transfers between devices, swap(): return lax.ppermute(array, axis, [(i, i ^ bits) for i in range(size)])  14.7 us
    pallas_call x1, Pallas kernels, local(): pl.pallas_call(functools.partial(block_kernel, sizes), out_shape=(half, h...  5.96 us
    pallas_call x1, Pallas kernels, local(): pl.pallas_call(functools.partial(slot_kernel, sizes), out_shape=tuple([sh...  4.11 us
  transfers between devices with their start and end apart: 17, of which 11 were waited for; matrix products, arithmetic and copies ran while one was open for 0% of the time, Pallas kernels for 9%

profile of v15, /device:TPU:0, one launch (start us, length us, event | category | flops | bytes accessed | tf_op | source)
XLA Modules:
  0.0 46.8 jit_solution(4744328326723439686)
XLA Ops:
  0.6 0.9 %pack.1.refs_3_ = bf16[144,128]{1,0:T(8,128)(2,1)S(1)} custom-call(f32[64,128]{1,0:T(8,128)} %bitcast.13, f32[64,128]{1,0:T(8,128)} %bitcast.15, f32[32,64]{1,0:T(8,128)} %refs_10_.1), custom_call_target="tpu_custom_call" | custom-call | tf_op jit(solution)/shard_map/pack/pallas_call | solution.py:362
  1.5 4.1 %collective-permute-start.2 = (bf16[144,128]{1,0:T(8,128)(2,1)S(1)}, bf16[144,128]{1,0:T(8,128)(2,1)S(1)}, u32[]{:S(2)}, u32[]{:S(2)}) collective-permute-start(bf16[144,128]{1,0:T(8,128)(2,1)S(1)} %pack.1.refs_3_), channel_id=1, source_target_pairs={{0,2},{1,3},{2,0},{3,1},{4,6},{5,7},{6,4},{7,5},{8,10},{9,11},{10,... | collective-permute-start | bytes 110600 | tf_op jit(solution)/shard_map/ppermute | solution.py:333
  5.6 1.3 %collective-permute-start.1 = (bf16[144,128]{1,0:T(8,128)(2,1)S(1)}, bf16[144,128]{1,0:T(8,128)(2,1)S(1)}, u32[]{:S(2)}, u32[]{:S(2)}) collective-permute-start(bf16[144,128]{1,0:T(8,128)(2,1)S(1)} %pack.1.refs_3_), channel_id=1, source_target_pairs={{0,3},{1,2},{2,1},{3,0},{4,7},{5,6},{6,5},{7,4},{8,11},{9,10},{10,... | collective-permute-start | bytes 110600 | tf_op jit(solution)/shard_map/ppermute | solution.py:333
  7.0 0.2 collective-permute-start
  7.2 0.8 %collective-permute-done.2.refs_2_ = bf16[144,128]{1,0:T(8,128)(2,1)S(1)} collective-permute-done((bf16[144,128]{1,0:T(8,128)(2,1)S(1)}, bf16[144,128]{1,0:T(8,128)(2,1)S(1)}, u32[]{:S(2)}, u32[]{:S(2)}) %collective-permute-start.2) | collective-permute-done | bytes 36896 | tf_op jit(solution)/shard_map/ppermute | solution.py:333
  8.0 3.4 %collective-permute-done.1.refs_1_ = bf16[144,128]{1,0:T(8,128)(2,1)S(1)} collective-permute-done((bf16[144,128]{1,0:T(8,128)(2,1)S(1)}, bf16[144,128]{1,0:T(8,128)(2,1)S(1)}, u32[]{:S(2)}, u32[]{:S(2)}) %collective-permute-start.1) | collective-permute-done | bytes 36896 | tf_op jit(solution)/shard_map/ppermute | solution.py:333
  11.4 0.1 table.1.refs_3_.refs_0_
  11.5 2.5 %collective-permute-start.8 = (bf16[576,128]{1,0:T(8,128)(2,1)S(1)}, bf16[576,128]{1,0:T(8,128)(2,1)S(1)}, u32[]{:S(2)}, u32[]{:S(2)}) collective-permute-start(bf16[576,128]{1,0:T(8,128)(2,1)S(1)} %table.1.refs_3_.refs_0_), channel_id=1, source_target_pairs={{0,24},{4,28},{8,16},{12,20},{16,8},{20,12},{24,0},{28,4},{1,25},{... | collective-permute-start | bytes 442376 | tf_op jit(solution)/shard_map/ppermute | solution.py:333
  14.0 0.5 %collective-permute-start.6 = (bf16[576,128]{1,0:T(8,128)(2,1)S(1)}, bf16[576,128]{1,0:T(8,128)(2,1)S(1)}, u32[]{:S(2)}, u32[]{:S(2)}) collective-permute-start(bf16[576,128]{1,0:T(8,128)(2,1)S(1)} %table.1.refs_3_.refs_0_), channel_id=1, source_target_pairs={{0,16},{4,20},{8,24},{12,28},{16,0},{20,4},{24,8},{28,12},{1,17},{... | collective-permute-start | bytes 442376 | tf_op jit(solution)/shard_map/ppermute | solution.py:333
  14.5 0.5 %collective-permute-start.4 = (bf16[576,128]{1,0:T(8,128)(2,1)S(1)}, bf16[576,128]{1,0:T(8,128)(2,1)S(1)}, u32[]{:S(2)}, u32[]{:S(2)}) collective-permute-start(bf16[576,128]{1,0:T(8,128)(2,1)S(1)} %table.1.refs_3_.refs_0_), channel_id=1, source_target_pairs={{0,8},{4,12},{8,0},{12,4},{16,24},{20,28},{24,16},{28,20},{1,9},{5... | collective-permute-start | bytes 442376 | tf_op jit(solution)/shard_map/ppermute | solution.py:333
  15.0 4.1 %slots.1 = (bf16[1024,256]{1,0:T(8,128)(2,1)S(1)}, bf16[1024,256]{1,0:T(8,128)(2,1)S(1)}, bf16[256,32]{1,0:T(8,128)(2,1)S(1)}, bf16[384,256]{1,0:T(8,128)(2,1)S(...) custom-call(s32[1]{0:T(128)} %bitcast.2.me_ref, ...), custom_call_target="tpu_custom_call" | custom-call | tf_op jit(solution)/shard_map/slots/pallas_call | solution.py:382
  19.2 0.0 copy-start.1
  19.3 0.6 %collective-permute-start.9 = (bf16[576,128]{1,0:T(8,128)(2,1)S(1)}, bf16[576,128]{1,0:T(8,128)(2,1)S(1)}, u32[]{:S(2)}, u32[]{:S(2)}) collective-permute-start(bf16[576,128]{1,0:T(8,128)(2,1)S(1)} %collective-permute-done.8.refs_6_), channel_id=1, source_target_pairs={{0,4},{4,0},{8,12},{12,8},{16,20},{20,16},{24,28},{28,24},{1,5},{5... | collective-permute-start | bytes 442376 | tf_op jit(solution)/shard_map/ppermute | solution.py:333
  19.8 0.1 collective-permute-done.6.refs_4_
  20.0 0.6 %collective-permute-start.5 = (bf16[576,128]{1,0:T(8,128)(2,1)S(1)}, bf16[576,128]{1,0:T(8,128)(2,1)S(1)}, u32[]{:S(2)}, u32[]{:S(2)}) collective-permute-start(bf16[576,128]{1,0:T(8,128)(2,1)S(1)} %hold.1.refs_2_), channel_id=1, source_target_pairs={{0,4},{4,0},{8,12},{12,8},{16,20},{20,16},{24,28},{28,24},{1,5},{5... | collective-permute-start | bytes 442376 | tf_op jit(solution)/shard_map/ppermute | solution.py:333
  20.5 0.3 collective-permute-done.9.refs_7_
  20.9 0.5 collective-permute-done.7.refs_5_
  21.3 0.2 collective-permute-done.5.refs_3_
  21.5 6.0 %block_gradients.1 = (bf16[448,256]{1,0:T(8,128)(2,1)S(1)}, bf16[448,256]{1,0:T(8,128)(2,1)S(1)}) custom-call(bf16[576,128]{1,0:T(8,128)(2,1)S(1)} %table.1.refs_3_.refs_0_, bf16[576,128]{1,0:T(8,128)(2,1)S(1)} %collective-permute-done.3.refs_1_, bf16[576,128]{1,0:T(8,128)(2,1)S(1)} %hold.1.refs_2_, bf16[576,128]{1,0:T(8,128)(2,1)S(1)} %collective-permute-done.5.refs_3_, ...), custom_call_target="tpu_custom_call" | custom-call | tf_op jit(solution)/shard_map/block_gradients/pallas_call | solution.py:415
  27.5 0.4 collective-permute-start.10
  27.9 1.1 %collective-permute-done.10.crossed_ref.refs_1_ = bf16[448,256]{1,0:T(8,128)(2,1)S(1)} collective-permute-done((bf16[448,256]{1,0:T(8,128)(2,1)S(1)}, bf16[448,256]{1,0:T(8,128)(2,1)S(1)}, u32[]{:S(2)}, u32[]{:S(2)}) %collective-permute-start.10) | collective-permute-done | bytes 229408 | tf_op jit(solution)/shard_map/ppermute | solution.py:333
  29.1 2.4 %collective-permute-start.11 = (bf16[224,256]{1,0:T(8,128)(2,1)S(1)}, bf16[224,256]{1,0:T(8,128)(2,1)S(1)}, u32[]{:S(2)}, u32[]{:S(2)}) collective-permute-start(bf16[224,256]{1,0:T(8,128)(2,1)S(1)} %get-tuple-element.45), channel_id=1, source_target_pairs={{0,24},{4,28},{8,16},{12,20},{16,8},{20,12},{24,0},{28,4},{1,25},{... | collective-permute-start | bytes 344072 | tf_op jit(solution)/shard_map/ppermute | solution.py:333
  31.5 0.5 %collective-permute-start.12 = (bf16[224,256]{1,0:T(8,128)(2,1)S(1)}, bf16[224,256]{1,0:T(8,128)(2,1)S(1)}, u32[]{:S(2)}, u32[]{:S(2)}) collective-permute-start(bf16[224,256]{1,0:T(8,128)(2,1)S(1)} %get-tuple-element.46), channel_id=1, source_target_pairs={{0,16},{4,20},{8,24},{12,28},{16,0},{20,4},{24,8},{28,12},{1,17},{... | collective-permute-start | bytes 344072 | tf_op jit(solution)/shard_map/ppermute | solution.py:333
  32.0 0.6 %collective-permute-start.13 = (bf16[224,256]{1,0:T(8,128)(2,1)S(1)}, bf16[224,256]{1,0:T(8,128)(2,1)S(1)}, u32[]{:S(2)}, u32[]{:S(2)}) collective-permute-start(bf16[224,256]{1,0:T(8,128)(2,1)S(1)} %get-tuple-element.47), channel_id=1, source_target_pairs={{0,8},{4,12},{8,0},{12,4},{16,24},{20,28},{24,16},{28,20},{1,9},{5... | collective-permute-start | bytes 344072 | tf_op jit(solution)/shard_map/ppermute | solution.py:333
  32.7 2.9 %collective-permute-done.11.refs_2_ = bf16[224,256]{1,0:T(8,128)(2,1)S(1)} collective-permute-done((bf16[224,256]{1,0:T(8,128)(2,1)S(1)}, bf16[224,256]{1,0:T(8,128)(2,1)S(1)}, u32[]{:S(2)}, u32[]{:S(2)}) %collective-permute-start.11) | collective-permute-done | bytes 114720 | tf_op jit(solution)/shard_map/ppermute | solution.py:333
  35.6 2.4 %collective-permute-done.12.refs_3_ = bf16[224,256]{1,0:T(8,128)(2,1)S(1)} collective-permute-done((bf16[224,256]{1,0:T(8,128)(2,1)S(1)}, bf16[224,256]{1,0:T(8,128)(2,1)S(1)}, u32[]{:S(2)}, u32[]{:S(2)}) %collective-permute-start.12) | collective-permute-done | bytes 114720 | tf_op jit(solution)/shard_map/ppermute | solution.py:333
  37.9 0.6 %row_sums.1 = (bf16[144,128]{1,0:T(8,128)(2,1)S(1)}, bf16[144,128]{1,0:T(8,128)(2,1)S(1)}, bf16[144,128]{1,0:T(8,128)(2,1)S(1)}, bf16[144,128]{1,0:T(8,128)(2,1)S(1)}) custom-call(bf16[448,256]{1,0:T(8,128)(2,1)S(1)} %get-tuple-element.43.own_ref.refs_0_, bf16[448,256]{1,0:T(8,128)(2,1)S(1)} %collective-permute-done.10.crossed_ref.refs_1_, ...), custom_call_target="tpu_custom_call" | custom-call | tf_op jit(solution)/shard_map/row_sums/pallas_call | solution.py:449
  38.5 2.6 %collective-permute-start.14 = (bf16[144,128]{1,0:T(8,128)(2,1)S(1)}, bf16[144,128]{1,0:T(8,128)(2,1)S(1)}, u32[]{:S(2)}, u32[]{:S(2)}) collective-permute-start(bf16[144,128]{1,0:T(8,128)(2,1)S(1)} %get-tuple-element.49), channel_id=1, source_target_pairs={{0,3},{1,2},{2,1},{3,0},{4,7},{5,6},{6,5},{7,4},{8,11},{9,10},{10,... | collective-permute-start | bytes 110600 | tf_op jit(solution)/shard_map/ppermute | solution.py:333
  41.1 1.8 %collective-permute-start.16 = (bf16[144,128]{1,0:T(8,128)(2,1)S(1)}, bf16[144,128]{1,0:T(8,128)(2,1)S(1)}, u32[]{:S(2)}, u32[]{:S(2)}) collective-permute-start(bf16[144,128]{1,0:T(8,128)(2,1)S(1)} %get-tuple-element.51), channel_id=1, source_target_pairs={{0,1},{1,0},{2,3},{3,2},{4,5},{5,4},{6,7},{7,6},{8,9},{9,8},{10,11... | collective-permute-start | bytes 110600 | tf_op jit(solution)/shard_map/ppermute | solution.py:333
  42.9 1.4 %collective-permute-done.14.refs_1_ = bf16[144,128]{1,0:T(8,128)(2,1)S(1)} collective-permute-done((bf16[144,128]{1,0:T(8,128)(2,1)S(1)}, bf16[144,128]{1,0:T(8,128)(2,1)S(1)}, u32[]{:S(2)}, u32[]{:S(2)}) %collective-permute-start.14) | collective-permute-done | bytes 36896 | tf_op jit(solution)/shard_map/ppermute | solution.py:333
  44.3 1.7 %collective-permute-done.15.refs_2_ = bf16[144,128]{1,0:T(8,128)(2,1)S(1)} collective-permute-done((bf16[144,128]{1,0:T(8,128)(2,1)S(1)}, bf16[144,128]{1,0:T(8,128)(2,1)S(1)}, u32[]{:S(2)}, u32[]{:S(2)}) %collective-permute-start.15) | collective-permute-done | bytes 36896 | tf_op jit(solution)/shard_map/ppermute | solution.py:333
  46.1 0.7 %adam.1 = (f32[64,128]{1,0:T(8,128)}, f32[64,128]{1,0:T(8,128)}, f32[64,128]{1,0:T(8,128)}, f32[64,128]{1,0:T(8,128)}, f32[64,128]{1,0:T(8,128)}, /*index=5*/f32...) custom-call(bf16[144,128]{1,0:T(8,128)(2,1)S(1)} %get-tuple-element.48.refs_0_, ...), custom_call_target="tpu_custom_call" | custom-call | tf_op jit(solution)/shard_map/adam/pallas_call | solution.py:470
  (28 shorter events, 0.1 us)
Async XLA Ops:
  1.5 6.4 %collective-permute-start.2 = (bf16[144,128]{1,0:T(8,128)(2,1)S(1)}, bf16[144,128]{1,0:T(8,128)(2,1)S(1)}, u32[]{:S(2)}, u32[]{:S(2)}) collective-permute-start(bf16[144,128]{1,0:T(8,128)(2,1)S(1)} %pack.1.refs_3_), channel_id=1, source_target_pairs={{0,2},{1,3},{2,0},{3,1},{4,6},{5,7},{6,4},{7,5},{8,10},{9,11},{10,... | collective-permute-start | bytes 110600 | tf_op jit(solution)/shard_map/ppermute | solution.py:333
  5.6 5.8 %collective-permute-start.1 = (bf16[144,128]{1,0:T(8,128)(2,1)S(1)}, bf16[144,128]{1,0:T(8,128)(2,1)S(1)}, u32[]{:S(2)}, u32[]{:S(2)}) collective-permute-start(bf16[144,128]{1,0:T(8,128)(2,1)S(1)} %pack.1.refs_3_), channel_id=1, source_target_pairs={{0,3},{1,2},{2,1},{3,0},{4,7},{5,6},{6,5},{7,4},{8,11},{9,10},{10,... | collective-permute-start | bytes 110600 | tf_op jit(solution)/shard_map/ppermute | solution.py:333
  7.0 4.4 %collective-permute-start = (bf16[144,128]{1,0:T(8,128)(2,1)S(1)}, bf16[144,128]{1,0:T(8,128)(2,1)S(1)}, u32[]{:S(2)}, u32[]{:S(2)}) collective-permute-start(bf16[144,128]{1,0:T(8,128)(2,1)S(1)} %pack.1.refs_3_), channel_id=1, source_target_pairs={{0,1},{1,0},{2,3},{3,2},{4,5},{5,4},{6,7},{7,6},{8,9},{9,8},{10,11... | collective-permute-start | bytes 110600 | tf_op jit(solution)/shard_map/ppermute | solution.py:333
  11.5 7.7 %collective-permute-start.8 = (bf16[576,128]{1,0:T(8,128)(2,1)S(1)}, bf16[576,128]{1,0:T(8,128)(2,1)S(1)}, u32[]{:S(2)}, u32[]{:S(2)}) collective-permute-start(bf16[576,128]{1,0:T(8,128)(2,1)S(1)} %table.1.refs_3_.refs_0_), channel_id=1, source_target_pairs={{0,24},{4,28},{8,16},{12,20},{16,8},{20,12},{24,0},{28,4},{1,25},{... | collective-permute-start | bytes 442376 | tf_op jit(solution)/shard_map/ppermute | solution.py:333
  14.0 6.0 %collective-permute-start.6 = (bf16[576,128]{1,0:T(8,128)(2,1)S(1)}, bf16[576,128]{1,0:T(8,128)(2,1)S(1)}, u32[]{:S(2)}, u32[]{:S(2)}) collective-permute-start(bf16[576,128]{1,0:T(8,128)(2,1)S(1)} %table.1.refs_3_.refs_0_), channel_id=1, source_target_pairs={{0,16},{4,20},{8,24},{12,28},{16,0},{20,4},{24,8},{28,12},{1,17},{... | collective-permute-start | bytes 442376 | tf_op jit(solution)/shard_map/ppermute | solution.py:333
  14.5 5.4 %collective-permute-start.4 = (bf16[576,128]{1,0:T(8,128)(2,1)S(1)}, bf16[576,128]{1,0:T(8,128)(2,1)S(1)}, u32[]{:S(2)}, u32[]{:S(2)}) collective-permute-start(bf16[576,128]{1,0:T(8,128)(2,1)S(1)} %table.1.refs_3_.refs_0_), channel_id=1, source_target_pairs={{0,8},{4,12},{8,0},{12,4},{16,24},{20,28},{24,16},{28,20},{1,9},{5... | collective-permute-start | bytes 442376 | tf_op jit(solution)/shard_map/ppermute | solution.py:333
  15.0 5.5 %collective-permute-start.3 = (bf16[576,128]{1,0:T(8,128)(2,1)S(1)}, bf16[576,128]{1,0:T(8,128)(2,1)S(1)}, u32[]{:S(2)}, u32[]{:S(2)}) collective-permute-start(bf16[576,128]{1,0:T(8,128)(2,1)S(1)} %table.1.refs_3_.refs_0_), channel_id=1, source_target_pairs={{0,4},{4,0},{8,12},{12,8},{16,20},{20,16},{24,28},{28,24},{1,5},{5... | collective-permute-start | bytes 442376 | tf_op jit(solution)/shard_map/ppermute | solution.py:333
  19.2 26.8 %copy-start = (f32[128,64]{0,1:T(8,128)S(1)}, f32[128,64]{0,1:T(8,128)}, u32[]{:S(2)}) copy-start(f32[128,64]{0,1:T(8,128)} %param.17) | copy-start | bytes 98308
  19.2 26.8 %copy-start.1 = (f32[128,64]{0,1:T(8,128)S(1)}, f32[128,64]{0,1:T(8,128)}, u32[]{:S(2)}) copy-start(f32[128,64]{0,1:T(8,128)} %param.20) | copy-start | bytes 98308
  19.2 26.8 %copy-start.2 = (f32[32,64]{1,0:T(8,128)S(1)}, f32[32,64]{1,0:T(8,128)}, u32[]{:S(2)}) copy-start(f32[32,64]{1,0:T(8,128)} %refs_10_.1) | copy-start | bytes 24580
  19.2 26.8 %copy-start.3 = (f32[128,64]{0,1:T(8,128)S(1)}, f32[128,64]{0,1:T(8,128)}, u32[]{:S(2)}) copy-start(f32[128,64]{0,1:T(8,128)} %param.18) | copy-start | bytes 98308
  19.2 26.8 %copy-start.4 = (f32[128,64]{0,1:T(8,128)S(1)}, f32[128,64]{0,1:T(8,128)}, u32[]{:S(2)}) copy-start(f32[128,64]{0,1:T(8,128)} %param.19) | copy-start | bytes 98308
  19.2 26.8 %copy-start.5 = (f32[128,64]{0,1:T(8,128)S(1)}, f32[128,64]{0,1:T(8,128)}, u32[]{:S(2)}) copy-start(f32[128,64]{0,1:T(8,128)} %param.21) | copy-start | bytes 98308
  19.2 26.8 %copy-start.6 = (f32[128,64]{0,1:T(8,128)S(1)}, f32[128,64]{0,1:T(8,128)}, u32[]{:S(2)}) copy-start(f32[128,64]{0,1:T(8,128)} %param.22) | copy-start | bytes 98308
  19.2 26.8 %copy-start.7 = (f32[32,64]{1,0:T(8,128)S(1)}, f32[32,64]{1,0:T(8,128)}, u32[]{:S(2)}) copy-start(f32[32,64]{1,0:T(8,128)} %refs_11_.1) | copy-start | bytes 24580
  19.3 26.8 %copy-start.8 = (f32[32,64]{1,0:T(8,128)S(1)}, f32[32,64]{1,0:T(8,128)}, u32[]{:S(2)}) copy-start(f32[32,64]{1,0:T(8,128)} %refs_12_.1) | copy-start | bytes 24580
  19.3 1.6 %collective-permute-start.9 = (bf16[576,128]{1,0:T(8,128)(2,1)S(1)}, bf16[576,128]{1,0:T(8,128)(2,1)S(1)}, u32[]{:S(2)}, u32[]{:S(2)}) collective-permute-start(bf16[576,128]{1,0:T(8,128)(2,1)S(1)} %collective-permute-done.8.refs_6_), channel_id=1, source_target_pairs={{0,4},{4,0},{8,12},{12,8},{16,20},{20,16},{24,28},{28,24},{1,5},{5... | collective-permute-start | bytes 442376 | tf_op jit(solution)/shard_map/ppermute | solution.py:333
  19.9 1.4 %collective-permute-start.7 = (bf16[576,128]{1,0:T(8,128)(2,1)S(1)}, bf16[576,128]{1,0:T(8,128)(2,1)S(1)}, u32[]{:S(2)}, u32[]{:S(2)}) collective-permute-start(bf16[576,128]{1,0:T(8,128)(2,1)S(1)} %collective-permute-done.6.refs_4_), channel_id=1, source_target_pairs={{0,4},{4,0},{8,12},{12,8},{16,20},{20,16},{24,28},{28,24},{1,5},{5... | collective-permute-start | bytes 442376 | tf_op jit(solution)/shard_map/ppermute | solution.py:333
  20.0 1.6 %collective-permute-start.5 = (bf16[576,128]{1,0:T(8,128)(2,1)S(1)}, bf16[576,128]{1,0:T(8,128)(2,1)S(1)}, u32[]{:S(2)}, u32[]{:S(2)}) collective-permute-start(bf16[576,128]{1,0:T(8,128)(2,1)S(1)} %hold.1.refs_2_), channel_id=1, source_target_pairs={{0,4},{4,0},{8,12},{12,8},{16,20},{20,16},{24,28},{28,24},{1,5},{5... | collective-permute-start | bytes 442376 | tf_op jit(solution)/shard_map/ppermute | solution.py:333
  27.5 1.6 %collective-permute-start.10 = (bf16[448,256]{1,0:T(8,128)(2,1)S(1)}, bf16[448,256]{1,0:T(8,128)(2,1)S(1)}, u32[]{:S(2)}, u32[]{:S(2)}) collective-permute-start(bf16[448,256]{1,0:T(8,128)(2,1)S(1)} %get-tuple-element.44), channel_id=1, source_target_pairs={{0,4},{4,0},{8,12},{12,8},{16,20},{20,16},{24,28},{28,24},{1,5},{5... | collective-permute-start | bytes 688136 | tf_op jit(solution)/shard_map/ppermute | solution.py:333
  29.1 6.5 %collective-permute-start.11 = (bf16[224,256]{1,0:T(8,128)(2,1)S(1)}, bf16[224,256]{1,0:T(8,128)(2,1)S(1)}, u32[]{:S(2)}, u32[]{:S(2)}) collective-permute-start(bf16[224,256]{1,0:T(8,128)(2,1)S(1)} %get-tuple-element.45), channel_id=1, source_target_pairs={{0,24},{4,28},{8,16},{12,20},{16,8},{20,12},{24,0},{28,4},{1,25},{... | collective-permute-start | bytes 344072 | tf_op jit(solution)/shard_map/ppermute | solution.py:333
  31.5 6.4 %collective-permute-start.12 = (bf16[224,256]{1,0:T(8,128)(2,1)S(1)}, bf16[224,256]{1,0:T(8,128)(2,1)S(1)}, u32[]{:S(2)}, u32[]{:S(2)}) collective-permute-start(bf16[224,256]{1,0:T(8,128)(2,1)S(1)} %get-tuple-element.46), channel_id=1, source_target_pairs={{0,16},{4,20},{8,24},{12,28},{16,0},{20,4},{24,8},{28,12},{1,17},{... | collective-permute-start | bytes 344072 | tf_op jit(solution)/shard_map/ppermute | solution.py:333
  32.0 5.9 %collective-permute-start.13 = (bf16[224,256]{1,0:T(8,128)(2,1)S(1)}, bf16[224,256]{1,0:T(8,128)(2,1)S(1)}, u32[]{:S(2)}, u32[]{:S(2)}) collective-permute-start(bf16[224,256]{1,0:T(8,128)(2,1)S(1)} %get-tuple-element.47), channel_id=1, source_target_pairs={{0,8},{4,12},{8,0},{12,4},{16,24},{20,28},{24,16},{28,20},{1,9},{5... | collective-permute-start | bytes 344072 | tf_op jit(solution)/shard_map/ppermute | solution.py:333
  38.5 5.8 %collective-permute-start.14 = (bf16[144,128]{1,0:T(8,128)(2,1)S(1)}, bf16[144,128]{1,0:T(8,128)(2,1)S(1)}, u32[]{:S(2)}, u32[]{:S(2)}) collective-permute-start(bf16[144,128]{1,0:T(8,128)(2,1)S(1)} %get-tuple-element.49), channel_id=1, source_target_pairs={{0,3},{1,2},{2,1},{3,0},{4,7},{5,6},{6,5},{7,4},{8,11},{9,10},{10,... | collective-permute-start | bytes 110600 | tf_op jit(solution)/shard_map/ppermute | solution.py:333
  41.1 4.9 %collective-permute-start.15 = (bf16[144,128]{1,0:T(8,128)(2,1)S(1)}, bf16[144,128]{1,0:T(8,128)(2,1)S(1)}, u32[]{:S(2)}, u32[]{:S(2)}) collective-permute-start(bf16[144,128]{1,0:T(8,128)(2,1)S(1)} %get-tuple-element.50), channel_id=1, source_target_pairs={{0,2},{1,3},{2,0},{3,1},{4,6},{5,7},{6,4},{7,5},{8,10},{9,11},{10,... | collective-permute-start | bytes 110600 | tf_op jit(solution)/shard_map/ppermute | solution.py:333
  41.1 4.9 %collective-permute-start.16 = (bf16[144,128]{1,0:T(8,128)(2,1)S(1)}, bf16[144,128]{1,0:T(8,128)(2,1)S(1)}, u32[]{:S(2)}, u32[]{:S(2)}) collective-permute-start(bf16[144,128]{1,0:T(8,128)(2,1)S(1)} %get-tuple-element.51), channel_id=1, source_target_pairs={{0,1},{1,0},{2,3},{3,2},{4,5},{5,4},{6,7},{7,6},{8,9},{9,8},{10,11... | collective-permute-start | bytes 110600 | tf_op jit(solution)/shard_map/ppermute | solution.py:333

commit v16 on v13

--- a/solution.py
+++ b/solution.py
@@ -175,6 +175,7 @@
     ) = refs[10:]
     pair = 4
     pairs = status.shape[0] // pair
+
     def pick(t):
         table = jnp.concatenate([ref[t * rank : (t + 1) * rank, :] for ref in tables], axis=1)
         return jnp.dot(table, picks[t][...], preferred_element_type=f32)
@@ -231,8 +232,7 @@
     even, odd = (scaled_even, residual_even), (scaled_odd, residual_odd)
     residuals(0, *even)
 
-    @pl.loop(0, pairs // 2 - 1)
-    def _(n):
+    for n in range(pairs // 2 - 1):
         first = 2 * n * pair
         residuals(first + pair, *odd)
         gradients(first, *even)

time: 46.6 us -> 45.9 us (0.985)
  Pallas kernels: 12 us -> 11.3 us
    pallas_call x1, Pallas kernels: 5.56 us -> 4.84 us  [local(): pl.pallas_call(functools.partial(block_kernel, sizes), out_shape=(half, h...]
where the time goes in v16:
time: 45.9 us; the launch traced here: 45.7 us
  starting transfers between devices  18.8 us (41%)
  waiting for transfers between devices  14.7 us (32%)
  Pallas kernels  11.3 us (25%)
  between operations  0.83 us (2%)
    ppermute x17, starting transfers between devices, swap(): return lax.ppermute(array, axis, [(i, i ^ bits) for i in range(size)])  18.8 us
    ppermute x17, waiting for transfers between devices, swap(): return lax.ppermute(array, axis, [(i, i ^ bits) for i in range(size)])  14.7 us
    pallas_call x1, Pallas kernels, local(): pl.pallas_call(functools.partial(block_kernel, sizes), out_shape=(half, h...  4.84 us
    pallas_call x1, Pallas kernels, local(): pl.pallas_call(functools.partial(slot_kernel, sizes), out_shape=tuple([sh...  4.11 us
  transfers between devices with their start and end apart: 17, of which 11 were waited for; matrix products, arithmetic and copies ran while one was open for 0% of the time, Pallas kernels for 9%

profile of v16, /device:TPU:0, one launch (start us, length us, event | category | flops | bytes accessed | tf_op | source)
XLA Modules:
  0.0 45.7 jit_solution(2571628738951227810)
XLA Ops:
  0.6 0.9 %pack.1.refs_3_ = bf16[144,128]{1,0:T(8,128)(2,1)S(1)} custom-call(f32[64,128]{1,0:T(8,128)} %bitcast.13, f32[64,128]{1,0:T(8,128)} %bitcast.15, f32[32,64]{1,0:T(8,128)} %refs_10_.1), custom_call_target="tpu_custom_call" | custom-call | tf_op jit(solution)/shard_map/pack/pallas_call | solution.py:362
  1.5 4.1 %collective-permute-start.2 = (bf16[144,128]{1,0:T(8,128)(2,1)S(1)}, bf16[144,128]{1,0:T(8,128)(2,1)S(1)}, u32[]{:S(2)}, u32[]{:S(2)}) collective-permute-start(bf16[144,128]{1,0:T(8,128)(2,1)S(1)} %pack.1.refs_3_), channel_id=1, source_target_pairs={{0,2},{1,3},{2,0},{3,1},{4,6},{5,7},{6,4},{7,5},{8,10},{9,11},{10,... | collective-permute-start | bytes 110600 | tf_op jit(solution)/shard_map/ppermute | solution.py:333
  5.6 1.3 %collective-permute-start.1 = (bf16[144,128]{1,0:T(8,128)(2,1)S(1)}, bf16[144,128]{1,0:T(8,128)(2,1)S(1)}, u32[]{:S(2)}, u32[]{:S(2)}) collective-permute-start(bf16[144,128]{1,0:T(8,128)(2,1)S(1)} %pack.1.refs_3_), channel_id=1, source_target_pairs={{0,3},{1,2},{2,1},{3,0},{4,7},{5,6},{6,5},{7,4},{8,11},{9,10},{10,... | collective-permute-start | bytes 110600 | tf_op jit(solution)/shard_map/ppermute | solution.py:333
  7.0 0.2 collective-permute-start
  7.2 0.8 %collective-permute-done.2.refs_2_ = bf16[144,128]{1,0:T(8,128)(2,1)S(1)} collective-permute-done((bf16[144,128]{1,0:T(8,128)(2,1)S(1)}, bf16[144,128]{1,0:T(8,128)(2,1)S(1)}, u32[]{:S(2)}, u32[]{:S(2)}) %collective-permute-start.2) | collective-permute-done | bytes 36896 | tf_op jit(solution)/shard_map/ppermute | solution.py:333
  8.0 3.4 %collective-permute-done.1.refs_1_ = bf16[144,128]{1,0:T(8,128)(2,1)S(1)} collective-permute-done((bf16[144,128]{1,0:T(8,128)(2,1)S(1)}, bf16[144,128]{1,0:T(8,128)(2,1)S(1)}, u32[]{:S(2)}, u32[]{:S(2)}) %collective-permute-start.1) | collective-permute-done | bytes 36896 | tf_op jit(solution)/shard_map/ppermute | solution.py:333
  11.4 0.1 table.1.refs_3_.refs_0_
  11.5 2.5 %collective-permute-start.8 = (bf16[576,128]{1,0:T(8,128)(2,1)S(1)}, bf16[576,128]{1,0:T(8,128)(2,1)S(1)}, u32[]{:S(2)}, u32[]{:S(2)}) collective-permute-start(bf16[576,128]{1,0:T(8,128)(2,1)S(1)} %table.1.refs_3_.refs_0_), channel_id=1, source_target_pairs={{0,24},{4,28},{8,16},{12,20},{16,8},{20,12},{24,0},{28,4},{1,25},{... | collective-permute-start | bytes 442376 | tf_op jit(solution)/shard_map/ppermute | solution.py:333
  14.0 0.5 %collective-permute-start.6 = (bf16[576,128]{1,0:T(8,128)(2,1)S(1)}, bf16[576,128]{1,0:T(8,128)(2,1)S(1)}, u32[]{:S(2)}, u32[]{:S(2)}) collective-permute-start(bf16[576,128]{1,0:T(8,128)(2,1)S(1)} %table.1.refs_3_.refs_0_), channel_id=1, source_target_pairs={{0,16},{4,20},{8,24},{12,28},{16,0},{20,4},{24,8},{28,12},{1,17},{... | collective-permute-start | bytes 442376 | tf_op jit(solution)/shard_map/ppermute | solution.py:333
  14.5 0.5 %collective-permute-start.4 = (bf16[576,128]{1,0:T(8,128)(2,1)S(1)}, bf16[576,128]{1,0:T(8,128)(2,1)S(1)}, u32[]{:S(2)}, u32[]{:S(2)}) collective-permute-start(bf16[576,128]{1,0:T(8,128)(2,1)S(1)} %table.1.refs_3_.refs_0_), channel_id=1, source_target_pairs={{0,8},{4,12},{8,0},{12,4},{16,24},{20,28},{24,16},{28,20},{1,9},{5... | collective-permute-start | bytes 442376 | tf_op jit(solution)/shard_map/ppermute | solution.py:333
  15.0 4.1 %slots.1 = (bf16[1024,256]{1,0:T(8,128)(2,1)S(1)}, bf16[1024,256]{1,0:T(8,128)(2,1)S(1)}, bf16[256,32]{1,0:T(8,128)(2,1)S(1)}, bf16[384,256]{1,0:T(8,128)(2,1)S(...) custom-call(s32[1]{0:T(128)} %bitcast.2.me_ref, ...), custom_call_target="tpu_custom_call" | custom-call | tf_op jit(solution)/shard_map/slots/pallas_call | solution.py:382
  19.2 0.0 copy-start
  19.3 0.6 %collective-permute-start.9 = (bf16[576,128]{1,0:T(8,128)(2,1)S(1)}, bf16[576,128]{1,0:T(8,128)(2,1)S(1)}, u32[]{:S(2)}, u32[]{:S(2)}) collective-permute-start(bf16[576,128]{1,0:T(8,128)(2,1)S(1)} %collective-permute-done.8.refs_6_), channel_id=1, source_target_pairs={{0,4},{4,0},{8,12},{12,8},{16,20},{20,16},{24,28},{28,24},{1,5},{5... | collective-permute-start | bytes 442376 | tf_op jit(solution)/shard_map/ppermute | solution.py:333
  19.8 0.1 collective-permute-done.6.refs_4_
  20.0 0.6 %collective-permute-start.5 = (bf16[576,128]{1,0:T(8,128)(2,1)S(1)}, bf16[576,128]{1,0:T(8,128)(2,1)S(1)}, u32[]{:S(2)}, u32[]{:S(2)}) collective-permute-start(bf16[576,128]{1,0:T(8,128)(2,1)S(1)} %hold.1.refs_2_), channel_id=1, source_target_pairs={{0,4},{4,0},{8,12},{12,8},{16,20},{20,16},{24,28},{28,24},{1,5},{5... | collective-permute-start | bytes 442376 | tf_op jit(solution)/shard_map/ppermute | solution.py:333
  20.5 0.3 collective-permute-done.9.refs_7_
  20.9 0.5 collective-permute-done.7.refs_5_
  21.3 0.2 collective-permute-done.5.refs_3_
  21.5 4.8 %block_gradients.1 = (bf16[448,256]{1,0:T(8,128)(2,1)S(1)}, bf16[448,256]{1,0:T(8,128)(2,1)S(1)}) custom-call(bf16[576,128]{1,0:T(8,128)(2,1)S(1)} %table.1.refs_3_.refs_0_, bf16[576,128]{1,0:T(8,128)(2,1)S(1)} %collective-permute-done.3.refs_1_, bf16[576,128]{1,0:T(8,128)(2,1)S(1)} %hold.1.refs_2_, bf16[576,128]{1,0:T(8,128)(2,1)S(1)} %collective-permute-done.5.refs_3_, ...), custom_call_target="tpu_custom_call" | custom-call | tf_op jit(solution)/shard_map/block_gradients/pallas_call | solution.py:415
  26.4 0.4 collective-permute-start.10
  26.8 1.1 %collective-permute-done.10.crossed_ref.refs_1_ = bf16[448,256]{1,0:T(8,128)(2,1)S(1)} collective-permute-done((bf16[448,256]{1,0:T(8,128)(2,1)S(1)}, bf16[448,256]{1,0:T(8,128)(2,1)S(1)}, u32[]{:S(2)}, u32[]{:S(2)}) %collective-permute-start.10) | collective-permute-done | bytes 229408 | tf_op jit(solution)/shard_map/ppermute | solution.py:333
  28.0 2.4 %collective-permute-start.11 = (bf16[224,256]{1,0:T(8,128)(2,1)S(1)}, bf16[224,256]{1,0:T(8,128)(2,1)S(1)}, u32[]{:S(2)}, u32[]{:S(2)}) collective-permute-start(bf16[224,256]{1,0:T(8,128)(2,1)S(1)} %get-tuple-element.45), channel_id=1, source_target_pairs={{0,24},{4,28},{8,16},{12,20},{16,8},{20,12},{24,0},{28,4},{1,25},{... | collective-permute-start | bytes 344072 | tf_op jit(solution)/shard_map/ppermute | solution.py:333
  30.4 0.5 %collective-permute-start.12 = (bf16[224,256]{1,0:T(8,128)(2,1)S(1)}, bf16[224,256]{1,0:T(8,128)(2,1)S(1)}, u32[]{:S(2)}, u32[]{:S(2)}) collective-permute-start(bf16[224,256]{1,0:T(8,128)(2,1)S(1)} %get-tuple-element.46), channel_id=1, source_target_pairs={{0,16},{4,20},{8,24},{12,28},{16,0},{20,4},{24,8},{28,12},{1,17},{... | collective-permute-start | bytes 344072 | tf_op jit(solution)/shard_map/ppermute | solution.py:333
  30.9 0.6 %collective-permute-start.13 = (bf16[224,256]{1,0:T(8,128)(2,1)S(1)}, bf16[224,256]{1,0:T(8,128)(2,1)S(1)}, u32[]{:S(2)}, u32[]{:S(2)}) collective-permute-start(bf16[224,256]{1,0:T(8,128)(2,1)S(1)} %get-tuple-element.47), channel_id=1, source_target_pairs={{0,8},{4,12},{8,0},{12,4},{16,24},{20,28},{24,16},{28,20},{1,9},{5... | collective-permute-start | bytes 344072 | tf_op jit(solution)/shard_map/ppermute | solution.py:333
  31.5 2.9 %collective-permute-done.11.refs_2_ = bf16[224,256]{1,0:T(8,128)(2,1)S(1)} collective-permute-done((bf16[224,256]{1,0:T(8,128)(2,1)S(1)}, bf16[224,256]{1,0:T(8,128)(2,1)S(1)}, u32[]{:S(2)}, u32[]{:S(2)}) %collective-permute-start.11) | collective-permute-done | bytes 114720 | tf_op jit(solution)/shard_map/ppermute | solution.py:333
  34.5 2.4 %collective-permute-done.12.refs_3_ = bf16[224,256]{1,0:T(8,128)(2,1)S(1)} collective-permute-done((bf16[224,256]{1,0:T(8,128)(2,1)S(1)}, bf16[224,256]{1,0:T(8,128)(2,1)S(1)}, u32[]{:S(2)}, u32[]{:S(2)}) %collective-permute-start.12) | collective-permute-done | bytes 114720 | tf_op jit(solution)/shard_map/ppermute | solution.py:333
  36.8 0.6 %row_sums.1 = (bf16[144,128]{1,0:T(8,128)(2,1)S(1)}, bf16[144,128]{1,0:T(8,128)(2,1)S(1)}, bf16[144,128]{1,0:T(8,128)(2,1)S(1)}, bf16[144,128]{1,0:T(8,128)(2,1)S(1)}) custom-call(bf16[448,256]{1,0:T(8,128)(2,1)S(1)} %get-tuple-element.43.own_ref.refs_0_, bf16[448,256]{1,0:T(8,128)(2,1)S(1)} %collective-permute-done.10.crossed_ref.refs_1_, ...), custom_call_target="tpu_custom_call" | custom-call | tf_op jit(solution)/shard_map/row_sums/pallas_call | solution.py:449
  37.4 2.6 %collective-permute-start.14 = (bf16[144,128]{1,0:T(8,128)(2,1)S(1)}, bf16[144,128]{1,0:T(8,128)(2,1)S(1)}, u32[]{:S(2)}, u32[]{:S(2)}) collective-permute-start(bf16[144,128]{1,0:T(8,128)(2,1)S(1)} %get-tuple-element.49), channel_id=1, source_target_pairs={{0,3},{1,2},{2,1},{3,0},{4,7},{5,6},{6,5},{7,4},{8,11},{9,10},{10,... | collective-permute-start | bytes 110600 | tf_op jit(solution)/shard_map/ppermute | solution.py:333
  40.0 1.8 %collective-permute-start.16 = (bf16[144,128]{1,0:T(8,128)(2,1)S(1)}, bf16[144,128]{1,0:T(8,128)(2,1)S(1)}, u32[]{:S(2)}, u32[]{:S(2)}) collective-permute-start(bf16[144,128]{1,0:T(8,128)(2,1)S(1)} %get-tuple-element.51), channel_id=1, source_target_pairs={{0,1},{1,0},{2,3},{3,2},{4,5},{5,4},{6,7},{7,6},{8,9},{9,8},{10,11... | collective-permute-start | bytes 110600 | tf_op jit(solution)/shard_map/ppermute | solution.py:333
  41.8 1.4 %collective-permute-done.14.refs_1_ = bf16[144,128]{1,0:T(8,128)(2,1)S(1)} collective-permute-done((bf16[144,128]{1,0:T(8,128)(2,1)S(1)}, bf16[144,128]{1,0:T(8,128)(2,1)S(1)}, u32[]{:S(2)}, u32[]{:S(2)}) %collective-permute-start.14) | collective-permute-done | bytes 36896 | tf_op jit(solution)/shard_map/ppermute | solution.py:333
  43.2 1.7 %collective-permute-done.15.refs_2_ = bf16[144,128]{1,0:T(8,128)(2,1)S(1)} collective-permute-done((bf16[144,128]{1,0:T(8,128)(2,1)S(1)}, bf16[144,128]{1,0:T(8,128)(2,1)S(1)}, u32[]{:S(2)}, u32[]{:S(2)}) %collective-permute-start.15) | collective-permute-done | bytes 36896 | tf_op jit(solution)/shard_map/ppermute | solution.py:333
  44.9 0.7 %adam.1 = (f32[64,128]{1,0:T(8,128)}, f32[64,128]{1,0:T(8,128)}, f32[64,128]{1,0:T(8,128)}, f32[64,128]{1,0:T(8,128)}, f32[64,128]{1,0:T(8,128)}, /*index=5*/f32...) custom-call(bf16[144,128]{1,0:T(8,128)(2,1)S(1)} %get-tuple-element.48.refs_0_, ...), custom_call_target="tpu_custom_call" | custom-call | tf_op jit(solution)/shard_map/adam/pallas_call | solution.py:470
  (28 shorter events, 0.1 us)
Async XLA Ops:
  1.5 6.4 %collective-permute-start.2 = (bf16[144,128]{1,0:T(8,128)(2,1)S(1)}, bf16[144,128]{1,0:T(8,128)(2,1)S(1)}, u32[]{:S(2)}, u32[]{:S(2)}) collective-permute-start(bf16[144,128]{1,0:T(8,128)(2,1)S(1)} %pack.1.refs_3_), channel_id=1, source_target_pairs={{0,2},{1,3},{2,0},{3,1},{4,6},{5,7},{6,4},{7,5},{8,10},{9,11},{10,... | collective-permute-start | bytes 110600 | tf_op jit(solution)/shard_map/ppermute | solution.py:333
  5.6 5.8 %collective-permute-start.1 = (bf16[144,128]{1,0:T(8,128)(2,1)S(1)}, bf16[144,128]{1,0:T(8,128)(2,1)S(1)}, u32[]{:S(2)}, u32[]{:S(2)}) collective-permute-start(bf16[144,128]{1,0:T(8,128)(2,1)S(1)} %pack.1.refs_3_), channel_id=1, source_target_pairs={{0,3},{1,2},{2,1},{3,0},{4,7},{5,6},{6,5},{7,4},{8,11},{9,10},{10,... | collective-permute-start | bytes 110600 | tf_op jit(solution)/shard_map/ppermute | solution.py:333
  7.0 4.4 %collective-permute-start = (bf16[144,128]{1,0:T(8,128)(2,1)S(1)}, bf16[144,128]{1,0:T(8,128)(2,1)S(1)}, u32[]{:S(2)}, u32[]{:S(2)}) collective-permute-start(bf16[144,128]{1,0:T(8,128)(2,1)S(1)} %pack.1.refs_3_), channel_id=1, source_target_pairs={{0,1},{1,0},{2,3},{3,2},{4,5},{5,4},{6,7},{7,6},{8,9},{9,8},{10,11... | collective-permute-start | bytes 110600 | tf_op jit(solution)/shard_map/ppermute | solution.py:333
  11.5 7.7 %collective-permute-start.8 = (bf16[576,128]{1,0:T(8,128)(2,1)S(1)}, bf16[576,128]{1,0:T(8,128)(2,1)S(1)}, u32[]{:S(2)}, u32[]{:S(2)}) collective-permute-start(bf16[576,128]{1,0:T(8,128)(2,1)S(1)} %table.1.refs_3_.refs_0_), channel_id=1, source_target_pairs={{0,24},{4,28},{8,16},{12,20},{16,8},{20,12},{24,0},{28,4},{1,25},{... | collective-permute-start | bytes 442376 | tf_op jit(solution)/shard_map/ppermute | solution.py:333
  14.0 6.0 %collective-permute-start.6 = (bf16[576,128]{1,0:T(8,128)(2,1)S(1)}, bf16[576,128]{1,0:T(8,128)(2,1)S(1)}, u32[]{:S(2)}, u32[]{:S(2)}) collective-permute-start(bf16[576,128]{1,0:T(8,128)(2,1)S(1)} %table.1.refs_3_.refs_0_), channel_id=1, source_target_pairs={{0,16},{4,20},{8,24},{12,28},{16,0},{20,4},{24,8},{28,12},{1,17},{... | collective-permute-start | bytes 442376 | tf_op jit(solution)/shard_map/ppermute | solution.py:333
  14.5 5.4 %collective-permute-start.4 = (bf16[576,128]{1,0:T(8,128)(2,1)S(1)}, bf16[576,128]{1,0:T(8,128)(2,1)S(1)}, u32[]{:S(2)}, u32[]{:S(2)}) collective-permute-start(bf16[576,128]{1,0:T(8,128)(2,1)S(1)} %table.1.refs_3_.refs_0_), channel_id=1, source_target_pairs={{0,8},{4,12},{8,0},{12,4},{16,24},{20,28},{24,16},{28,20},{1,9},{5... | collective-permute-start | bytes 442376 | tf_op jit(solution)/shard_map/ppermute | solution.py:333
  15.0 5.5 %collective-permute-start.3 = (bf16[576,128]{1,0:T(8,128)(2,1)S(1)}, bf16[576,128]{1,0:T(8,128)(2,1)S(1)}, u32[]{:S(2)}, u32[]{:S(2)}) collective-permute-start(bf16[576,128]{1,0:T(8,128)(2,1)S(1)} %table.1.refs_3_.refs_0_), channel_id=1, source_target_pairs={{0,4},{4,0},{8,12},{12,8},{16,20},{20,16},{24,28},{28,24},{1,5},{5... | collective-permute-start | bytes 442376 | tf_op jit(solution)/shard_map/ppermute | solution.py:333
  19.2 25.7 %copy-start = (f32[128,64]{0,1:T(8,128)S(1)}, f32[128,64]{0,1:T(8,128)}, u32[]{:S(2)}) copy-start(f32[128,64]{0,1:T(8,128)} %param.17) | copy-start | bytes 98308
  19.2 25.7 %copy-start.1 = (f32[128,64]{0,1:T(8,128)S(1)}, f32[128,64]{0,1:T(8,128)}, u32[]{:S(2)}) copy-start(f32[128,64]{0,1:T(8,128)} %param.20) | copy-start | bytes 98308
  19.2 25.7 %copy-start.2 = (f32[32,64]{1,0:T(8,128)S(1)}, f32[32,64]{1,0:T(8,128)}, u32[]{:S(2)}) copy-start(f32[32,64]{1,0:T(8,128)} %refs_10_.1) | copy-start | bytes 24580
  19.2 25.7 %copy-start.3 = (f32[128,64]{0,1:T(8,128)S(1)}, f32[128,64]{0,1:T(8,128)}, u32[]{:S(2)}) copy-start(f32[128,64]{0,1:T(8,128)} %param.18) | copy-start | bytes 98308
  19.2 25.7 %copy-start.4 = (f32[128,64]{0,1:T(8,128)S(1)}, f32[128,64]{0,1:T(8,128)}, u32[]{:S(2)}) copy-start(f32[128,64]{0,1:T(8,128)} %param.19) | copy-start | bytes 98308
  19.2 25.7 %copy-start.5 = (f32[128,64]{0,1:T(8,128)S(1)}, f32[128,64]{0,1:T(8,128)}, u32[]{:S(2)}) copy-start(f32[128,64]{0,1:T(8,128)} %param.21) | copy-start | bytes 98308
  19.2 25.7 %copy-start.6 = (f32[128,64]{0,1:T(8,128)S(1)}, f32[128,64]{0,1:T(8,128)}, u32[]{:S(2)}) copy-start(f32[128,64]{0,1:T(8,128)} %param.22) | copy-start | bytes 98308
  19.2 25.7 %copy-start.7 = (f32[32,64]{1,0:T(8,128)S(1)}, f32[32,64]{1,0:T(8,128)}, u32[]{:S(2)}) copy-start(f32[32,64]{1,0:T(8,128)} %refs_11_.1) | copy-start | bytes 24580
  19.3 25.7 %copy-start.8 = (f32[32,64]{1,0:T(8,128)S(1)}, f32[32,64]{1,0:T(8,128)}, u32[]{:S(2)}) copy-start(f32[32,64]{1,0:T(8,128)} %refs_12_.1) | copy-start | bytes 24580
  19.3 1.6 %collective-permute-start.9 = (bf16[576,128]{1,0:T(8,128)(2,1)S(1)}, bf16[576,128]{1,0:T(8,128)(2,1)S(1)}, u32[]{:S(2)}, u32[]{:S(2)}) collective-permute-start(bf16[576,128]{1,0:T(8,128)(2,1)S(1)} %collective-permute-done.8.refs_6_), channel_id=1, source_target_pairs={{0,4},{4,0},{8,12},{12,8},{16,20},{20,16},{24,28},{28,24},{1,5},{5... | collective-permute-start | bytes 442376 | tf_op jit(solution)/shard_map/ppermute | solution.py:333
  19.9 1.4 %collective-permute-start.7 = (bf16[576,128]{1,0:T(8,128)(2,1)S(1)}, bf16[576,128]{1,0:T(8,128)(2,1)S(1)}, u32[]{:S(2)}, u32[]{:S(2)}) collective-permute-start(bf16[576,128]{1,0:T(8,128)(2,1)S(1)} %collective-permute-done.6.refs_4_), channel_id=1, source_target_pairs={{0,4},{4,0},{8,12},{12,8},{16,20},{20,16},{24,28},{28,24},{1,5},{5... | collective-permute-start | bytes 442376 | tf_op jit(solution)/shard_map/ppermute | solution.py:333
  20.0 1.6 %collective-permute-start.5 = (bf16[576,128]{1,0:T(8,128)(2,1)S(1)}, bf16[576,128]{1,0:T(8,128)(2,1)S(1)}, u32[]{:S(2)}, u32[]{:S(2)}) collective-permute-start(bf16[576,128]{1,0:T(8,128)(2,1)S(1)} %hold.1.refs_2_), channel_id=1, source_target_pairs={{0,4},{4,0},{8,12},{12,8},{16,20},{20,16},{24,28},{28,24},{1,5},{5... | collective-permute-start | bytes 442376 | tf_op jit(solution)/shard_map/ppermute | solution.py:333
  26.4 1.6 %collective-permute-start.10 = (bf16[448,256]{1,0:T(8,128)(2,1)S(1)}, bf16[448,256]{1,0:T(8,128)(2,1)S(1)}, u32[]{:S(2)}, u32[]{:S(2)}) collective-permute-start(bf16[448,256]{1,0:T(8,128)(2,1)S(1)} %get-tuple-element.44), channel_id=1, source_target_pairs={{0,4},{4,0},{8,12},{12,8},{16,20},{20,16},{24,28},{28,24},{1,5},{5... | collective-permute-start | bytes 688136 | tf_op jit(solution)/shard_map/ppermute | solution.py:333
  28.0 6.5 %collective-permute-start.11 = (bf16[224,256]{1,0:T(8,128)(2,1)S(1)}, bf16[224,256]{1,0:T(8,128)(2,1)S(1)}, u32[]{:S(2)}, u32[]{:S(2)}) collective-permute-start(bf16[224,256]{1,0:T(8,128)(2,1)S(1)} %get-tuple-element.45), channel_id=1, source_target_pairs={{0,24},{4,28},{8,16},{12,20},{16,8},{20,12},{24,0},{28,4},{1,25},{... | collective-permute-start | bytes 344072 | tf_op jit(solution)/shard_map/ppermute | solution.py:333
  30.4 6.4 %collective-permute-start.12 = (bf16[224,256]{1,0:T(8,128)(2,1)S(1)}, bf16[224,256]{1,0:T(8,128)(2,1)S(1)}, u32[]{:S(2)}, u32[]{:S(2)}) collective-permute-start(bf16[224,256]{1,0:T(8,128)(2,1)S(1)} %get-tuple-element.46), channel_id=1, source_target_pairs={{0,16},{4,20},{8,24},{12,28},{16,0},{20,4},{24,8},{28,12},{1,17},{... | collective-permute-start | bytes 344072 | tf_op jit(solution)/shard_map/ppermute | solution.py:333
  30.9 5.9 %collective-permute-start.13 = (bf16[224,256]{1,0:T(8,128)(2,1)S(1)}, bf16[224,256]{1,0:T(8,128)(2,1)S(1)}, u32[]{:S(2)}, u32[]{:S(2)}) collective-permute-start(bf16[224,256]{1,0:T(8,128)(2,1)S(1)} %get-tuple-element.47), channel_id=1, source_target_pairs={{0,8},{4,12},{8,0},{12,4},{16,24},{20,28},{24,16},{28,20},{1,9},{5... | collective-permute-start | bytes 344072 | tf_op jit(solution)/shard_map/ppermute | solution.py:333
  37.4 5.8 %collective-permute-start.14 = (bf16[144,128]{1,0:T(8,128)(2,1)S(1)}, bf16[144,128]{1,0:T(8,128)(2,1)S(1)}, u32[]{:S(2)}, u32[]{:S(2)}) collective-permute-start(bf16[144,128]{1,0:T(8,128)(2,1)S(1)} %get-tuple-element.49), channel_id=1, source_target_pairs={{0,3},{1,2},{2,1},{3,0},{4,7},{5,6},{6,5},{7,4},{8,11},{9,10},{10,... | collective-permute-start | bytes 110600 | tf_op jit(solution)/shard_map/ppermute | solution.py:333
  40.0 4.9 %collective-permute-start.15 = (bf16[144,128]{1,0:T(8,128)(2,1)S(1)}, bf16[144,128]{1,0:T(8,128)(2,1)S(1)}, u32[]{:S(2)}, u32[]{:S(2)}) collective-permute-start(bf16[144,128]{1,0:T(8,128)(2,1)S(1)} %get-tuple-element.50), channel_id=1, source_target_pairs={{0,2},{1,3},{2,0},{3,1},{4,6},{5,7},{6,4},{7,5},{8,10},{9,11},{10,... | collective-permute-start | bytes 110600 | tf_op jit(solution)/shard_map/ppermute | solution.py:333
  40.0 4.9 %collective-permute-start.16 = (bf16[144,128]{1,0:T(8,128)(2,1)S(1)}, bf16[144,128]{1,0:T(8,128)(2,1)S(1)}, u32[]{:S(2)}, u32[]{:S(2)}) collective-permute-start(bf16[144,128]{1,0:T(8,128)(2,1)S(1)} %get-tuple-element.51), channel_id=1, source_target_pairs={{0,1},{1,0},{2,3},{3,2},{4,5},{5,4},{6,7},{7,6},{8,9},{9,8},{10,11... | collective-permute-start | bytes 110600 | tf_op jit(solution)/shard_map/ppermute | solution.py:333

commit v17 on v16

--- a/solution.py
+++ b/solution.py
@@ -173,7 +173,7 @@
         residual_even,
         residual_odd,
     ) = refs[10:]
-    pair = 4
+    pair = 8
     pairs = status.shape[0] // pair
 
     def pick(t):
@@ -270,14 +270,8 @@
         out[rows:, :] = crossed_ref[start : start + rows, :]
 
 
-def sum_kernel(sizes, *refs):
-    holders, columns = sizes.holders, sizes.columns
-    inputs = sizes.owners // 2 + 1
-    arrived, outs = refs[:inputs], refs[inputs:]
+def add_messages(sizes, totals, messages):
     day_start = sizes.slot_starts[2]
-    totals = [0.0, 0.0, 0.0]
-    messages = [ref.at[: sizes.slot_rows] for ref in arrived]
-    messages += [ref.at[sizes.slot_rows :] for ref in arrived[2:]]
     for ref in messages:
         notes = ref[day_start : day_start + sizes.slots[2], :].astype(f32)
         rows = notes[sizes.note_row : sizes.note_row + 1, : sizes.slot_rows].astype(jnp.int32)
@@ -288,6 +282,22 @@
             mine = (slot >= start) & (slot < start + slots)
             selector = onehot((iota(shape, 0) == rows) & mine)
             totals[t] = totals[t] + jnp.dot(selector, ref[...], preferred_element_type=f32)
+    return totals
+
+
+def early_sum_kernel(sizes, own_ref, crossed_ref, arrived_ref, *outs):
+    rows = sizes.slot_rows
+    messages = [own_ref.at[:rows], crossed_ref.at[:rows]]
+    messages += [arrived_ref.at[:rows], arrived_ref.at[rows:]]
+    for out, total in zip(outs, add_messages(sizes, [0.0, 0.0, 0.0], messages)):
+        out[...] = total
+
+
+def sum_kernel(sizes, *refs):
+    holders, columns, rows = sizes.holders, sizes.columns, sizes.slot_rows
+    early, arrived, outs = refs[:3], refs[3:-holders], refs[-holders:]
+    messages = [ref.at[:rows] for ref in arrived] + [ref.at[rows:] for ref in arrived]
+    totals = add_messages(sizes, [ref[...] for ref in early], messages)
     for t in range(3):
         if t < 2:
             turned = totals[t].T.astype(bf16)
@@ -425,10 +435,10 @@
             pltpu.VMEM((users, sizes.rank), f32),
             pltpu.VMEM((items, sizes.rank), f32),
             pltpu.VMEM((days, sizes.rank), f32),
-            pltpu.VMEM((4 * users, sizes.rank), bf16),
-            pltpu.VMEM((4 * users, sizes.rank), bf16),
-            pltpu.VMEM((4 * users, items), bf16),
-            pltpu.VMEM((4 * users, items), bf16),
+            pltpu.VMEM((8 * users, sizes.rank), bf16),
+            pltpu.VMEM((8 * users, sizes.rank), bf16),
+            pltpu.VMEM((8 * users, items), bf16),
+            pltpu.VMEM((8 * users, items), bf16),
         ],
         compiler_params=pltpu.CompilerParams(vmem_limit_bytes=BLOCK_VMEM),
         name="block_gradients",
@@ -446,12 +456,18 @@
         swap(merged[bits // 2 - 1], "dp", owners, bits) for bits in range(owners - 2, 0, -2)
     ]
 
+    early = pl.pallas_call(
+        functools.partial(early_sum_kernel, sizes),
+        out_shape=tuple(shape((rows, sizes.rank), f32) for rows in row_counts),
+        compiler_params=small,
+        name="early_sums",
+    )(*returned[:3])
     totals = pl.pallas_call(
         functools.partial(sum_kernel, sizes),
         out_shape=tuple([shape(piece.shape, bf16)] * holders),
         compiler_params=small,
         name="row_sums",
-    )(*returned)
+    )(*early, *returned[3:])
     column_totals = [totals[0]] + [
         swap(totals[bits], "mp", holders, bits) for bits in range(holders - 1, 0, -1)
     ]

time: 45.9 us -> 46 us (level)
  transfers between devices with their start and end apart: 17 -> 17, of which waited for: 11 -> 11; matrix products, arithmetic and copies ran while one was open for 0% -> 0% of each run, Pallas kernels for 9% -> 10%
where the time goes in v17:
time: 46 us; the launch traced here: 45.7 us
  starting transfers between devices  18.8 us (41%)
  waiting for transfers between devices  14.4 us (31%)
  Pallas kernels  11.7 us (25%)
  between operations  0.83 us (2%)
    ppermute x17, starting transfers between devices, swap(): return lax.ppermute(array, axis, [(i, i ^ bits) for i in range(size)])  18.8 us
    ppermute x17, waiting for transfers between devices, swap(): return lax.ppermute(array, axis, [(i, i ^ bits) for i in range(size)])  14.4 us
    pallas_call x1, Pallas kernels, local(): pl.pallas_call(functools.partial(block_kernel, sizes), out_shape=(half, h...  5.03 us
    pallas_call x1, Pallas kernels, local(): pl.pallas_call(functools.partial(slot_kernel, sizes), out_shape=tuple([sh...  4.11 us
  transfers between devices with their start and end apart: 17, of which 11 were waited for; matrix products, arithmetic and copies ran while one was open for 0% of the time, Pallas kernels for 10%

profile of v17, /device:TPU:0, one launch (start us, length us, event | category | flops | bytes accessed | tf_op | source)
XLA Modules:
  0.0 45.7 jit_solution(12340468780121208575)
XLA Ops:
  0.6 0.9 %pack.1.refs_3_ = bf16[144,128]{1,0:T(8,128)(2,1)S(1)} custom-call(f32[64,128]{1,0:T(8,128)} %bitcast.13, f32[64,128]{1,0:T(8,128)} %bitcast.15, f32[32,64]{1,0:T(8,128)} %refs_10_.1), custom_call_target="tpu_custom_call" | custom-call | tf_op jit(solution)/shard_map/pack/pallas_call | solution.py:372
  1.5 4.1 %collective-permute-start.2 = (bf16[144,128]{1,0:T(8,128)(2,1)S(1)}, bf16[144,128]{1,0:T(8,128)(2,1)S(1)}, u32[]{:S(2)}, u32[]{:S(2)}) collective-permute-start(bf16[144,128]{1,0:T(8,128)(2,1)S(1)} %pack.1.refs_3_), channel_id=1, source_target_pairs={{0,2},{1,3},{2,0},{3,1},{4,6},{5,7},{6,4},{7,5},{8,10},{9,11},{10,... | collective-permute-start | bytes 110600 | tf_op jit(solution)/shard_map/ppermute | solution.py:343
  5.6 1.3 %collective-permute-start.1 = (bf16[144,128]{1,0:T(8,128)(2,1)S(1)}, bf16[144,128]{1,0:T(8,128)(2,1)S(1)}, u32[]{:S(2)}, u32[]{:S(2)}) collective-permute-start(bf16[144,128]{1,0:T(8,128)(2,1)S(1)} %pack.1.refs_3_), channel_id=1, source_target_pairs={{0,3},{1,2},{2,1},{3,0},{4,7},{5,6},{6,5},{7,4},{8,11},{9,10},{10,... | collective-permute-start | bytes 110600 | tf_op jit(solution)/shard_map/ppermute | solution.py:343
  7.0 0.2 collective-permute-start
  7.2 0.8 %collective-permute-done.2.refs_2_ = bf16[144,128]{1,0:T(8,128)(2,1)S(1)} collective-permute-done((bf16[144,128]{1,0:T(8,128)(2,1)S(1)}, bf16[144,128]{1,0:T(8,128)(2,1)S(1)}, u32[]{:S(2)}, u32[]{:S(2)}) %collective-permute-start.2) | collective-permute-done | bytes 36896 | tf_op jit(solution)/shard_map/ppermute | solution.py:343
  8.0 3.4 %collective-permute-done.1.refs_1_ = bf16[144,128]{1,0:T(8,128)(2,1)S(1)} collective-permute-done((bf16[144,128]{1,0:T(8,128)(2,1)S(1)}, bf16[144,128]{1,0:T(8,128)(2,1)S(1)}, u32[]{:S(2)}, u32[]{:S(2)}) %collective-permute-start.1) | collective-permute-done | bytes 36896 | tf_op jit(solution)/shard_map/ppermute | solution.py:343
  11.4 0.1 table.1.refs_3_.refs_0_
  11.5 2.5 %collective-permute-start.8 = (bf16[576,128]{1,0:T(8,128)(2,1)S(1)}, bf16[576,128]{1,0:T(8,128)(2,1)S(1)}, u32[]{:S(2)}, u32[]{:S(2)}) collective-permute-start(bf16[576,128]{1,0:T(8,128)(2,1)S(1)} %table.1.refs_3_.refs_0_), channel_id=1, source_target_pairs={{0,24},{4,28},{8,16},{12,20},{16,8},{20,12},{24,0},{28,4},{1,25},{... | collective-permute-start | bytes 442376 | tf_op jit(solution)/shard_map/ppermute | solution.py:343
  14.0 0.5 %collective-permute-start.6 = (bf16[576,128]{1,0:T(8,128)(2,1)S(1)}, bf16[576,128]{1,0:T(8,128)(2,1)S(1)}, u32[]{:S(2)}, u32[]{:S(2)}) collective-permute-start(bf16[576,128]{1,0:T(8,128)(2,1)S(1)} %table.1.refs_3_.refs_0_), channel_id=1, source_target_pairs={{0,16},{4,20},{8,24},{12,28},{16,0},{20,4},{24,8},{28,12},{1,17},{... | collective-permute-start | bytes 442376 | tf_op jit(solution)/shard_map/ppermute | solution.py:343
  14.5 0.5 %collective-permute-start.4 = (bf16[576,128]{1,0:T(8,128)(2,1)S(1)}, bf16[576,128]{1,0:T(8,128)(2,1)S(1)}, u32[]{:S(2)}, u32[]{:S(2)}) collective-permute-start(bf16[576,128]{1,0:T(8,128)(2,1)S(1)} %table.1.refs_3_.refs_0_), channel_id=1, source_target_pairs={{0,8},{4,12},{8,0},{12,4},{16,24},{20,28},{24,16},{28,20},{1,9},{5... | collective-permute-start | bytes 442376 | tf_op jit(solution)/shard_map/ppermute | solution.py:343
  15.0 4.1 %slots.1 = (bf16[1024,256]{1,0:T(8,128)(2,1)S(1)}, bf16[1024,256]{1,0:T(8,128)(2,1)S(1)}, bf16[256,32]{1,0:T(8,128)(2,1)S(1)}, bf16[384,256]{1,0:T(8,128)(2,1)S(...) custom-call(s32[1]{0:T(128)} %bitcast.2.me_ref, ...), custom_call_target="tpu_custom_call" | custom-call | tf_op jit(solution)/shard_map/slots/pallas_call | solution.py:392
  19.3 0.6 %collective-permute-start.9 = (bf16[576,128]{1,0:T(8,128)(2,1)S(1)}, bf16[576,128]{1,0:T(8,128)(2,1)S(1)}, u32[]{:S(2)}, u32[]{:S(2)}) collective-permute-start(bf16[576,128]{1,0:T(8,128)(2,1)S(1)} %collective-permute-done.8.refs_6_), channel_id=1, source_target_pairs={{0,4},{4,0},{8,12},{12,8},{16,20},{20,16},{24,28},{28,24},{1,5},{5... | collective-permute-start | bytes 442376 | tf_op jit(solution)/shard_map/ppermute | solution.py:343
  19.8 0.1 collective-permute-done.6.refs_4_
  20.0 0.6 %collective-permute-start.5 = (bf16[576,128]{1,0:T(8,128)(2,1)S(1)}, bf16[576,128]{1,0:T(8,128)(2,1)S(1)}, u32[]{:S(2)}, u32[]{:S(2)}) collective-permute-start(bf16[576,128]{1,0:T(8,128)(2,1)S(1)} %hold.1.refs_2_), channel_id=1, source_target_pairs={{0,4},{4,0},{8,12},{12,8},{16,20},{20,16},{24,28},{28,24},{1,5},{5... | collective-permute-start | bytes 442376 | tf_op jit(solution)/shard_map/ppermute | solution.py:343
  20.5 0.3 collective-permute-done.9.refs_7_
  20.9 0.5 collective-permute-done.7.refs_5_
  21.3 0.2 collective-permute-done.5.refs_3_
  21.5 5.0 %block_gradients.1 = (bf16[448,256]{1,0:T(8,128)(2,1)S(1)}, bf16[448,256]{1,0:T(8,128)(2,1)S(1)}) custom-call(bf16[576,128]{1,0:T(8,128)(2,1)S(1)} %table.1.refs_3_.refs_0_, bf16[576,128]{1,0:T(8,128)(2,1)S(1)} %collective-permute-done.3.refs_1_, bf16[576,128]{1,0:T(8,128)(2,1)S(1)} %hold.1.refs_2_, bf16[576,128]{1,0:T(8,128)(2,1)S(1)} %collective-permute-done.5.refs_3_, ...), custom_call_target="tpu_custom_call" | custom-call | tf_op jit(solution)/shard_map/block_gradients/pallas_call | solution.py:425
  26.6 0.4 collective-permute-start.10
  27.0 1.1 %collective-permute-done.10.crossed_ref = bf16[448,256]{1,0:T(8,128)(2,1)S(1)} collective-permute-done((bf16[448,256]{1,0:T(8,128)(2,1)S(1)}, bf16[448,256]{1,0:T(8,128)(2,1)S(1)}, u32[]{:S(2)}, u32[]{:S(2)}) %collective-permute-start.10) | collective-permute-done | bytes 229408 | tf_op jit(solution)/shard_map/ppermute | solution.py:343
  28.2 2.4 %collective-permute-start.11 = (bf16[224,256]{1,0:T(8,128)(2,1)S(1)}, bf16[224,256]{1,0:T(8,128)(2,1)S(1)}, u32[]{:S(2)}, u32[]{:S(2)}) collective-permute-start(bf16[224,256]{1,0:T(8,128)(2,1)S(1)} %get-tuple-element.48), channel_id=1, source_target_pairs={{0,24},{4,28},{8,16},{12,20},{16,8},{20,12},{24,0},{28,4},{1,25},{... | collective-permute-start | bytes 344072 | tf_op jit(solution)/shard_map/ppermute | solution.py:343
  30.6 0.5 %collective-permute-start.12 = (bf16[224,256]{1,0:T(8,128)(2,1)S(1)}, bf16[224,256]{1,0:T(8,128)(2,1)S(1)}, u32[]{:S(2)}, u32[]{:S(2)}) collective-permute-start(bf16[224,256]{1,0:T(8,128)(2,1)S(1)} %get-tuple-element.52), channel_id=1, source_target_pairs={{0,16},{4,20},{8,24},{12,28},{16,0},{20,4},{24,8},{28,12},{1,17},{... | collective-permute-start | bytes 344072 | tf_op jit(solution)/shard_map/ppermute | solution.py:343
  31.1 0.6 %collective-permute-start.13 = (bf16[224,256]{1,0:T(8,128)(2,1)S(1)}, bf16[224,256]{1,0:T(8,128)(2,1)S(1)}, u32[]{:S(2)}, u32[]{:S(2)}) collective-permute-start(bf16[224,256]{1,0:T(8,128)(2,1)S(1)} %get-tuple-element.53), channel_id=1, source_target_pairs={{0,8},{4,12},{8,0},{12,4},{16,24},{20,28},{24,16},{28,20},{1,9},{5... | collective-permute-start | bytes 344072 | tf_op jit(solution)/shard_map/ppermute | solution.py:343
  31.7 2.9 %collective-permute-done.11.arrived_ref = bf16[224,256]{1,0:T(8,128)(2,1)S(1)} collective-permute-done((bf16[224,256]{1,0:T(8,128)(2,1)S(1)}, bf16[224,256]{1,0:T(8,128)(2,1)S(1)}, u32[]{:S(2)}, u32[]{:S(2)}) %collective-permute-start.11) | collective-permute-done | bytes 114720 | tf_op jit(solution)/shard_map/ppermute | solution.py:343
  34.6 0.3 early_sums.1
  35.0 2.0 %collective-permute-done.12.refs_3_ = bf16[224,256]{1,0:T(8,128)(2,1)S(1)} collective-permute-done((bf16[224,256]{1,0:T(8,128)(2,1)S(1)}, bf16[224,256]{1,0:T(8,128)(2,1)S(1)}, u32[]{:S(2)}, u32[]{:S(2)}) %collective-permute-start.12) | collective-permute-done | bytes 114720 | tf_op jit(solution)/shard_map/ppermute | solution.py:343
  37.0 0.4 row_sums.1
  37.4 2.6 %collective-permute-start.14 = (bf16[144,128]{1,0:T(8,128)(2,1)S(1)}, bf16[144,128]{1,0:T(8,128)(2,1)S(1)}, u32[]{:S(2)}, u32[]{:S(2)}) collective-permute-start(bf16[144,128]{1,0:T(8,128)(2,1)S(1)} %get-tuple-element.55), channel_id=1, source_target_pairs={{0,3},{1,2},{2,1},{3,0},{4,7},{5,6},{6,5},{7,4},{8,11},{9,10},{10,... | collective-permute-start | bytes 110600 | tf_op jit(solution)/shard_map/ppermute | solution.py:343
  40.1 1.8 %collective-permute-start.16 = (bf16[144,128]{1,0:T(8,128)(2,1)S(1)}, bf16[144,128]{1,0:T(8,128)(2,1)S(1)}, u32[]{:S(2)}, u32[]{:S(2)}) collective-permute-start(bf16[144,128]{1,0:T(8,128)(2,1)S(1)} %get-tuple-element.57), channel_id=1, source_target_pairs={{0,1},{1,0},{2,3},{3,2},{4,5},{5,4},{6,7},{7,6},{8,9},{9,8},{10,11... | collective-permute-start | bytes 110600 | tf_op jit(solution)/shard_map/ppermute | solution.py:343
  41.9 1.4 %collective-permute-done.14.refs_1_ = bf16[144,128]{1,0:T(8,128)(2,1)S(1)} collective-permute-done((bf16[144,128]{1,0:T(8,128)(2,1)S(1)}, bf16[144,128]{1,0:T(8,128)(2,1)S(1)}, u32[]{:S(2)}, u32[]{:S(2)}) %collective-permute-start.14) | collective-permute-done | bytes 36896 | tf_op jit(solution)/shard_map/ppermute | solution.py:343
  43.3 1.7 %collective-permute-done.15.refs_2_ = bf16[144,128]{1,0:T(8,128)(2,1)S(1)} collective-permute-done((bf16[144,128]{1,0:T(8,128)(2,1)S(1)}, bf16[144,128]{1,0:T(8,128)(2,1)S(1)}, u32[]{:S(2)}, u32[]{:S(2)}) %collective-permute-start.15) | collective-permute-done | bytes 36896 | tf_op jit(solution)/shard_map/ppermute | solution.py:343
  45.0 0.7 %adam.1 = (f32[64,128]{1,0:T(8,128)}, f32[64,128]{1,0:T(8,128)}, f32[64,128]{1,0:T(8,128)}, f32[64,128]{1,0:T(8,128)}, f32[64,128]{1,0:T(8,128)}, /*index=5*/f32...) custom-call(bf16[144,128]{1,0:T(8,128)(2,1)S(1)} %get-tuple-element.54.refs_0_, ...), custom_call_target="tpu_custom_call" | custom-call | tf_op jit(solution)/shard_map/adam/pallas_call | solution.py:486
  (29 shorter events, 0.1 us)
Async XLA Ops:
  1.5 6.4 %collective-permute-start.2 = (bf16[144,128]{1,0:T(8,128)(2,1)S(1)}, bf16[144,128]{1,0:T(8,128)(2,1)S(1)}, u32[]{:S(2)}, u32[]{:S(2)}) collective-permute-start(bf16[144,128]{1,0:T(8,128)(2,1)S(1)} %pack.1.refs_3_), channel_id=1, source_target_pairs={{0,2},{1,3},{2,0},{3,1},{4,6},{5,7},{6,4},{7,5},{8,10},{9,11},{10,... | collective-permute-start | bytes 110600 | tf_op jit(solution)/shard_map/ppermute | solution.py:343
  5.6 5.8 %collective-permute-start.1 = (bf16[144,128]{1,0:T(8,128)(2,1)S(1)}, bf16[144,128]{1,0:T(8,128)(2,1)S(1)}, u32[]{:S(2)}, u32[]{:S(2)}) collective-permute-start(bf16[144,128]{1,0:T(8,128)(2,1)S(1)} %pack.1.refs_3_), channel_id=1, source_target_pairs={{0,3},{1,2},{2,1},{3,0},{4,7},{5,6},{6,5},{7,4},{8,11},{9,10},{10,... | collective-permute-start | bytes 110600 | tf_op jit(solution)/shard_map/ppermute | solution.py:343
  7.0 4.4 %collective-permute-start = (bf16[144,128]{1,0:T(8,128)(2,1)S(1)}, bf16[144,128]{1,0:T(8,128)(2,1)S(1)}, u32[]{:S(2)}, u32[]{:S(2)}) collective-permute-start(bf16[144,128]{1,0:T(8,128)(2,1)S(1)} %pack.1.refs_3_), channel_id=1, source_target_pairs={{0,1},{1,0},{2,3},{3,2},{4,5},{5,4},{6,7},{7,6},{8,9},{9,8},{10,11... | collective-permute-start | bytes 110600 | tf_op jit(solution)/shard_map/ppermute | solution.py:343
  11.5 7.7 %collective-permute-start.8 = (bf16[576,128]{1,0:T(8,128)(2,1)S(1)}, bf16[576,128]{1,0:T(8,128)(2,1)S(1)}, u32[]{:S(2)}, u32[]{:S(2)}) collective-permute-start(bf16[576,128]{1,0:T(8,128)(2,1)S(1)} %table.1.refs_3_.refs_0_), channel_id=1, source_target_pairs={{0,24},{4,28},{8,16},{12,20},{16,8},{20,12},{24,0},{28,4},{1,25},{... | collective-permute-start | bytes 442376 | tf_op jit(solution)/shard_map/ppermute | solution.py:343
  14.0 6.0 %collective-permute-start.6 = (bf16[576,128]{1,0:T(8,128)(2,1)S(1)}, bf16[576,128]{1,0:T(8,128)(2,1)S(1)}, u32[]{:S(2)}, u32[]{:S(2)}) collective-permute-start(bf16[576,128]{1,0:T(8,128)(2,1)S(1)} %table.1.refs_3_.refs_0_), channel_id=1, source_target_pairs={{0,16},{4,20},{8,24},{12,28},{16,0},{20,4},{24,8},{28,12},{1,17},{... | collective-permute-start | bytes 442376 | tf_op jit(solution)/shard_map/ppermute | solution.py:343
  14.5 5.4 %collective-permute-start.4 = (bf16[576,128]{1,0:T(8,128)(2,1)S(1)}, bf16[576,128]{1,0:T(8,128)(2,1)S(1)}, u32[]{:S(2)}, u32[]{:S(2)}) collective-permute-start(bf16[576,128]{1,0:T(8,128)(2,1)S(1)} %table.1.refs_3_.refs_0_), channel_id=1, source_target_pairs={{0,8},{4,12},{8,0},{12,4},{16,24},{20,28},{24,16},{28,20},{1,9},{5... | collective-permute-start | bytes 442376 | tf_op jit(solution)/shard_map/ppermute | solution.py:343
  15.0 5.5 %collective-permute-start.3 = (bf16[576,128]{1,0:T(8,128)(2,1)S(1)}, bf16[576,128]{1,0:T(8,128)(2,1)S(1)}, u32[]{:S(2)}, u32[]{:S(2)}) collective-permute-start(bf16[576,128]{1,0:T(8,128)(2,1)S(1)} %table.1.refs_3_.refs_0_), channel_id=1, source_target_pairs={{0,4},{4,0},{8,12},{12,8},{16,20},{20,16},{24,28},{28,24},{1,5},{5... | collective-permute-start | bytes 442376 | tf_op jit(solution)/shard_map/ppermute | solution.py:343
  19.2 25.8 %copy-start = (f32[128,64]{0,1:T(8,128)S(1)}, f32[128,64]{0,1:T(8,128)}, u32[]{:S(2)}) copy-start(f32[128,64]{0,1:T(8,128)} %param.17) | copy-start | bytes 98308
  19.2 25.8 %copy-start.1 = (f32[128,64]{0,1:T(8,128)S(1)}, f32[128,64]{0,1:T(8,128)}, u32[]{:S(2)}) copy-start(f32[128,64]{0,1:T(8,128)} %param.20) | copy-start | bytes 98308
  19.2 25.7 %copy-start.2 = (f32[32,64]{1,0:T(8,128)S(1)}, f32[32,64]{1,0:T(8,128)}, u32[]{:S(2)}) copy-start(f32[32,64]{1,0:T(8,128)} %refs_10_.1) | copy-start | bytes 24580
  19.2 25.7 %copy-start.3 = (f32[128,64]{0,1:T(8,128)S(1)}, f32[128,64]{0,1:T(8,128)}, u32[]{:S(2)}) copy-start(f32[128,64]{0,1:T(8,128)} %param.18) | copy-start | bytes 98308
  19.2 25.7 %copy-start.4 = (f32[128,64]{0,1:T(8,128)S(1)}, f32[128,64]{0,1:T(8,128)}, u32[]{:S(2)}) copy-start(f32[128,64]{0,1:T(8,128)} %param.19) | copy-start | bytes 98308
  19.2 25.7 %copy-start.5 = (f32[128,64]{0,1:T(8,128)S(1)}, f32[128,64]{0,1:T(8,128)}, u32[]{:S(2)}) copy-start(f32[128,64]{0,1:T(8,128)} %param.21) | copy-start | bytes 98308
  19.2 25.7 %copy-start.6 = (f32[128,64]{0,1:T(8,128)S(1)}, f32[128,64]{0,1:T(8,128)}, u32[]{:S(2)}) copy-start(f32[128,64]{0,1:T(8,128)} %param.22) | copy-start | bytes 98308
  19.2 25.7 %copy-start.7 = (f32[32,64]{1,0:T(8,128)S(1)}, f32[32,64]{1,0:T(8,128)}, u32[]{:S(2)}) copy-start(f32[32,64]{1,0:T(8,128)} %refs_11_.1) | copy-start | bytes 24580
  19.3 25.7 %copy-start.8 = (f32[32,64]{1,0:T(8,128)S(1)}, f32[32,64]{1,0:T(8,128)}, u32[]{:S(2)}) copy-start(f32[32,64]{1,0:T(8,128)} %refs_12_.1) | copy-start | bytes 24580
  19.3 1.6 %collective-permute-start.9 = (bf16[576,128]{1,0:T(8,128)(2,1)S(1)}, bf16[576,128]{1,0:T(8,128)(2,1)S(1)}, u32[]{:S(2)}, u32[]{:S(2)}) collective-permute-start(bf16[576,128]{1,0:T(8,128)(2,1)S(1)} %collective-permute-done.8.refs_6_), channel_id=1, source_target_pairs={{0,4},{4,0},{8,12},{12,8},{16,20},{20,16},{24,28},{28,24},{1,5},{5... | collective-permute-start | bytes 442376 | tf_op jit(solution)/shard_map/ppermute | solution.py:343
  19.9 1.4 %collective-permute-start.7 = (bf16[576,128]{1,0:T(8,128)(2,1)S(1)}, bf16[576,128]{1,0:T(8,128)(2,1)S(1)}, u32[]{:S(2)}, u32[]{:S(2)}) collective-permute-start(bf16[576,128]{1,0:T(8,128)(2,1)S(1)} %collective-permute-done.6.refs_4_), channel_id=1, source_target_pairs={{0,4},{4,0},{8,12},{12,8},{16,20},{20,16},{24,28},{28,24},{1,5},{5... | collective-permute-start | bytes 442376 | tf_op jit(solution)/shard_map/ppermute | solution.py:343
  20.0 1.6 %collective-permute-start.5 = (bf16[576,128]{1,0:T(8,128)(2,1)S(1)}, bf16[576,128]{1,0:T(8,128)(2,1)S(1)}, u32[]{:S(2)}, u32[]{:S(2)}) collective-permute-start(bf16[576,128]{1,0:T(8,128)(2,1)S(1)} %hold.1.refs_2_), channel_id=1, source_target_pairs={{0,4},{4,0},{8,12},{12,8},{16,20},{20,16},{24,28},{28,24},{1,5},{5... | collective-permute-start | bytes 442376 | tf_op jit(solution)/shard_map/ppermute | solution.py:343
  26.6 1.6 %collective-permute-start.10 = (bf16[448,256]{1,0:T(8,128)(2,1)S(1)}, bf16[448,256]{1,0:T(8,128)(2,1)S(1)}, u32[]{:S(2)}, u32[]{:S(2)}) collective-permute-start(bf16[448,256]{1,0:T(8,128)(2,1)S(1)} %get-tuple-element.47), channel_id=1, source_target_pairs={{0,4},{4,0},{8,12},{12,8},{16,20},{20,16},{24,28},{28,24},{1,5},{5... | collective-permute-start | bytes 688136 | tf_op jit(solution)/shard_map/ppermute | solution.py:343
  28.2 6.5 %collective-permute-start.11 = (bf16[224,256]{1,0:T(8,128)(2,1)S(1)}, bf16[224,256]{1,0:T(8,128)(2,1)S(1)}, u32[]{:S(2)}, u32[]{:S(2)}) collective-permute-start(bf16[224,256]{1,0:T(8,128)(2,1)S(1)} %get-tuple-element.48), channel_id=1, source_target_pairs={{0,24},{4,28},{8,16},{12,20},{16,8},{20,12},{24,0},{28,4},{1,25},{... | collective-permute-start | bytes 344072 | tf_op jit(solution)/shard_map/ppermute | solution.py:343
  30.6 6.4 %collective-permute-start.12 = (bf16[224,256]{1,0:T(8,128)(2,1)S(1)}, bf16[224,256]{1,0:T(8,128)(2,1)S(1)}, u32[]{:S(2)}, u32[]{:S(2)}) collective-permute-start(bf16[224,256]{1,0:T(8,128)(2,1)S(1)} %get-tuple-element.52), channel_id=1, source_target_pairs={{0,16},{4,20},{8,24},{12,28},{16,0},{20,4},{24,8},{28,12},{1,17},{... | collective-permute-start | bytes 344072 | tf_op jit(solution)/shard_map/ppermute | solution.py:343
  31.1 5.9 %collective-permute-start.13 = (bf16[224,256]{1,0:T(8,128)(2,1)S(1)}, bf16[224,256]{1,0:T(8,128)(2,1)S(1)}, u32[]{:S(2)}, u32[]{:S(2)}) collective-permute-start(bf16[224,256]{1,0:T(8,128)(2,1)S(1)} %get-tuple-element.53), channel_id=1, source_target_pairs={{0,8},{4,12},{8,0},{12,4},{16,24},{20,28},{24,16},{28,20},{1,9},{5... | collective-permute-start | bytes 344072 | tf_op jit(solution)/shard_map/ppermute | solution.py:343
  37.4 5.8 %collective-permute-start.14 = (bf16[144,128]{1,0:T(8,128)(2,1)S(1)}, bf16[144,128]{1,0:T(8,128)(2,1)S(1)}, u32[]{:S(2)}, u32[]{:S(2)}) collective-permute-start(bf16[144,128]{1,0:T(8,128)(2,1)S(1)} %get-tuple-element.55), channel_id=1, source_target_pairs={{0,3},{1,2},{2,1},{3,0},{4,7},{5,6},{6,5},{7,4},{8,11},{9,10},{10,... | collective-permute-start | bytes 110600 | tf_op jit(solution)/shard_map/ppermute | solution.py:343
  40.1 4.9 %collective-permute-start.15 = (bf16[144,128]{1,0:T(8,128)(2,1)S(1)}, bf16[144,128]{1,0:T(8,128)(2,1)S(1)}, u32[]{:S(2)}, u32[]{:S(2)}) collective-permute-start(bf16[144,128]{1,0:T(8,128)(2,1)S(1)} %get-tuple-element.56), channel_id=1, source_target_pairs={{0,2},{1,3},{2,0},{3,1},{4,6},{5,7},{6,4},{7,5},{8,10},{9,11},{10,... | collective-permute-start | bytes 110600 | tf_op jit(solution)/shard_map/ppermute | solution.py:343
  40.1 4.9 %collective-permute-start.16 = (bf16[144,128]{1,0:T(8,128)(2,1)S(1)}, bf16[144,128]{1,0:T(8,128)(2,1)S(1)}, u32[]{:S(2)}, u32[]{:S(2)}) collective-permute-start(bf16[144,128]{1,0:T(8,128)(2,1)S(1)} %get-tuple-element.57), channel_id=1, source_target_pairs={{0,1},{1,0},{2,3},{3,2},{4,5},{5,4},{6,7},{7,6},{8,9},{9,8},{10,11... | collective-permute-start | bytes 110600 | tf_op jit(solution)/shard_map/ppermute | solution.py:343

commit v18 on v17

--- a/solution.py
+++ b/solution.py
@@ -154,9 +154,15 @@
         out_ref[start : start + day_rows, :] = days[:, chunk * LANES : (chunk + 1) * LANES]
 
 
+def table_order(owners):
+    return [0, 2] + list(range(owners - 2, 2, -2))
+
+
 def block_kernel(sizes, *refs):
     owners, rank, day_rows = sizes.owners, sizes.rank, sizes.row_counts[2]
-    tables, refs = refs[:owners], refs[owners:]
+    order = table_order(owners)
+    tables = [refs[2 * order.index(n - n % 2) + n % 2] for n in range(owners)]
+    refs = refs[owners:]
     picks, places = refs[:3], refs[3:6]
     note_ref, status, own_ref, other_ref = refs[6:10]
     (
@@ -173,7 +179,7 @@
         residual_even,
         residual_odd,
     ) = refs[10:]
-    pair = 8
+    pair = 2
     pairs = status.shape[0] // pair
 
     def pick(t):
@@ -417,7 +423,7 @@
         name="hold",
     )(arrived[HOLD], picks_places_notes[6])
     tables = [table, own_crossed]
-    for bits in range(2, owners, 2):
+    for bits in table_order(owners)[1:]:
         tables += [arrived[bits], swap(arrived[bits], "dp", owners, 1)]
     inputs = [*tables, *picks_places_notes]
     users, items, days = list_counts
@@ -435,10 +441,10 @@
             pltpu.VMEM((users, sizes.rank), f32),
             pltpu.VMEM((items, sizes.rank), f32),
             pltpu.VMEM((days, sizes.rank), f32),
-            pltpu.VMEM((8 * users, sizes.rank), bf16),
-            pltpu.VMEM((8 * users, sizes.rank), bf16),
-            pltpu.VMEM((8 * users, items), bf16),
-            pltpu.VMEM((8 * users, items), bf16),
+            pltpu.VMEM((2 * users, sizes.rank), bf16),
+            pltpu.VMEM((2 * users, sizes.rank), bf16),
+            pltpu.VMEM((2 * users, items), bf16),
+            pltpu.VMEM((2 * users, items), bf16),
         ],
         compiler_params=pltpu.CompilerParams(vmem_limit_bytes=BLOCK_VMEM),
         name="block_gradients",

time: 46 us -> 45.6 us (level)
  transfers between devices with their start and end apart: 17 -> 17, of which waited for: 11 -> 12; matrix products, arithmetic and copies ran while one was open for 0% -> 0% of each run, Pallas kernels for 10% -> 10%
where the time goes in v18:
time: 45.6 us; the launch traced here: 45.4 us
  starting transfers between devices  18.4 us (40%)
  waiting for transfers between devices  14.7 us (32%)
  Pallas kernels  11.4 us (25%)
  between operations  0.83 us (2%)
    ppermute x17, starting transfers between devices, swap(): return lax.ppermute(array, axis, [(i, i ^ bits) for i in range(size)])  18.4 us
    ppermute x17, waiting for transfers between devices, swap(): return lax.ppermute(array, axis, [(i, i ^ bits) for i in range(size)])  14.7 us
    pallas_call x1, Pallas kernels, local(): pl.pallas_call(functools.partial(block_kernel, sizes), out_shape=(half, h...  4.71 us
    pallas_call x1, Pallas kernels, local(): pl.pallas_call(functools.partial(slot_kernel, sizes), out_shape=tuple([sh...  4.11 us
  transfers between devices with their start and end apart: 17, of which 12 were waited for; matrix products, arithmetic and copies ran while one was open for 0% of the time, Pallas kernels for 10%

profile of v18, /device:TPU:0, one launch (start us, length us, event | category | flops | bytes accessed | tf_op | source)
XLA Modules:
  0.0 45.4 jit_solution(16259557228706291742)
XLA Ops:
  0.6 0.9 %pack.1.refs_3_ = bf16[144,128]{1,0:T(8,128)(2,1)S(1)} custom-call(f32[64,128]{1,0:T(8,128)} %bitcast.13, f32[64,128]{1,0:T(8,128)} %bitcast.15, f32[32,64]{1,0:T(8,128)} %refs_10_.1), custom_call_target="tpu_custom_call" | custom-call | tf_op jit(solution)/shard_map/pack/pallas_call | solution.py:378
  1.5 4.1 %collective-permute-start.2 = (bf16[144,128]{1,0:T(8,128)(2,1)S(1)}, bf16[144,128]{1,0:T(8,128)(2,1)S(1)}, u32[]{:S(2)}, u32[]{:S(2)}) collective-permute-start(bf16[144,128]{1,0:T(8,128)(2,1)S(1)} %pack.1.refs_3_), channel_id=1, source_target_pairs={{0,2},{1,3},{2,0},{3,1},{4,6},{5,7},{6,4},{7,5},{8,10},{9,11},{10,... | collective-permute-start | bytes 110600 | tf_op jit(solution)/shard_map/ppermute | solution.py:349
  5.6 1.3 %collective-permute-start.1 = (bf16[144,128]{1,0:T(8,128)(2,1)S(1)}, bf16[144,128]{1,0:T(8,128)(2,1)S(1)}, u32[]{:S(2)}, u32[]{:S(2)}) collective-permute-start(bf16[144,128]{1,0:T(8,128)(2,1)S(1)} %pack.1.refs_3_), channel_id=1, source_target_pairs={{0,3},{1,2},{2,1},{3,0},{4,7},{5,6},{6,5},{7,4},{8,11},{9,10},{10,... | collective-permute-start | bytes 110600 | tf_op jit(solution)/shard_map/ppermute | solution.py:349
  7.0 0.2 collective-permute-start
  7.2 0.8 %collective-permute-done.2.refs_2_ = bf16[144,128]{1,0:T(8,128)(2,1)S(1)} collective-permute-done((bf16[144,128]{1,0:T(8,128)(2,1)S(1)}, bf16[144,128]{1,0:T(8,128)(2,1)S(1)}, u32[]{:S(2)}, u32[]{:S(2)}) %collective-permute-start.2) | collective-permute-done | bytes 36896 | tf_op jit(solution)/shard_map/ppermute | solution.py:349
  8.0 3.4 %collective-permute-done.1.refs_1_ = bf16[144,128]{1,0:T(8,128)(2,1)S(1)} collective-permute-done((bf16[144,128]{1,0:T(8,128)(2,1)S(1)}, bf16[144,128]{1,0:T(8,128)(2,1)S(1)}, u32[]{:S(2)}, u32[]{:S(2)}) %collective-permute-start.1) | collective-permute-done | bytes 36896 | tf_op jit(solution)/shard_map/ppermute | solution.py:349
  11.4 0.1 table.1.refs_3_.refs_0_
  11.5 1.5 %collective-permute-start.8 = (bf16[576,128]{1,0:T(8,128)(2,1)S(1)}, bf16[576,128]{1,0:T(8,128)(2,1)S(1)}, u32[]{:S(2)}, u32[]{:S(2)}) collective-permute-start(bf16[576,128]{1,0:T(8,128)(2,1)S(1)} %table.1.refs_3_.refs_0_), channel_id=1, source_target_pairs={{0,16},{4,20},{8,24},{12,28},{16,0},{20,4},{24,8},{28,12},{1,17},{... | collective-permute-start | bytes 442376 | tf_op jit(solution)/shard_map/ppermute | solution.py:349
  13.1 1.4 %collective-permute-start.6 = (bf16[576,128]{1,0:T(8,128)(2,1)S(1)}, bf16[576,128]{1,0:T(8,128)(2,1)S(1)}, u32[]{:S(2)}, u32[]{:S(2)}) collective-permute-start(bf16[576,128]{1,0:T(8,128)(2,1)S(1)} %table.1.refs_3_.refs_0_), channel_id=1, source_target_pairs={{0,24},{4,28},{8,16},{12,20},{16,8},{20,12},{24,0},{28,4},{1,25},{... | collective-permute-start | bytes 442376 | tf_op jit(solution)/shard_map/ppermute | solution.py:349
  14.5 0.5 %collective-permute-start.4 = (bf16[576,128]{1,0:T(8,128)(2,1)S(1)}, bf16[576,128]{1,0:T(8,128)(2,1)S(1)}, u32[]{:S(2)}, u32[]{:S(2)}) collective-permute-start(bf16[576,128]{1,0:T(8,128)(2,1)S(1)} %table.1.refs_3_.refs_0_), channel_id=1, source_target_pairs={{0,8},{4,12},{8,0},{12,4},{16,24},{20,28},{24,16},{28,20},{1,9},{5... | collective-permute-start | bytes 442376 | tf_op jit(solution)/shard_map/ppermute | solution.py:349
  15.0 4.1 %slots.1 = (bf16[1024,256]{1,0:T(8,128)(2,1)S(1)}, bf16[1024,256]{1,0:T(8,128)(2,1)S(1)}, bf16[256,32]{1,0:T(8,128)(2,1)S(1)}, bf16[384,256]{1,0:T(8,128)(2,1)S(...) custom-call(s32[1]{0:T(128)} %bitcast.2.me_ref, ...), custom_call_target="tpu_custom_call" | custom-call | tf_op jit(solution)/shard_map/slots/pallas_call | solution.py:398
  19.3 0.6 %collective-permute-start.9 = (bf16[576,128]{1,0:T(8,128)(2,1)S(1)}, bf16[576,128]{1,0:T(8,128)(2,1)S(1)}, u32[]{:S(2)}, u32[]{:S(2)}) collective-permute-start(bf16[576,128]{1,0:T(8,128)(2,1)S(1)} %collective-permute-done.8.refs_6_), channel_id=1, source_target_pairs={{0,4},{4,0},{8,12},{12,8},{16,20},{20,16},{24,28},{28,24},{1,5},{5... | collective-permute-start | bytes 442376 | tf_op jit(solution)/shard_map/ppermute | solution.py:349
  19.9 0.2 collective-permute-done.4.arrived_ref
  20.1 0.3 collective-permute-start.5
  20.4 0.4 collective-permute-done.9.refs_7_
  20.9 0.4 collective-permute-done.7.refs_5_
  21.2 0.4 collective-permute-done.5.refs_3_
  21.6 4.7 %block_gradients.1 = (bf16[448,256]{1,0:T(8,128)(2,1)S(1)}, bf16[448,256]{1,0:T(8,128)(2,1)S(1)}) custom-call(bf16[576,128]{1,0:T(8,128)(2,1)S(1)} %table.1.refs_3_.refs_0_, bf16[576,128]{1,0:T(8,128)(2,1)S(1)} %collective-permute-done.3.refs_1_, bf16[576,128]{1,0:T(8,128)(2,1)S(1)} %hold.1.refs_2_, bf16[576,128]{1,0:T(8,128)(2,1)S(1)} %collective-permute-done.5.refs_3_, ...), custom_call_target="tpu_custom_call" | custom-call | tf_op jit(solution)/shard_map/block_gradients/pallas_call | solution.py:431
  26.3 0.3 collective-permute-start.10
  26.6 1.3 %collective-permute-done.10.crossed_ref = bf16[448,256]{1,0:T(8,128)(2,1)S(1)} collective-permute-done((bf16[448,256]{1,0:T(8,128)(2,1)S(1)}, bf16[448,256]{1,0:T(8,128)(2,1)S(1)}, u32[]{:S(2)}, u32[]{:S(2)}) %collective-permute-start.10) | collective-permute-done | bytes 229408 | tf_op jit(solution)/shard_map/ppermute | solution.py:349
  27.9 2.4 %collective-permute-start.11 = (bf16[224,256]{1,0:T(8,128)(2,1)S(1)}, bf16[224,256]{1,0:T(8,128)(2,1)S(1)}, u32[]{:S(2)}, u32[]{:S(2)}) collective-permute-start(bf16[224,256]{1,0:T(8,128)(2,1)S(1)} %get-tuple-element.48), channel_id=1, source_target_pairs={{0,24},{4,28},{8,16},{12,20},{16,8},{20,12},{24,0},{28,4},{1,25},{... | collective-permute-start | bytes 344072 | tf_op jit(solution)/shard_map/ppermute | solution.py:349
  30.3 0.6 %collective-permute-start.12 = (bf16[224,256]{1,0:T(8,128)(2,1)S(1)}, bf16[224,256]{1,0:T(8,128)(2,1)S(1)}, u32[]{:S(2)}, u32[]{:S(2)}) collective-permute-start(bf16[224,256]{1,0:T(8,128)(2,1)S(1)} %get-tuple-element.52), channel_id=1, source_target_pairs={{0,16},{4,20},{8,24},{12,28},{16,0},{20,4},{24,8},{28,12},{1,17},{... | collective-permute-start | bytes 344072 | tf_op jit(solution)/shard_map/ppermute | solution.py:349
  30.9 0.5 %collective-permute-start.13 = (bf16[224,256]{1,0:T(8,128)(2,1)S(1)}, bf16[224,256]{1,0:T(8,128)(2,1)S(1)}, u32[]{:S(2)}, u32[]{:S(2)}) collective-permute-start(bf16[224,256]{1,0:T(8,128)(2,1)S(1)} %get-tuple-element.53), channel_id=1, source_target_pairs={{0,8},{4,12},{8,0},{12,4},{16,24},{20,28},{24,16},{28,20},{1,9},{5... | collective-permute-start | bytes 344072 | tf_op jit(solution)/shard_map/ppermute | solution.py:349
  31.4 2.8 %collective-permute-done.11.arrived_ref = bf16[224,256]{1,0:T(8,128)(2,1)S(1)} collective-permute-done((bf16[224,256]{1,0:T(8,128)(2,1)S(1)}, bf16[224,256]{1,0:T(8,128)(2,1)S(1)}, u32[]{:S(2)}, u32[]{:S(2)}) %collective-permute-start.11) | collective-permute-done | bytes 114720 | tf_op jit(solution)/shard_map/ppermute | solution.py:349
  34.2 0.3 early_sums.1
  34.5 2.0 %collective-permute-done.12.refs_3_ = bf16[224,256]{1,0:T(8,128)(2,1)S(1)} collective-permute-done((bf16[224,256]{1,0:T(8,128)(2,1)S(1)}, bf16[224,256]{1,0:T(8,128)(2,1)S(1)}, u32[]{:S(2)}, u32[]{:S(2)}) %collective-permute-start.12) | collective-permute-done | bytes 114720 | tf_op jit(solution)/shard_map/ppermute | solution.py:349
  36.7 0.4 row_sums.1
  37.1 2.6 %collective-permute-start.14 = (bf16[144,128]{1,0:T(8,128)(2,1)S(1)}, bf16[144,128]{1,0:T(8,128)(2,1)S(1)}, u32[]{:S(2)}, u32[]{:S(2)}) collective-permute-start(bf16[144,128]{1,0:T(8,128)(2,1)S(1)} %get-tuple-element.55), channel_id=1, source_target_pairs={{0,3},{1,2},{2,1},{3,0},{4,7},{5,6},{6,5},{7,4},{8,11},{9,10},{10,... | collective-permute-start | bytes 110600 | tf_op jit(solution)/shard_map/ppermute | solution.py:349
  39.7 1.8 %collective-permute-start.16 = (bf16[144,128]{1,0:T(8,128)(2,1)S(1)}, bf16[144,128]{1,0:T(8,128)(2,1)S(1)}, u32[]{:S(2)}, u32[]{:S(2)}) collective-permute-start(bf16[144,128]{1,0:T(8,128)(2,1)S(1)} %get-tuple-element.57), channel_id=1, source_target_pairs={{0,1},{1,0},{2,3},{3,2},{4,5},{5,4},{6,7},{7,6},{8,9},{9,8},{10,11... | collective-permute-start | bytes 110600 | tf_op jit(solution)/shard_map/ppermute | solution.py:349
  41.5 1.4 %collective-permute-done.14.refs_1_ = bf16[144,128]{1,0:T(8,128)(2,1)S(1)} collective-permute-done((bf16[144,128]{1,0:T(8,128)(2,1)S(1)}, bf16[144,128]{1,0:T(8,128)(2,1)S(1)}, u32[]{:S(2)}, u32[]{:S(2)}) %collective-permute-start.14) | collective-permute-done | bytes 36896 | tf_op jit(solution)/shard_map/ppermute | solution.py:349
  42.9 1.6 %collective-permute-done.15.refs_2_ = bf16[144,128]{1,0:T(8,128)(2,1)S(1)} collective-permute-done((bf16[144,128]{1,0:T(8,128)(2,1)S(1)}, bf16[144,128]{1,0:T(8,128)(2,1)S(1)}, u32[]{:S(2)}, u32[]{:S(2)}) %collective-permute-start.15) | collective-permute-done | bytes 36896 | tf_op jit(solution)/shard_map/ppermute | solution.py:349
  44.6 0.7 %adam.1 = (f32[64,128]{1,0:T(8,128)}, f32[64,128]{1,0:T(8,128)}, f32[64,128]{1,0:T(8,128)}, f32[64,128]{1,0:T(8,128)}, f32[64,128]{1,0:T(8,128)}, /*index=5*/f32...) custom-call(bf16[144,128]{1,0:T(8,128)(2,1)S(1)} %get-tuple-element.54.refs_0_, ...), custom_call_target="tpu_custom_call" | custom-call | tf_op jit(solution)/shard_map/adam/pallas_call | solution.py:492
  (29 shorter events, 0.3 us)
Async XLA Ops:
  1.5 6.4 %collective-permute-start.2 = (bf16[144,128]{1,0:T(8,128)(2,1)S(1)}, bf16[144,128]{1,0:T(8,128)(2,1)S(1)}, u32[]{:S(2)}, u32[]{:S(2)}) collective-permute-start(bf16[144,128]{1,0:T(8,128)(2,1)S(1)} %pack.1.refs_3_), channel_id=1, source_target_pairs={{0,2},{1,3},{2,0},{3,1},{4,6},{5,7},{6,4},{7,5},{8,10},{9,11},{10,... | collective-permute-start | bytes 110600 | tf_op jit(solution)/shard_map/ppermute | solution.py:349
  5.6 5.8 %collective-permute-start.1 = (bf16[144,128]{1,0:T(8,128)(2,1)S(1)}, bf16[144,128]{1,0:T(8,128)(2,1)S(1)}, u32[]{:S(2)}, u32[]{:S(2)}) collective-permute-start(bf16[144,128]{1,0:T(8,128)(2,1)S(1)} %pack.1.refs_3_), channel_id=1, source_target_pairs={{0,3},{1,2},{2,1},{3,0},{4,7},{5,6},{6,5},{7,4},{8,11},{9,10},{10,... | collective-permute-start | bytes 110600 | tf_op jit(solution)/shard_map/ppermute | solution.py:349
  7.0 4.4 %collective-permute-start = (bf16[144,128]{1,0:T(8,128)(2,1)S(1)}, bf16[144,128]{1,0:T(8,128)(2,1)S(1)}, u32[]{:S(2)}, u32[]{:S(2)}) collective-permute-start(bf16[144,128]{1,0:T(8,128)(2,1)S(1)} %pack.1.refs_3_), channel_id=1, source_target_pairs={{0,1},{1,0},{2,3},{3,2},{4,5},{5,4},{6,7},{7,6},{8,9},{9,8},{10,11... | collective-permute-start | bytes 110600 | tf_op jit(solution)/shard_map/ppermute | solution.py:349
  11.5 7.7 %collective-permute-start.8 = (bf16[576,128]{1,0:T(8,128)(2,1)S(1)}, bf16[576,128]{1,0:T(8,128)(2,1)S(1)}, u32[]{:S(2)}, u32[]{:S(2)}) collective-permute-start(bf16[576,128]{1,0:T(8,128)(2,1)S(1)} %table.1.refs_3_.refs_0_), channel_id=1, source_target_pairs={{0,16},{4,20},{8,24},{12,28},{16,0},{20,4},{24,8},{28,12},{1,17},{... | collective-permute-start | bytes 442376 | tf_op jit(solution)/shard_map/ppermute | solution.py:349
  13.1 6.8 %collective-permute-start.6 = (bf16[576,128]{1,0:T(8,128)(2,1)S(1)}, bf16[576,128]{1,0:T(8,128)(2,1)S(1)}, u32[]{:S(2)}, u32[]{:S(2)}) collective-permute-start(bf16[576,128]{1,0:T(8,128)(2,1)S(1)} %table.1.refs_3_.refs_0_), channel_id=1, source_target_pairs={{0,24},{4,28},{8,16},{12,20},{16,8},{20,12},{24,0},{28,4},{1,25},{... | collective-permute-start | bytes 442376 | tf_op jit(solution)/shard_map/ppermute | solution.py:349
  14.5 5.6 %collective-permute-start.4 = (bf16[576,128]{1,0:T(8,128)(2,1)S(1)}, bf16[576,128]{1,0:T(8,128)(2,1)S(1)}, u32[]{:S(2)}, u32[]{:S(2)}) collective-permute-start(bf16[576,128]{1,0:T(8,128)(2,1)S(1)} %table.1.refs_3_.refs_0_), channel_id=1, source_target_pairs={{0,8},{4,12},{8,0},{12,4},{16,24},{20,28},{24,16},{28,20},{1,9},{5... | collective-permute-start | bytes 442376 | tf_op jit(solution)/shard_map/ppermute | solution.py:349
  15.0 5.4 %collective-permute-start.3 = (bf16[576,128]{1,0:T(8,128)(2,1)S(1)}, bf16[576,128]{1,0:T(8,128)(2,1)S(1)}, u32[]{:S(2)}, u32[]{:S(2)}) collective-permute-start(bf16[576,128]{1,0:T(8,128)(2,1)S(1)} %table.1.refs_3_.refs_0_), channel_id=1, source_target_pairs={{0,4},{4,0},{8,12},{12,8},{16,20},{20,16},{24,28},{28,24},{1,5},{5... | collective-permute-start | bytes 442376 | tf_op jit(solution)/shard_map/ppermute | solution.py:349
  19.2 25.4 %copy-start = (f32[128,64]{0,1:T(8,128)S(1)}, f32[128,64]{0,1:T(8,128)}, u32[]{:S(2)}) copy-start(f32[128,64]{0,1:T(8,128)} %param.17) | copy-start | bytes 98308
  19.2 25.4 %copy-start.1 = (f32[128,64]{0,1:T(8,128)S(1)}, f32[128,64]{0,1:T(8,128)}, u32[]{:S(2)}) copy-start(f32[128,64]{0,1:T(8,128)} %param.20) | copy-start | bytes 98308
  19.2 25.4 %copy-start.2 = (f32[32,64]{1,0:T(8,128)S(1)}, f32[32,64]{1,0:T(8,128)}, u32[]{:S(2)}) copy-start(f32[32,64]{1,0:T(8,128)} %refs_10_.1) | copy-start | bytes 24580
  19.2 25.4 %copy-start.3 = (f32[128,64]{0,1:T(8,128)S(1)}, f32[128,64]{0,1:T(8,128)}, u32[]{:S(2)}) copy-start(f32[128,64]{0,1:T(8,128)} %param.18) | copy-start | bytes 98308
  19.2 25.4 %copy-start.4 = (f32[128,64]{0,1:T(8,128)S(1)}, f32[128,64]{0,1:T(8,128)}, u32[]{:S(2)}) copy-start(f32[128,64]{0,1:T(8,128)} %param.19) | copy-start | bytes 98308
  19.2 25.4 %copy-start.5 = (f32[128,64]{0,1:T(8,128)S(1)}, f32[128,64]{0,1:T(8,128)}, u32[]{:S(2)}) copy-start(f32[128,64]{0,1:T(8,128)} %param.21) | copy-start | bytes 98308
  19.2 25.4 %copy-start.6 = (f32[128,64]{0,1:T(8,128)S(1)}, f32[128,64]{0,1:T(8,128)}, u32[]{:S(2)}) copy-start(f32[128,64]{0,1:T(8,128)} %param.22) | copy-start | bytes 98308
  19.2 25.4 %copy-start.7 = (f32[32,64]{1,0:T(8,128)S(1)}, f32[32,64]{1,0:T(8,128)}, u32[]{:S(2)}) copy-start(f32[32,64]{1,0:T(8,128)} %refs_11_.1) | copy-start | bytes 24580
  19.3 25.4 %copy-start.8 = (f32[32,64]{1,0:T(8,128)S(1)}, f32[32,64]{1,0:T(8,128)}, u32[]{:S(2)}) copy-start(f32[32,64]{1,0:T(8,128)} %refs_12_.1) | copy-start | bytes 24580
  19.3 1.6 %collective-permute-start.9 = (bf16[576,128]{1,0:T(8,128)(2,1)S(1)}, bf16[576,128]{1,0:T(8,128)(2,1)S(1)}, u32[]{:S(2)}, u32[]{:S(2)}) collective-permute-start(bf16[576,128]{1,0:T(8,128)(2,1)S(1)} %collective-permute-done.8.refs_6_), channel_id=1, source_target_pairs={{0,4},{4,0},{8,12},{12,8},{16,20},{20,16},{24,28},{28,24},{1,5},{5... | collective-permute-start | bytes 442376 | tf_op jit(solution)/shard_map/ppermute | solution.py:349
  19.9 1.4 %collective-permute-start.7 = (bf16[576,128]{1,0:T(8,128)(2,1)S(1)}, bf16[576,128]{1,0:T(8,128)(2,1)S(1)}, u32[]{:S(2)}, u32[]{:S(2)}) collective-permute-start(bf16[576,128]{1,0:T(8,128)(2,1)S(1)} %collective-permute-done.6.refs_4_), channel_id=1, source_target_pairs={{0,4},{4,0},{8,12},{12,8},{16,20},{20,16},{24,28},{28,24},{1,5},{5... | collective-permute-start | bytes 442376 | tf_op jit(solution)/shard_map/ppermute | solution.py:349
  20.1 1.4 %collective-permute-start.5 = (bf16[576,128]{1,0:T(8,128)(2,1)S(1)}, bf16[576,128]{1,0:T(8,128)(2,1)S(1)}, u32[]{:S(2)}, u32[]{:S(2)}) collective-permute-start(bf16[576,128]{1,0:T(8,128)(2,1)S(1)} %hold.1.refs_2_), channel_id=1, source_target_pairs={{0,4},{4,0},{8,12},{12,8},{16,20},{20,16},{24,28},{28,24},{1,5},{5... | collective-permute-start | bytes 442376 | tf_op jit(solution)/shard_map/ppermute | solution.py:349
  26.3 1.6 %collective-permute-start.10 = (bf16[448,256]{1,0:T(8,128)(2,1)S(1)}, bf16[448,256]{1,0:T(8,128)(2,1)S(1)}, u32[]{:S(2)}, u32[]{:S(2)}) collective-permute-start(bf16[448,256]{1,0:T(8,128)(2,1)S(1)} %get-tuple-element.47), channel_id=1, source_target_pairs={{0,4},{4,0},{8,12},{12,8},{16,20},{20,16},{24,28},{28,24},{1,5},{5... | collective-permute-start | bytes 688136 | tf_op jit(solution)/shard_map/ppermute | solution.py:349
  27.9 6.3 %collective-permute-start.11 = (bf16[224,256]{1,0:T(8,128)(2,1)S(1)}, bf16[224,256]{1,0:T(8,128)(2,1)S(1)}, u32[]{:S(2)}, u32[]{:S(2)}) collective-permute-start(bf16[224,256]{1,0:T(8,128)(2,1)S(1)} %get-tuple-element.48), channel_id=1, source_target_pairs={{0,24},{4,28},{8,16},{12,20},{16,8},{20,12},{24,0},{28,4},{1,25},{... | collective-permute-start | bytes 344072 | tf_op jit(solution)/shard_map/ppermute | solution.py:349
  30.3 6.3 %collective-permute-start.12 = (bf16[224,256]{1,0:T(8,128)(2,1)S(1)}, bf16[224,256]{1,0:T(8,128)(2,1)S(1)}, u32[]{:S(2)}, u32[]{:S(2)}) collective-permute-start(bf16[224,256]{1,0:T(8,128)(2,1)S(1)} %get-tuple-element.52), channel_id=1, source_target_pairs={{0,16},{4,20},{8,24},{12,28},{16,0},{20,4},{24,8},{28,12},{1,17},{... | collective-permute-start | bytes 344072 | tf_op jit(solution)/shard_map/ppermute | solution.py:349
  30.9 5.7 %collective-permute-start.13 = (bf16[224,256]{1,0:T(8,128)(2,1)S(1)}, bf16[224,256]{1,0:T(8,128)(2,1)S(1)}, u32[]{:S(2)}, u32[]{:S(2)}) collective-permute-start(bf16[224,256]{1,0:T(8,128)(2,1)S(1)} %get-tuple-element.53), channel_id=1, source_target_pairs={{0,8},{4,12},{8,0},{12,4},{16,24},{20,28},{24,16},{28,20},{1,9},{5... | collective-permute-start | bytes 344072 | tf_op jit(solution)/shard_map/ppermute | solution.py:349
  37.1 5.8 %collective-permute-start.14 = (bf16[144,128]{1,0:T(8,128)(2,1)S(1)}, bf16[144,128]{1,0:T(8,128)(2,1)S(1)}, u32[]{:S(2)}, u32[]{:S(2)}) collective-permute-start(bf16[144,128]{1,0:T(8,128)(2,1)S(1)} %get-tuple-element.55), channel_id=1, source_target_pairs={{0,3},{1,2},{2,1},{3,0},{4,7},{5,6},{6,5},{7,4},{8,11},{9,10},{10,... | collective-permute-start | bytes 110600 | tf_op jit(solution)/shard_map/ppermute | solution.py:349
  39.7 4.9 %collective-permute-start.15 = (bf16[144,128]{1,0:T(8,128)(2,1)S(1)}, bf16[144,128]{1,0:T(8,128)(2,1)S(1)}, u32[]{:S(2)}, u32[]{:S(2)}) collective-permute-start(bf16[144,128]{1,0:T(8,128)(2,1)S(1)} %get-tuple-element.56), channel_id=1, source_target_pairs={{0,2},{1,3},{2,0},{3,1},{4,6},{5,7},{6,4},{7,5},{8,10},{9,11},{10,... | collective-permute-start | bytes 110600 | tf_op jit(solution)/shard_map/ppermute | solution.py:349
  39.7 4.9 %collective-permute-start.16 = (bf16[144,128]{1,0:T(8,128)(2,1)S(1)}, bf16[144,128]{1,0:T(8,128)(2,1)S(1)}, u32[]{:S(2)}, u32[]{:S(2)}) collective-permute-start(bf16[144,128]{1,0:T(8,128)(2,1)S(1)} %get-tuple-element.57), channel_id=1, source_target_pairs={{0,1},{1,0},{2,3},{3,2},{4,5},{5,4},{6,7},{7,6},{8,9},{9,8},{10,11... | collective-permute-start | bytes 110600 | tf_op jit(solution)/shard_map/ppermute | solution.py:349

commit v19 on v18

--- a/solution.py
+++ b/solution.py
@@ -158,11 +158,45 @@
     return [0, 2] + list(range(owners - 2, 2, -2))
 
 
+def pick_rows(sizes, tables, picks):
+    rank, day_rows = sizes.rank, sizes.row_counts[2]
+    selectors = []
+    for t in range(3):
+        rows = sizes.row_counts[t]
+        selectors.append(
+            jnp.concatenate([picks[t][n * rows : (n + 1) * rows, :] for n in tables], axis=0)
+        )
+    picked = []
+    for t in range(2):
+        table = jnp.concatenate(
+            [ref[t * rank : (t + 1) * rank, :] for ref in tables.values()], axis=1
+        )
+        picked.append(jnp.dot(table, selectors[t], preferred_element_type=f32))
+    starts = [2 * rank + chunk * day_rows for chunk in range(sizes.day_chunks)]
+    day_table = jnp.concatenate(
+        [
+            jnp.concatenate([ref[start : start + day_rows, :] for start in starts], axis=1)
+            for ref in tables.values()
+        ],
+        axis=0,
+    )
+    picked.append(
+        lax.dot_general(
+            selectors[2], day_table, (((0,), (0,)), ((), ())), preferred_element_type=f32
+        )
+    )
+    return picked
+
+
+def early_pick_kernel(sizes, numbers, *refs):
+    tables, picks, outs = refs[: len(numbers)], refs[len(numbers) : -3], refs[-3:]
+    for out, rows in zip(outs, pick_rows(sizes, dict(zip(numbers, tables)), picks)):
+        out[...] = rows
+
+
 def block_kernel(sizes, *refs):
-    owners, rank, day_rows = sizes.owners, sizes.rank, sizes.row_counts[2]
-    order = table_order(owners)
-    tables = [refs[2 * order.index(n - n % 2) + n % 2] for n in range(owners)]
-    refs = refs[owners:]
+    owners = sizes.owners
+    table, early, refs = refs[0], refs[1:4], refs[4:]
     picks, places = refs[:3], refs[3:6]
     note_ref, status, own_ref, other_ref = refs[6:10]
     (
@@ -182,27 +216,14 @@
     pair = 2
     pairs = status.shape[0] // pair
 
-    def pick(t):
-        table = jnp.concatenate([ref[t * rank : (t + 1) * rank, :] for ref in tables], axis=1)
-        return jnp.dot(table, picks[t][...], preferred_element_type=f32)
-
-    user_values = pick(0).T
+    last = pick_rows(sizes, {HOLD + 1: table}, picks)
+    users_t, items_t, day_values = [ref[...] + rows for ref, rows in zip(early, last)]
+    user_values = users_t.T
     users[...] = user_values
     users_low[...] = user_values.astype(bf16)
-    items_t = pick(1)
     items[...] = items_t.T.astype(bf16)
     items_half_t[...] = (0.5 * items_t).astype(bf16)
-    starts = [2 * rank + chunk * day_rows for chunk in range(sizes.day_chunks)]
-    day_table = jnp.concatenate(
-        [
-            jnp.concatenate([ref[start : start + day_rows, :] for start in starts], axis=1)
-            for ref in tables
-        ],
-        axis=0,
-    )
-    days[...] = lax.dot_general(
-        picks[2][...], day_table, (((0,), (0,)), ((), ())), preferred_element_type=f32
-    )
+    days[...] = day_values
     user_gradient[...] = jnp.zeros_like(user_gradient)
     item_gradient[...] = jnp.zeros_like(item_gradient)
     count = users.shape[0]
@@ -416,16 +437,29 @@
         in_hbm(status),
     )
 
-    arrived[HOLD] = pl.pallas_call(
+    hold = pl.pallas_call(
         hold_kernel,
         out_shape=shape(table.shape, bf16),
         compiler_params=small,
         name="hold",
-    )(arrived[HOLD], picks_places_notes[6])
-    tables = [table, own_crossed]
+    )
+    arrived = {bits: hold(a, picks_places_notes[6]) for bits, a in arrived.items()}
+    tables = {0: table, 1: own_crossed}
     for bits in table_order(owners)[1:]:
-        tables += [arrived[bits], swap(arrived[bits], "dp", owners, 1)]
-    inputs = [*tables, *picks_places_notes]
+        tables[bits] = arrived[bits]
+        tables[bits + 1] = swap(arrived[bits], "dp", owners, 1)
+    last = tables.pop(HOLD + 1)
+    early = pl.pallas_call(
+        functools.partial(early_pick_kernel, sizes, tuple(tables)),
+        out_shape=(
+            shape((sizes.rank, list_counts[0]), f32),
+            shape((sizes.rank, list_counts[1]), f32),
+            shape((list_counts[2], sizes.rank), f32),
+        ),
+        compiler_params=small,
+        name="early_picks",
+    )(*tables.values(), *picks_places_notes[:3])
+    inputs = [last, *early, *picks_places_notes]
     users, items, days = list_counts
     half = shape((owners // 2 * sizes.slot_rows, sizes.rank), bf16)
     own, other = pl.pallas_call(

time: 45.6 us -> 46.2 us (1.013)
    pallas_call x1 -> x4, Pallas kernels: 0.01 us -> 0.48 us  [the longest x1 0.44 us: local(): pl.pallas_call(functools.partial(early_pick_kernel, sizes, tuple(tables))...]
  transfers between devices with their start and end apart: 17 -> 17, of which waited for: 12 -> 10; matrix products, arithmetic and copies ran while one was open for 0% -> 0% of each run, Pallas kernels for 10% -> 11%
where the time goes in v19:
time: 46.2 us; the launch traced here: 46 us
  starting transfers between devices  18.6 us (40%)
  waiting for transfers between devices  14.9 us (32%)
  Pallas kernels  11.6 us (25%)
  between operations  0.87 us (2%)
    ppermute x17, starting transfers between devices, swap(): return lax.ppermute(array, axis, [(i, i ^ bits) for i in range(size)])  18.6 us
    ppermute x17, waiting for transfers between devices, swap(): return lax.ppermute(array, axis, [(i, i ^ bits) for i in range(size)])  14.9 us
    pallas_call x1, Pallas kernels, local(): pl.pallas_call(functools.partial(block_kernel, sizes), out_shape=(half, h...  4.48 us
    pallas_call x1, Pallas kernels, local(): pl.pallas_call(functools.partial(slot_kernel, sizes), out_shape=tuple([sh...  4.11 us
  transfers between devices with their start and end apart: 17, of which 10 were waited for; matrix products, arithmetic and copies ran while one was open for 0% of the time, Pallas kernels for 11%

profile of v19, /device:TPU:0, one launch (start us, length us, event | category | flops | bytes accessed | tf_op | source)
XLA Modules:
  0.0 46.0 jit_solution(8684784493810787386)
XLA Ops:
  0.6 0.9 %pack.1.refs_3_ = bf16[144,128]{1,0:T(8,128)(2,1)S(1)} custom-call(f32[64,128]{1,0:T(8,128)} %bitcast.13, f32[64,128]{1,0:T(8,128)} %bitcast.15, f32[32,64]{1,0:T(8,128)} %refs_10_.1), custom_call_target="tpu_custom_call" | custom-call | tf_op jit(solution)/shard_map/pack/pallas_call | solution.py:399
  1.5 3.1 %collective-permute-start = (bf16[144,128]{1,0:T(8,128)(2,1)S(1)}, bf16[144,128]{1,0:T(8,128)(2,1)S(1)}, u32[]{:S(2)}, u32[]{:S(2)}) collective-permute-start(bf16[144,128]{1,0:T(8,128)(2,1)S(1)} %pack.1.refs_3_), channel_id=1, source_target_pairs={{0,1},{1,0},{2,3},{3,2},{4,5},{5,4},{6,7},{7,6},{8,9},{9,8},{10,11... | collective-permute-start | bytes 110600 | tf_op jit(solution)/shard_map/ppermute | solution.py:370
  4.6 2.5 %collective-permute-start.1 = (bf16[144,128]{1,0:T(8,128)(2,1)S(1)}, bf16[144,128]{1,0:T(8,128)(2,1)S(1)}, u32[]{:S(2)}, u32[]{:S(2)}) collective-permute-start(bf16[144,128]{1,0:T(8,128)(2,1)S(1)} %pack.1.refs_3_), channel_id=1, source_target_pairs={{0,3},{1,2},{2,1},{3,0},{4,7},{5,6},{6,5},{7,4},{8,11},{9,10},{10,... | collective-permute-start | bytes 110600 | tf_op jit(solution)/shard_map/ppermute | solution.py:370
  7.1 0.1 collective-permute-start.2
  7.2 3.7 %collective-permute-done.1.refs_1_ = bf16[144,128]{1,0:T(8,128)(2,1)S(1)} collective-permute-done((bf16[144,128]{1,0:T(8,128)(2,1)S(1)}, bf16[144,128]{1,0:T(8,128)(2,1)S(1)}, u32[]{:S(2)}, u32[]{:S(2)}) %collective-permute-start.1) | collective-permute-done | bytes 36896 | tf_op jit(solution)/shard_map/ppermute | solution.py:370
  10.9 1.5 %collective-permute-done.2.refs_2_ = bf16[144,128]{1,0:T(8,128)(2,1)S(1)} collective-permute-done((bf16[144,128]{1,0:T(8,128)(2,1)S(1)}, bf16[144,128]{1,0:T(8,128)(2,1)S(1)}, u32[]{:S(2)}, u32[]{:S(2)}) %collective-permute-start.2) | collective-permute-done | bytes 36896 | tf_op jit(solution)/shard_map/ppermute | solution.py:370
  12.3 0.1 table.1.refs_3_.refs_0_
  12.5 2.5 %collective-permute-start.6 = (bf16[576,128]{1,0:T(8,128)(2,1)S(1)}, bf16[576,128]{1,0:T(8,128)(2,1)S(1)}, u32[]{:S(2)}, u32[]{:S(2)}) collective-permute-start(bf16[576,128]{1,0:T(8,128)(2,1)S(1)} %table.1.refs_3_.refs_0_), channel_id=1, source_target_pairs={{0,24},{4,28},{8,16},{12,20},{16,8},{20,12},{24,0},{28,4},{1,25},{... | collective-permute-start | bytes 442376 | tf_op jit(solution)/shard_map/ppermute | solution.py:370
  14.9 0.5 %collective-permute-start.8 = (bf16[576,128]{1,0:T(8,128)(2,1)S(1)}, bf16[576,128]{1,0:T(8,128)(2,1)S(1)}, u32[]{:S(2)}, u32[]{:S(2)}) collective-permute-start(bf16[576,128]{1,0:T(8,128)(2,1)S(1)} %table.1.refs_3_.refs_0_), channel_id=1, source_target_pairs={{0,16},{4,20},{8,24},{12,28},{16,0},{20,4},{24,8},{28,12},{1,17},{... | collective-permute-start | bytes 442376 | tf_op jit(solution)/shard_map/ppermute | solution.py:370
  15.5 0.5 %collective-permute-start.3 = (bf16[576,128]{1,0:T(8,128)(2,1)S(1)}, bf16[576,128]{1,0:T(8,128)(2,1)S(1)}, u32[]{:S(2)}, u32[]{:S(2)}) collective-permute-start(bf16[576,128]{1,0:T(8,128)(2,1)S(1)} %table.1.refs_3_.refs_0_), channel_id=1, source_target_pairs={{0,8},{4,12},{8,0},{12,4},{16,24},{20,28},{24,16},{28,20},{1,9},{5... | collective-permute-start | bytes 442376 | tf_op jit(solution)/shard_map/ppermute | solution.py:370
  16.0 4.1 %slots.1 = (bf16[1024,256]{1,0:T(8,128)(2,1)S(1)}, bf16[1024,256]{1,0:T(8,128)(2,1)S(1)}, bf16[256,32]{1,0:T(8,128)(2,1)S(1)}, bf16[384,256]{1,0:T(8,128)(2,1)S(...) custom-call(s32[1]{0:T(128)} %bitcast.2.me_ref, ...), custom_call_target="tpu_custom_call" | custom-call | tf_op jit(solution)/shard_map/slots/pallas_call | solution.py:419
  20.2 0.6 %collective-permute-start.7 = (bf16[576,128]{1,0:T(8,128)(2,1)S(1)}, bf16[576,128]{1,0:T(8,128)(2,1)S(1)}, u32[]{:S(2)}, u32[]{:S(2)}) collective-permute-start(bf16[576,128]{1,0:T(8,128)(2,1)S(1)} %hold.4.refs_3_), channel_id=1, source_target_pairs={{0,4},{4,0},{8,12},{12,8},{16,20},{20,16},{24,28},{28,24},{1,5},{5... | collective-permute-start | bytes 442376 | tf_op jit(solution)/shard_map/ppermute | solution.py:370
  20.9 0.1 collective-permute-start.9
  21.0 0.5 %collective-permute-start.4 = (bf16[576,128]{1,0:T(8,128)(2,1)S(1)}, bf16[576,128]{1,0:T(8,128)(2,1)S(1)}, u32[]{:S(2)}, u32[]{:S(2)}) collective-permute-start(bf16[576,128]{1,0:T(8,128)(2,1)S(1)} %hold.3.refs_2_), channel_id=1, source_target_pairs={{0,4},{4,0},{8,12},{12,8},{16,20},{20,16},{24,28},{28,24},{1,5},{5... | collective-permute-start | bytes 442376 | tf_op jit(solution)/shard_map/ppermute | solution.py:370
  21.6 0.3 collective-permute-done.7.refs_4_
  21.8 0.5 %collective-permute-done.9.refs_6_ = bf16[576,128]{1,0:T(8,128)(2,1)S(1)} collective-permute-done((bf16[576,128]{1,0:T(8,128)(2,1)S(1)}, bf16[576,128]{1,0:T(8,128)(2,1)S(1)}, u32[]{:S(2)}, u32[]{:S(2)}) %collective-permute-start.9) | collective-permute-done | bytes 147488 | tf_op jit(solution)/shard_map/ppermute | solution.py:370
  22.3 0.4 early_picks.1
  22.8 4.5 %block_gradients.1 = (bf16[448,256]{1,0:T(8,128)(2,1)S(1)}, bf16[448,256]{1,0:T(8,128)(2,1)S(1)}) custom-call(bf16[576,128]{1,0:T(8,128)(2,1)S(1)} %collective-permute-done.4.refs_0_, f32[256,256]{1,0:T(8,128)S(1)} %get-tuple-element.45.refs_1_, f32[256,256]{1,0:T(8,128)S(1)} %get-tuple-element.46.refs_2_, f32[32,256]{1,0:T(8,128)S(1)} %get-tuple-element.47.refs_3_, ...), custom_call_target="tpu_custom_call" | custom-call | tf_op jit(solution)/shard_map/block_gradients/pallas_call | solution.py:465
  27.3 0.2 collective-permute-start.10
  27.5 1.3 %collective-permute-done.10.crossed_ref = bf16[448,256]{1,0:T(8,128)(2,1)S(1)} collective-permute-done((bf16[448,256]{1,0:T(8,128)(2,1)S(1)}, bf16[448,256]{1,0:T(8,128)(2,1)S(1)}, u32[]{:S(2)}, u32[]{:S(2)}) %collective-permute-start.10) | collective-permute-done | bytes 229408 | tf_op jit(solution)/shard_map/ppermute | solution.py:370
  28.9 2.4 %collective-permute-start.11 = (bf16[224,256]{1,0:T(8,128)(2,1)S(1)}, bf16[224,256]{1,0:T(8,128)(2,1)S(1)}, u32[]{:S(2)}, u32[]{:S(2)}) collective-permute-start(bf16[224,256]{1,0:T(8,128)(2,1)S(1)} %get-tuple-element.54), channel_id=1, source_target_pairs={{0,24},{4,28},{8,16},{12,20},{16,8},{20,12},{24,0},{28,4},{1,25},{... | collective-permute-start | bytes 344072 | tf_op jit(solution)/shard_map/ppermute | solution.py:370
  31.3 0.5 %collective-permute-start.12 = (bf16[224,256]{1,0:T(8,128)(2,1)S(1)}, bf16[224,256]{1,0:T(8,128)(2,1)S(1)}, u32[]{:S(2)}, u32[]{:S(2)}) collective-permute-start(bf16[224,256]{1,0:T(8,128)(2,1)S(1)} %get-tuple-element.58), channel_id=1, source_target_pairs={{0,16},{4,20},{8,24},{12,28},{16,0},{20,4},{24,8},{28,12},{1,17},{... | collective-permute-start | bytes 344072 | tf_op jit(solution)/shard_map/ppermute | solution.py:370
  31.8 0.6 %collective-permute-start.13 = (bf16[224,256]{1,0:T(8,128)(2,1)S(1)}, bf16[224,256]{1,0:T(8,128)(2,1)S(1)}, u32[]{:S(2)}, u32[]{:S(2)}) collective-permute-start(bf16[224,256]{1,0:T(8,128)(2,1)S(1)} %get-tuple-element.59), channel_id=1, source_target_pairs={{0,8},{4,12},{8,0},{12,4},{16,24},{20,28},{24,16},{28,20},{1,9},{5... | collective-permute-start | bytes 344072 | tf_op jit(solution)/shard_map/ppermute | solution.py:370
  32.4 2.7 %collective-permute-done.11.arrived_ref = bf16[224,256]{1,0:T(8,128)(2,1)S(1)} collective-permute-done((bf16[224,256]{1,0:T(8,128)(2,1)S(1)}, bf16[224,256]{1,0:T(8,128)(2,1)S(1)}, u32[]{:S(2)}, u32[]{:S(2)}) %collective-permute-start.11) | collective-permute-done | bytes 114720 | tf_op jit(solution)/shard_map/ppermute | solution.py:370
  35.1 0.3 early_sums.1
  35.4 2.0 %collective-permute-done.12.refs_3_ = bf16[224,256]{1,0:T(8,128)(2,1)S(1)} collective-permute-done((bf16[224,256]{1,0:T(8,128)(2,1)S(1)}, bf16[224,256]{1,0:T(8,128)(2,1)S(1)}, u32[]{:S(2)}, u32[]{:S(2)}) %collective-permute-start.12) | collective-permute-done | bytes 114720 | tf_op jit(solution)/shard_map/ppermute | solution.py:370
  37.5 0.4 row_sums.1
  37.9 2.4 %collective-permute-start.14 = (bf16[144,128]{1,0:T(8,128)(2,1)S(1)}, bf16[144,128]{1,0:T(8,128)(2,1)S(1)}, u32[]{:S(2)}, u32[]{:S(2)}) collective-permute-start(bf16[144,128]{1,0:T(8,128)(2,1)S(1)} %get-tuple-element.61), channel_id=1, source_target_pairs={{0,3},{1,2},{2,1},{3,0},{4,7},{5,6},{6,5},{7,4},{8,11},{9,10},{10,... | collective-permute-start | bytes 110600 | tf_op jit(solution)/shard_map/ppermute | solution.py:370
  40.3 2.1 %collective-permute-start.16 = (bf16[144,128]{1,0:T(8,128)(2,1)S(1)}, bf16[144,128]{1,0:T(8,128)(2,1)S(1)}, u32[]{:S(2)}, u32[]{:S(2)}) collective-permute-start(bf16[144,128]{1,0:T(8,128)(2,1)S(1)} %get-tuple-element.63), channel_id=1, source_target_pairs={{0,1},{1,0},{2,3},{3,2},{4,5},{5,4},{6,7},{7,6},{8,9},{9,8},{10,11... | collective-permute-start | bytes 110600 | tf_op jit(solution)/shard_map/ppermute | solution.py:370
  42.4 1.4 %collective-permute-done.14.refs_1_ = bf16[144,128]{1,0:T(8,128)(2,1)S(1)} collective-permute-done((bf16[144,128]{1,0:T(8,128)(2,1)S(1)}, bf16[144,128]{1,0:T(8,128)(2,1)S(1)}, u32[]{:S(2)}, u32[]{:S(2)}) %collective-permute-start.14) | collective-permute-done | bytes 36896 | tf_op jit(solution)/shard_map/ppermute | solution.py:370
  43.8 1.4 %collective-permute-done.15.refs_2_ = bf16[144,128]{1,0:T(8,128)(2,1)S(1)} collective-permute-done((bf16[144,128]{1,0:T(8,128)(2,1)S(1)}, bf16[144,128]{1,0:T(8,128)(2,1)S(1)}, u32[]{:S(2)}, u32[]{:S(2)}) %collective-permute-start.15) | collective-permute-done | bytes 36896 | tf_op jit(solution)/shard_map/ppermute | solution.py:370
  45.3 0.7 %adam.1 = (f32[64,128]{1,0:T(8,128)}, f32[64,128]{1,0:T(8,128)}, f32[64,128]{1,0:T(8,128)}, f32[64,128]{1,0:T(8,128)}, f32[64,128]{1,0:T(8,128)}, /*index=5*/f32...) custom-call(bf16[144,128]{1,0:T(8,128)(2,1)S(1)} %get-tuple-element.60.refs_0_, ...), custom_call_target="tpu_custom_call" | custom-call | tf_op jit(solution)/shard_map/adam/pallas_call | solution.py:526
  (32 shorter events, 0.2 us)
Async XLA Ops:
  1.5 5.7 %collective-permute-start = (bf16[144,128]{1,0:T(8,128)(2,1)S(1)}, bf16[144,128]{1,0:T(8,128)(2,1)S(1)}, u32[]{:S(2)}, u32[]{:S(2)}) collective-permute-start(bf16[144,128]{1,0:T(8,128)(2,1)S(1)} %pack.1.refs_3_), channel_id=1, source_target_pairs={{0,1},{1,0},{2,3},{3,2},{4,5},{5,4},{6,7},{7,6},{8,9},{9,8},{10,11... | collective-permute-start | bytes 110600 | tf_op jit(solution)/shard_map/ppermute | solution.py:370
  4.6 6.2 %collective-permute-start.1 = (bf16[144,128]{1,0:T(8,128)(2,1)S(1)}, bf16[144,128]{1,0:T(8,128)(2,1)S(1)}, u32[]{:S(2)}, u32[]{:S(2)}) collective-permute-start(bf16[144,128]{1,0:T(8,128)(2,1)S(1)} %pack.1.refs_3_), channel_id=1, source_target_pairs={{0,3},{1,2},{2,1},{3,0},{4,7},{5,6},{6,5},{7,4},{8,11},{9,10},{10,... | collective-permute-start | bytes 110600 | tf_op jit(solution)/shard_map/ppermute | solution.py:370
  7.1 5.3 %collective-permute-start.2 = (bf16[144,128]{1,0:T(8,128)(2,1)S(1)}, bf16[144,128]{1,0:T(8,128)(2,1)S(1)}, u32[]{:S(2)}, u32[]{:S(2)}) collective-permute-start(bf16[144,128]{1,0:T(8,128)(2,1)S(1)} %pack.1.refs_3_), channel_id=1, source_target_pairs={{0,2},{1,3},{2,0},{3,1},{4,6},{5,7},{6,4},{7,5},{8,10},{9,11},{10,... | collective-permute-start | bytes 110600 | tf_op jit(solution)/shard_map/ppermute | solution.py:370
  12.5 7.7 %collective-permute-start.6 = (bf16[576,128]{1,0:T(8,128)(2,1)S(1)}, bf16[576,128]{1,0:T(8,128)(2,1)S(1)}, u32[]{:S(2)}, u32[]{:S(2)}) collective-permute-start(bf16[576,128]{1,0:T(8,128)(2,1)S(1)} %table.1.refs_3_.refs_0_), channel_id=1, source_target_pairs={{0,24},{4,28},{8,16},{12,20},{16,8},{20,12},{24,0},{28,4},{1,25},{... | collective-permute-start | bytes 442376 | tf_op jit(solution)/shard_map/ppermute | solution.py:370
  14.9 5.9 %collective-permute-start.8 = (bf16[576,128]{1,0:T(8,128)(2,1)S(1)}, bf16[576,128]{1,0:T(8,128)(2,1)S(1)}, u32[]{:S(2)}, u32[]{:S(2)}) collective-permute-start(bf16[576,128]{1,0:T(8,128)(2,1)S(1)} %table.1.refs_3_.refs_0_), channel_id=1, source_target_pairs={{0,16},{4,20},{8,24},{12,28},{16,0},{20,4},{24,8},{28,12},{1,17},{... | collective-permute-start | bytes 442376 | tf_op jit(solution)/shard_map/ppermute | solution.py:370
  15.5 5.5 %collective-permute-start.3 = (bf16[576,128]{1,0:T(8,128)(2,1)S(1)}, bf16[576,128]{1,0:T(8,128)(2,1)S(1)}, u32[]{:S(2)}, u32[]{:S(2)}) collective-permute-start(bf16[576,128]{1,0:T(8,128)(2,1)S(1)} %table.1.refs_3_.refs_0_), channel_id=1, source_target_pairs={{0,8},{4,12},{8,0},{12,4},{16,24},{20,28},{24,16},{28,20},{1,9},{5... | collective-permute-start | bytes 442376 | tf_op jit(solution)/shard_map/ppermute | solution.py:370
  16.0 5.6 %collective-permute-start.5 = (bf16[576,128]{1,0:T(8,128)(2,1)S(1)}, bf16[576,128]{1,0:T(8,128)(2,1)S(1)}, u32[]{:S(2)}, u32[]{:S(2)}) collective-permute-start(bf16[576,128]{1,0:T(8,128)(2,1)S(1)} %table.1.refs_3_.refs_0_), channel_id=1, source_target_pairs={{0,4},{4,0},{8,12},{12,8},{16,20},{20,16},{24,28},{28,24},{1,5},{5... | collective-permute-start | bytes 442376 | tf_op jit(solution)/shard_map/ppermute | solution.py:370
  20.1 25.1 %copy-start = (f32[128,64]{0,1:T(8,128)S(1)}, f32[128,64]{0,1:T(8,128)}, u32[]{:S(2)}) copy-start(f32[128,64]{0,1:T(8,128)} %param.17) | copy-start | bytes 98308
  20.1 25.1 %copy-start.1 = (f32[128,64]{0,1:T(8,128)S(1)}, f32[128,64]{0,1:T(8,128)}, u32[]{:S(2)}) copy-start(f32[128,64]{0,1:T(8,128)} %param.20) | copy-start | bytes 98308
  20.1 25.1 %copy-start.2 = (f32[32,64]{1,0:T(8,128)S(1)}, f32[32,64]{1,0:T(8,128)}, u32[]{:S(2)}) copy-start(f32[32,64]{1,0:T(8,128)} %refs_10_.1) | copy-start | bytes 24580
  20.1 25.0 %copy-start.3 = (f32[128,64]{0,1:T(8,128)S(1)}, f32[128,64]{0,1:T(8,128)}, u32[]{:S(2)}) copy-start(f32[128,64]{0,1:T(8,128)} %param.18) | copy-start | bytes 98308
  20.2 25.0 %copy-start.4 = (f32[128,64]{0,1:T(8,128)S(1)}, f32[128,64]{0,1:T(8,128)}, u32[]{:S(2)}) copy-start(f32[128,64]{0,1:T(8,128)} %param.19) | copy-start | bytes 98308
  20.2 25.0 %copy-start.5 = (f32[128,64]{0,1:T(8,128)S(1)}, f32[128,64]{0,1:T(8,128)}, u32[]{:S(2)}) copy-start(f32[128,64]{0,1:T(8,128)} %param.21) | copy-start | bytes 98308
  20.2 25.0 %copy-start.6 = (f32[128,64]{0,1:T(8,128)S(1)}, f32[128,64]{0,1:T(8,128)}, u32[]{:S(2)}) copy-start(f32[128,64]{0,1:T(8,128)} %param.22) | copy-start | bytes 98308
  20.2 25.0 %copy-start.7 = (f32[32,64]{1,0:T(8,128)S(1)}, f32[32,64]{1,0:T(8,128)}, u32[]{:S(2)}) copy-start(f32[32,64]{1,0:T(8,128)} %refs_11_.1) | copy-start | bytes 24580
  20.2 25.0 %copy-start.8 = (f32[32,64]{1,0:T(8,128)S(1)}, f32[32,64]{1,0:T(8,128)}, u32[]{:S(2)}) copy-start(f32[32,64]{1,0:T(8,128)} %refs_12_.1) | copy-start | bytes 24580
  20.2 1.6 %collective-permute-start.7 = (bf16[576,128]{1,0:T(8,128)(2,1)S(1)}, bf16[576,128]{1,0:T(8,128)(2,1)S(1)}, u32[]{:S(2)}, u32[]{:S(2)}) collective-permute-start(bf16[576,128]{1,0:T(8,128)(2,1)S(1)} %hold.4.refs_3_), channel_id=1, source_target_pairs={{0,4},{4,0},{8,12},{12,8},{16,20},{20,16},{24,28},{28,24},{1,5},{5... | collective-permute-start | bytes 442376 | tf_op jit(solution)/shard_map/ppermute | solution.py:370
  20.9 1.4 %collective-permute-start.9 = (bf16[576,128]{1,0:T(8,128)(2,1)S(1)}, bf16[576,128]{1,0:T(8,128)(2,1)S(1)}, u32[]{:S(2)}, u32[]{:S(2)}) collective-permute-start(bf16[576,128]{1,0:T(8,128)(2,1)S(1)} %hold.5.refs_5_), channel_id=1, source_target_pairs={{0,4},{4,0},{8,12},{12,8},{16,20},{20,16},{24,28},{28,24},{1,5},{5... | collective-permute-start | bytes 442376 | tf_op jit(solution)/shard_map/ppermute | solution.py:370
  21.0 1.8 %collective-permute-start.4 = (bf16[576,128]{1,0:T(8,128)(2,1)S(1)}, bf16[576,128]{1,0:T(8,128)(2,1)S(1)}, u32[]{:S(2)}, u32[]{:S(2)}) collective-permute-start(bf16[576,128]{1,0:T(8,128)(2,1)S(1)} %hold.3.refs_2_), channel_id=1, source_target_pairs={{0,4},{4,0},{8,12},{12,8},{16,20},{20,16},{24,28},{28,24},{1,5},{5... | collective-permute-start | bytes 442376 | tf_op jit(solution)/shard_map/ppermute | solution.py:370
  27.3 1.6 %collective-permute-start.10 = (bf16[448,256]{1,0:T(8,128)(2,1)S(1)}, bf16[448,256]{1,0:T(8,128)(2,1)S(1)}, u32[]{:S(2)}, u32[]{:S(2)}) collective-permute-start(bf16[448,256]{1,0:T(8,128)(2,1)S(1)} %get-tuple-element.53), channel_id=1, source_target_pairs={{0,4},{4,0},{8,12},{12,8},{16,20},{20,16},{24,28},{28,24},{1,5},{5... | collective-permute-start | bytes 688136 | tf_op jit(solution)/shard_map/ppermute | solution.py:370
  28.9 6.3 %collective-permute-start.11 = (bf16[224,256]{1,0:T(8,128)(2,1)S(1)}, bf16[224,256]{1,0:T(8,128)(2,1)S(1)}, u32[]{:S(2)}, u32[]{:S(2)}) collective-permute-start(bf16[224,256]{1,0:T(8,128)(2,1)S(1)} %get-tuple-element.54), channel_id=1, source_target_pairs={{0,24},{4,28},{8,16},{12,20},{16,8},{20,12},{24,0},{28,4},{1,25},{... | collective-permute-start | bytes 344072 | tf_op jit(solution)/shard_map/ppermute | solution.py:370
  31.3 6.2 %collective-permute-start.12 = (bf16[224,256]{1,0:T(8,128)(2,1)S(1)}, bf16[224,256]{1,0:T(8,128)(2,1)S(1)}, u32[]{:S(2)}, u32[]{:S(2)}) collective-permute-start(bf16[224,256]{1,0:T(8,128)(2,1)S(1)} %get-tuple-element.58), channel_id=1, source_target_pairs={{0,16},{4,20},{8,24},{12,28},{16,0},{20,4},{24,8},{28,12},{1,17},{... | collective-permute-start | bytes 344072 | tf_op jit(solution)/shard_map/ppermute | solution.py:370
  31.8 5.7 %collective-permute-start.13 = (bf16[224,256]{1,0:T(8,128)(2,1)S(1)}, bf16[224,256]{1,0:T(8,128)(2,1)S(1)}, u32[]{:S(2)}, u32[]{:S(2)}) collective-permute-start(bf16[224,256]{1,0:T(8,128)(2,1)S(1)} %get-tuple-element.59), channel_id=1, source_target_pairs={{0,8},{4,12},{8,0},{12,4},{16,24},{20,28},{24,16},{28,20},{1,9},{5... | collective-permute-start | bytes 344072 | tf_op jit(solution)/shard_map/ppermute | solution.py:370
  37.9 5.8 %collective-permute-start.14 = (bf16[144,128]{1,0:T(8,128)(2,1)S(1)}, bf16[144,128]{1,0:T(8,128)(2,1)S(1)}, u32[]{:S(2)}, u32[]{:S(2)}) collective-permute-start(bf16[144,128]{1,0:T(8,128)(2,1)S(1)} %get-tuple-element.61), channel_id=1, source_target_pairs={{0,3},{1,2},{2,1},{3,0},{4,7},{5,6},{6,5},{7,4},{8,11},{9,10},{10,... | collective-permute-start | bytes 110600 | tf_op jit(solution)/shard_map/ppermute | solution.py:370
  40.3 4.9 %collective-permute-start.15 = (bf16[144,128]{1,0:T(8,128)(2,1)S(1)}, bf16[144,128]{1,0:T(8,128)(2,1)S(1)}, u32[]{:S(2)}, u32[]{:S(2)}) collective-permute-start(bf16[144,128]{1,0:T(8,128)(2,1)S(1)} %get-tuple-element.62), channel_id=1, source_target_pairs={{0,2},{1,3},{2,0},{3,1},{4,6},{5,7},{6,4},{7,5},{8,10},{9,11},{10,... | collective-permute-start | bytes 110600 | tf_op jit(solution)/shard_map/ppermute | solution.py:370
  40.3 4.9 %collective-permute-start.16 = (bf16[144,128]{1,0:T(8,128)(2,1)S(1)}, bf16[144,128]{1,0:T(8,128)(2,1)S(1)}, u32[]{:S(2)}, u32[]{:S(2)}) collective-permute-start(bf16[144,128]{1,0:T(8,128)(2,1)S(1)} %get-tuple-element.63), channel_id=1, source_target_pairs={{0,1},{1,0},{2,3},{3,2},{4,5},{5,4},{6,7},{7,6},{8,9},{9,8},{10,11... | collective-permute-start | bytes 110600 | tf_op jit(solution)/shard_map/ppermute | solution.py:370
